TPU v7x, 32 devices: a whole 2x2x4 slice. The times are simulated.
32 devices in a mesh: section: 2 (over x), ctx: 16 (over z, y, core).
Axes of the slice: x: 2, y: 2, z: 4, core: 2. Of those that a mesh axis runs over, the one named last changes fastest.
Arguments:
- inputs: bfloat16 [2048, 2048], P('ctx', 'section'), may hold values from -8 to 8
- out_grads: bfloat16 [2048, 2048], P('ctx', 'section'), may hold values from -6 to 6
- conv_weight: float32 [3, 4, 2048], P(None, None, 'section'), may hold values from -3 to 3
- log_decay: float32 [2048, 2048], P('ctx', 'section'), may hold values from -1 to 0
- beta: float32 [2048, 16], P('ctx', 'section'), may hold values from 0 to 1
Outputs:
- stream_out: bfloat16 [2048, 2048], P('ctx', 'section')
- input_grad: bfloat16 [2048, 2048], P('ctx', 'section')
All inputs are finite; a program needn't handle non-finite values.
Results may differ from a plain program's by a relative error of at most 0.001.
Values sent between devices are 32-bit elements; how exact they have to be, the bound alone decides.
No kernel may reach another device: no remote copies, remote signals or barrier semaphores. Data moves between devices by JAX's collectives and lax.ppermute only.
A program may use at most 128 MiB of HBM per device.

v0:
```python
import jax
import jax.numpy as jnp
from jax import lax
from jax.sharding import PartitionSpec as P

HEAD_DIM = 128


epsilon = 1e-06
norm_eps = 1e-05
highest = lax.Precision.HIGHEST


def passed_along(block, axis, distance):
    devices = range(lax.axis_size(axis))
    route = [(i - distance, i) for i in devices if i - distance in devices]
    return lax.ppermute(block, axis, route)


def entering(part, axis, combine, identity, reverse):
    count = lax.axis_size(axis)
    place = lax.axis_index(axis)
    ahead = count - 1 - place if reverse else place
    gathered = jax.tree.map(lambda a: lax.all_gather(a, axis), part)
    state = jax.tree.map(lambda a, e: jnp.zeros_like(a) + jnp.asarray(e, a.dtype), part, identity)

    def one(hop, state):
        source = count - 1 - hop if reverse else hop
        return combine(
            state, jax.tree.map(lambda a: lax.dynamic_index_in_dim(a, source, 0, False), gathered)
        )

    return lax.fori_loop(0, ahead, one, state)


def unit_rows(mixed):
    act = jax.nn.silu(mixed).reshape(mixed.shape[0], -1, HEAD_DIM)
    return act / jnp.sqrt(jnp.sum(act * act, axis=-1, keepdims=True) + epsilon)


def features(padded, kern):
    taps_count = kern.shape[1]
    length = padded.shape[0] - taps_count + 1
    mixes = [
        sum((kern[j, i] * padded[i : i + length] for i in range(taps_count))) for j in range(3)
    ]
    queries = unit_rows(mixes[0])
    keys = unit_rows(mixes[1])
    values = jax.nn.silu(mixes[2]).reshape(length, -1, HEAD_DIM)
    return (queries, keys, values)


def solve_block(keys, values, cumulative, rates):
    length = keys.shape[0]
    middle = cumulative[length // 2]
    key_fwd = keys * jnp.exp(cumulative - middle)
    key_back = keys * jnp.exp(middle - cumulative)
    products = jnp.einsum("thc,shc->hts", key_fwd, key_back, precision=highest)
    strict_mask = jnp.tril(jnp.ones((length, length), jnp.float32), -1)
    rate_col = jnp.swapaxes(rates, 0, 1)[:, :, None]
    system = jnp.eye(length, dtype=jnp.float32) + rate_col * products * strict_mask
    rhs_keys = rate_col * jnp.swapaxes(keys * jnp.exp(cumulative), 0, 1)
    rhs_values = rate_col * jnp.swapaxes(values, 0, 1)
    solved = lax.linalg.triangular_solve(
        system,
        jnp.concatenate([rhs_keys, rhs_values], axis=-1),
        left_side=True,
        lower=True,
        unit_diagonal=True,
    )
    return (solved[..., :HEAD_DIM], solved[..., HEAD_DIM:])


def transition(keys, cumulative, w_rows, u_rows):
    final_decay = cumulative[-1]
    key_end = keys * jnp.exp(final_decay - cumulative)
    retained = jnp.exp(final_decay)[:, :, None] * jnp.eye(HEAD_DIM, dtype=jnp.float32)
    transit = retained - jnp.einsum("thd,hte->hde", key_end, w_rows, precision=highest)
    inject = jnp.einsum("thd,hte->hde", key_end, u_rows, precision=highest)
    return (transit, inject)


def block_out(queries, keys, cumulative, w_rows, u_rows, start):
    length = queries.shape[0]
    middle = cumulative[length // 2]
    query_fwd = queries * jnp.exp(cumulative - middle)
    key_back = keys * jnp.exp(middle - cumulative)
    full_mask = jnp.tril(jnp.ones((length, length), jnp.float32))
    scores = jnp.einsum("thc,shc->hts", query_fwd, key_back, precision=highest) * full_mask
    fresh = u_rows - jnp.einsum("htd,hde->hte", w_rows, start, precision=highest)
    output = jnp.einsum("thd,hde->the", queries * jnp.exp(cumulative), start, precision=highest)
    output = output + jnp.einsum("hts,hse->the", scores, fresh, precision=highest)
    return output.reshape(length, -1)


def compose(earlier, later):
    first_map, first_add = earlier
    second_map, second_add = later
    joined_map = jnp.einsum("hab,hbc->hac", second_map, first_map, precision=highest)
    joined_add = jnp.einsum("hab,hbc->hac", second_map, first_add, precision=highest) + second_add
    return (joined_map, joined_add)


def unit_pair(elements):
    return (
        jnp.broadcast_to(jnp.eye(HEAD_DIM, dtype=jnp.float32), elements[0].shape),
        jnp.zeros_like(elements[1]),
    )


def pass_rim(piece, offset):
    return passed_along(piece, "ctx", offset)


def section_sum(values):
    return lax.psum(values, "section")


def shards(inputs, out_grads, conv_weight, log_decay, beta):
    length, channels = inputs.shape
    tail = conv_weight.shape[1] - 1
    width_all = channels * lax.axis_size("section")
    cumulative = jnp.cumsum(log_decay.reshape(length, -1, HEAD_DIM), axis=0)
    stream = inputs.astype(jnp.float32)
    scale = 1.0 / jnp.sqrt(section_sum(jnp.sum(stream * stream, axis=1)) / width_all + norm_eps)
    normed = stream * scale[:, None]
    rim = pass_rim(normed[length - tail :], 1)

    def front(stream_part, rim_part):
        return features(jnp.concatenate([rim_part, stream_part], axis=0), conv_weight)

    queries, keys, values = front(normed, rim)
    w_rows, u_rows = solve_block(keys, values, cumulative, beta)
    transit, inject = transition(keys, cumulative, w_rows, u_rows)
    start = entering((transit, inject), "ctx", compose, unit_pair((transit, inject)), False)[1]
    output = (stream + block_out(queries, keys, cumulative, w_rows, u_rows, start)).astype(
        jnp.bfloat16
    )
    _, pull_front = jax.vjp(front, normed, rim)
    _, pull_solve = jax.vjp(
        lambda key_x, value_x: solve_block(key_x, value_x, cumulative, beta), keys, values
    )
    _, pull_trans = jax.vjp(
        lambda key_x, w_x, u_x: transition(key_x, cumulative, w_x, u_x), keys, w_rows, u_rows
    )
    grad_out = out_grads.astype(jnp.float32)
    _, pull_out = jax.vjp(
        lambda q_x, k_x, w_x, u_x, s_x: block_out(q_x, k_x, cumulative, w_x, u_x, s_x),
        queries,
        keys,
        w_rows,
        u_rows,
        start,
    )
    grad_query, grad_key_out, grad_w_out, grad_u_out, grad_start = pull_out(grad_out)
    back_elements = (jnp.swapaxes(transit, 1, 2), grad_start)
    _, grad_end = entering(back_elements, "ctx", compose, unit_pair(back_elements), True)
    grad_transit = jnp.einsum("hde,hfe->hdf", grad_end, start, precision=highest)
    grad_key_trans, grad_w_trans, grad_u_trans = pull_trans((grad_transit, grad_end))
    grad_key_solve, grad_value = pull_solve((grad_w_out + grad_w_trans, grad_u_out + grad_u_trans))
    grad_normed, grad_rim = pull_front(
        (grad_query, grad_key_out + grad_key_trans + grad_key_solve, grad_value)
    )
    from_next = pass_rim(grad_rim, -1)
    grad_normed = jnp.concatenate(
        [grad_normed[: length - tail], grad_normed[length - tail :] + from_next], axis=0
    )
    inner = section_sum(jnp.sum(grad_normed * stream, axis=1))
    cubed = scale * scale * scale
    total = grad_out + grad_normed * scale[:, None] - stream * (cubed * inner / width_all)[:, None]
    return (output, total.astype(jnp.bfloat16))


def solution(mesh):
    in_specs = (
        P("ctx", "section"),
        P("ctx", "section"),
        P(None, None, "section"),
        P("ctx", "section"),
        P("ctx", "section"),
    )
    out_specs = (P("ctx", "section"), P("ctx", "section"))
    return jax.shard_map(shards, mesh=mesh, in_specs=in_specs, out_specs=out_specs, check_vma=False)
```

profile of v0, /device:TPU:1, one launch (start us, length us, event | category | flops | bytes accessed | tf_op | source)
XLA Modules:
  0.0 514.3 jit_solution(11965710267889819540)
XLA Ops:
  7.2 1.1 copy.76
  8.5 4.3 psum.14
  13.1 5.1 collective-permute-start
  19.6 1.1 copy.138
  20.7 23.3 %fusion.107 = f32[128,8,128]{2,1,0:T(8,128)S(1)} fusion(f32[128,8,128]{2,1,0:T(8,128)S(1)} %bitcast.183), kind=kOutput, calls=%fused_computation.188 | output fusion | flops 16646144 | bytes 1048576 | tf_op jit(solution)/shard_map/jit(cumsum)/reduce_window_sum | solution.py:123
  44.6 2.1 fusion.53
  47.0 4.1 multiply_reduce_fusion.2
  52.0 1.4 fusion.13
  53.5 78.6 %custom-call.9 = f32[8,1,128,128]{2,3,1,0:T(8,128)S(1)} custom-call(f32[8,1,128,128]{3,2,1,0:T(8,128)S(1)} %fusion.13), custom_call_target="InvertDiagBlocksLowerTriangular" | custom-call | tf_op jit(solution)/shard_map/triangular_solve/custom-call.1 | solution.py:64
  133.3 1.0 fusion.27
  134.4 1.8 fusion.61
  136.3 2.0 multiply_subtract_fusion
  138.4 2.1 bitcast_subtract_fusion
  140.4 2.0 copy.93
  142.5 1.8 copy.90
  144.3 2.1 copy.87
  146.4 1.3 multiply_divide_fusion
  147.7 63.7 %all-gather.11.cloned.1.call-done = f32[128,128,128]{2,1,0:T(8,128)} async-done(((f32[8,128,128]{2,1,0:T(8,128)}), f32[128,128,128]{2,1,0:T(8,128)}) %all-gather.11.cloned.1.call-update) | async-done | bytes 8388624 | tf_op jit(solution)/shard_map/all_gather | solution.py:24
  211.5 75.3 %all-gather.9.cloned.1.call-done = f32[128,128,128]{2,1,0:T(8,128)} async-done(((f32[8,128,128]{2,1,0:T(8,128)}), f32[128,128,128]{2,1,0:T(8,128)}) %all-gather.9.cloned.1.call-update) | async-done | bytes 8388624 | tf_op jit(solution)/shard_map/all_gather | solution.py:24
  286.8 2.1 while.26
  286.9 1.9 convolution_add_fusion.9
  290.4 1.6 fusion.25
  292.1 1.8 fusion.26
  293.9 2.8 multiply_reduce_fusion
  296.7 1.3 multiply_multiply_fusion
  298.0 2.5 convolution_multiply_fusion
  302.0 1.8 convolution_add_fusion.5
  303.8 2.4 add_add_fusion
  306.2 2.1 copy.114
  308.2 2.0 fusion.55
  310.2 3.1 fusion.90
  313.3 3.2 fusion.24
  316.5 45.7 %all-gather.13.cloned.1.call-done = f32[128,128,128]{2,1,0:T(8,128)} async-done(((f32[8,128,128]{2,1,0:T(8,128)}), f32[128,128,128]{2,1,0:T(8,128)}) %all-gather.13.cloned.1.call-update) | async-done | bytes 8388624 | tf_op jit(solution)/shard_map/all_gather | solution.py:24
  362.1 75.2 %all-gather.15.cloned.1.call-done = f32[128,128,128]{2,1,0:T(8,128)} async-done(((f32[8,128,128]{2,1,0:T(8,128)}), f32[128,128,128]{2,1,0:T(8,128)}) %all-gather.15.cloned.1.call-update) | async-done | bytes 8388624 | tf_op jit(solution)/shard_map/all_gather | solution.py:24
  437.4 27.1 %while.27 = (s32[]{:T(128)}, f32[8,128,128]{2,1,0:T(8,128)S(1)}, s32[]{:T(128)}, f32[16,8,128,128]{3,2,1,0:T(8,128)}, f32[16,8,128,128]{3,2,1,0:T(8,128)}, /*index=5*/s32[]{:T(128)}, s32[]{:T(128)}, s32[]{:T(128)}, s32[]{:T(128)}) while((s32[]{:T(128)}, f32[8,128,128]{2,1,0:T(8,128)S(1)}, s32[]{:T(128)}, f32[16,8,128,128]{3,2,1,0:T(8,128)}, ...), condition=%wide.region_8.10_spmd, body=%wide.region_7.9_spmd.sunk | while | flops 201457664 | bytes 3146899 | solution.py:33
  437.5 1.9 convolution_add_fusion.10
  439.4 1.8 convolution_add_fusion.10
  441.3 1.8 convolution_add_fusion.10
  443.2 1.8 convolution_add_fusion.10
  445.1 1.9 convolution_add_fusion.10
  447.1 1.9 convolution_add_fusion.10
  449.0 1.9 convolution_add_fusion.10
  450.9 1.8 convolution_add_fusion.10
  452.8 1.8 convolution_add_fusion.10
  454.7 1.9 convolution_add_fusion.10
  456.7 1.9 convolution_add_fusion.10
  458.6 1.9 convolution_add_fusion.10
  460.5 1.8 convolution_add_fusion.10
  462.4 1.8 convolution_add_fusion.10
  464.5 1.2 convolution_negate_fusion.1
  465.8 1.9 convolution_add_fusion.4
  467.7 1.2 fusion.59
  468.9 1.7 convolution_add_fusion.3
  470.7 1.1 fusion.31
  474.6 2.1 fusion.20
  476.7 2.1 copy.96
  478.7 2.3 fusion.8
  481.1 2.4 multiply_reduce_fusion.1
  484.1 1.8 broadcast_multiply_fusion
  488.0 2.5 pad_add_fusion
  490.5 4.1 collective-permute-start.1
  494.6 1.0 convolution_add_fusion.6
  495.9 5.4 %collective-permute-done.1 = f32[3,1024]{0,1:T(8,128)S(1)} collective-permute-done((f32[3,1024]{0,1:T(8,128)S(1)}, f32[3,1024]{0,1:T(8,128)S(1)}, u32[]{:S(2)}, u32[]{:S(2)}) %collective-permute-start.1) | collective-permute-done | bytes 12320 | tf_op jit(solution)/shard_map/ppermute | solution.py:17
  501.6 3.8 psum.15
  (176 shorter events, 16.0 us)
Async XLA Ops:
  7.2 44.8 %copy-start.22 = (f32[128,8]{0,1:T(8,128)S(1)}, f32[128,8]{0,1:T(8,128)}, u32[]{:S(2)}) copy-start(f32[128,8]{0,1:T(8,128)} %param.15) | copy-start | bytes 12292
  7.2 204.3 %all-gather.11.cloned.1.call-start = ((), (), s32[]{:S(2)}) async-start(), calls=%async_computation.1 | async-start | bytes 8912896 | tf_op jit(solution)/shard_map/all_gather | solution.py:24
  12.8 7.9 %copy-start.53 = (f32[128]{0:T(128)}, f32[128]{0:T(128)S(1)}, u32[]{:S(2)}) copy-start(f32[128]{0:T(128)S(1)} %psum.14) | copy-start | bytes 1540
  12.9 39.0 %copy-start.48 = (f32[128]{0:T(128)}, f32[128]{0:T(128)S(1)}, u32[]{:S(2)}) copy-start(f32[128]{0:T(128)S(1)} %add_rsqrt_fusion) | copy-start | bytes 1540
  13.1 31.5 %collective-permute-start = (f32[3,1024]{0,1:T(8,128)S(1)}, f32[3,1024]{0,1:T(8,128)S(1)}, u32[]{:S(2)}, u32[]{:S(2)}) collective-permute-start(f32[3,1024]{0,1:T(8,128)S(1)} %slice.132), channel_id=1, source_target_pairs={{0,1},{1,2},{2,3},{3,4},{4,5},{5,6},{6,7},{7,8},{8,9},{9,10},{10,1... | collective-permute-start | bytes 36872 | tf_op jit(solution)/shard_map/ppermute | solution.py:17
  18.3 33.5 %copy-start.20 = (pred[128,128]{1,0:T(8,128)(4,1)}, pred[128,128]{1,0:T(8,128)(4,1)S(1)}, u32[]{:S(2)}) copy-start(pred[128,128]{1,0:T(8,128)(4,1)S(1)} %iota_compare_fusion.1) | copy-start | bytes 49156
  19.5 31.6 %copy-start.23 = (f32[1,1,1024]{2,1,0:T(1,128)}, f32[1,1,1024]{2,1,0:T(1,128)S(1)}, u32[]{:S(2)}) copy-start(f32[1,1,1024]{2,1,0:T(1,128)S(1)} %get-tuple-element.202) | copy-start | bytes 12292
  19.5 32.4 %copy-start.25 = (f32[1,1,1024]{2,1,0:T(1,128)}, f32[1,1,1024]{2,1,0:T(1,128)S(1)}, u32[]{:S(2)}) copy-start(f32[1,1,1024]{2,1,0:T(1,128)S(1)} %get-tuple-element.199) | copy-start | bytes 12292
  19.5 32.4 %copy-start.27 = (f32[1,1,1024]{2,1,0:T(1,128)}, f32[1,1,1024]{2,1,0:T(1,128)S(1)}, u32[]{:S(2)}) copy-start(f32[1,1,1024]{2,1,0:T(1,128)S(1)} %get-tuple-element.204) | copy-start | bytes 12292
  19.5 32.4 %copy-start.29 = (f32[1,1,1024]{2,1,0:T(1,128)}, f32[1,1,1024]{2,1,0:T(1,128)S(1)}, u32[]{:S(2)}) copy-start(f32[1,1,1024]{2,1,0:T(1,128)S(1)} %get-tuple-element.205) | copy-start | bytes 12292
  19.5 32.4 %copy-start.31 = (f32[1,1,1024]{2,1,0:T(1,128)}, f32[1,1,1024]{2,1,0:T(1,128)S(1)}, u32[]{:S(2)}) copy-start(f32[1,1,1024]{2,1,0:T(1,128)S(1)} %get-tuple-element.206) | copy-start | bytes 12292
  19.5 32.4 %copy-start.33 = (f32[1,1,1024]{2,1,0:T(1,128)}, f32[1,1,1024]{2,1,0:T(1,128)S(1)}, u32[]{:S(2)}) copy-start(f32[1,1,1024]{2,1,0:T(1,128)S(1)} %get-tuple-element.197) | copy-start | bytes 12292
  19.5 32.4 %copy-start.35 = (f32[1,1,1024]{2,1,0:T(1,128)}, f32[1,1,1024]{2,1,0:T(1,128)S(1)}, u32[]{:S(2)}) copy-start(f32[1,1,1024]{2,1,0:T(1,128)S(1)} %get-tuple-element.198) | copy-start | bytes 12292
  19.5 32.4 %copy-start.37 = (f32[1,1,1024]{2,1,0:T(1,128)}, f32[1,1,1024]{2,1,0:T(1,128)S(1)}, u32[]{:S(2)}) copy-start(f32[1,1,1024]{2,1,0:T(1,128)S(1)} %get-tuple-element.208) | copy-start | bytes 12292
  19.5 32.4 %copy-start.43 = (f32[1,1,1024]{2,1,0:T(1,128)}, f32[1,1,1024]{2,1,0:T(1,128)S(1)}, u32[]{:S(2)}) copy-start(f32[1,1,1024]{2,1,0:T(1,128)S(1)} %get-tuple-element.203) | copy-start | bytes 12292
  19.6 32.4 %copy-start.45 = (f32[1,1,1024]{2,1,0:T(1,128)}, f32[1,1,1024]{2,1,0:T(1,128)S(1)}, u32[]{:S(2)}) copy-start(f32[1,1,1024]{2,1,0:T(1,128)S(1)} %get-tuple-element.207) | copy-start | bytes 12292
  44.6 7.4 %copy-start.51 = (f32[8,128]{1,0:T(8,128)}, f32[8,128]{1,0:T(8,128)S(1)}, u32[]{:S(2)}) copy-start(f32[8,128]{1,0:T(8,128)S(1)} %get-tuple-element.193) | copy-start | bytes 12292
  51.1 0.9 copy-start.41
  51.9 246.1 %copy-start = (f32[128,8,128]{2,0,1:T(8,128)}, f32[128,8,128]{2,0,1:T(8,128)S(1)}, u32[]{:S(2)}) copy-start(f32[128,8,128]{2,0,1:T(8,128)S(1)} %copy.77) | copy-start | bytes 1572868
  132.1 154.7 %copy-start.6 = (f32[8,1,128,128]{2,3,1,0:T(8,128)}, f32[8,1,128,128]{2,3,1,0:T(8,128)S(1)}, u32[]{:S(2)}) copy-start(f32[8,1,128,128]{2,3,1,0:T(8,128)S(1)} %custom-call.9) | copy-start | bytes 1572868
  136.2 150.6 %all-gather.9.cloned.1.call-start = ((), (), s32[]{:S(2)}) async-start(), calls=%async_computation | async-start | bytes 8912896 | tf_op jit(solution)/shard_map/all_gather | solution.py:24
  136.3 2.0 copy-start.39
  138.3 223.9 %all-gather.13.cloned.1.call-start = ((), (), s32[]{:S(2)}) async-start(), calls=%async_computation.2 | async-start | bytes 8912896 | tf_op jit(solution)/shard_map/all_gather | solution.py:24
  142.5 294.9 %all-gather.15.cloned.1.call-start = ((), (), s32[]{:S(2)}) async-start(), calls=%async_computation.3 | async-start | bytes 8912896 | tf_op jit(solution)/shard_map/all_gather | solution.py:24
  288.9 11.5 %copy-start.4 = (bf16[128,1024]{0,1:T(8,128)(2,1)S(1)}, bf16[128,1024]{0,1:T(8,128)(2,1)}, u32[]{:S(2)}) copy-start(bf16[128,1024]{0,1:T(8,128)(2,1)} %copy.90) | copy-start | bytes 786436
  289.0 12.2 %copy-start.12 = (f32[128,8,128]{2,0,1:T(8,128)S(1)}, f32[128,8,128]{2,0,1:T(8,128)}, u32[]{:S(2)}) copy-start(f32[128,8,128]{2,0,1:T(8,128)} %copy.87) | copy-start | bytes 1572868
  289.6 0.8 copy-start.8
  292.1 9.8 %copy-start.18 = (f32[8,128,128]{2,1,0:T(8,128)}, f32[8,128,128]{2,1,0:T(8,128)S(1)}, u32[]{:S(2)}) copy-start(f32[8,128,128]{2,1,0:T(8,128)S(1)} %fusion.25) | copy-start | bytes 1572868
  298.0 3.9 copy-start.47
  300.5 1.5 copy-start.13
  300.5 12.8 %copy-start.52 = (f32[8,128]{1,0:T(8,128)S(1)}, f32[8,128]{1,0:T(8,128)}, u32[]{:S(2)}) copy-start(f32[8,128]{1,0:T(8,128)} %copy-done.51) | copy-start | bytes 12292
  301.1 136.2 %copy-start.3 = (f32[8,128,128]{2,1,0:T(8,128)}, f32[8,128,128]{2,1,0:T(8,128)S(1)}, u32[]{:S(2)}) copy-start(f32[8,128,128]{2,1,0:T(8,128)S(1)} %fusion.108) | copy-start | bytes 1572868
  464.5 7.3 %copy-start.7 = (f32[8,1,128,128]{2,3,1,0:T(8,128)S(1)}, f32[8,1,128,128]{2,3,1,0:T(8,128)}, u32[]{:S(2)}) copy-start(f32[8,1,128,128]{2,3,1,0:T(8,128)} %copy-done.6) | copy-start | bytes 1572868
  464.5 8.3 %copy-start.21 = (pred[128,128]{1,0:T(8,128)(4,1)S(1)}, pred[128,128]{1,0:T(8,128)(4,1)}, u32[]{:S(2)}) copy-start(pred[128,128]{1,0:T(8,128)(4,1)} %copy-done.20) | copy-start | bytes 49156
  464.5 10.1 %copy-start.1 = (f32[128,8,128]{2,0,1:T(8,128)S(1)}, f32[128,8,128]{2,0,1:T(8,128)}, u32[]{:S(2)}) copy-start(f32[128,8,128]{2,0,1:T(8,128)} %copy-done) | copy-start | bytes 1572868
  465.8 3.1 copy-start.10
  467.6 11.1 %copy-start.40 = (f32[8,128]{1,0:T(8,128)S(1)}, f32[8,128]{1,0:T(8,128)}, u32[]{:S(2)}) copy-start(f32[8,128]{1,0:T(8,128)} %get-tuple-element.194) | copy-start | bytes 12292
  468.9 12.2 %copy-start.2 = (f32[128,8,128]{2,0,1:T(8,128)S(1)}, f32[128,8,128]{2,0,1:T(8,128)}, u32[]{:S(2)}) copy-start(f32[128,8,128]{2,0,1:T(8,128)} %copy-done) | copy-start | bytes 1572868
  468.9 12.2 %copy-start.50 = (f32[128,8]{0,1:T(8,128)S(1)}, f32[128,8]{0,1:T(8,128)}, u32[]{:S(2)}) copy-start(f32[128,8]{0,1:T(8,128)} %get-tuple-element.209) | copy-start | bytes 12292
  470.6 8.1 %copy-start.11 = (f32[8,128,128]{2,1,0:T(8,128)S(1)}, f32[8,128,128]{2,1,0:T(8,128)}, u32[]{:S(2)}) copy-start(f32[8,128,128]{2,1,0:T(8,128)} %copy-done.10) | copy-start | bytes 1572868
  471.8 11.7 %copy-start.42 = (f32[128,8]{0,1:T(8,128)S(1)}, f32[128,8]{0,1:T(8,128)}, u32[]{:S(2)}) copy-start(f32[128,8]{0,1:T(8,128)} %copy-done.41) | copy-start | bytes 12292
  472.8 11.2 %copy-start.44 = (f32[1,1,1024]{2,1,0:T(1,128)S(1)}, f32[1,1,1024]{2,1,0:T(1,128)}, u32[]{:S(2)}) copy-start(f32[1,1,1024]{2,1,0:T(1,128)} %copy-done.43) | copy-start | bytes 12292
  472.9 11.2 %copy-start.46 = (f32[1,1,1024]{2,1,0:T(1,128)S(1)}, f32[1,1,1024]{2,1,0:T(1,128)}, u32[]{:S(2)}) copy-start(f32[1,1,1024]{2,1,0:T(1,128)} %copy-done.45) | copy-start | bytes 12292
  473.6 1.0 copy-start.17
  474.6 11.3 %copy-start.34 = (f32[1,1,1024]{2,1,0:T(1,128)S(1)}, f32[1,1,1024]{2,1,0:T(1,128)}, u32[]{:S(2)}) copy-start(f32[1,1,1024]{2,1,0:T(1,128)} %copy-done.33) | copy-start | bytes 12292
  474.6 11.3 %copy-start.36 = (f32[1,1,1024]{2,1,0:T(1,128)S(1)}, f32[1,1,1024]{2,1,0:T(1,128)}, u32[]{:S(2)}) copy-start(f32[1,1,1024]{2,1,0:T(1,128)} %copy-done.35) | copy-start | bytes 12292
  474.6 11.3 %copy-start.38 = (f32[1,1,1024]{2,1,0:T(1,128)S(1)}, f32[1,1,1024]{2,1,0:T(1,128)}, u32[]{:S(2)}) copy-start(f32[1,1,1024]{2,1,0:T(1,128)} %copy-done.37) | copy-start | bytes 12292
  476.7 9.8 %copy-start.28 = (f32[1,1,1024]{2,1,0:T(1,128)S(1)}, f32[1,1,1024]{2,1,0:T(1,128)}, u32[]{:S(2)}) copy-start(f32[1,1,1024]{2,1,0:T(1,128)} %copy-done.27) | copy-start | bytes 12292
  476.7 9.8 %copy-start.30 = (f32[1,1,1024]{2,1,0:T(1,128)S(1)}, f32[1,1,1024]{2,1,0:T(1,128)}, u32[]{:S(2)}) copy-start(f32[1,1,1024]{2,1,0:T(1,128)} %copy-done.29) | copy-start | bytes 12292
  476.7 9.8 %copy-start.32 = (f32[1,1,1024]{2,1,0:T(1,128)S(1)}, f32[1,1,1024]{2,1,0:T(1,128)}, u32[]{:S(2)}) copy-start(f32[1,1,1024]{2,1,0:T(1,128)} %copy-done.31) | copy-start | bytes 12292
  478.7 8.2 %copy-start.26 = (f32[1,1,1024]{2,1,0:T(1,128)S(1)}, f32[1,1,1024]{2,1,0:T(1,128)}, u32[]{:S(2)}) copy-start(f32[1,1,1024]{2,1,0:T(1,128)} %copy-done.25) | copy-start | bytes 12292
  481.1 5.9 %copy-start.15 = (f32[128,8,128]{0,2,1:T(8,128)S(1)}, f32[128,8,128]{0,2,1:T(8,128)}, u32[]{:S(2)}) copy-start(f32[128,8,128]{0,2,1:T(8,128)} %copy.96) | copy-start | bytes 1572868
  481.1 5.9 %copy-start.16 = (f32[128,1024]{0,1:T(8,128)S(1)}, f32[128,1024]{0,1:T(8,128)}, u32[]{:S(2)}) copy-start(f32[128,1024]{0,1:T(8,128)} %get-tuple-element.177) | copy-start | bytes 1572868
  481.1 6.1 %copy-start.24 = (f32[1,1,1024]{2,1,0:T(1,128)S(1)}, f32[1,1,1024]{2,1,0:T(1,128)}, u32[]{:S(2)}) copy-start(f32[1,1,1024]{2,1,0:T(1,128)} %copy-done.23) | copy-start | bytes 12292
  485.9 8.7 %copy-start.9 = (f32[8,128,128]{2,1,0:T(8,128)S(1)}, f32[8,128,128]{2,1,0:T(8,128)}, u32[]{:S(2)}) copy-start(f32[8,128,128]{2,1,0:T(8,128)} %copy-done.8) | copy-start | bytes 1572868
  485.9 8.7 %copy-start.14 = (f32[8,128,128]{2,1,0:T(8,128)S(1)}, f32[8,128,128]{2,1,0:T(8,128)}, u32[]{:S(2)}) copy-start(f32[8,128,128]{2,1,0:T(8,128)} %copy-done.13) | copy-start | bytes 1572868
  485.9 8.7 %copy-start.19 = (f32[8,128,128]{2,1,0:T(8,128)S(1)}, f32[8,128,128]{2,1,0:T(8,128)}, u32[]{:S(2)}) copy-start(f32[8,128,128]{2,1,0:T(8,128)} %fusion.90) | copy-start | bytes 1572868
  487.2 18.2 %copy-start.54 = (f32[128]{0:T(128)S(1)}, f32[128]{0:T(128)}, u32[]{:S(2)}) copy-start(f32[128]{0:T(128)} %copy-done.53) | copy-start | bytes 1540
  487.2 18.2 %copy-start.5 = (bf16[128,1024]{0,1:T(8,128)(2,1)S(1)}, bf16[128,1024]{0,1:T(8,128)(2,1)}, u32[]{:S(2)}) copy-start(bf16[128,1024]{0,1:T(8,128)(2,1)} %copy.90) | copy-start | bytes 786436
  487.2 18.2 %copy-start.49 = (f32[128]{0:T(128)S(1)}, f32[128]{0:T(128)}, u32[]{:S(2)}) copy-start(f32[128]{0:T(128)} %copy-done.48) | copy-start | bytes 1540
  490.5 10.8 %collective-permute-start.1 = (f32[3,1024]{0,1:T(8,128)S(1)}, f32[3,1024]{0,1:T(8,128)S(1)}, u32[]{:S(2)}, u32[]{:S(2)}) collective-permute-start(f32[3,1024]{0,1:T(8,128)S(1)} %split.15), channel_id=1, source_target_pairs={{1,0},{2,1},{3,2},{4,3},{5,4},{6,5},{7,6},{8,7},{9,8},{10,9},{11,1... | collective-permute-start | bytes 36872 | tf_op jit(solution)/shard_map/ppermute | solution.py:17
Sparse Core Ops, SparseCore 0:
  136.3 75.0 all-gather.10
  213.6 73.1 all-gather.8
  289.0 73.1 all-gather.12
  364.2 73.1 all-gather.14
where the time goes:
time: 524 us; the launch traced here: 514 us
  waiting for transfers between devices  265 us (51%)
  other arithmetic  125 us (24%)
  matrix products  71.5 us (14%)
  local copies, waits for them, and re-layouts  18.3 us (3%)
  between operations  15.3 us (3%)
  starting transfers between devices  9.37 us (2%)
  blocking collectives  8.14 us (2%)
    all_gather x4, waiting for transfers between devices, entering(): gathered = jax.tree.map(lambda a: lax.all_gather(a, axis), part)  260 us
    another operation x4, other arithmetic, solve_block(): lax.linalg.triangular_solve(system, jnp.concatenate([rhs_keys, rhs_values...  78.7 us
    dot_general x15, matrix products, compose(): jnp.einsum('hab,hbc->hac', second_map, first_add, precision=highest)  27.8 us
    another operation x1, other arithmetic, shards(): cumulative = jnp.cumsum(log_decay.reshape(length, -1, HEAD_DIM), axis=0)  23.3 us
  transfers between devices with their start and end apart: 6, of which 5 were waited for; matrix products, arithmetic and copies ran while one was open for 13% of the time, Pallas kernels for 0%

commit v1 on v0

v1 whole, which is shorter than its diff:
```python
import functools

import jax
import jax.numpy as jnp
from jax import lax
from jax.experimental import pallas as pl
from jax.experimental.pallas import tpu as pltpu
from jax.sharding import PartitionSpec as P

HEAD_DIM = 128
RIM = 8
epsilon = 1e-06
norm_eps = 1e-05
f32 = jnp.float32
bf16 = jnp.bfloat16
VMEM_LIMIT = 56 * 1024 * 1024

DIMS = {
    "nn": (((1,), (0,)), ((), ())),
    "nt": (((1,), (1,)), ((), ())),
    "tn": (((0,), (0,)), ((), ())),
}


def split(a):
    high = a.astype(bf16)
    return high, (a - high.astype(f32)).astype(bf16)


def exact(a):
    return a, None


def rows_of(*parts):
    highs = jnp.concatenate([p[0] for p in parts], axis=0)
    lows = [jnp.zeros_like(p[0]) if p[1] is None else p[1] for p in parts]
    return highs, jnp.concatenate(lows, axis=0)


def cols_of(*parts):
    return tuple(jnp.concatenate([p[i] for p in parts], axis=1) for i in range(2))


def mm(a, b, form):
    pairs = [(a[0], b[0])]
    if a[1] is not None:
        pairs.append((a[1], b[0]))
    if b[1] is not None:
        pairs.append((a[0], b[1]))
    left = jnp.concatenate([p[0] for p in pairs], axis=0 if form == "tn" else 1)
    right = jnp.concatenate([p[1] for p in pairs], axis=1 if form == "nt" else 0)
    return lax.dot_general(left, right, DIMS[form], preferred_element_type=f32)


def row_sums(a):
    high = a.astype(bf16)
    rest = a - high.astype(f32)
    mid = rest.astype(bf16)
    low = (rest - mid.astype(f32)).astype(bf16)
    terms = jnp.concatenate([high, mid, low], axis=1)
    ones = jnp.ones((RIM, terms.shape[1]), bf16)
    return lax.dot_general(ones, terms, DIMS["nt"], preferred_element_type=f32)


def down_rows(row):
    return jnp.transpose(jnp.broadcast_to(row[0:1], (HEAD_DIM, row.shape[1])))


def iotas(n=HEAD_DIM):
    return (
        lax.broadcasted_iota(jnp.int32, (n, n), 0),
        lax.broadcasted_iota(jnp.int32, (n, n), 1),
    )


def lane_slice(place):
    return pl.ds(pl.multiple_of(place * HEAD_DIM, HEAD_DIM), HEAD_DIM)


def prelude_kernel(x_ref, payload_ref, sums_ref):
    x = x_ref[...].astype(f32)
    channels = x.shape[1]
    sums = row_sums(x * x)
    sums_ref[...] = sums
    payload_ref[:, :channels] = x[x.shape[0] - RIM :]
    payload_ref[:, channels:] = sums


def inverse_all(systems):
    row, col = iotas()
    found = [jnp.where(row == col, 1.0, 0.0) - jnp.where((row >> 1 == col >> 1), n, 0.0) for n in systems]
    level = 1
    while (2 << level) <= HEAD_DIM:
        mask = (row >> (level + 1) == col >> (level + 1)) & (row >> level != col >> level)
        parts = [split(a) for a in found]
        cross = [split(jnp.where(mask, n, 0.0)) for n in systems]
        right = [split(mm(c, p, "nn")) for c, p in zip(cross, parts)]
        found = [a - mm(p, r, "nn") for a, p, r in zip(found, parts, right)]
        level += 1
    return found


def mixes_of(normed, rim, kern):
    row8 = lax.broadcasted_iota(jnp.int32, (RIM, HEAD_DIM), 0)
    taps = kern.shape[1]
    shifted = [normed]
    for s in range(1, taps):
        moved = pltpu.roll(normed, s, 0)
        first = jnp.where(row8 < s, pltpu.roll(rim, s, 0), moved[:RIM])
        shifted.append(jnp.concatenate([first, moved[RIM:]], axis=0))
    return [
        sum(kern[j, i : i + 1] * shifted[taps - 1 - i] for i in range(taps)) for j in range(3)
    ]


def local_kernel(
    heads, base, flags, x_ref, go_ref, kern_ref, decay_ref, beta_ref, rim_ref, scale_ref, rim_scale_ref,
    comp_ref, saved_ref,
):
    mask = flags[0]
    length = x_ref.shape[0]
    row, col = iotas()
    strict, full = row > col, row >= col
    scale = down_rows(scale_ref[...])
    rim_scale = down_rows(rim_scale_ref[...])[length - RIM :]
    lane8 = lax.broadcasted_iota(jnp.int32, beta_ref.shape, 1)
    tril = jnp.where(full, 1.0, 0.0).astype(bf16)
    tril = jnp.concatenate([tril] * 3, axis=1)
    data = []
    for j in range(heads):
        place = (j ^ mask) & (heads - 1)
        at = lane_slice(place)
        head = (base + j) ^ mask
        x = x_ref[:, at].astype(f32)
        kern = kern_ref[:, :, at]
        mixes = mixes_of(x * scale, rim_ref[:, at] * rim_scale, kern)
        sig = [1.0 / (1.0 + jnp.exp(-m)) for m in mixes]
        act = [m * s for m, s in zip(mixes, sig)]
        slope = [s * (1.0 + m * (1.0 - s)) for m, s in zip(mixes, sig)]
        inv = [lax.rsqrt(jnp.sum(a * a, axis=1, keepdims=True) + epsilon) for a in act[:2]]
        q, k = act[0] * inv[0], act[1] * inv[1]
        gq, gk = slope[0] * inv[0], slope[1] * inv[1]
        beta = jnp.sum(jnp.where(lane8 == head, beta_ref[...], 0.0), axis=1, keepdims=True)
        decay = decay_ref[:, at]
        high = decay.astype(bf16)
        rest = decay - high.astype(f32)
        mid = rest.astype(bf16)
        low = (rest - mid.astype(f32)).astype(bf16)
        cumulative = lax.dot_general(
            tril, jnp.concatenate([high, mid, low], axis=0), DIMS["nn"], preferred_element_type=f32
        )
        middle = cumulative[length // 2 : length // 2 + 1]
        final = cumulative[length - 1 : length]
        e1 = jnp.exp(cumulative - middle)
        e2 = jnp.exp(middle - cumulative)
        em = jnp.exp(middle)
        ecm = jnp.exp(final - middle)
        kf, qf, kb = k * e1, q * e1, k * e2
        data.append(
            dict(q=q, gq=gq, k=k, gk=gk, v=act[2], gv=slope[2], beta=beta, e1=e1, e2=e2, em=em, ecm=ecm,
                 ef=jnp.exp(final), kf=kf, qf=qf, kb=kb, at=at)
        )
    for d in data:
        d["skb"] = split(d["kb"])
        products = mm(rows_of(split(d["kf"]), split(d["qf"])), d["skb"], "nt")
        d["system"] = jnp.where(strict, d["beta"] * products[:length], 0.0)
        d["scores"] = split(jnp.where(full, products[length:], 0.0))
    inverses = inverse_all([d["system"] for d in data])
    for d, inverse in zip(data, inverses):
        d["inv"] = split(inverse)
        rhs = cols_of(split(d["beta"] * d["kf"] * d["em"]), split(d["beta"] * d["v"]))
        d["wu"] = mm(d["inv"], rhs, "nn")
        d["swu"] = split(d["wu"])
    for j, d in enumerate(data):
        ke = split(d["kb"] * d["ecm"])
        d["ke"] = ke
        maps = mm(ke, d["swu"], "tn")
        comp_ref[j, 0:128] = jnp.where(row == col, d["ef"], 0.0) - maps[:, :HEAD_DIM]
        comp_ref[j, 128:256] = maps[:, HEAD_DIM:]
        swu = mm(d["scores"], d["swu"], "nn")
        qs = d["qf"] * d["em"] - swu[:, :HEAD_DIM]
        go = exact(go_ref[:, d["at"]])
        comp_ref[j, 256:384] = mm(split(qs), go, "tn")
        fresh_grad = split(mm(d["scores"], go, "tn"))
        back = mm(d["inv"], cols_of(fresh_grad, ke), "tn")
        saved = [
            d["q"], d["gq"], d["k"], d["gk"], d["gv"], d["e1"], d["e2"], qs, d["wu"][:, :HEAD_DIM],
            swu[:, HEAD_DIM:], d["wu"][:, HEAD_DIM:], back[:, :HEAD_DIM], back[:, HEAD_DIM:],
        ]
        for n, a in enumerate(saved):
            saved_ref[j, n] = a
        saved_ref[j, len(saved), 0:8] = jnp.broadcast_to(d["em"], (8, HEAD_DIM))
        saved_ref[j, len(saved), 8:16] = jnp.broadcast_to(d["ecm"], (8, HEAD_DIM))


N_SAVED = 14


def compose_kernel(heads, bit, flags, keep_ref, recv_ref, *outs):
    later = flags[bit] != 0
    half = outs[0].shape[0]
    for j in range(heads):
        keep, recv = keep_ref[j], recv_ref[j]
        lo = jnp.where(later, recv, keep)
        hi = jnp.where(later, keep, recv)
        lo_map, hi_map = split(lo[0:128]), split(hi[0:128])
        forward = mm(hi_map, cols_of(lo_map, split(lo[128:256])), "nn")
        back = mm(lo_map, split(hi[256:384]), "tn")
        out, at = outs[j // half], j % half
        out[at, 0:128] = forward[:, :HEAD_DIM]
        out[at, 128:256] = forward[:, HEAD_DIM:] + hi[128:256]
        out[at, 256:384] = back + lo[256:384]


def last_compose_kernel(heads, bit, flags, keep_ref, recv_ref, t_ref, u_ref, g_ref):
    later = flags[bit] != 0
    for j in range(heads):
        keep, recv = keep_ref[j], recv_ref[j]
        lo = jnp.where(later, recv, keep)
        hi = jnp.where(later, keep, recv)
        lo_map, hi_map = split(lo[0:128]), split(hi[0:128])
        forward = mm(hi_map, cols_of(lo_map, split(lo[128:256])), "nn")
        back = mm(lo_map, split(hi[256:384]), "tn")
        t_ref[j] = forward[:, :HEAD_DIM]
        u_ref[j] = forward[:, HEAD_DIM:] + hi[128:256]
        g_ref[j] = back + lo[256:384]


def hop_kernel(t_ref, u_ref, g_ref, s_ref, e_ref, s_out, e_out):
    for j in range(t_ref.shape[0]):
        t = split(t_ref[j])
        s_out[j] = mm(t, split(s_ref[j]), "nn") + u_ref[j]
        e_out[j] = mm(t, split(e_ref[j]), "tn") + g_ref[j]


def down_kernel(bit, n_in, flags, keep_ref, recv_ref, *refs):
    ins, (mine_ref, send_ref) = refs[:n_in], refs[n_in:]
    later = flags[bit] != 0
    heads = keep_ref.shape[0]
    for j in range(heads):
        half = ins[0].shape[0]
        at = j % half
        if ins[0].shape[1] == HEAD_DIM:
            start, end = ins[0][at], ins[1][at]
        else:
            both = ins[j // half][at]
            start, end = both[:HEAD_DIM], both[HEAD_DIM:]
        keep, recv = keep_ref[j], recv_ref[j]
        lo = jnp.where(later, recv, keep)
        hi = jnp.where(later, keep, recv)
        start_hi = mm(split(lo[0:128]), split(start), "nn") + lo[128:256]
        end_lo = mm(split(hi[0:128]), split(end), "tn") + hi[256:384]
        mine_ref[j, 0:128] = jnp.where(later, start_hi, start)
        mine_ref[j, 128:256] = jnp.where(later, end, end_lo)
        send_ref[j, 0:128] = jnp.where(later, start, start_hi)
        send_ref[j, 128:256] = jnp.where(later, end_lo, end)


def back_kernel(
    heads, base, chained, flags, x_ref, go_ref, kern_ref, beta_ref, rim_ref, saved_ref, state_ref, *rest
):
    if chained:
        rest = rest[1:]
    out_ref, grad_ref, rim_grad_ref, sums_ref, rim_sums_ref = rest
    mask = flags[0]
    length = x_ref.shape[0]
    row, col = iotas()
    strict, full = row > col, row >= col
    lane8 = lax.broadcasted_iota(jnp.int32, beta_ref.shape, 1)
    taps = kern_ref.shape[1]
    dot_all = rim_dot = 0.0
    data = []
    for j in range(heads):
        place = (j ^ mask) & (heads - 1)
        at = lane_slice(place)
        head = (base + j) ^ mask
        start, end = split(state_ref[j, 0:128]), split(state_ref[j, 128:256])
        qs, w, o0, u, z0, kea = [saved_ref[j, 7 + n] for n in range(6)]
        first = mm(rows_of(split(qs), split(w)), start, "nn")
        z = z0 + mm(split(kea), end, "nn")
        x = x_ref[:, at].astype(f32)
        out_ref[:, at] = (x + (o0 + first[:length])).astype(bf16)
        data.append(
            dict(at=at, head=head, x=x, start=start, end=end, z=z, fresh=split(u - first[length:]))
        )
    for j, d in enumerate(data):
        q, gq, k, gk, gv, e1, e2 = [saved_ref[j, n] for n in range(7)]
        em, ecm = saved_ref[j, 13, 0:1], saved_ref[j, 13, 8:9]
        at = d["at"]
        beta = jnp.sum(jnp.where(lane8 == d["head"], beta_ref[...], 0.0), axis=1, keepdims=True)
        go = exact(go_ref[:, at])
        second = mm(rows_of(go, split(d["z"])), rows_of(d["fresh"], d["start"]), "nt")
        score_grad = split(jnp.where(full, second[:length, :HEAD_DIM], 0.0))
        product_grad = split(jnp.where(strict, -beta * second[length:, :HEAD_DIM], 0.0))
        qg_grad = second[:length, HEAD_DIM:]
        kg_grad = -beta * second[length:, HEAD_DIM:]
        ke_grad = mm(d["fresh"], d["end"], "nt")
        pair = rows_of(score_grad, product_grad)
        third = mm(pair, split(k * e2), "nn")
        kb_grad = mm(pair, rows_of(split(q * e1), split(k * e1)), "tn")
        q_grad = e1 * (third[:length] + em * qg_grad)
        k_grad = e1 * (third[length:] + em * kg_grad) + e2 * (kb_grad + ecm * ke_grad)
        mix_grads = [
            gq * (q_grad - q * jnp.sum(q * q_grad, axis=1, keepdims=True)),
            gk * (k_grad - k * jnp.sum(k * k_grad, axis=1, keepdims=True)),
            gv * (beta * d["z"]),
        ]
        kern = kern_ref[:, :, at]
        normed_grad = rim_grad = 0.0
        for i in range(taps):
            each = sum(kern[n, i : i + 1] * mix_grads[n] for n in range(3))
            s = taps - 1 - i
            if s == 0:
                normed_grad = normed_grad + each
            else:
                moved = pltpu.roll(each, length - s, 0)
                normed_grad = normed_grad + jnp.where(row < length - s, moved, 0.0)
                row8 = lax.broadcasted_iota(jnp.int32, (RIM, HEAD_DIM), 0)
                rim_grad = rim_grad + jnp.where(row8 >= RIM - s, moved[length - RIM :], 0.0)
        grad_ref[:, at] = normed_grad
        rim_grad_ref[:, at] = rim_grad
        dot_all = dot_all + normed_grad * d["x"]
        rim_dot = rim_dot + rim_grad * rim_ref[:, at]
    sums_ref[...] = row_sums(dot_all)
    rim_sums_ref[...] = jnp.broadcast_to(jnp.sum(rim_dot, axis=1, keepdims=True), rim_dot.shape)


def finish_kernel(
    groups, width, flags, x_ref, go_ref, scale_ref, inner_ref, next_sums_ref, *refs
):
    grads, next_rims, out_ref = refs[:groups], refs[groups : 2 * groups], refs[2 * groups]
    length = x_ref.shape[0]
    mask = flags[0]
    scale = down_rows(scale_ref[...])
    inner = down_rows(inner_ref[...])
    inner = jnp.concatenate([inner[: length - RIM], inner[length - RIM :] + next_sums_ref[...]], axis=0)
    cubed = scale * scale * scale * inner * (1.0 / width)
    span = grads[0].shape[1]
    per = span // HEAD_DIM
    for g in range(groups):
        grad_ref, next_ref = grads[g], next_rims[g]
        place = ((g * per) ^ mask) // per if groups > 1 else 0
        for n in range(per):
            here = slice(n * HEAD_DIM, (n + 1) * HEAD_DIM)
            at = lane_slice(place * per + n)
            grad = grad_ref[:, here]
            grad = jnp.concatenate([grad[: length - RIM], grad[length - RIM :] + next_ref[:, here]], axis=0)
            total = go_ref[:, at].astype(f32) + grad * scale - x_ref[:, at].astype(f32) * cubed
            out_ref[:, at] = total.astype(bf16)


def whole_call(kernel, outs, flags, *args, name=None, aliases=None, scalar=True):
    params = pltpu.CompilerParams(vmem_limit_bytes=VMEM_LIMIT)
    if not scalar:
        return pl.pallas_call(kernel, out_shape=outs, compiler_params=params, name=name)(*args)
    spec = pl.BlockSpec(memory_space=pltpu.VMEM)
    return pl.pallas_call(
        kernel,
        out_shape=outs,
        in_specs=[pl.BlockSpec(memory_space=pltpu.SMEM)] + [spec] * len(args),
        out_specs=jax.tree.map(lambda _: spec, outs),
        compiler_params=params,
        name=name,
    )(flags, *args)


def array(*shape, dtype=f32):
    return jax.ShapeDtypeStruct(shape, dtype)


def shards(inputs, out_grads, conv_weight, log_decay, beta):
    length, channels = inputs.shape
    heads = channels // HEAD_DIM
    sections, spots = lax.axis_size("section"), lax.axis_size("ctx")
    width = channels * sections
    me = lax.axis_index("ctx")
    levels = 0
    while (heads >> (levels + 1)) >= 1 and spots % (2 << levels) == 0:
        levels += 1
    slabs = spots >> levels
    bits = [(me >> n) & 1 for n in range(levels)]
    mask = sum(b * (heads >> (n + 1)) for n, b in enumerate(bits))
    flags = jnp.stack([mask] + bits).astype(jnp.int32)

    def turned(value, sec, shift):
        route = []
        for s in range(sections):
            for c in range(spots):
                if 0 <= c + shift < spots:
                    route.append((s * spots + c, ((s + sec) % sections) * spots + c + shift))
        return lax.ppermute(value, ("section", "ctx"), route)

    def swapped(value, level):
        return lax.ppermute(value, "ctx", [(i, i ^ (1 << level)) for i in range(spots)])

    def moved(value, shift):
        return lax.ppermute(
            value, "ctx", [(i, i + shift) for i in range(spots) if 0 <= i + shift < spots]
        )

    payload, sums = whole_call(
        prelude_kernel, (array(RIM, channels + length), array(RIM, length)), None, inputs,
        name="prelude", scalar=False,
    )
    rim = turned(payload, 0, 1)
    total = sums
    rim_total = rim[:, channels:]
    for sec in range(1, sections):
        total = total + turned(sums, sec, 0)
        rim_total = rim_total + turned(sums, sec, 1)
    scale = lax.rsqrt(total / width + norm_eps)
    rim_scale = lax.rsqrt(rim_total / width + norm_eps)

    groups = 2 if levels > 0 else 1
    per = heads // groups
    span = per * HEAD_DIM

    def block(shape, at, wide):
        lead = (0,) * (len(shape) - 1)
        return pl.BlockSpec(
            shape[:-1] + (span,), lambda i, f, lead=lead: lead + (((at * per) ^ f[0]) // per,)
        )

    def fixed(shape):
        return pl.BlockSpec(shape, lambda i, f, n=len(shape): (0,) * n)

    def grid_call(kernel, in_specs, out_specs, outs, args, name, aliases=None):
        return pl.pallas_call(
            kernel,
            grid_spec=pltpu.PrefetchScalarGridSpec(
                num_scalar_prefetch=1, grid=(1,), in_specs=in_specs, out_specs=out_specs
            ),
            out_shape=outs,
            input_output_aliases=aliases or {},
            compiler_params=pltpu.CompilerParams(vmem_limit_bytes=VMEM_LIMIT),
            name=name,
        )(flags, *args)

    rim_raw = rim[:, :channels]
    comps, saves = [None] * groups, [None] * groups
    for g in reversed(range(groups)):
        comps[g], saves[g] = grid_call(
            functools.partial(local_kernel, per, g * per),
            [
                block(inputs.shape, g, span), block(out_grads.shape, g, span), block(conv_weight.shape, g, span),
                block(log_decay.shape, g, span), fixed(beta.shape), block(rim_raw.shape, g, span),
                fixed(scale.shape), fixed(rim_scale.shape),
            ],
            [fixed((per, 384, HEAD_DIM)), fixed((per, N_SAVED, HEAD_DIM, HEAD_DIM))],
            [array(per, 384, HEAD_DIM), array(per, N_SAVED, HEAD_DIM, HEAD_DIM)],
            (inputs, out_grads, conv_weight, log_decay, beta, rim_raw, scale, rim_scale),
            name=f"local{g}",
        )

    history = []
    keep, send = comps[0], comps[-1]
    for level in range(levels):
        recv = swapped(send, level)
        history.append((keep, recv))
        n = keep.shape[0]
        if level + 1 < levels:
            keep, send = whole_call(
                functools.partial(compose_kernel, n, level + 1),
                (array(n // 2, 384, HEAD_DIM), array(n // 2, 384, HEAD_DIM)),
                flags, keep, recv, name=f"compose{level}",
            )
        else:
            t, u, g = whole_call(
                functools.partial(last_compose_kernel, n, level + 1),
                (array(n, HEAD_DIM, HEAD_DIM),) * 3,
                flags, keep, recv, name=f"compose{level}",
            )
    if levels == 0:
        t, u, g = keep[:, :128], keep[:, 128:256], keep[:, 256:]
    step = 1 << levels
    start, end = jnp.zeros_like(u), jnp.zeros_like(g)
    for hop in range(slabs - 1):
        if hop == 0:
            start, end = u, g
        else:
            start, end = whole_call(
                lambda flags, *refs: hop_kernel(*refs), (array(*u.shape),) * 2, flags, t, u, g, start, end,
                name=f"hop{hop}",
            )
        start, end = moved(start, step), moved(end, -step)
    states = (start, end)
    for level in reversed(range(levels)):
        keep, recv = history[level]
        n = keep.shape[0]
        mine, send = whole_call(
            functools.partial(down_kernel, level + 1, len(states)),
            (array(n, 256, HEAD_DIM),) * 2,
            flags, keep, recv, *states, name=f"down{level}",
        )
        states = (mine, swapped(send, level))
    if levels == 0:
        states = (jnp.concatenate([start, end], axis=1),)

    stream_out = None
    grads, rim_grads, inner, rim_sums = [], [], 0.0, 0.0
    for g in range(groups):
        args = [inputs, out_grads, conv_weight, beta, rim_raw, saves[g], states[g]]
        specs = [
            block(inputs.shape, g, span), block(out_grads.shape, g, span), block(conv_weight.shape, g, span),
            fixed(beta.shape), block(rim_raw.shape, g, span), fixed(saves[g].shape), fixed(states[g].shape),
        ]
        aliases = None
        if g > 0:
            args.append(stream_out)
            specs.append(pl.BlockSpec(memory_space=pl.ANY))
            aliases = {len(args): 0}
        stream_out, grad, rim_grad, part, rim_part = grid_call(
            functools.partial(back_kernel, per, g * per, g > 0),
            specs,
            [
                block(inputs.shape, g, span), fixed((length, span)), fixed((RIM, span)),
                fixed((RIM, length)), fixed((RIM, HEAD_DIM)),
            ],
            [
                array(*inputs.shape, dtype=bf16), array(length, span), array(RIM, span),
                array(RIM, length), array(RIM, HEAD_DIM),
            ],
            args, name=f"back{g}", aliases=aliases,
        )
        grads.append(grad)
        rim_grads.append(rim_grad)
        inner = inner + part
        rim_sums = rim_sums + rim_part

    next_rims = [turned(a, 0, -1) for a in reversed(rim_grads)]
    inner_total = inner
    next_sums = turned(rim_sums, 0, -1)
    for sec in range(1, sections):
        inner_total = inner_total + turned(inner, sec, 0)
        next_sums = next_sums + turned(rim_sums, sec, -1)
    input_grad = finish(
        flags, groups, width, inputs, out_grads, scale, inner_total, next_sums, grads, next_rims
    )
    return (stream_out, input_grad)


def finish(flags, groups, width, inputs, out_grads, scale, inner_total, next_sums, grads, next_rims):
    return whole_call(
        functools.partial(finish_kernel, groups, width),
        array(*inputs.shape, dtype=bf16),
        flags, inputs, out_grads, scale, inner_total, next_sums, *grads, *next_rims, name="finish",
    )


def solution(mesh):
    in_specs = (
        P("ctx", "section"),
        P("ctx", "section"),
        P(None, None, "section"),
        P("ctx", "section"),
        P("ctx", "section"),
    )
    out_specs = (P("ctx", "section"), P("ctx", "section"))
    return jax.shard_map(shards, mesh=mesh, in_specs=in_specs, out_specs=out_specs, check_vma=False)
```

time: 524 us -> 125 us (0.24)
  the two profiles are of different devices: /device:TPU:1 before, /device:TPU:11 now
where the time goes in v1:
time: 125 us
  Pallas kernels  47.9 us (38%)
  starting transfers between devices  32.6 us (26%)
  waiting for transfers between devices  30.3 us (24%)
  local copies, waits for them, and re-layouts  7.82 us (6%)
  other arithmetic  5.09 us (4%)
    pallas_call x4, Pallas kernels, grid_call(): pl.pallas_call(kernel, grid_spec=pltpu.PrefetchScalarGridSpec(num_scalar_...  30 us
    ppermute x6, waiting for transfers between devices, swapped(): lax.ppermute(value, 'ctx', [(i, i ^ 1 << level) for i in range(spots)])  23.3 us
    ppermute x8, starting transfers between devices, turned(): return lax.ppermute(value, ('section', 'ctx'), route)  18.6 us
    pallas_call x7, Pallas kernels, whole_call(): pl.pallas_call(kernel, out_shape=outs, in_specs=[pl.BlockSpec(memory_spac...  16 us
    ppermute x6, starting transfers between devices, swapped(): lax.ppermute(value, 'ctx', [(i, i ^ 1 << level) for i in range(spots)])  8.34 us
    unnamed x25, local copies, waits for them, and re-layouts  7.22 us
    ppermute x2, starting transfers between devices, moved(): lax.ppermute(value, 'ctx', [(i, i + shift) for i in range(spots) if 0 <=...  5.7 us
    ppermute x2, waiting for transfers between devices, moved(): lax.ppermute(value, 'ctx', [(i, i + shift) for i in range(spots) if 0 <=...  4.64 us
  transfers between devices with their start and end apart: 16, of which 7 were waited for; matrix products, arithmetic and copies ran while one was open for 5% of the time, Pallas kernels for 17%

profile of v1, /device:TPU:11, one launch (start us, length us, event | category | flops | bytes accessed | tf_op | source)
XLA Modules:
  0.0 124.5 jit_solution(3266842959755924236)
XLA Ops:
  0.6 1.9 %prelude.1 = (f32[8,1152]{1,0:T(8,128)}, f32[8,128]{1,0:T(8,128)}) custom-call(bf16[128,1024]{1,0:T(8,128)(2,1)} %x_ref.11), custom_call_target="tpu_custom_call" | custom-call | tf_op jit(solution)/shard_map/prelude/pallas_call | solution.py:355
  2.5 3.7 %collective-permute-start.2 = (f32[8,128]{1,0:T(8,128)}, f32[8,128]{1,0:T(8,128)S(1)}, u32[]{:S(2)}, u32[]{:S(2)}) collective-permute-start(f32[8,128]{1,0:T(8,128)} %get-tuple-element.31), channel_id=1, source_target_pairs={{0,17},{1,18},{2,19},{3,20},{4,21},{5,22},{6,23},{7,24},{8,25},{9,... | collective-permute-start | bytes 12296 | tf_op jit(solution)/shard_map/ppermute | solution.py:391
  6.2 1.3 %collective-permute-start.1 = (f32[8,128]{1,0:T(8,128)}, f32[8,128]{1,0:T(8,128)S(1)}, u32[]{:S(2)}, u32[]{:S(2)}) collective-permute-start(f32[8,128]{1,0:T(8,128)} %get-tuple-element.31), channel_id=1, source_target_pairs={{0,16},{1,17},{2,18},{3,19},{4,20},{5,21},{6,22},{7,23},{8,24},{9,... | collective-permute-start | bytes 12296 | tf_op jit(solution)/shard_map/ppermute | solution.py:391
  7.5 2.2 %collective-permute-start = (f32[8,1152]{1,0:T(8,128)}, f32[8,1152]{1,0:T(8,128)S(1)}, u32[]{:S(2)}, u32[]{:S(2)}) collective-permute-start(f32[8,1152]{1,0:T(8,128)} %get-tuple-element.30), channel_id=1, source_target_pairs={{0,1},{1,2},{2,3},{3,4},{4,5},{5,6},{6,7},{7,8},{8,9},{9,10},{10,1... | collective-permute-start | bytes 110600 | tf_op jit(solution)/shard_map/ppermute | solution.py:391
  9.7 0.7 pad_add_fusion.flags
  10.3 1.4 %copy.11.beta_ref = f32[128,8]{1,0:T(8,128)} copy(f32[128,8]{0,1:T(8,128)} %param.9) | data formatting | bytes 8192 | tf_op args[4]
  11.8 0.0 collective-permute-done.1
  11.8 1.3 %add_rsqrt_fusion.scale_ref = f32[8,128]{1,0:T(8,128)} fusion(f32[8,128]{1,0:T(8,128)} %get-tuple-element.31, f32[8,128]{1,0:T(8,128)S(1)} %collective-permute-done.1), kind=kLoop, calls=%fused_computation.4 | loop fusion | flops 3072 | bytes 12288 | tf_op jit(solution)/shard_map/rsqrt | solution.py:411
  13.0 0.0 collective-permute-done
  13.1 0.6 slice.8.rim_ref
  13.7 0.0 collective-permute-done.2
  13.7 0.6 fusion.2.rim_scale_ref
  14.3 9.0 %local1.1 = (f32[4,384,128]{2,1,0:T(8,128)}, f32[4,14,128,128]{3,2,1,0:T(8,128)}) custom-call(s32[4]{0:T(128)} %pad_add_fusion.flags, bf16[128,1024]{1,0:T(8,128)(2,1)} %x_ref.11, bf16[128,1024]{1,0:T(8,128)(2,1)} %go_ref.9, f32[3,4,1024]{2,1,0:T(4,128)} %kern_ref.7, f32[128,1024]{1,0:T(8,128)} %decay_ref.3, f32[128,8]{1,0:T(8,128)} %copy.11.beta_ref, ...), custom_call_target="tpu_custom_call" | custom-call | tf_op jit(solution)/shard_map/local1/pallas_call | solution.py:428
  23.2 0.2 collective-permute-start.3
  23.5 9.0 %local0.1 = (f32[4,384,128]{2,1,0:T(8,128)}, f32[4,14,128,128]{3,2,1,0:T(8,128)}) custom-call(s32[4]{0:T(128)} %pad_add_fusion.flags, bf16[128,1024]{1,0:T(8,128)(2,1)} %x_ref.11, bf16[128,1024]{1,0:T(8,128)(2,1)} %go_ref.9, f32[3,4,1024]{2,1,0:T(4,128)} %kern_ref.7, f32[128,1024]{1,0:T(8,128)} %decay_ref.3, f32[128,8]{1,0:T(8,128)} %copy.11.beta_ref, ...), custom_call_target="tpu_custom_call" | custom-call | tf_op jit(solution)/shard_map/local0/pallas_call | solution.py:428
  32.4 0.0 collective-permute-done.3.recv_ref
  32.4 1.0 copy-done
  33.4 2.6 %compose0.1 = (f32[2,384,128]{2,1,0:T(8,128)}, f32[2,384,128]{2,1,0:T(8,128)}) custom-call(s32[4]{0:T(128)} %pad_add_fusion.flags, f32[4,384,128]{2,1,0:T(8,128)} %get-tuple-element.33.keep_ref, f32[4,384,128]{2,1,0:T(8,128)} %copy-done), custom_call_target="tpu_custom_call" | custom-call | tf_op jit(solution)/shard_map/compose0/pallas_call | solution.py:357
  36.0 1.2 collective-permute-start.4
  37.2 9.4 %collective-permute-done.4.recv_ref = f32[2,384,128]{2,1,0:T(8,128)S(1)} collective-permute-done((f32[2,384,128]{2,1,0:T(8,128)}, f32[2,384,128]{2,1,0:T(8,128)S(1)}, u32[]{:S(2)}, u32[]{:S(2)}) %collective-permute-start.4) | collective-permute-done | bytes 393248 | tf_op jit(solution)/shard_map/ppermute | solution.py:394
  46.6 0.8 copy-done.1
  47.4 2.1 %compose1.1 = (f32[1,384,128]{2,1,0:T(8,128)}, f32[1,384,128]{2,1,0:T(8,128)}) custom-call(s32[4]{0:T(128)} %pad_add_fusion.flags, f32[2,384,128]{2,1,0:T(8,128)} %get-tuple-element.35.keep_ref, f32[2,384,128]{2,1,0:T(8,128)} %copy-done.1), custom_call_target="tpu_custom_call" | custom-call | tf_op jit(solution)/shard_map/compose1/pallas_call | solution.py:357
  49.5 0.2 collective-permute-start.5
  49.7 5.3 %collective-permute-done.5.recv_ref = f32[1,384,128]{2,1,0:T(8,128)S(1)} collective-permute-done((f32[1,384,128]{2,1,0:T(8,128)}, f32[1,384,128]{2,1,0:T(8,128)S(1)}, u32[]{:S(2)}, u32[]{:S(2)}) %collective-permute-start.5) | collective-permute-done | bytes 196640 | tf_op jit(solution)/shard_map/ppermute | solution.py:394
  55.0 0.7 copy-done.2
  55.7 1.9 %compose2.1 = (f32[1,128,128]{2,1,0:T(8,128)}, f32[1,128,128]{2,1,0:T(8,128)}, f32[1,128,128]{2,1,0:T(8,128)}) custom-call(s32[4]{0:T(128)} %pad_add_fusion.flags, f32[1,384,128]{2,1,0:T(8,128)} %get-tuple-element.37.keep_ref, f32[1,384,128]{2,1,0:T(8,128)} %copy-done.2), custom_call_target="tpu_custom_call" | custom-call | tf_op jit(solution)/shard_map/compose2/pallas_call | solution.py:357
  57.6 4.2 %collective-permute-start.6 = (f32[1,128,128]{2,1,0:T(8,128)}, f32[1,128,128]{2,1,0:T(8,128)S(1)}, u32[]{:S(2)}, u32[]{:S(2)}) collective-permute-start(f32[1,128,128]{2,1,0:T(8,128)} %get-tuple-element.39), channel_id=1, source_target_pairs={{0,8},{1,9},{2,10},{3,11},{4,12},{5,13},{6,14},{7,15},{16,24},{17,... | collective-permute-start | bytes 196616 | tf_op jit(solution)/shard_map/ppermute | solution.py:397
  61.9 1.5 %collective-permute-start.7 = (f32[1,128,128]{2,1,0:T(8,128)}, f32[1,128,128]{2,1,0:T(8,128)S(1)}, u32[]{:S(2)}, u32[]{:S(2)}) collective-permute-start(f32[1,128,128]{2,1,0:T(8,128)} %get-tuple-element.40), channel_id=1, source_target_pairs={{8,0},{9,1},{10,2},{11,3},{12,4},{13,5},{14,6},{15,7},{24,16},{25,... | collective-permute-start | bytes 196616 | tf_op jit(solution)/shard_map/ppermute | solution.py:397
  63.4 0.6 collective-permute-done.6.refs_0_
  64.0 4.0 %collective-permute-done.7.refs_1_ = f32[1,128,128]{2,1,0:T(8,128)S(1)} collective-permute-done((f32[1,128,128]{2,1,0:T(8,128)}, f32[1,128,128]{2,1,0:T(8,128)S(1)}, u32[]{:S(2)}, u32[]{:S(2)}) %collective-permute-start.7) | collective-permute-done | bytes 65568 | tf_op jit(solution)/shard_map/ppermute | solution.py:397
  68.0 0.0 copy-done.6
  68.0 0.6 copy-done.7
  68.6 2.0 %down2.1 = (f32[1,256,128]{2,1,0:T(8,128)}, f32[1,256,128]{2,1,0:T(8,128)}) custom-call(s32[4]{0:T(128)} %pad_add_fusion.flags, f32[1,384,128]{2,1,0:T(8,128)} %get-tuple-element.37.keep_ref, f32[1,384,128]{2,1,0:T(8,128)} %copy-done.2, f32[1,128,128]{2,1,0:T(8,128)} %copy-done.6, f32[1,128,128]{2,1,0:T(8,128)} %copy-done.7), custom_call_target="tpu_custom_call" | custom-call | tf_op jit(solution)/shard_map/down2/pallas_call | solution.py:357
  70.6 0.2 collective-permute-start.8
  70.8 3.8 %collective-permute-done.8.refs_1_ = f32[1,256,128]{2,1,0:T(8,128)S(1)} collective-permute-done((f32[1,256,128]{2,1,0:T(8,128)}, f32[1,256,128]{2,1,0:T(8,128)S(1)}, u32[]{:S(2)}, u32[]{:S(2)}) %collective-permute-start.8) | collective-permute-done | bytes 131104 | tf_op jit(solution)/shard_map/ppermute | solution.py:394
  74.7 0.7 copy-done.5
  75.3 2.3 %down1.1 = (f32[2,256,128]{2,1,0:T(8,128)}, f32[2,256,128]{2,1,0:T(8,128)}) custom-call(s32[4]{0:T(128)} %pad_add_fusion.flags, f32[2,384,128]{2,1,0:T(8,128)} %get-tuple-element.35.keep_ref, f32[2,384,128]{2,1,0:T(8,128)} %copy-done.1, f32[1,256,128]{2,1,0:T(8,128)} %get-tuple-element.41.refs_0_, f32[1,256,128]{2,1,0:T(8,128)} %copy-done.5), custom_call_target="tpu_custom_call" | custom-call | tf_op jit(solution)/shard_map/down1/pallas_call | solution.py:357
  77.6 0.8 collective-permute-start.9
  78.4 4.7 %collective-permute-done.9.refs_1_ = f32[2,256,128]{2,1,0:T(8,128)S(1)} collective-permute-done((f32[2,256,128]{2,1,0:T(8,128)}, f32[2,256,128]{2,1,0:T(8,128)S(1)}, u32[]{:S(2)}, u32[]{:S(2)}) %collective-permute-start.9) | collective-permute-done | bytes 262176 | tf_op jit(solution)/shard_map/ppermute | solution.py:394
  83.0 0.7 copy-done.4
  83.7 2.9 %down0.1 = (f32[4,256,128]{2,1,0:T(8,128)}, f32[4,256,128]{2,1,0:T(8,128)}) custom-call(s32[4]{0:T(128)} %pad_add_fusion.flags, f32[4,384,128]{2,1,0:T(8,128)} %get-tuple-element.33.keep_ref, f32[4,384,128]{2,1,0:T(8,128)} %copy-done, f32[2,256,128]{2,1,0:T(8,128)} %get-tuple-element.43.refs_0_, f32[2,256,128]{2,1,0:T(8,128)} %copy-done.4), custom_call_target="tpu_custom_call" | custom-call | tf_op jit(solution)/shard_map/down0/pallas_call | solution.py:357
  86.6 5.7 %collective-permute-start.10 = (f32[4,256,128]{2,1,0:T(8,128)}, f32[4,256,128]{2,1,0:T(8,128)S(1)}, u32[]{:S(2)}, u32[]{:S(2)}) collective-permute-start(f32[4,256,128]{2,1,0:T(8,128)} %get-tuple-element.45), channel_id=1, source_target_pairs={{0,1},{1,0},{2,3},{3,2},{4,5},{5,4},{6,7},{7,6},{8,9},{9,8},{10,11... | collective-permute-start | bytes 1572872 | tf_op jit(solution)/shard_map/ppermute | solution.py:394
  92.3 6.0 %back0.1 = (bf16[128,1024]{1,0:T(8,128)(2,1)}, f32[128,512]{1,0:T(8,128)}, f32[8,512]{1,0:T(8,128)}, f32[8,128]{1,0:T(8,128)}, f32[8,128]{1,0:T(8,128)}) custom-call(s32[4]{0:T(128)} %pad_add_fusion.flags, bf16[128,1024]{1,0:T(8,128)(2,1)} %x_ref.11, bf16[128,1024]{1,0:T(8,128)(2,1)} %go_ref.9, f32[3,4,1024]{2,1,0:T(4,128)} %kern_ref.7, ...), custom_call_target="tpu_custom_call" | custom-call | tf_op jit(solution)/shard_map/back0/pallas_call | solution.py:428
  98.4 1.9 %collective-permute-start.15 = (f32[8,512]{1,0:T(8,128)}, f32[8,512]{1,0:T(8,128)S(1)}, u32[]{:S(2)}, u32[]{:S(2)}) collective-permute-start(f32[8,512]{1,0:T(8,128)} %get-tuple-element.57), channel_id=1, source_target_pairs={{1,0},{2,1},{3,2},{4,3},{5,4},{6,5},{7,6},{8,7},{9,8},{10,9},{11,1... | collective-permute-start | bytes 49160 | tf_op jit(solution)/shard_map/ppermute | solution.py:391
  100.3 0.0 collective-permute-done.10.state_ref
  100.3 0.8 copy-done.3
  101.1 6.0 %back1.1 = (bf16[128,1024]{1,0:T(8,128)(2,1)}, f32[128,512]{1,0:T(8,128)}, f32[8,512]{1,0:T(8,128)}, f32[8,128]{1,0:T(8,128)}, f32[8,128]{1,0:T(8,128)}) custom-call(s32[4]{0:T(128)} %pad_add_fusion.flags, bf16[128,1024]{1,0:T(8,128)(2,1)} %x_ref.11, bf16[128,1024]{1,0:T(8,128)(2,1)} %go_ref.9, ...), custom_call_target="tpu_custom_call", output_to_operand_aliasing={{0}: (8, {})} | custom-call | tf_op jit(solution)/shard_map/back1/pallas_call | solution.py:428
  107.1 4.1 %collective-permute-start.14 = (f32[8,512]{1,0:T(8,128)}, f32[8,512]{1,0:T(8,128)S(1)}, u32[]{:S(2)}, u32[]{:S(2)}) collective-permute-start(f32[8,512]{1,0:T(8,128)} %get-tuple-element.56), channel_id=1, source_target_pairs={{1,0},{2,1},{3,2},{4,3},{5,4},{6,5},{7,6},{8,7},{9,8},{10,9},{11,1... | collective-permute-start | bytes 49160 | tf_op jit(solution)/shard_map/ppermute | solution.py:391
  111.2 0.0 copy-done.11
  111.3 0.7 add.36
  111.9 0.2 collective-permute-start.11
  112.2 0.7 add.38
  112.9 3.3 %collective-permute-start.13 = (f32[8,128]{1,0:T(8,128)S(1)}, f32[8,128]{1,0:T(8,128)S(1)}, u32[]{:S(2)}, u32[]{:S(2)}) collective-permute-start(f32[8,128]{1,0:T(8,128)S(1)} %add.38), channel_id=1, source_target_pairs={{1,16},{2,17},{3,18},{4,19},{5,20},{6,21},{7,22},{8,23},{9,24},{10... | collective-permute-start | bytes 12296 | tf_op jit(solution)/shard_map/ppermute | solution.py:391
  116.2 1.9 %collective-permute-start.12 = (f32[8,128]{1,0:T(8,128)S(1)}, f32[8,128]{1,0:T(8,128)S(1)}, u32[]{:S(2)}, u32[]{:S(2)}) collective-permute-start(f32[8,128]{1,0:T(8,128)S(1)} %add.38), channel_id=1, source_target_pairs={{1,0},{2,1},{3,2},{4,3},{5,4},{6,5},{7,6},{8,7},{9,8},{10,9},{11,1... | collective-permute-start | bytes 12296 | tf_op jit(solution)/shard_map/ppermute | solution.py:391
  118.1 0.0 collective-permute-done.11
  118.1 0.6 add.37.inner_ref
  118.7 0.0 collective-permute-done.13
  118.7 2.4 %collective-permute-done.12 = f32[8,128]{1,0:T(8,128)S(1)} collective-permute-done((f32[8,128]{1,0:T(8,128)S(1)}, f32[8,128]{1,0:T(8,128)S(1)}, u32[]{:S(2)}, u32[]{:S(2)}) %collective-permute-start.12) | collective-permute-done | bytes 4128 | tf_op jit(solution)/shard_map/ppermute | solution.py:391
  121.1 0.6 add.39.next_sums_ref
  121.7 0.0 collective-permute-done.15.refs_3_
  121.7 0.0 collective-permute-done.14.refs_2_
  121.7 0.6 copy-done.8
  122.3 0.0 copy-done.9
  122.3 2.2 %finish.1 = bf16[128,1024]{1,0:T(8,128)(2,1)} custom-call(s32[4]{0:T(128)} %pad_add_fusion.flags, bf16[128,1024]{1,0:T(8,128)(2,1)} %x_ref.11, bf16[128,1024]{1,0:T(8,128)(2,1)} %go_ref.9, f32[8,128]{1,0:T(8,128)} %add_rsqrt_fusion.scale_ref, f32[8,128]{1,0:T(8,128)} %add.37.inner_ref, f32[8,128]{1,0:T(8,128)} %add.39.next_sums_ref, ...), custom_call_target="tpu_custom_call" | custom-call | tf_op jit(solution)/shard_map/finish/pallas_call | solution.py:357
  (13 shorter events, 0.0 us)
Async XLA Ops:
  2.5 11.1 %collective-permute-start.2 = (f32[8,128]{1,0:T(8,128)}, f32[8,128]{1,0:T(8,128)S(1)}, u32[]{:S(2)}, u32[]{:S(2)}) collective-permute-start(f32[8,128]{1,0:T(8,128)} %get-tuple-element.31), channel_id=1, source_target_pairs={{0,17},{1,18},{2,19},{3,20},{4,21},{5,22},{6,23},{7,24},{8,25},{9,... | collective-permute-start | bytes 12296 | tf_op jit(solution)/shard_map/ppermute | solution.py:391
  6.2 5.6 %collective-permute-start.1 = (f32[8,128]{1,0:T(8,128)}, f32[8,128]{1,0:T(8,128)S(1)}, u32[]{:S(2)}, u32[]{:S(2)}) collective-permute-start(f32[8,128]{1,0:T(8,128)} %get-tuple-element.31), channel_id=1, source_target_pairs={{0,16},{1,17},{2,18},{3,19},{4,20},{5,21},{6,22},{7,23},{8,24},{9,... | collective-permute-start | bytes 12296 | tf_op jit(solution)/shard_map/ppermute | solution.py:391
  7.5 5.6 %collective-permute-start = (f32[8,1152]{1,0:T(8,128)}, f32[8,1152]{1,0:T(8,128)S(1)}, u32[]{:S(2)}, u32[]{:S(2)}) collective-permute-start(f32[8,1152]{1,0:T(8,128)} %get-tuple-element.30), channel_id=1, source_target_pairs={{0,1},{1,2},{2,3},{3,4},{4,5},{5,6},{6,7},{7,8},{8,9},{9,10},{10,1... | collective-permute-start | bytes 110600 | tf_op jit(solution)/shard_map/ppermute | solution.py:391
  23.2 9.2 %collective-permute-start.3 = (f32[4,384,128]{2,1,0:T(8,128)}, f32[4,384,128]{2,1,0:T(8,128)S(1)}, u32[]{:S(2)}, u32[]{:S(2)}) collective-permute-start(f32[4,384,128]{2,1,0:T(8,128)} %get-tuple-element.34), channel_id=1, source_target_pairs={{0,1},{1,0},{2,3},{3,2},{4,5},{5,4},{6,7},{7,6},{8,9},{9,8},{10,11... | collective-permute-start | bytes 2359304 | tf_op jit(solution)/shard_map/ppermute | solution.py:394
  32.4 1.0 copy-start
  36.0 10.6 %collective-permute-start.4 = (f32[2,384,128]{2,1,0:T(8,128)}, f32[2,384,128]{2,1,0:T(8,128)S(1)}, u32[]{:S(2)}, u32[]{:S(2)}) collective-permute-start(f32[2,384,128]{2,1,0:T(8,128)} %get-tuple-element.36), channel_id=1, source_target_pairs={{0,2},{1,3},{2,0},{3,1},{4,6},{5,7},{6,4},{7,5},{8,10},{9,11},{10,... | collective-permute-start | bytes 1179656 | tf_op jit(solution)/shard_map/ppermute | solution.py:394
  46.6 0.8 copy-start.1
  49.5 5.5 %collective-permute-start.5 = (f32[1,384,128]{2,1,0:T(8,128)}, f32[1,384,128]{2,1,0:T(8,128)S(1)}, u32[]{:S(2)}, u32[]{:S(2)}) collective-permute-start(f32[1,384,128]{2,1,0:T(8,128)} %get-tuple-element.38), channel_id=1, source_target_pairs={{0,4},{1,5},{2,6},{3,7},{4,0},{5,1},{6,2},{7,3},{8,12},{9,13},{10,... | collective-permute-start | bytes 589832 | tf_op jit(solution)/shard_map/ppermute | solution.py:394
  55.0 0.7 copy-start.2
  57.6 6.3 %collective-permute-start.6 = (f32[1,128,128]{2,1,0:T(8,128)}, f32[1,128,128]{2,1,0:T(8,128)S(1)}, u32[]{:S(2)}, u32[]{:S(2)}) collective-permute-start(f32[1,128,128]{2,1,0:T(8,128)} %get-tuple-element.39), channel_id=1, source_target_pairs={{0,8},{1,9},{2,10},{3,11},{4,12},{5,13},{6,14},{7,15},{16,24},{17,... | collective-permute-start | bytes 196616 | tf_op jit(solution)/shard_map/ppermute | solution.py:397
  61.9 6.1 %collective-permute-start.7 = (f32[1,128,128]{2,1,0:T(8,128)}, f32[1,128,128]{2,1,0:T(8,128)S(1)}, u32[]{:S(2)}, u32[]{:S(2)}) collective-permute-start(f32[1,128,128]{2,1,0:T(8,128)} %get-tuple-element.40), channel_id=1, source_target_pairs={{8,0},{9,1},{10,2},{11,3},{12,4},{13,5},{14,6},{15,7},{24,16},{25,... | collective-permute-start | bytes 196616 | tf_op jit(solution)/shard_map/ppermute | solution.py:397
  64.0 4.0 %copy-start.6 = (f32[1,128,128]{2,1,0:T(8,128)}, f32[1,128,128]{2,1,0:T(8,128)S(1)}, u32[]{:S(2)}) copy-start(f32[1,128,128]{2,1,0:T(8,128)S(1)} %collective-permute-done.6.refs_0_) | copy-start | bytes 196612
  68.0 0.6 copy-start.7
  70.6 4.0 %collective-permute-start.8 = (f32[1,256,128]{2,1,0:T(8,128)}, f32[1,256,128]{2,1,0:T(8,128)S(1)}, u32[]{:S(2)}, u32[]{:S(2)}) collective-permute-start(f32[1,256,128]{2,1,0:T(8,128)} %get-tuple-element.42), channel_id=1, source_target_pairs={{0,4},{1,5},{2,6},{3,7},{4,0},{5,1},{6,2},{7,3},{8,12},{9,13},{10,... | collective-permute-start | bytes 393224 | tf_op jit(solution)/shard_map/ppermute | solution.py:394
  74.6 0.7 copy-start.5
  77.6 5.4 %collective-permute-start.9 = (f32[2,256,128]{2,1,0:T(8,128)}, f32[2,256,128]{2,1,0:T(8,128)S(1)}, u32[]{:S(2)}, u32[]{:S(2)}) collective-permute-start(f32[2,256,128]{2,1,0:T(8,128)} %get-tuple-element.44), channel_id=1, source_target_pairs={{0,2},{1,3},{2,0},{3,1},{4,6},{5,7},{6,4},{7,5},{8,10},{9,11},{10,... | collective-permute-start | bytes 786440 | tf_op jit(solution)/shard_map/ppermute | solution.py:394
  83.0 0.7 copy-start.4
  86.6 13.7 %collective-permute-start.10 = (f32[4,256,128]{2,1,0:T(8,128)}, f32[4,256,128]{2,1,0:T(8,128)S(1)}, u32[]{:S(2)}, u32[]{:S(2)}) collective-permute-start(f32[4,256,128]{2,1,0:T(8,128)} %get-tuple-element.45), channel_id=1, source_target_pairs={{0,1},{1,0},{2,3},{3,2},{4,5},{5,4},{6,7},{7,6},{8,9},{9,8},{10,11... | collective-permute-start | bytes 1572872 | tf_op jit(solution)/shard_map/ppermute | solution.py:394
  98.4 12.9 %copy-start.11 = (f32[8,128]{1,0:T(8,128)S(1)}, f32[8,128]{1,0:T(8,128)}, u32[]{:S(2)}) copy-start(f32[8,128]{1,0:T(8,128)} %get-tuple-element.50) | copy-start | bytes 12292
  98.4 13.8 %copy-start.10 = (f32[8,128]{1,0:T(8,128)S(1)}, f32[8,128]{1,0:T(8,128)}, u32[]{:S(2)}) copy-start(f32[8,128]{1,0:T(8,128)} %get-tuple-element.52) | copy-start | bytes 12292
  98.4 23.3 %collective-permute-start.15 = (f32[8,512]{1,0:T(8,128)}, f32[8,512]{1,0:T(8,128)S(1)}, u32[]{:S(2)}, u32[]{:S(2)}) collective-permute-start(f32[8,512]{1,0:T(8,128)} %get-tuple-element.57), channel_id=1, source_target_pairs={{1,0},{2,1},{3,2},{4,3},{5,4},{6,5},{7,6},{8,7},{9,8},{10,9},{11,1... | collective-permute-start | bytes 49160 | tf_op jit(solution)/shard_map/ppermute | solution.py:391
  100.3 0.8 copy-start.3
  107.1 14.6 %collective-permute-start.14 = (f32[8,512]{1,0:T(8,128)}, f32[8,512]{1,0:T(8,128)S(1)}, u32[]{:S(2)}, u32[]{:S(2)}) collective-permute-start(f32[8,512]{1,0:T(8,128)} %get-tuple-element.56), channel_id=1, source_target_pairs={{1,0},{2,1},{3,2},{4,3},{5,4},{6,5},{7,6},{8,7},{9,8},{10,9},{11,1... | collective-permute-start | bytes 49160 | tf_op jit(solution)/shard_map/ppermute | solution.py:391
  111.9 6.2 %collective-permute-start.11 = (f32[8,128]{1,0:T(8,128)S(1)}, f32[8,128]{1,0:T(8,128)S(1)}, u32[]{:S(2)}, u32[]{:S(2)}) collective-permute-start(f32[8,128]{1,0:T(8,128)S(1)} %add.36), channel_id=1, source_target_pairs={{0,16},{1,17},{2,18},{3,19},{4,20},{5,21},{6,22},{7,23},{8,24},{9,... | collective-permute-start | bytes 12296 | tf_op jit(solution)/shard_map/ppermute | solution.py:391
  112.9 5.8 %collective-permute-start.13 = (f32[8,128]{1,0:T(8,128)S(1)}, f32[8,128]{1,0:T(8,128)S(1)}, u32[]{:S(2)}, u32[]{:S(2)}) collective-permute-start(f32[8,128]{1,0:T(8,128)S(1)} %add.38), channel_id=1, source_target_pairs={{1,16},{2,17},{3,18},{4,19},{5,20},{6,21},{7,22},{8,23},{9,24},{10... | collective-permute-start | bytes 12296 | tf_op jit(solution)/shard_map/ppermute | solution.py:391
  116.2 4.9 %collective-permute-start.12 = (f32[8,128]{1,0:T(8,128)S(1)}, f32[8,128]{1,0:T(8,128)S(1)}, u32[]{:S(2)}, u32[]{:S(2)}) collective-permute-start(f32[8,128]{1,0:T(8,128)S(1)} %add.38), channel_id=1, source_target_pairs={{1,0},{2,1},{3,2},{4,3},{5,4},{6,5},{7,6},{8,7},{9,8},{10,9},{11,1... | collective-permute-start | bytes 12296 | tf_op jit(solution)/shard_map/ppermute | solution.py:391
  121.7 0.6 copy-start.8
  121.7 0.6 copy-start.9

commit v2 on v1

--- a/solution.py
+++ b/solution.py
@@ -13,7 +13,7 @@
 norm_eps = 1e-05
 f32 = jnp.float32
 bf16 = jnp.bfloat16
-VMEM_LIMIT = 56 * 1024 * 1024
+VMEM_LIMIT = 24 * 1024 * 1024
 
 DIMS = {
     "nn": (((1,), (0,)), ((), ())),

time: 125 us -> 99.1 us (0.79)
  the two profiles are of different devices: /device:TPU:11 before, /device:TPU:13 now
where the time goes in v2:
time: 99.1 us; the launch traced here: 98.6 us
  starting transfers between devices  34 us (34%)
  waiting for transfers between devices  31.3 us (32%)
  Pallas kernels  26.9 us (27%)
  local copies, waits for them, and re-layouts  5.49 us (6%)
    ppermute x6, waiting for transfers between devices, swapped(): lax.ppermute(value, 'ctx', [(i, i ^ 1 << level) for i in range(spots)])  22.8 us
    pallas_call x4, Pallas kernels, grid_call(): pl.pallas_call(kernel, grid_spec=pltpu.PrefetchScalarGridSpec(num_scalar_...  19.3 us
    ppermute x8, starting transfers between devices, turned(): return lax.ppermute(value, ('section', 'ctx'), route)  18.1 us
    ppermute x6, starting transfers between devices, swapped(): lax.ppermute(value, 'ctx', [(i, i ^ 1 << level) for i in range(spots)])  10.3 us
    pallas_call x7, Pallas kernels, whole_call(): pl.pallas_call(kernel, out_shape=outs, in_specs=[pl.BlockSpec(memory_spac...  7.31 us
    ppermute x2, starting transfers between devices, moved(): lax.ppermute(value, 'ctx', [(i, i + shift) for i in range(spots) if 0 <=...  5.68 us
    unnamed x17, local copies, waits for them, and re-layouts  5.49 us
    ppermute x2, waiting for transfers between devices, moved(): lax.ppermute(value, 'ctx', [(i, i + shift) for i in range(spots) if 0 <=...  4.43 us
  transfers between devices with their start and end apart: 16, of which 9 were waited for; matrix products, arithmetic and copies ran while one was open for 1% of the time, Pallas kernels for 13%

profile of v2, /device:TPU:13, one launch (start us, length us, event | category | flops | bytes accessed | tf_op | source)
XLA Modules:
  0.0 98.6 jit_solution(7845660038660335869)
XLA Ops:
  0.6 0.0 copy-start
  0.6 0.9 copy-done
  1.6 0.3 prelude.1
  1.9 4.6 %collective-permute-start.2 = (f32[8,128]{1,0:T(8,128)S(1)}, f32[8,128]{1,0:T(8,128)S(1)}, u32[]{:S(2)}, u32[]{:S(2)}) collective-permute-start(f32[8,128]{1,0:T(8,128)S(1)} %get-tuple-element.31), channel_id=1, source_target_pairs={{0,17},{1,18},{2,19},{3,20},{4,21},{5,22},{6,23},{7,24},{8,25},{9,... | collective-permute-start | bytes 12296 | tf_op jit(solution)/shard_map/ppermute | solution.py:391
  6.5 0.3 collective-permute-start.1
  6.9 2.2 %collective-permute-start = (f32[8,1152]{1,0:T(8,128)S(1)}, f32[8,1152]{1,0:T(8,128)S(1)}, u32[]{:S(2)}, u32[]{:S(2)}) collective-permute-start(f32[8,1152]{1,0:T(8,128)S(1)} %get-tuple-element.30), channel_id=1, source_target_pairs={{0,1},{1,2},{2,3},{3,4},{4,5},{5,6},{6,7},{7,8},{8,9},{9,10},{10,1... | collective-permute-start | bytes 110600 | tf_op jit(solution)/shard_map/ppermute | solution.py:391
  9.1 0.1 pad_add_fusion.flags
  9.2 0.8 copy.11.beta_ref
  10.0 0.0 collective-permute-done.1
  10.0 0.1 collective-permute-done
  10.1 0.0 collective-permute-done.2
  10.2 0.0 copy-start.1
  10.2 0.9 copy-done.1
  11.1 0.0 copy-start.3
  11.1 0.9 copy-done.3
  12.1 0.0 copy-start.5
  12.1 1.0 %copy-done.5 = f32[128,1024]{1,0:T(8,128)S(1)} copy-done((f32[128,1024]{1,0:T(8,128)S(1)}, f32[128,1024]{1,0:T(8,128)}, u32[]{:S(2)}) %copy-start.5) | copy-done | bytes 524312
  13.1 0.0 copy-start.6
  13.1 0.8 copy-done.6
  13.9 6.0 %local1.1 = (f32[4,384,128]{2,1,0:T(8,128)S(1)}, f32[4,14,128,128]{3,2,1,0:T(8,128)S(1)}) custom-call(s32[4]{0:T(128)S(1)} %pad_add_fusion.flags, bf16[128,1024]{1,0:T(8,128)(2,1)S(1)} %copy-done.1, bf16[128,1024]{1,0:T(8,128)(2,1)S(1)} %copy-done.3, f32[3,4,1024]{2,1,0:T(4,128)S(1)} %copy-done.6, f32[128,1024]{1,0:T(8,128)S(1)} %copy-done.5, ...), custom_call_target="tpu_custom_call" | custom-call | tf_op jit(solution)/shard_map/local1/pallas_call | solution.py:428
  19.9 0.0 copy-start.2
  19.9 0.0 copy-start.4
  20.0 0.0 copy-start.7
  20.0 1.3 %collective-permute-start.3 = (f32[4,384,128]{2,1,0:T(8,128)S(1)}, f32[4,384,128]{2,1,0:T(8,128)S(1)}, u32[]{:S(2)}, u32[]{:S(2)}) collective-permute-start(f32[4,384,128]{2,1,0:T(8,128)S(1)} %get-tuple-element.34), channel_id=1, source_target_pairs={{0,1},{1,0},{2,3},{3,2},{4,5},{5,4},{6,7},{7,6},{8,9},{9,8},{10,11... | collective-permute-start | bytes 2359304 | tf_op jit(solution)/shard_map/ppermute | solution.py:394
  21.2 6.0 %local0.1 = (f32[4,384,128]{2,1,0:T(8,128)S(1)}, f32[4,14,128,128]{3,2,1,0:T(8,128)S(1)}) custom-call(s32[4]{0:T(128)S(1)} %pad_add_fusion.flags, bf16[128,1024]{1,0:T(8,128)(2,1)S(1)} %copy-done.1, bf16[128,1024]{1,0:T(8,128)(2,1)S(1)} %copy-done.3, f32[3,4,1024]{2,1,0:T(4,128)S(1)} %copy-done.6, f32[128,1024]{1,0:T(8,128)S(1)} %copy-done.5, ...), custom_call_target="tpu_custom_call" | custom-call | tf_op jit(solution)/shard_map/local0/pallas_call | solution.py:428
  27.3 0.0 collective-permute-done.3.recv_ref
  27.3 1.0 %compose0.1 = (f32[2,384,128]{2,1,0:T(8,128)S(1)}, f32[2,384,128]{2,1,0:T(8,128)S(1)}) custom-call(s32[4]{0:T(128)S(1)} %pad_add_fusion.flags, f32[4,384,128]{2,1,0:T(8,128)S(1)} %get-tuple-element.33.keep_ref, f32[4,384,128]{2,1,0:T(8,128)S(1)} %collective-permute-done.3.recv_ref), custom_call_target="tpu_custom_call" | custom-call | tf_op jit(solution)/shard_map/compose0/pallas_call | solution.py:357
  28.3 1.2 %collective-permute-start.4 = (f32[2,384,128]{2,1,0:T(8,128)S(1)}, f32[2,384,128]{2,1,0:T(8,128)S(1)}, u32[]{:S(2)}, u32[]{:S(2)}) collective-permute-start(f32[2,384,128]{2,1,0:T(8,128)S(1)} %get-tuple-element.36), channel_id=1, source_target_pairs={{0,2},{1,3},{2,0},{3,1},{4,6},{5,7},{6,4},{7,5},{8,10},{9,11},{10,... | collective-permute-start | bytes 1179656 | tf_op jit(solution)/shard_map/ppermute | solution.py:394
  29.5 9.6 %collective-permute-done.4.recv_ref = f32[2,384,128]{2,1,0:T(8,128)S(1)} collective-permute-done((f32[2,384,128]{2,1,0:T(8,128)S(1)}, f32[2,384,128]{2,1,0:T(8,128)S(1)}, u32[]{:S(2)}, u32[]{:S(2)}) %collective-permute-start.4) | collective-permute-done | bytes 393248 | tf_op jit(solution)/shard_map/ppermute | solution.py:394
  39.1 0.9 compose1.1
  40.0 0.2 collective-permute-start.5
  40.2 5.5 %collective-permute-done.5.recv_ref = f32[1,384,128]{2,1,0:T(8,128)S(1)} collective-permute-done((f32[1,384,128]{2,1,0:T(8,128)S(1)}, f32[1,384,128]{2,1,0:T(8,128)S(1)}, u32[]{:S(2)}, u32[]{:S(2)}) %collective-permute-start.5) | collective-permute-done | bytes 196640 | tf_op jit(solution)/shard_map/ppermute | solution.py:394
  45.7 1.4 %compose2.1 = (f32[1,128,128]{2,1,0:T(8,128)}, f32[1,128,128]{2,1,0:T(8,128)S(1)}, f32[1,128,128]{2,1,0:T(8,128)S(1)}) custom-call(s32[4]{0:T(128)S(1)} %pad_add_fusion.flags, f32[1,384,128]{2,1,0:T(8,128)S(1)} %get-tuple-element.37.keep_ref, f32[1,384,128]{2,1,0:T(8,128)S(1)} %collective-permute-done.5.recv_ref), custom_call_target="tpu_custom_call" | custom-call | tf_op jit(solution)/shard_map/compose2/pallas_call | solution.py:357
  47.0 4.2 %collective-permute-start.6 = (f32[1,128,128]{2,1,0:T(8,128)S(1)}, f32[1,128,128]{2,1,0:T(8,128)S(1)}, u32[]{:S(2)}, u32[]{:S(2)}) collective-permute-start(f32[1,128,128]{2,1,0:T(8,128)S(1)} %get-tuple-element.39), channel_id=1, source_target_pairs={{0,8},{1,9},{2,10},{3,11},{4,12},{5,13},{6,14},{7,15},{16,24},{17,... | collective-permute-start | bytes 196616 | tf_op jit(solution)/shard_map/ppermute | solution.py:397
  51.3 1.5 %collective-permute-start.7 = (f32[1,128,128]{2,1,0:T(8,128)S(1)}, f32[1,128,128]{2,1,0:T(8,128)S(1)}, u32[]{:S(2)}, u32[]{:S(2)}) collective-permute-start(f32[1,128,128]{2,1,0:T(8,128)S(1)} %get-tuple-element.40), channel_id=1, source_target_pairs={{8,0},{9,1},{10,2},{11,3},{12,4},{13,5},{14,6},{15,7},{24,16},{25,... | collective-permute-start | bytes 196616 | tf_op jit(solution)/shard_map/ppermute | solution.py:397
  52.7 0.3 collective-permute-done.6.refs_0_
  53.0 4.1 %collective-permute-done.7.refs_1_ = f32[1,128,128]{2,1,0:T(8,128)S(1)} collective-permute-done((f32[1,128,128]{2,1,0:T(8,128)S(1)}, f32[1,128,128]{2,1,0:T(8,128)S(1)}, u32[]{:S(2)}, u32[]{:S(2)}) %collective-permute-start.7) | collective-permute-done | bytes 65568 | tf_op jit(solution)/shard_map/ppermute | solution.py:397
  57.2 0.8 down2.1
  57.9 0.2 collective-permute-start.8
  58.2 3.6 %collective-permute-done.8.refs_1_ = f32[1,256,128]{2,1,0:T(8,128)S(1)} collective-permute-done((f32[1,256,128]{2,1,0:T(8,128)S(1)}, f32[1,256,128]{2,1,0:T(8,128)S(1)}, u32[]{:S(2)}, u32[]{:S(2)}) %collective-permute-start.8) | collective-permute-done | bytes 131104 | tf_op jit(solution)/shard_map/ppermute | solution.py:394
  61.8 0.8 down1.1
  62.6 1.2 %collective-permute-start.9 = (f32[2,256,128]{2,1,0:T(8,128)S(1)}, f32[2,256,128]{2,1,0:T(8,128)S(1)}, u32[]{:S(2)}, u32[]{:S(2)}) collective-permute-start(f32[2,256,128]{2,1,0:T(8,128)S(1)} %get-tuple-element.44), channel_id=1, source_target_pairs={{0,2},{1,3},{2,0},{3,1},{4,6},{5,7},{6,4},{7,5},{8,10},{9,11},{10,... | collective-permute-start | bytes 786440 | tf_op jit(solution)/shard_map/ppermute | solution.py:394
  63.8 4.1 %collective-permute-done.9.refs_1_ = f32[2,256,128]{2,1,0:T(8,128)S(1)} collective-permute-done((f32[2,256,128]{2,1,0:T(8,128)S(1)}, f32[2,256,128]{2,1,0:T(8,128)S(1)}, u32[]{:S(2)}, u32[]{:S(2)}) %collective-permute-start.9) | collective-permute-done | bytes 262176 | tf_op jit(solution)/shard_map/ppermute | solution.py:394
  67.9 0.9 down0.1
  68.9 6.2 %collective-permute-start.10 = (f32[4,256,128]{2,1,0:T(8,128)S(1)}, f32[4,256,128]{2,1,0:T(8,128)S(1)}, u32[]{:S(2)}, u32[]{:S(2)}) collective-permute-start(f32[4,256,128]{2,1,0:T(8,128)S(1)} %get-tuple-element.45), channel_id=1, source_target_pairs={{0,1},{1,0},{2,3},{3,2},{4,5},{5,4},{6,7},{7,6},{8,9},{9,8},{10,11... | collective-permute-start | bytes 1572872 | tf_op jit(solution)/shard_map/ppermute | solution.py:394
  75.1 0.0 copy-done.2
  75.1 0.0 copy-done.4
  75.1 0.0 copy-done.7
  75.1 3.6 %back0.1 = (bf16[128,1024]{1,0:T(8,128)(2,1)}, f32[128,512]{1,0:T(8,128)S(1)}, f32[8,512]{1,0:T(8,128)S(1)}, f32[8,128]{1,0:T(8,128)S(1)}, f32[8,128]{1,0:T(8,128)S(1)}) custom-call(s32[4]{0:T(128)S(1)} %pad_add_fusion.flags, bf16[128,1024]{1,0:T(8,128)(2,1)S(1)} %copy-done.2, bf16[128,1024]{1,0:T(8,128)(2,1)S(1)} %copy-done.4, f32[3,4,1024]{2,1,0:T(4,128)S(1)} %copy-done.7, ...), custom_call_target="tpu_custom_call" | custom-call | tf_op jit(solution)/shard_map/back0/pallas_call | solution.py:428
  78.7 1.9 %collective-permute-start.15 = (f32[8,512]{1,0:T(8,128)S(1)}, f32[8,512]{1,0:T(8,128)S(1)}, u32[]{:S(2)}, u32[]{:S(2)}) collective-permute-start(f32[8,512]{1,0:T(8,128)S(1)} %get-tuple-element.57), channel_id=1, source_target_pairs={{1,0},{2,1},{3,2},{4,3},{5,4},{6,5},{7,6},{8,7},{9,8},{10,9},{11,1... | collective-permute-start | bytes 49160 | tf_op jit(solution)/shard_map/ppermute | solution.py:391
  80.6 0.0 collective-permute-done.10.state_ref
  80.6 3.6 %back1.1 = (bf16[128,1024]{1,0:T(8,128)(2,1)}, f32[128,512]{1,0:T(8,128)S(1)}, f32[8,512]{1,0:T(8,128)S(1)}, f32[8,128]{1,0:T(8,128)S(1)}, f32[8,128]{1,0:T(8,128)S(1)}) custom-call(s32[4]{0:T(128)S(1)} %pad_add_fusion.flags, bf16[128,1024]{1,0:T(8,128)(2,1)S(1)} %copy-done.2, bf16[128,1024]{1,0:T(8,128)(2,1)S(1)} %copy-done.4, ...), custom_call_target="tpu_custom_call", output_to_operand_aliasing={{0}: (8, {})} | custom-call | tf_op jit(solution)/shard_map/back1/pallas_call | solution.py:428
  84.2 3.4 %collective-permute-start.14 = (f32[8,512]{1,0:T(8,128)S(1)}, f32[8,512]{1,0:T(8,128)S(1)}, u32[]{:S(2)}, u32[]{:S(2)}) collective-permute-start(f32[8,512]{1,0:T(8,128)S(1)} %get-tuple-element.56), channel_id=1, source_target_pairs={{1,0},{2,1},{3,2},{4,3},{5,4},{6,5},{7,6},{8,7},{9,8},{10,9},{11,1... | collective-permute-start | bytes 49160 | tf_op jit(solution)/shard_map/ppermute | solution.py:391
  87.6 1.2 %collective-permute-start.11 = (f32[8,128]{1,0:T(8,128)S(1)}, f32[8,128]{1,0:T(8,128)S(1)}, u32[]{:S(2)}, u32[]{:S(2)}) collective-permute-start(f32[8,128]{1,0:T(8,128)S(1)} %add.36), channel_id=1, source_target_pairs={{0,16},{1,17},{2,18},{3,19},{4,20},{5,21},{6,22},{7,23},{8,24},{9,... | collective-permute-start | bytes 12296 | tf_op jit(solution)/shard_map/ppermute | solution.py:391
  88.9 2.4 %collective-permute-start.13 = (f32[8,128]{1,0:T(8,128)S(1)}, f32[8,128]{1,0:T(8,128)S(1)}, u32[]{:S(2)}, u32[]{:S(2)}) collective-permute-start(f32[8,128]{1,0:T(8,128)S(1)} %add.38), channel_id=1, source_target_pairs={{1,16},{2,17},{3,18},{4,19},{5,20},{6,21},{7,22},{8,23},{9,24},{10... | collective-permute-start | bytes 12296 | tf_op jit(solution)/shard_map/ppermute | solution.py:391
  91.3 1.9 %collective-permute-start.12 = (f32[8,128]{1,0:T(8,128)S(1)}, f32[8,128]{1,0:T(8,128)S(1)}, u32[]{:S(2)}, u32[]{:S(2)}) collective-permute-start(f32[8,128]{1,0:T(8,128)S(1)} %add.38), channel_id=1, source_target_pairs={{1,0},{2,1},{3,2},{4,3},{5,4},{6,5},{7,6},{8,7},{9,8},{10,9},{11,1... | collective-permute-start | bytes 12296 | tf_op jit(solution)/shard_map/ppermute | solution.py:391
  93.2 0.0 collective-permute-done.11
  93.2 2.4 %collective-permute-done.13 = f32[8,128]{1,0:T(8,128)S(1)} collective-permute-done((f32[8,128]{1,0:T(8,128)S(1)}, f32[8,128]{1,0:T(8,128)S(1)}, u32[]{:S(2)}, u32[]{:S(2)}) %collective-permute-start.13) | collective-permute-done | bytes 4128 | tf_op jit(solution)/shard_map/ppermute | solution.py:391
  95.6 1.5 %collective-permute-done.12 = f32[8,128]{1,0:T(8,128)S(1)} collective-permute-done((f32[8,128]{1,0:T(8,128)S(1)}, f32[8,128]{1,0:T(8,128)S(1)}, u32[]{:S(2)}, u32[]{:S(2)}) %collective-permute-start.12) | collective-permute-done | bytes 4128 | tf_op jit(solution)/shard_map/ppermute | solution.py:391
  97.1 0.0 collective-permute-done.15.refs_3_
  97.1 0.0 collective-permute-done.14.refs_2_
  97.1 1.5 %finish.1 = bf16[128,1024]{1,0:T(8,128)(2,1)} custom-call(s32[4]{0:T(128)S(1)} %pad_add_fusion.flags, bf16[128,1024]{1,0:T(8,128)(2,1)S(1)} %copy-done.2, bf16[128,1024]{1,0:T(8,128)(2,1)S(1)} %copy-done.4, f32[8,128]{1,0:T(8,128)S(1)} %add_rsqrt_fusion.scale_ref, f32[8,128]{1,0:T(8,128)S(1)} %add.37.inner_ref, f32[8,128]{1,0:T(8,128)S(1)} %add.39.next_sums_ref, ...), custom_call_target="tpu_custom_call" | custom-call | tf_op jit(solution)/shard_map/finish/pallas_call | solution.py:357
  (7 shorter events, 0.0 us)
Async XLA Ops:
  0.6 1.0 copy-start
  1.9 8.2 %collective-permute-start.2 = (f32[8,128]{1,0:T(8,128)S(1)}, f32[8,128]{1,0:T(8,128)S(1)}, u32[]{:S(2)}, u32[]{:S(2)}) collective-permute-start(f32[8,128]{1,0:T(8,128)S(1)} %get-tuple-element.31), channel_id=1, source_target_pairs={{0,17},{1,18},{2,19},{3,20},{4,21},{5,22},{6,23},{7,24},{8,25},{9,... | collective-permute-start | bytes 12296 | tf_op jit(solution)/shard_map/ppermute | solution.py:391
  6.5 3.4 %collective-permute-start.1 = (f32[8,128]{1,0:T(8,128)S(1)}, f32[8,128]{1,0:T(8,128)S(1)}, u32[]{:S(2)}, u32[]{:S(2)}) collective-permute-start(f32[8,128]{1,0:T(8,128)S(1)} %get-tuple-element.31), channel_id=1, source_target_pairs={{0,16},{1,17},{2,18},{3,19},{4,20},{5,21},{6,22},{7,23},{8,24},{9,... | collective-permute-start | bytes 12296 | tf_op jit(solution)/shard_map/ppermute | solution.py:391
  6.9 3.3 %collective-permute-start = (f32[8,1152]{1,0:T(8,128)S(1)}, f32[8,1152]{1,0:T(8,128)S(1)}, u32[]{:S(2)}, u32[]{:S(2)}) collective-permute-start(f32[8,1152]{1,0:T(8,128)S(1)} %get-tuple-element.30), channel_id=1, source_target_pairs={{0,1},{1,2},{2,3},{3,4},{4,5},{5,6},{6,7},{7,8},{8,9},{9,10},{10,1... | collective-permute-start | bytes 110600 | tf_op jit(solution)/shard_map/ppermute | solution.py:391
  10.2 1.0 copy-start.1
  11.1 0.9 copy-start.3
  12.1 1.0 %copy-start.5 = (f32[128,1024]{1,0:T(8,128)S(1)}, f32[128,1024]{1,0:T(8,128)}, u32[]{:S(2)}) copy-start(f32[128,1024]{1,0:T(8,128)} %decay_ref.3) | copy-start | bytes 1572868
  13.1 0.8 copy-start.6
  19.9 55.1 %copy-start.2 = (bf16[128,1024]{1,0:T(8,128)(2,1)S(1)}, bf16[128,1024]{1,0:T(8,128)(2,1)}, u32[]{:S(2)}) copy-start(bf16[128,1024]{1,0:T(8,128)(2,1)} %x_ref.11) | copy-start | bytes 786436
  19.9 55.1 %copy-start.4 = (bf16[128,1024]{1,0:T(8,128)(2,1)S(1)}, bf16[128,1024]{1,0:T(8,128)(2,1)}, u32[]{:S(2)}) copy-start(bf16[128,1024]{1,0:T(8,128)(2,1)} %go_ref.9) | copy-start | bytes 786436
  20.0 55.1 %copy-start.7 = (f32[3,4,1024]{2,1,0:T(4,128)S(1)}, f32[3,4,1024]{2,1,0:T(4,128)}, u32[]{:S(2)}) copy-start(f32[3,4,1024]{2,1,0:T(4,128)} %kern_ref.7) | copy-start | bytes 147460
  20.0 7.3 %collective-permute-start.3 = (f32[4,384,128]{2,1,0:T(8,128)S(1)}, f32[4,384,128]{2,1,0:T(8,128)S(1)}, u32[]{:S(2)}, u32[]{:S(2)}) collective-permute-start(f32[4,384,128]{2,1,0:T(8,128)S(1)} %get-tuple-element.34), channel_id=1, source_target_pairs={{0,1},{1,0},{2,3},{3,2},{4,5},{5,4},{6,7},{7,6},{8,9},{9,8},{10,11... | collective-permute-start | bytes 2359304 | tf_op jit(solution)/shard_map/ppermute | solution.py:394
  28.3 10.8 %collective-permute-start.4 = (f32[2,384,128]{2,1,0:T(8,128)S(1)}, f32[2,384,128]{2,1,0:T(8,128)S(1)}, u32[]{:S(2)}, u32[]{:S(2)}) collective-permute-start(f32[2,384,128]{2,1,0:T(8,128)S(1)} %get-tuple-element.36), channel_id=1, source_target_pairs={{0,2},{1,3},{2,0},{3,1},{4,6},{5,7},{6,4},{7,5},{8,10},{9,11},{10,... | collective-permute-start | bytes 1179656 | tf_op jit(solution)/shard_map/ppermute | solution.py:394
  40.0 5.7 %collective-permute-start.5 = (f32[1,384,128]{2,1,0:T(8,128)S(1)}, f32[1,384,128]{2,1,0:T(8,128)S(1)}, u32[]{:S(2)}, u32[]{:S(2)}) collective-permute-start(f32[1,384,128]{2,1,0:T(8,128)S(1)} %get-tuple-element.38), channel_id=1, source_target_pairs={{0,4},{1,5},{2,6},{3,7},{4,0},{5,1},{6,2},{7,3},{8,12},{9,13},{10,... | collective-permute-start | bytes 589832 | tf_op jit(solution)/shard_map/ppermute | solution.py:394
  47.0 6.0 %collective-permute-start.6 = (f32[1,128,128]{2,1,0:T(8,128)S(1)}, f32[1,128,128]{2,1,0:T(8,128)S(1)}, u32[]{:S(2)}, u32[]{:S(2)}) collective-permute-start(f32[1,128,128]{2,1,0:T(8,128)S(1)} %get-tuple-element.39), channel_id=1, source_target_pairs={{0,8},{1,9},{2,10},{3,11},{4,12},{5,13},{6,14},{7,15},{16,24},{17,... | collective-permute-start | bytes 196616 | tf_op jit(solution)/shard_map/ppermute | solution.py:397
  51.3 5.9 %collective-permute-start.7 = (f32[1,128,128]{2,1,0:T(8,128)S(1)}, f32[1,128,128]{2,1,0:T(8,128)S(1)}, u32[]{:S(2)}, u32[]{:S(2)}) collective-permute-start(f32[1,128,128]{2,1,0:T(8,128)S(1)} %get-tuple-element.40), channel_id=1, source_target_pairs={{8,0},{9,1},{10,2},{11,3},{12,4},{13,5},{14,6},{15,7},{24,16},{25,... | collective-permute-start | bytes 196616 | tf_op jit(solution)/shard_map/ppermute | solution.py:397
  57.9 3.9 %collective-permute-start.8 = (f32[1,256,128]{2,1,0:T(8,128)S(1)}, f32[1,256,128]{2,1,0:T(8,128)S(1)}, u32[]{:S(2)}, u32[]{:S(2)}) collective-permute-start(f32[1,256,128]{2,1,0:T(8,128)S(1)} %get-tuple-element.42), channel_id=1, source_target_pairs={{0,4},{1,5},{2,6},{3,7},{4,0},{5,1},{6,2},{7,3},{8,12},{9,13},{10,... | collective-permute-start | bytes 393224 | tf_op jit(solution)/shard_map/ppermute | solution.py:394
  62.6 5.3 %collective-permute-start.9 = (f32[2,256,128]{2,1,0:T(8,128)S(1)}, f32[2,256,128]{2,1,0:T(8,128)S(1)}, u32[]{:S(2)}, u32[]{:S(2)}) collective-permute-start(f32[2,256,128]{2,1,0:T(8,128)S(1)} %get-tuple-element.44), channel_id=1, source_target_pairs={{0,2},{1,3},{2,0},{3,1},{4,6},{5,7},{6,4},{7,5},{8,10},{9,11},{10,... | collective-permute-start | bytes 786440 | tf_op jit(solution)/shard_map/ppermute | solution.py:394
  68.9 11.7 %collective-permute-start.10 = (f32[4,256,128]{2,1,0:T(8,128)S(1)}, f32[4,256,128]{2,1,0:T(8,128)S(1)}, u32[]{:S(2)}, u32[]{:S(2)}) collective-permute-start(f32[4,256,128]{2,1,0:T(8,128)S(1)} %get-tuple-element.45), channel_id=1, source_target_pairs={{0,1},{1,0},{2,3},{3,2},{4,5},{5,4},{6,7},{7,6},{8,9},{9,8},{10,11... | collective-permute-start | bytes 1572872 | tf_op jit(solution)/shard_map/ppermute | solution.py:394
  78.7 18.4 %collective-permute-start.15 = (f32[8,512]{1,0:T(8,128)S(1)}, f32[8,512]{1,0:T(8,128)S(1)}, u32[]{:S(2)}, u32[]{:S(2)}) collective-permute-start(f32[8,512]{1,0:T(8,128)S(1)} %get-tuple-element.57), channel_id=1, source_target_pairs={{1,0},{2,1},{3,2},{4,3},{5,4},{6,5},{7,6},{8,7},{9,8},{10,9},{11,1... | collective-permute-start | bytes 49160 | tf_op jit(solution)/shard_map/ppermute | solution.py:391
  84.2 12.9 %collective-permute-start.14 = (f32[8,512]{1,0:T(8,128)S(1)}, f32[8,512]{1,0:T(8,128)S(1)}, u32[]{:S(2)}, u32[]{:S(2)}) collective-permute-start(f32[8,512]{1,0:T(8,128)S(1)} %get-tuple-element.56), channel_id=1, source_target_pairs={{1,0},{2,1},{3,2},{4,3},{5,4},{6,5},{7,6},{8,7},{9,8},{10,9},{11,1... | collective-permute-start | bytes 49160 | tf_op jit(solution)/shard_map/ppermute | solution.py:391
  87.6 5.6 %collective-permute-start.11 = (f32[8,128]{1,0:T(8,128)S(1)}, f32[8,128]{1,0:T(8,128)S(1)}, u32[]{:S(2)}, u32[]{:S(2)}) collective-permute-start(f32[8,128]{1,0:T(8,128)S(1)} %add.36), channel_id=1, source_target_pairs={{0,16},{1,17},{2,18},{3,19},{4,20},{5,21},{6,22},{7,23},{8,24},{9,... | collective-permute-start | bytes 12296 | tf_op jit(solution)/shard_map/ppermute | solution.py:391
  88.9 6.7 %collective-permute-start.13 = (f32[8,128]{1,0:T(8,128)S(1)}, f32[8,128]{1,0:T(8,128)S(1)}, u32[]{:S(2)}, u32[]{:S(2)}) collective-permute-start(f32[8,128]{1,0:T(8,128)S(1)} %add.38), channel_id=1, source_target_pairs={{1,16},{2,17},{3,18},{4,19},{5,20},{6,21},{7,22},{8,23},{9,24},{10... | collective-permute-start | bytes 12296 | tf_op jit(solution)/shard_map/ppermute | solution.py:391
  91.3 5.8 %collective-permute-start.12 = (f32[8,128]{1,0:T(8,128)S(1)}, f32[8,128]{1,0:T(8,128)S(1)}, u32[]{:S(2)}, u32[]{:S(2)}) collective-permute-start(f32[8,128]{1,0:T(8,128)S(1)} %add.38), channel_id=1, source_target_pairs={{1,0},{2,1},{3,2},{4,3},{5,4},{6,5},{7,6},{8,7},{9,8},{10,9},{11,1... | collective-permute-start | bytes 12296 | tf_op jit(solution)/shard_map/ppermute | solution.py:391

commit v3 on v2

v3 whole, which is shorter than its diff:
```python
import functools

import jax
import jax.numpy as jnp
from jax import lax
from jax.experimental import pallas as pl
from jax.experimental.pallas import tpu as pltpu
from jax.sharding import PartitionSpec as P

HEAD_DIM = 128
RIM = 8
epsilon = 1e-06
norm_eps = 1e-05
f32 = jnp.float32
bf16 = jnp.bfloat16
VMEM_LIMIT = 24 * 1024 * 1024

DIMS = {
    "nn": (((1,), (0,)), ((), ())),
    "nt": (((1,), (1,)), ((), ())),
    "tn": (((0,), (0,)), ((), ())),
}


def split(a):
    high = a.astype(bf16)
    return high, (a - high.astype(f32)).astype(bf16)


def exact(a):
    return a, None


def rows_of(*parts):
    highs = jnp.concatenate([p[0] for p in parts], axis=0)
    lows = [jnp.zeros_like(p[0]) if p[1] is None else p[1] for p in parts]
    return highs, jnp.concatenate(lows, axis=0)


def cols_of(*parts):
    return tuple(jnp.concatenate([p[i] for p in parts], axis=1) for i in range(2))


def mm(a, b, form):
    pairs = [(a[0], b[0])]
    if a[1] is not None:
        pairs.append((a[1], b[0]))
    if b[1] is not None:
        pairs.append((a[0], b[1]))
    left = jnp.concatenate([p[0] for p in pairs], axis=0 if form == "tn" else 1)
    right = jnp.concatenate([p[1] for p in pairs], axis=1 if form == "nt" else 0)
    return lax.dot_general(left, right, DIMS[form], preferred_element_type=f32)


def row_sums(a):
    high = a.astype(bf16)
    rest = a - high.astype(f32)
    mid = rest.astype(bf16)
    low = (rest - mid.astype(f32)).astype(bf16)
    terms = jnp.concatenate([high, mid, low], axis=1)
    ones = jnp.ones((RIM, terms.shape[1]), bf16)
    return lax.dot_general(ones, terms, DIMS["nt"], preferred_element_type=f32)


def down_rows(row):
    return jnp.transpose(jnp.broadcast_to(row[0:1], (HEAD_DIM, row.shape[1])))


def iotas(n=HEAD_DIM):
    return (
        lax.broadcasted_iota(jnp.int32, (n, n), 0),
        lax.broadcasted_iota(jnp.int32, (n, n), 1),
    )


def lane_slice(place):
    return pl.ds(pl.multiple_of(place * HEAD_DIM, HEAD_DIM), HEAD_DIM)


def prelude_kernel(x_hbm, go_hbm, kern_hbm, decay_hbm, payload_ref, sums_ref, x_ref, go_ref, kern_ref, decay_ref, sems):
    pairs = ((x_hbm, x_ref), (go_hbm, go_ref), (kern_hbm, kern_ref), (decay_hbm, decay_ref))
    copies = [pltpu.make_async_copy(src, dst, sems.at[n]) for n, (src, dst) in enumerate(pairs)]
    for copy in copies:
        copy.start()
    copies[0].wait()
    x = x_ref[...].astype(f32)
    channels = x.shape[1]
    sums = row_sums(x * x)
    sums_ref[...] = sums
    payload_ref[:, :channels] = x[x.shape[0] - RIM :]
    payload_ref[:, channels:] = sums
    for copy in copies[1:]:
        copy.wait()


def inverse_all(systems):
    row, col = iotas()
    own = row >> 3 == col >> 3
    row8 = lax.broadcasted_iota(jnp.int32, (RIM, HEAD_DIM), 0)
    col8 = lax.broadcasted_iota(jnp.int32, (RIM, HEAD_DIM), 1)
    found = []
    for n in systems:
        blocks = jnp.sum(jnp.where(own, n, 0.0).reshape(-1, RIM, HEAD_DIM), axis=0)
        rows = jnp.where(row8 == (col8 & 7), 1.0, 0.0)
        for s in range(RIM - 1):
            column = jnp.take_along_axis(blocks, ((col8 >> 3) << 3) + s, axis=1, mode="promise_in_bounds")
            rows = rows - column * rows[s : s + 1]
        found.append(jnp.where(own, jnp.concatenate([rows] * (HEAD_DIM // RIM), axis=0), 0.0))
    level = 3
    while (1 << level) < HEAD_DIM:
        mask = (row >> (level + 2) == col >> (level + 2)) & (row >> level != col >> level)
        parts = [split(d) for d in found]
        cross = [split(jnp.where(mask, n, 0.0)) for n in systems]
        maps = [split(mm(p, c, "nn")) for p, c in zip(parts, cross)]
        twice = [mm(m, cols_of(m, p), "nn") for m, p in zip(maps, parts)]
        less = [d - t[:, HEAD_DIM:] for d, t in zip(found, twice)]
        found = [y + mm(split(t[:, :HEAD_DIM]), split(y), "nn") for y, t in zip(less, twice)]
        level += 2
    return found


def mixes_of(normed, rim, kern):
    row8 = lax.broadcasted_iota(jnp.int32, (RIM, HEAD_DIM), 0)
    taps = kern.shape[1]
    shifted = [normed]
    for s in range(1, taps):
        moved = pltpu.roll(normed, s, 0)
        first = jnp.where(row8 < s, pltpu.roll(rim, s, 0), moved[:RIM])
        shifted.append(jnp.concatenate([first, moved[RIM:]], axis=0))
    return [
        sum(kern[j, i : i + 1] * shifted[taps - 1 - i] for i in range(taps)) for j in range(3)
    ]


def gates_kernel(decay_ref, beta_ref, e1_ref, e2_ref, edge_ref, rate_ref):
    length = decay_ref.shape[0]
    row, col = iotas()
    tril = jnp.where(row >= col, 1.0, 0.0).astype(bf16)
    tril = jnp.concatenate([tril] * 3, axis=1)
    for head in range(decay_ref.shape[1] // HEAD_DIM):
        here = slice(head * HEAD_DIM, (head + 1) * HEAD_DIM)
        decay = decay_ref[:, here]
        high = decay.astype(bf16)
        rest = decay - high.astype(f32)
        mid = rest.astype(bf16)
        low = (rest - mid.astype(f32)).astype(bf16)
        cumulative = lax.dot_general(
            tril, jnp.concatenate([high, mid, low], axis=0), DIMS["nn"], preferred_element_type=f32
        )
        middle = cumulative[length // 2 : length // 2 + 1]
        final = cumulative[length - 1 : length]
        e1_ref[:, here] = jnp.exp(cumulative - middle)
        e2_ref[:, here] = jnp.exp(middle - cumulative)
        edge_ref[0:8, here] = jnp.broadcast_to(jnp.exp(middle), (8, HEAD_DIM))
        edge_ref[8:16, here] = jnp.broadcast_to(jnp.exp(final - middle), (8, HEAD_DIM))
        edge_ref[16:24, here] = jnp.broadcast_to(jnp.exp(final), (8, HEAD_DIM))
        rate_ref[:, here] = down_rows(beta_ref[head : head + 1])


def scaled(x_ref, rim_ref, kern_ref, scale, rim_scale, at):
    x = x_ref[:, at].astype(f32)
    return mixes_of(x * scale, rim_ref[:, at] * rim_scale, kern_ref[:, :, at])


def scales(flags, scale_ref, rim_scale_ref):
    rim_scale = down_rows(rim_scale_ref[...])
    rim_scale = jnp.where(flags[4] != 0, rim_scale[rim_scale.shape[0] - RIM :], 0.0)
    return down_rows(scale_ref[...]), rim_scale


def keep_split(ref, j, n, parts):
    ref[j, n] = parts[0]
    ref[j, n + 1] = parts[1]


def kept(ref, j, n):
    return ref[j, n], ref[j, n + 1]


def local_kernel(
    heads, flags, x_ref, go_ref, kern_ref, e1_ref, e2_ref, edge_ref, rate_ref, rim_ref, scale_ref, rim_scale_ref,
    comp_ref, wide_ref, narrow_ref,
):
    mask = flags[0]
    length = x_ref.shape[0]
    row, col = iotas()
    strict, full = row > col, row >= col
    scale, rim_scale = scales(flags, scale_ref, rim_scale_ref)
    data = []
    for j in range(heads):
        at = lane_slice((j ^ mask) & (heads - 1))
        mixes = scaled(x_ref, rim_ref, kern_ref, scale, rim_scale, at)
        act = [m / (1.0 + jnp.exp(-m)) for m in mixes]
        q, k = [a * lax.rsqrt(jnp.sum(a * a, axis=1, keepdims=True) + epsilon) for a in act[:2]]
        rate, e1, e2 = rate_ref[:, at], e1_ref[:, at], e2_ref[:, at]
        em, ecm, ef = [edge_ref[n : n + 1, at] for n in (0, 8, 16)]
        qf, kf, kb = q * e1, k * e1, k * e2
        skf, sqf, skb = split(kf), split(qf), split(kb)
        products = mm(rows_of(skf, sqf), skb, "nt")
        system = jnp.where(strict, rate * products[:length], 0.0)
        scores = split(jnp.where(full, products[length:], 0.0))
        go = exact(go_ref[:, at])
        fresh_grad = split(mm(scores, go, "tn"))
        wide_ref[j, 0], wide_ref[j, 1] = q, k
        for n, parts in enumerate((skf, sqf, skb, scores, fresh_grad)):
            keep_split(narrow_ref, j, 2 * n, parts)
        data.append(
            dict(system=system, go=go, rhs=cols_of(split(rate * kf * em), split(rate * act[2])), ke=split(kb * ecm),
                 qg=qf * em, fresh_grad=fresh_grad, ef=ef)
        )
    inverses = inverse_all([d["system"] for d in data])
    for j, (d, inverse) in enumerate(zip(data, inverses)):
        inverse = split(inverse)
        keep_split(narrow_ref, j, 10, inverse)
        solved = mm(inverse, d["rhs"], "nn")
        wide_ref[j, 2] = solved[:, HEAD_DIM:]
        d["solved"] = split(solved)
    for j, d in enumerate(data):
        solved = d["solved"]
        keep_split(narrow_ref, j, 12, (solved[0][:, :HEAD_DIM], solved[1][:, :HEAD_DIM]))
        keep_split(narrow_ref, j, 14, (solved[0][:, HEAD_DIM:], solved[1][:, HEAD_DIM:]))
        maps = mm(d["ke"], solved, "tn")
        comp_ref[j, 0:128] = jnp.where(row == col, d["ef"], 0.0) - maps[:, :HEAD_DIM]
        comp_ref[j, 128:256] = maps[:, HEAD_DIM:]
        w = (solved[0][:, :HEAD_DIM], solved[1][:, :HEAD_DIM])
        comp_ref[j, 256:384] = mm(split(d["qg"]), d["go"], "tn") - mm(w, d["fresh_grad"], "tn")


WIDE, NARROW = 3, 16


def ready_kernel(
    heads, flags, x_ref, kern_ref, e2_ref, edge_ref, rim_ref, scale_ref, rim_scale_ref, wide_ref, narrow_ref,
    more_ref, pairs_ref,
):
    mask = flags[0]
    scale, rim_scale = scales(flags, scale_ref, rim_scale_ref)
    for j in range(heads):
        at = lane_slice((j ^ mask) & (heads - 1))
        mixes = scaled(x_ref, rim_ref, kern_ref, scale, rim_scale, at)
        sig = [1.0 / (1.0 + jnp.exp(-m)) for m in mixes]
        slope = [s * (1.0 + m * (1.0 - s)) for m, s in zip(mixes, sig)]
        act = [m * s for m, s in zip(mixes[:2], sig)]
        inv = [lax.rsqrt(jnp.sum(a * a, axis=1, keepdims=True) + epsilon) for a in act]
        em, ecm = edge_ref[0:1, at], edge_ref[8:9, at]
        scores, fresh_grad, inverse = [kept(narrow_ref, j, n) for n in (6, 8, 10)]
        solved = cols_of(kept(narrow_ref, j, 12), kept(narrow_ref, j, 14))
        seen = mm(scores, solved, "nn")
        ke = split(wide_ref[j, 1] * e2_ref[:, at] * ecm)
        back = mm(inverse, cols_of(fresh_grad, ke), "tn")
        more_ref[j, 0] = slope[0] * inv[0]
        more_ref[j, 1] = slope[1] * inv[1]
        more_ref[j, 2] = slope[2]
        more_ref[j, 3] = seen[:, HEAD_DIM:]
        more_ref[j, 4] = back[:, :HEAD_DIM]
        qf = narrow_ref[j, 2].astype(f32) + narrow_ref[j, 3].astype(f32)
        keep_split(pairs_ref, j, 0, split(qf * em - seen[:, :HEAD_DIM]))
        keep_split(pairs_ref, j, 2, split(back[:, HEAD_DIM:]))


MORE, PAIRS = 5, 4


def join_kernel(flags, keep_ref, recv_ref, *outs):
    later = flags[1] != 0
    for j, out in enumerate(outs):
        keep, recv = keep_ref[j], recv_ref[j]
        lo = jnp.where(later, recv, keep)
        hi = jnp.where(later, keep, recv)
        lo_map, hi_map = split(lo[0:128]), split(hi[0:128])
        forward = mm(hi_map, cols_of(lo_map, split(lo[128:256])), "nn")
        back = mm(lo_map, split(hi[256:384]), "tn")
        out[0:128] = forward[:, :HEAD_DIM]
        out[128:256] = forward[:, HEAD_DIM:] + hi[128:256]
        out[256:384] = back + lo[256:384]


def collect(place, parts, held):
    for n, part in enumerate(parts):
        held[place ^ n] = part[...]


def gather_kernel(count, waits, with_map, flags, *refs):
    parts, outs, held = refs[:count], refs[count + waits : -1], refs[-1]
    collect(flags[2], parts, held)
    maps = [split(held[p, 0:128]) for p in range(count)]
    state, grad = held[0, 128:256], held[count - 1, 256:384]
    whole = held[0, 0:128]
    for p in range(1, count):
        state = mm(maps[p], split(state), "nn") + held[p, 128:256]
        grad = mm(maps[count - 1 - p], split(grad), "tn") + held[count - 1 - p, 256:384]
        if with_map:
            whole = mm(maps[p], split(whole), "nn")
    if with_map:
        outs[0][...], outs[1][...], outs[2][...] = whole, state, grad
    else:
        outs[0][...] = jnp.where(flags[3] != 0, grad, state)


def hop_kernel(flags, t_ref, u_ref, g_ref, s_ref, e_ref, s_out, e_out):
    t = split(t_ref[...])
    s_out[...] = mm(t, split(s_ref[...]), "nn") + u_ref[...]
    e_out[...] = mm(t, split(e_ref[...]), "tn") + g_ref[...]


def spread_kernel(count, single, flags, *refs):
    parts, ins, outs, held, found = refs[:count], refs[count : -2 - count], refs[-2 - count : -2], refs[-2], refs[-1]
    collect(flags[2], parts, held)
    if single:
        upper = flags[3] != 0
        state = jnp.where(upper, ins[0][...], 0.0)
        grad = jnp.where(upper, 0.0, ins[0][...])
    else:
        state, grad = ins[0][...], ins[1][...]
    for p in range(count):
        back = count - 1 - p
        found[p, 0:128] = state
        found[back, 128:256] = grad
        if p + 1 < count:
            state = mm(split(held[p, 0:128]), split(state), "nn") + held[p, 128:256]
            grad = mm(split(held[back, 0:128]), split(grad), "tn") + held[back, 256:384]
    for n, out in enumerate(outs):
        out[...] = found[flags[2] ^ n]


def part_kernel(flags, keep_ref, recv_ref, *refs):
    ins, (mine_ref, send_ref) = refs[:-2], refs[-2:]
    later = flags[1] != 0
    for j, ref in enumerate(ins):
        start, end = ref[0:128], ref[128:256]
        keep, recv = keep_ref[j], recv_ref[j]
        lo = jnp.where(later, recv, keep)
        hi = jnp.where(later, keep, recv)
        start_hi = mm(split(lo[0:128]), split(start), "nn") + lo[128:256]
        end_lo = mm(split(hi[0:128]), split(end), "tn") + hi[256:384]
        mine_ref[j, 0:128] = jnp.where(later, start_hi, start)
        mine_ref[j, 128:256] = jnp.where(later, end, end_lo)
        send_ref[j, 0:128] = jnp.where(later, start, start_hi)
        send_ref[j, 128:256] = jnp.where(later, end_lo, end)


def back_kernel(
    heads, chained, flags, x_ref, go_ref, kern_ref, e1_ref, e2_ref, edge_ref, rate_ref, rim_ref, wide_ref, narrow_ref,
    more_ref, pairs_ref, state_ref, *rest,
):
    if chained:
        sums_in, rim_sums_in, rim_grad_in, rest = rest[0], rest[1], rest[2], rest[4:]
    out_hbm, rim_grad_ref, grad_ref, sums_ref, rim_sums_ref, out_ref, sems = rest
    mask = flags[0]
    length = x_ref.shape[0]
    row, col = iotas()
    row8 = lax.broadcasted_iota(jnp.int32, (RIM, HEAD_DIM), 0)
    strict, full = row > col, row >= col
    taps = kern_ref.shape[1]
    first_head = (heads if chained else 0) ^ (mask & heads)
    dot_all = rim_dot = 0.0
    data, copies = [], []
    for j in range(heads):
        near = (j ^ mask) & (heads - 1)
        at = lane_slice(near)
        start, end = split(state_ref[j, 0:128]), split(state_ref[j, 128:256])
        first = mm(rows_of(kept(pairs_ref, j, 0), kept(narrow_ref, j, 12)), start, "nn")
        z = more_ref[j, 4] + mm(kept(pairs_ref, j, 2), end, "nn")
        x = x_ref[:, at].astype(f32)
        out_ref[j] = (x + (more_ref[j, 3] + first[:length])).astype(bf16)
        copies.append(
            pltpu.make_async_copy(out_ref.at[j], out_hbm.at[:, lane_slice(first_head + near)], sems.at[j])
        )
        copies[-1].start()
        data.append(dict(at=at, x=x, start=start, end=end, z=z, fresh=split(wide_ref[j, 2] - first[length:])))
    for j, d in enumerate(data):
        at = d["at"]
        q, k = wide_ref[j, 0], wide_ref[j, 1]
        gq, gk, gv = [more_ref[j, n] for n in range(3)]
        skf, sqf, skb = [kept(narrow_ref, j, n) for n in (0, 2, 4)]
        e1, e2, rate = e1_ref[:, at], e2_ref[:, at], rate_ref[:, at]
        em, ecm = edge_ref[0:1, at], edge_ref[8:9, at]
        go = exact(go_ref[:, at])
        second = mm(rows_of(go, split(d["z"])), rows_of(d["fresh"], d["start"]), "nt")
        score_grad = split(jnp.where(full, second[:length, :HEAD_DIM], 0.0))
        product_grad = split(jnp.where(strict, -rate * second[length:, :HEAD_DIM], 0.0))
        qg_grad = second[:length, HEAD_DIM:]
        kg_grad = -rate * second[length:, HEAD_DIM:]
        ke_grad = mm(d["fresh"], d["end"], "nt")
        pair = rows_of(score_grad, product_grad)
        third = mm(pair, skb, "nn")
        kb_grad = mm(pair, rows_of(sqf, skf), "tn")
        q_grad = e1 * (third[:length] + em * qg_grad)
        k_grad = e1 * (third[length:] + em * kg_grad) + e2 * (kb_grad + ecm * ke_grad)
        mix_grads = [
            gq * (q_grad - q * jnp.sum(q * q_grad, axis=1, keepdims=True)),
            gk * (k_grad - k * jnp.sum(k * k_grad, axis=1, keepdims=True)),
            gv * (rate * d["z"]),
        ]
        kern = kern_ref[:, :, at]
        normed_grad = rim_grad = 0.0
        for i in range(taps):
            each = sum(kern[n, i : i + 1] * mix_grads[n] for n in range(3))
            s = taps - 1 - i
            if s == 0:
                normed_grad = normed_grad + each
            else:
                moved = pltpu.roll(each, length - s, 0)
                normed_grad = normed_grad + jnp.where(row < length - s, moved, 0.0)
                rim_grad = rim_grad + jnp.where(row8 >= RIM - s, moved[length - RIM :], 0.0)
        grad_ref[:, at] = normed_grad
        if chained:
            rim_grad_ref[:, lane_slice(first_head + ((j ^ mask) & (heads - 1)))] = rim_grad
        else:
            rim_grad_ref[:, at] = rim_grad
        dot_all = dot_all + normed_grad * d["x"]
        rim_dot = rim_dot + rim_grad * rim_ref[:, at]
    sums = row_sums(dot_all)
    rim_sums = jnp.broadcast_to(jnp.sum(rim_dot, axis=1, keepdims=True), rim_dot.shape)
    if chained:
        sums, rim_sums = sums + sums_in[...], rim_sums + rim_sums_in[...]
        for n in range(heads):
            here = slice(n * HEAD_DIM, (n + 1) * HEAD_DIM)
            rim_grad_ref[:, lane_slice((first_head ^ heads) + n)] = rim_grad_in[:, here]
        rim_grad_ref[:, 2 * heads * HEAD_DIM :] = rim_sums
    sums_ref[...] = sums
    rim_sums_ref[...] = rim_sums
    for copy in copies:
        copy.wait()


def finish_kernel(groups, width, flags, x_ref, go_ref, scale_ref, inner_ref, next_sums_ref, next_ref, *refs):
    grads, (out_hbm, out_ref, sems) = refs[:groups], refs[groups:]
    length = x_ref.shape[0]
    scale = down_rows(scale_ref[...])
    inner = down_rows(inner_ref[...])
    last = flags[5] == 0
    next_sums = jnp.where(last, 0.0, next_sums_ref[...])
    inner = jnp.concatenate([inner[: length - RIM], inner[length - RIM :] + next_sums], axis=0)
    cubed = scale * scale * scale * inner * (1.0 / width)
    per = grads[0].shape[1] // HEAD_DIM
    copies = []
    for g, grad_ref in enumerate(grads):
        place = ((g * per) ^ flags[0]) // per
        for n in range(per):
            at = lane_slice(place * per + n)
            grad = grad_ref[:, n * HEAD_DIM : (n + 1) * HEAD_DIM]
            next_grad = jnp.where(last, 0.0, next_ref[:, at])
            grad = jnp.concatenate([grad[: length - RIM], grad[length - RIM :] + next_grad], axis=0)
            total = go_ref[:, at].astype(f32) + grad * scale - x_ref[:, at].astype(f32) * cubed
            out_ref[g * per + n] = total.astype(bf16)
            copies.append(
                pltpu.make_async_copy(out_ref.at[g * per + n], out_hbm.at[:, at], sems.at[g * per + n])
            )
            copies[-1].start()
    for copy in copies:
        copy.wait()


def whole_call(kernel, outs, *args, name=None, scratch=(), scalar=True, cost=None, far=False, unread=0):
    spec = pl.BlockSpec(memory_space=pltpu.VMEM)
    hbm = pl.BlockSpec(memory_space=pltpu.HBM)
    first = [pl.BlockSpec(memory_space=pltpu.SMEM)] if scalar else []
    return pl.pallas_call(
        kernel,
        out_shape=outs,
        in_specs=first + [hbm if far == "in" else spec] * (len(args) - len(first) - unread)
        + [pl.BlockSpec(memory_space=pl.ANY)] * unread,
        out_specs=jax.tree.map(lambda _: hbm if far == "out" else spec, outs),
        scratch_shapes=scratch,
        compiler_params=pltpu.CompilerParams(vmem_limit_bytes=VMEM_LIMIT),
        cost_estimate=cost,
        name=name,
    )(*args)


BESIDE = pl.CostEstimate(flops=10**9, bytes_accessed=10**7, transcendentals=0)


def array(*shape, dtype=f32):
    return jax.ShapeDtypeStruct(shape, dtype)


def shards(inputs, out_grads, conv_weight, log_decay, beta):
    length, channels = inputs.shape
    heads = channels // HEAD_DIM
    sections, spots = lax.axis_size("section"), lax.axis_size("ctx")
    width = channels * sections
    groups, per = 2, heads // 2
    count = per
    slabs = spots // (2 * count)
    me = lax.axis_index("ctx")
    place = (me >> 1) % count
    later = me & 1
    mask = later * per + place
    flags = [mask, later, place, (me // (2 * count)) % 2, me != 0, me != spots - 1]
    flags = jnp.stack([jnp.asarray(f, jnp.int32) for f in flags])

    def turned(value, sec, shift):
        route = [
            (s * spots + c, ((s + sec) % sections) * spots + (c + shift) % spots)
            for s in range(sections)
            for c in range(spots)
        ]
        return lax.ppermute(value, ("section", "ctx"), route)

    def swapped(value, distance):
        return lax.ppermute(value, "ctx", [(i, i ^ distance) for i in range(spots)])

    def moved(value, shift):
        return lax.ppermute(
            value, "ctx", [(i, i + shift) for i in range(spots) if 0 <= i + shift < spots]
        )

    payload, sums, x, go, kern, decay = whole_call(
        prelude_kernel,
        (
            array(RIM, channels + length), array(RIM, length), array(*inputs.shape, dtype=bf16),
            array(*inputs.shape, dtype=bf16), array(*conv_weight.shape), array(*inputs.shape),
        ),
        *[pltpu.with_memory_space_constraint(a, pltpu.HBM) for a in (inputs, out_grads, conv_weight, log_decay)],
        name="prelude", scalar=False, far="in", scratch=[pltpu.SemaphoreType.DMA((4,))],
    )
    total = sums
    rim_total = 0.0
    for sec in range(1, sections):
        total = total + turned(sums, sec, 0)
        rim_total = rim_total + turned(sums, sec, 1)
    rim = turned(payload, 0, 1)
    e1, e2, edge, rate = whole_call(
        gates_kernel,
        (array(length, channels), array(length, channels), array(24, channels), array(length, channels)),
        decay, beta.T, name="gates", scalar=False, cost=BESIDE,
    )
    scale = lax.rsqrt(total / width + norm_eps)
    rim_scale = lax.rsqrt((rim_total + rim[:, channels:]) / width + norm_eps)
    rim_raw = rim[:, :channels]

    span = per * HEAD_DIM

    def block(a, g):
        lead = (0,) * (len(a.shape) - 1)
        return pl.BlockSpec(a.shape[:-1] + (span,), lambda i, f: lead + (((g * per) ^ f[0]) // per,))

    def fixed(a):
        return pl.BlockSpec(a.shape, lambda i, f: (0,) * len(a.shape))

    def grid_call(kernel, in_specs, out_specs, outs, args, name, aliases=None, scratch=(), cost=None):
        return pl.pallas_call(
            kernel,
            grid_spec=pltpu.PrefetchScalarGridSpec(
                num_scalar_prefetch=1, grid=(1,), in_specs=in_specs, out_specs=out_specs, scratch_shapes=scratch
            ),
            out_shape=outs,
            input_output_aliases=aliases or {},
            compiler_params=pltpu.CompilerParams(vmem_limit_bytes=VMEM_LIMIT),
            cost_estimate=cost,
            name=name,
        )(flags, *args)

    square = (HEAD_DIM, HEAD_DIM)
    sliced = (x, go, kern, e1, e2, edge, rate, rim_raw)
    comps, saves = [None] * groups, [None] * groups
    for g in reversed(range(groups)):
        outs = [array(per, 384, HEAD_DIM), array(per, WIDE, *square), array(per, NARROW, *square, dtype=bf16)]
        comps[g], *saves[g] = grid_call(
            functools.partial(local_kernel, per),
            [block(a, g) for a in sliced] + [fixed(scale), fixed(rim_scale)],
            [fixed(a) for a in outs], outs, sliced + (scale, rim_scale), name=f"local{g}",
        )

    keep, recv = comps[0], swapped(comps[1], 1)
    joined = whole_call(join_kernel, (array(384, HEAD_DIM),) * per, flags, keep, recv, name="join")
    parts = [joined[0]] + [swapped(joined[n], 2 * n) for n in range(1, count)]
    for g in range(groups):
        outs = [array(per, MORE, HEAD_DIM, HEAD_DIM), array(per, PAIRS, HEAD_DIM, HEAD_DIM, dtype=bf16)]
        some = (x, kern, e2, edge, rim_raw)
        rest = (scale, rim_scale, *saves[g])
        saves[g] += grid_call(
            functools.partial(ready_kernel, per),
            [block(a, g) for a in some] + [fixed(a) for a in rest],
            [fixed(a) for a in outs], outs, some + rest, name=f"ready{g}", cost=BESIDE,
        )
    held = pltpu.VMEM((count, 384, HEAD_DIM), f32)
    square = array(*square)
    single = slabs == 2
    gathered = whole_call(
        functools.partial(gather_kernel, count, groups, not single), (square,) if single else (square,) * 3,
        flags, *parts, *[saves[g][2] for g in range(groups)], name="gather", scratch=[held], unread=groups,
    )
    step = 2 * count
    if single:
        states = (swapped(gathered[0], step),)
    else:
        states = (jnp.zeros(square.shape, f32),) * 2
        for hop in range(slabs - 1):
            if hop == 0:
                states = gathered[1:]
            else:
                states = whole_call(hop_kernel, (square,) * 2, flags, *gathered, *states, name=f"hop{hop}")
            states = (moved(states[0], step), moved(states[1], -step))
    spread = whole_call(
        functools.partial(spread_kernel, count, single), (array(256, HEAD_DIM),) * count,
        flags, *parts, *states, name="spread", scratch=[held, pltpu.VMEM((count, 256, HEAD_DIM), f32)],
    )
    spread = [spread[0]] + [swapped(spread[n], 2 * n) for n in range(1, count)]
    mine, send = whole_call(
        part_kernel, (array(per, 256, HEAD_DIM),) * 2, flags, keep, recv, *spread, name="part"
    )
    states = (mine, swapped(send, 1))

    chain = None
    grads = []
    far = pl.BlockSpec(memory_space=pltpu.HBM)
    for g in range(groups):
        rest = (*saves[g], states[g])
        aliases = None
        if chain is not None:
            rest = rest + (chain[3], chain[4], chain[1])
        args = sliced + rest
        specs = [block(a, g) for a in sliced] + [fixed(a) for a in rest]
        if chain is not None:
            args = args + (chain[0],)
            specs = specs + [far]
            aliases = {len(args): 0}
        rim_width = span if chain is None else channels + HEAD_DIM
        outs = [
            array(*inputs.shape, dtype=bf16), array(RIM, rim_width), array(length, span),
            array(RIM, length), array(RIM, HEAD_DIM),
        ]
        chain = grid_call(
            functools.partial(back_kernel, per, chain is not None),
            specs, [far] + [fixed(a) for a in outs[1:]], outs, args, name=f"back{g}", aliases=aliases,
            scratch=[pltpu.VMEM((per, length, HEAD_DIM), bf16), pltpu.SemaphoreType.DMA((per,))],
        )
        grads.append(chain[2])
    stream_out, rim_grad, _, inner, rim_sums = chain

    inner_total, next_sums = inner, 0.0
    for sec in range(1, sections):
        inner_total = inner_total + turned(inner, sec, 0)
        next_sums = next_sums + turned(rim_sums, sec, -1)
    next_rim = turned(rim_grad, 0, -1)
    input_grad = whole_call(
        functools.partial(finish_kernel, groups, width), array(*inputs.shape, dtype=bf16),
        flags, x, go, scale, inner_total, next_sums + next_rim[:, channels:], next_rim, *grads, name="finish",
        far="out", scratch=[pltpu.VMEM((heads, length, HEAD_DIM), bf16), pltpu.SemaphoreType.DMA((heads,))],
    )
    return (stream_out, input_grad)


def solution(mesh):
    in_specs = (
        P("ctx", "section"),
        P("ctx", "section"),
        P(None, None, "section"),
        P("ctx", "section"),
        P("ctx", "section"),
    )
    out_specs = (P("ctx", "section"), P("ctx", "section"))
    return jax.shard_map(shards, mesh=mesh, in_specs=in_specs, out_specs=out_specs, check_vma=False)
```

time: 99.1 us -> 65.1 us (0.66)
  the two profiles are of different devices: /device:TPU:13 before, /device:TPU:0 now
where the time goes in v3:
time: 65.1 us; the launch traced here: 64.9 us
  Pallas kernels  25.2 us (39%)
  waiting for transfers between devices  22 us (34%)
  starting transfers between devices  15.9 us (24%)
  between operations  0.97 us (1%)
  local copies, waits for them, and re-layouts  0.77 us (1%)
    pallas_call x6, Pallas kernels, grid_call(): pl.pallas_call(kernel, grid_spec=pltpu.PrefetchScalarGridSpec(num_scalar_...  17.6 us
    ppermute x9, waiting for transfers between devices, swapped(): return lax.ppermute(value, 'ctx', [(i, i ^ distance) for i in range(spots)])  15.4 us
    ppermute x9, starting transfers between devices, swapped(): return lax.ppermute(value, 'ctx', [(i, i ^ distance) for i in range(spots)])  8.1 us
    ppermute x6, starting transfers between devices, turned(): return lax.ppermute(value, ('section', 'ctx'), route)  7.77 us
    pallas_call x7, Pallas kernels, whole_call(): pl.pallas_call(kernel, out_shape=outs, in_specs=first + [hbm if far == 'i...  7.57 us
    ppermute x6, waiting for transfers between devices, turned(): return lax.ppermute(value, ('section', 'ctx'), route)  6.61 us
  transfers between devices with their start and end apart: 15, of which 10 were waited for; matrix products, arithmetic and copies ran while one was open for 0% of the time, Pallas kernels for 17%

profile of v3, /device:TPU:0, one launch (start us, length us, event | category | flops | bytes accessed | tf_op | source)
XLA Modules:
  0.0 64.9 jit_solution(11188553883021510125)
XLA Ops:
  0.6 1.3 %prelude.1 = (f32[8,1152]{1,0:T(8,128)S(1)}, f32[8,128]{1,0:T(8,128)S(1)}, bf16[128,1024]{1,0:T(8,128)(2,1)S(1)}, bf16[128,1024]{1,0:T(8,128)(2,1)S(1)}, f32[3,4...) custom-call(bf16[128,1024]{1,0:T(8,128)(2,1)} %x_hbm.1, bf16[128,1024]{1,0:T(8,128)(2,1)} %go_hbm.1, f32[3,4,1024]{2,1,0:T(4,128)} %kern_hbm.1, ...), custom_call_target="tpu_custom_call" | custom-call | tf_op jit(solution)/shard_map/prelude/pallas_call | solution.py:459
  2.0 2.4 %collective-permute-start.2 = (f32[8,128]{1,0:T(8,128)S(1)}, f32[8,128]{1,0:T(8,128)S(1)}, u32[]{:S(2)}, u32[]{:S(2)}) collective-permute-start(f32[8,128]{1,0:T(8,128)S(1)} %get-tuple-element.51), channel_id=1, source_target_pairs={{0,17},{1,18},{2,19},{3,20},{4,21},{5,22},{6,23},{7,24},{8,25},{9,... | collective-permute-start | bytes 12296 | tf_op jit(solution)/shard_map/ppermute | solution.py:500
  4.4 0.6 collective-permute-start.1
  5.0 1.2 %collective-permute-start = (f32[8,1152]{1,0:T(8,128)S(1)}, f32[8,1152]{1,0:T(8,128)S(1)}, u32[]{:S(2)}, u32[]{:S(2)}) collective-permute-start(f32[8,1152]{1,0:T(8,128)S(1)} %get-tuple-element.50), channel_id=1, source_target_pairs={{0,1},{1,2},{2,3},{3,4},{4,5},{5,6},{6,7},{7,8},{8,9},{9,10},{10,1... | collective-permute-start | bytes 110600 | tf_op jit(solution)/shard_map/ppermute | solution.py:500
  6.3 0.0 copy-start
  6.3 0.7 %copy-done = f32[128,8]{0,1:T(8,128)S(1)} copy-done((f32[128,8]{0,1:T(8,128)S(1)}, f32[128,8]{0,1:T(8,128)}, u32[]{:S(2)}) %copy-start) | copy-done | bytes 4120
  7.0 0.4 gates.1
  7.4 0.1 stack.35.flags
  7.5 0.5 collective-permute-done.1
  8.0 3.1 %collective-permute-done = f32[8,1152]{1,0:T(8,128)S(1)} collective-permute-done((f32[8,1152]{1,0:T(8,128)S(1)}, f32[8,1152]{1,0:T(8,128)S(1)}, u32[]{:S(2)}, u32[]{:S(2)}) %collective-permute-start) | collective-permute-done | bytes 36896 | tf_op jit(solution)/shard_map/ppermute | solution.py:500
  11.1 0.0 collective-permute-done.2
  11.1 3.6 %local1.1 = (f32[4,384,128]{2,1,0:T(8,128)S(1)}, f32[4,3,128,128]{3,2,1,0:T(8,128)S(1)}, bf16[4,16,128,128]{3,2,1,0:T(8,128)(2,1)S(1)}) custom-call(s32[6]{0:T(128)S(1)} %stack.35.flags, bf16[128,1024]{1,0:T(8,128)(2,1)S(1)} %get-tuple-element.42.x_ref, bf16[128,1024]{1,0:T(8,128)(2,1)S(1)} %get-tuple-element.43.go_ref, ...), custom_call_target="tpu_custom_call" | custom-call | tf_op jit(solution)/shard_map/local1/pallas_call | solution.py:544
  14.7 0.1 collective-permute-start.3
  14.8 3.6 %local0.1 = (f32[4,384,128]{2,1,0:T(8,128)S(1)}, f32[4,3,128,128]{3,2,1,0:T(8,128)S(1)}, bf16[4,16,128,128]{3,2,1,0:T(8,128)(2,1)S(1)}) custom-call(s32[6]{0:T(128)S(1)} %stack.35.flags, bf16[128,1024]{1,0:T(8,128)(2,1)S(1)} %get-tuple-element.42.x_ref, bf16[128,1024]{1,0:T(8,128)(2,1)S(1)} %get-tuple-element.43.go_ref, ...), custom_call_target="tpu_custom_call" | custom-call | tf_op jit(solution)/shard_map/local0/pallas_call | solution.py:544
  18.4 0.0 collective-permute-done.3.recv_ref
  18.5 1.0 %join.1 = (f32[384,128]{1,0:T(8,128)S(1)}, f32[384,128]{1,0:T(8,128)S(1)}, f32[384,128]{1,0:T(8,128)S(1)}, f32[384,128]{1,0:T(8,128)S(1)}) custom-call(s32[6]{0:T(128)S(1)} %stack.35.flags, f32[4,384,128]{2,1,0:T(8,128)S(1)} %get-tuple-element.56.keep_ref, f32[4,384,128]{2,1,0:T(8,128)S(1)} %collective-permute-done.3.recv_ref), custom_call_target="tpu_custom_call" | custom-call | tf_op jit(solution)/shard_map/join/pallas_call | solution.py:459
  19.5 0.1 collective-permute-start.4
  19.6 0.6 collective-permute-start.5
  20.1 2.9 %collective-permute-start.6 = (f32[384,128]{1,0:T(8,128)S(1)}, f32[384,128]{1,0:T(8,128)S(1)}, u32[]{:S(2)}, u32[]{:S(2)}) collective-permute-start(f32[384,128]{1,0:T(8,128)S(1)} %get-tuple-element.61), channel_id=1, source_target_pairs={{0,6},{1,7},{2,4},{3,5},{4,2},{5,3},{6,0},{7,1},{8,14},{9,15},{10,... | collective-permute-start | bytes 589832 | tf_op jit(solution)/shard_map/ppermute | solution.py:503
  23.0 1.5 %ready0.1 = (f32[4,5,128,128]{3,2,1,0:T(8,128)S(1)}, bf16[4,4,128,128]{3,2,1,0:T(8,128)(2,1)S(1)}) custom-call(s32[6]{0:T(128)S(1)} %stack.35.flags, bf16[128,1024]{1,0:T(8,128)(2,1)S(1)} %get-tuple-element.42.x_ref, f32[3,4,1024]{2,1,0:T(4,128)S(1)} %get-tuple-element.44.kern_ref, f32[128,1024]{1,0:T(8,128)S(1)} %get-tuple-element.47.e2_ref, ...), custom_call_target="tpu_custom_call" | custom-call | flops 1000000000 | bytes 10000000 | tf_op jit(solution)/shard_map/ready0/pallas_call | solution.py:544
  24.6 1.5 %ready1.1 = (f32[4,5,128,128]{3,2,1,0:T(8,128)S(1)}, bf16[4,4,128,128]{3,2,1,0:T(8,128)(2,1)S(1)}) custom-call(s32[6]{0:T(128)S(1)} %stack.35.flags, bf16[128,1024]{1,0:T(8,128)(2,1)S(1)} %get-tuple-element.42.x_ref, f32[3,4,1024]{2,1,0:T(4,128)S(1)} %get-tuple-element.44.kern_ref, f32[128,1024]{1,0:T(8,128)S(1)} %get-tuple-element.47.e2_ref, ...), custom_call_target="tpu_custom_call" | custom-call | flops 1000000000 | bytes 10000000 | tf_op jit(solution)/shard_map/ready1/pallas_call | solution.py:544
  26.1 0.8 %collective-permute-done.4.refs_1_ = f32[384,128]{1,0:T(8,128)S(1)} collective-permute-done((f32[384,128]{1,0:T(8,128)S(1)}, f32[384,128]{1,0:T(8,128)S(1)}, u32[]{:S(2)}, u32[]{:S(2)}) %collective-permute-start.4) | collective-permute-done | bytes 196640 | tf_op jit(solution)/shard_map/ppermute | solution.py:503
  26.8 0.5 collective-permute-done.5.refs_2_
  27.3 4.9 %collective-permute-done.6.refs_3_ = f32[384,128]{1,0:T(8,128)S(1)} collective-permute-done((f32[384,128]{1,0:T(8,128)S(1)}, f32[384,128]{1,0:T(8,128)S(1)}, u32[]{:S(2)}, u32[]{:S(2)}) %collective-permute-start.6) | collective-permute-done | bytes 196640 | tf_op jit(solution)/shard_map/ppermute | solution.py:503
  32.2 1.1 %gather.1 = f32[128,128]{1,0:T(8,128)S(1)} custom-call(s32[6]{0:T(128)S(1)} %stack.35.flags, f32[384,128]{1,0:T(8,128)S(1)} %get-tuple-element.58.refs_0_, f32[384,128]{1,0:T(8,128)S(1)} %collective-permute-done.4.refs_1_, f32[384,128]{1,0:T(8,128)S(1)} %collective-permute-done.5.refs_2_, f32[384,128]{1,0:T(8,128)S(1)} %collective-permute-done.6.refs_3_, ...), custom_call_target="tpu_custom_call" | custom-call | tf_op jit(solution)/shard_map/gather/pallas_call | solution.py:459
  33.4 0.9 %collective-permute-start.7 = (f32[128,128]{1,0:T(8,128)S(1)}, f32[128,128]{1,0:T(8,128)S(1)}, u32[]{:S(2)}, u32[]{:S(2)}) collective-permute-start(f32[128,128]{1,0:T(8,128)S(1)} %gather.1), channel_id=1, source_target_pairs={{0,8},{1,9},{2,10},{3,11},{4,12},{5,13},{6,14},{7,15},{8,0},{9,1},... | collective-permute-start | bytes 196616 | tf_op jit(solution)/shard_map/ppermute | solution.py:503
  34.2 4.9 %collective-permute-done.7.refs_4_ = f32[128,128]{1,0:T(8,128)S(1)} collective-permute-done((f32[128,128]{1,0:T(8,128)S(1)}, f32[128,128]{1,0:T(8,128)S(1)}, u32[]{:S(2)}, u32[]{:S(2)}) %collective-permute-start.7) | collective-permute-done | bytes 65568 | tf_op jit(solution)/shard_map/ppermute | solution.py:503
  39.1 1.2 %spread.1 = (f32[256,128]{1,0:T(8,128)S(1)}, f32[256,128]{1,0:T(8,128)S(1)}, f32[256,128]{1,0:T(8,128)S(1)}, f32[256,128]{1,0:T(8,128)S(1)}) custom-call(s32[6]{0:T(128)S(1)} %stack.35.flags, f32[384,128]{1,0:T(8,128)S(1)} %get-tuple-element.58.refs_0_, f32[384,128]{1,0:T(8,128)S(1)} %collective-permute-done.4.refs_1_, ...), custom_call_target="tpu_custom_call" | custom-call | tf_op jit(solution)/shard_map/spread/pallas_call | solution.py:459
  40.3 0.3 collective-permute-start.8
  40.6 0.0 collective-permute-start.9
  40.7 3.2 %collective-permute-start.10 = (f32[256,128]{1,0:T(8,128)S(1)}, f32[256,128]{1,0:T(8,128)S(1)}, u32[]{:S(2)}, u32[]{:S(2)}) collective-permute-start(f32[256,128]{1,0:T(8,128)S(1)} %get-tuple-element.68), channel_id=1, source_target_pairs={{0,6},{1,7},{2,4},{3,5},{4,2},{5,3},{6,0},{7,1},{8,14},{9,15},{10,... | collective-permute-start | bytes 393224 | tf_op jit(solution)/shard_map/ppermute | solution.py:503
  43.9 2.9 %collective-permute-done.8.refs_1_ = f32[256,128]{1,0:T(8,128)S(1)} collective-permute-done((f32[256,128]{1,0:T(8,128)S(1)}, f32[256,128]{1,0:T(8,128)S(1)}, u32[]{:S(2)}, u32[]{:S(2)}) %collective-permute-start.8) | collective-permute-done | bytes 131104 | tf_op jit(solution)/shard_map/ppermute | solution.py:503
  46.8 0.0 collective-permute-done.9.refs_2_
  46.8 1.5 %collective-permute-done.10.refs_3_ = f32[256,128]{1,0:T(8,128)S(1)} collective-permute-done((f32[256,128]{1,0:T(8,128)S(1)}, f32[256,128]{1,0:T(8,128)S(1)}, u32[]{:S(2)}, u32[]{:S(2)}) %collective-permute-start.10) | collective-permute-done | bytes 131104 | tf_op jit(solution)/shard_map/ppermute | solution.py:503
  48.3 1.0 %part.1 = (f32[4,256,128]{2,1,0:T(8,128)S(1)}, f32[4,256,128]{2,1,0:T(8,128)S(1)}) custom-call(s32[6]{0:T(128)S(1)} %stack.35.flags, f32[4,384,128]{2,1,0:T(8,128)S(1)} %get-tuple-element.56.keep_ref, f32[4,384,128]{2,1,0:T(8,128)S(1)} %collective-permute-done.3.recv_ref, f32[256,128]{1,0:T(8,128)S(1)} %get-tuple-element.65.refs_0_, ...), custom_call_target="tpu_custom_call" | custom-call | tf_op jit(solution)/shard_map/part/pallas_call | solution.py:459
  49.2 0.1 collective-permute-start.11
  49.3 3.8 %back0.1 = (bf16[128,1024]{1,0:T(8,128)(2,1)}, f32[8,512]{1,0:T(8,128)S(1)}, f32[128,512]{1,0:T(8,128)S(1)}, f32[8,128]{1,0:T(8,128)S(1)}, f32[8,128]{1,0:T(8,128)S(1)}) custom-call(s32[6]{0:T(128)S(1)} %stack.35.flags, bf16[128,1024]{1,0:T(8,128)(2,1)S(1)} %get-tuple-element.42.x_ref, bf16[128,1024]{1,0:T(8,128)(2,1)S(1)} %get-tuple-element.43.go_ref, ...), custom_call_target="tpu_custom_call" | custom-call | tf_op jit(solution)/shard_map/back0/pallas_call | solution.py:544
  53.1 0.0 collective-permute-done.11.state_ref
  53.1 3.6 %back1.1 = (bf16[128,1024]{1,0:T(8,128)(2,1)}, f32[8,1152]{1,0:T(8,128)S(1)}, f32[128,512]{1,0:T(8,128)S(1)}, f32[8,128]{1,0:T(8,128)S(1)}, f32[8,128]{1,0:T(8,128)S(1)}) custom-call(s32[6]{0:T(128)S(1)} %stack.35.flags, bf16[128,1024]{1,0:T(8,128)(2,1)S(1)} %get-tuple-element.42.x_ref, ...), custom_call_target="tpu_custom_call", output_to_operand_aliasing={{0}: (17, {})} | custom-call | tf_op jit(solution)/shard_map/back1/pallas_call | solution.py:544
  56.7 2.1 %collective-permute-start.14 = (f32[8,1152]{1,0:T(8,128)S(1)}, f32[8,1152]{1,0:T(8,128)S(1)}, u32[]{:S(2)}, u32[]{:S(2)}) collective-permute-start(f32[8,1152]{1,0:T(8,128)S(1)} %get-tuple-element.79), channel_id=1, source_target_pairs={{0,15},{1,0},{2,1},{3,2},{4,3},{5,4},{6,5},{7,6},{8,7},{9,8},{10,9... | collective-permute-start | bytes 110600 | tf_op jit(solution)/shard_map/ppermute | solution.py:500
  58.7 1.4 %collective-permute-start.12 = (f32[8,128]{1,0:T(8,128)S(1)}, f32[8,128]{1,0:T(8,128)S(1)}, u32[]{:S(2)}, u32[]{:S(2)}) collective-permute-start(f32[8,128]{1,0:T(8,128)S(1)} %get-tuple-element.77), channel_id=1, source_target_pairs={{0,16},{1,17},{2,18},{3,19},{4,20},{5,21},{6,22},{7,23},{8,24},{9,... | collective-permute-start | bytes 12296 | tf_op jit(solution)/shard_map/ppermute | solution.py:500
  60.1 0.0 collective-permute-start.13
  60.1 2.2 %collective-permute-done.12 = f32[8,128]{1,0:T(8,128)S(1)} collective-permute-done((f32[8,128]{1,0:T(8,128)S(1)}, f32[8,128]{1,0:T(8,128)S(1)}, u32[]{:S(2)}, u32[]{:S(2)}) %collective-permute-start.12) | collective-permute-done | bytes 4128 | tf_op jit(solution)/shard_map/ppermute | solution.py:500
  62.4 0.8 %collective-permute-done.13 = f32[8,128]{1,0:T(8,128)S(1)} collective-permute-done((f32[8,128]{1,0:T(8,128)S(1)}, f32[8,128]{1,0:T(8,128)S(1)}, u32[]{:S(2)}, u32[]{:S(2)}) %collective-permute-start.13) | collective-permute-done | bytes 4128 | tf_op jit(solution)/shard_map/ppermute | solution.py:500
  63.2 0.0 collective-permute-done.14.next_ref
  63.2 1.5 %finish.1 = bf16[128,1024]{1,0:T(8,128)(2,1)} custom-call(s32[6]{0:T(128)S(1)} %stack.35.flags, bf16[128,1024]{1,0:T(8,128)(2,1)S(1)} %get-tuple-element.42.x_ref, bf16[128,1024]{1,0:T(8,128)(2,1)S(1)} %get-tuple-element.43.go_ref, f32[8,128]{1,0:T(8,128)S(1)} %add_rsqrt_fusion.scale_ref, f32[8,128]{1,0:T(8,128)S(1)} %add.36.inner_ref, ...), custom_call_target="tpu_custom_call" | custom-call | tf_op jit(solution)/shard_map/finish/pallas_call | solution.py:459
  (5 shorter events, 0.0 us)
Async XLA Ops:
  2.0 9.2 %collective-permute-start.2 = (f32[8,128]{1,0:T(8,128)S(1)}, f32[8,128]{1,0:T(8,128)S(1)}, u32[]{:S(2)}, u32[]{:S(2)}) collective-permute-start(f32[8,128]{1,0:T(8,128)S(1)} %get-tuple-element.51), channel_id=1, source_target_pairs={{0,17},{1,18},{2,19},{3,20},{4,21},{5,22},{6,23},{7,24},{8,25},{9,... | collective-permute-start | bytes 12296 | tf_op jit(solution)/shard_map/ppermute | solution.py:500
  4.4 3.6 %collective-permute-start.1 = (f32[8,128]{1,0:T(8,128)S(1)}, f32[8,128]{1,0:T(8,128)S(1)}, u32[]{:S(2)}, u32[]{:S(2)}) collective-permute-start(f32[8,128]{1,0:T(8,128)S(1)} %get-tuple-element.51), channel_id=1, source_target_pairs={{0,16},{1,17},{2,18},{3,19},{4,20},{5,21},{6,22},{7,23},{8,24},{9,... | collective-permute-start | bytes 12296 | tf_op jit(solution)/shard_map/ppermute | solution.py:500
  5.0 6.1 %collective-permute-start = (f32[8,1152]{1,0:T(8,128)S(1)}, f32[8,1152]{1,0:T(8,128)S(1)}, u32[]{:S(2)}, u32[]{:S(2)}) collective-permute-start(f32[8,1152]{1,0:T(8,128)S(1)} %get-tuple-element.50), channel_id=1, source_target_pairs={{0,1},{1,2},{2,3},{3,4},{4,5},{5,6},{6,7},{7,8},{8,9},{9,10},{10,1... | collective-permute-start | bytes 110600 | tf_op jit(solution)/shard_map/ppermute | solution.py:500
  6.3 0.7 %copy-start = (f32[128,8]{0,1:T(8,128)S(1)}, f32[128,8]{0,1:T(8,128)}, u32[]{:S(2)}) copy-start(f32[128,8]{0,1:T(8,128)} %param.9) | copy-start | bytes 12292
  14.7 3.7 %collective-permute-start.3 = (f32[4,384,128]{2,1,0:T(8,128)S(1)}, f32[4,384,128]{2,1,0:T(8,128)S(1)}, u32[]{:S(2)}, u32[]{:S(2)}) collective-permute-start(f32[4,384,128]{2,1,0:T(8,128)S(1)} %get-tuple-element.57), channel_id=1, source_target_pairs={{0,1},{1,0},{2,3},{3,2},{4,5},{5,4},{6,7},{7,6},{8,9},{9,8},{10,11... | collective-permute-start | bytes 2359304 | tf_op jit(solution)/shard_map/ppermute | solution.py:503
  19.5 7.4 %collective-permute-start.4 = (f32[384,128]{1,0:T(8,128)S(1)}, f32[384,128]{1,0:T(8,128)S(1)}, u32[]{:S(2)}, u32[]{:S(2)}) collective-permute-start(f32[384,128]{1,0:T(8,128)S(1)} %get-tuple-element.59), channel_id=1, source_target_pairs={{0,2},{1,3},{2,0},{3,1},{4,6},{5,7},{6,4},{7,5},{8,10},{9,11},{10,... | collective-permute-start | bytes 589832 | tf_op jit(solution)/shard_map/ppermute | solution.py:503
  19.6 7.8 %collective-permute-start.5 = (f32[384,128]{1,0:T(8,128)S(1)}, f32[384,128]{1,0:T(8,128)S(1)}, u32[]{:S(2)}, u32[]{:S(2)}) collective-permute-start(f32[384,128]{1,0:T(8,128)S(1)} %get-tuple-element.60), channel_id=1, source_target_pairs={{0,4},{1,5},{2,6},{3,7},{4,0},{5,1},{6,2},{7,3},{8,12},{9,13},{10,... | collective-permute-start | bytes 589832 | tf_op jit(solution)/shard_map/ppermute | solution.py:503
  20.1 12.1 %collective-permute-start.6 = (f32[384,128]{1,0:T(8,128)S(1)}, f32[384,128]{1,0:T(8,128)S(1)}, u32[]{:S(2)}, u32[]{:S(2)}) collective-permute-start(f32[384,128]{1,0:T(8,128)S(1)} %get-tuple-element.61), channel_id=1, source_target_pairs={{0,6},{1,7},{2,4},{3,5},{4,2},{5,3},{6,0},{7,1},{8,14},{9,15},{10,... | collective-permute-start | bytes 589832 | tf_op jit(solution)/shard_map/ppermute | solution.py:503
  33.4 5.8 %collective-permute-start.7 = (f32[128,128]{1,0:T(8,128)S(1)}, f32[128,128]{1,0:T(8,128)S(1)}, u32[]{:S(2)}, u32[]{:S(2)}) collective-permute-start(f32[128,128]{1,0:T(8,128)S(1)} %gather.1), channel_id=1, source_target_pairs={{0,8},{1,9},{2,10},{3,11},{4,12},{5,13},{6,14},{7,15},{8,0},{9,1},... | collective-permute-start | bytes 196616 | tf_op jit(solution)/shard_map/ppermute | solution.py:503
  40.3 6.4 %collective-permute-start.8 = (f32[256,128]{1,0:T(8,128)S(1)}, f32[256,128]{1,0:T(8,128)S(1)}, u32[]{:S(2)}, u32[]{:S(2)}) collective-permute-start(f32[256,128]{1,0:T(8,128)S(1)} %get-tuple-element.66), channel_id=1, source_target_pairs={{0,2},{1,3},{2,0},{3,1},{4,6},{5,7},{6,4},{7,5},{8,10},{9,11},{10,... | collective-permute-start | bytes 393224 | tf_op jit(solution)/shard_map/ppermute | solution.py:503
  40.6 6.1 %collective-permute-start.9 = (f32[256,128]{1,0:T(8,128)S(1)}, f32[256,128]{1,0:T(8,128)S(1)}, u32[]{:S(2)}, u32[]{:S(2)}) collective-permute-start(f32[256,128]{1,0:T(8,128)S(1)} %get-tuple-element.67), channel_id=1, source_target_pairs={{0,4},{1,5},{2,6},{3,7},{4,0},{5,1},{6,2},{7,3},{8,12},{9,13},{10,... | collective-permute-start | bytes 393224 | tf_op jit(solution)/shard_map/ppermute | solution.py:503
  40.7 7.6 %collective-permute-start.10 = (f32[256,128]{1,0:T(8,128)S(1)}, f32[256,128]{1,0:T(8,128)S(1)}, u32[]{:S(2)}, u32[]{:S(2)}) collective-permute-start(f32[256,128]{1,0:T(8,128)S(1)} %get-tuple-element.68), channel_id=1, source_target_pairs={{0,6},{1,7},{2,4},{3,5},{4,2},{5,3},{6,0},{7,1},{8,14},{9,15},{10,... | collective-permute-start | bytes 393224 | tf_op jit(solution)/shard_map/ppermute | solution.py:503
  49.2 3.9 %collective-permute-start.11 = (f32[4,256,128]{2,1,0:T(8,128)S(1)}, f32[4,256,128]{2,1,0:T(8,128)S(1)}, u32[]{:S(2)}, u32[]{:S(2)}) collective-permute-start(f32[4,256,128]{2,1,0:T(8,128)S(1)} %get-tuple-element.69), channel_id=1, source_target_pairs={{0,1},{1,0},{2,3},{3,2},{4,5},{5,4},{6,7},{7,6},{8,9},{9,8},{10,11... | collective-permute-start | bytes 1572872 | tf_op jit(solution)/shard_map/ppermute | solution.py:503
  56.7 6.5 %collective-permute-start.14 = (f32[8,1152]{1,0:T(8,128)S(1)}, f32[8,1152]{1,0:T(8,128)S(1)}, u32[]{:S(2)}, u32[]{:S(2)}) collective-permute-start(f32[8,1152]{1,0:T(8,128)S(1)} %get-tuple-element.79), channel_id=1, source_target_pairs={{0,15},{1,0},{2,1},{3,2},{4,3},{5,4},{6,5},{7,6},{8,7},{9,8},{10,9... | collective-permute-start | bytes 110600 | tf_op jit(solution)/shard_map/ppermute | solution.py:500
  58.7 3.6 %collective-permute-start.12 = (f32[8,128]{1,0:T(8,128)S(1)}, f32[8,128]{1,0:T(8,128)S(1)}, u32[]{:S(2)}, u32[]{:S(2)}) collective-permute-start(f32[8,128]{1,0:T(8,128)S(1)} %get-tuple-element.77), channel_id=1, source_target_pairs={{0,16},{1,17},{2,18},{3,19},{4,20},{5,21},{6,22},{7,23},{8,24},{9,... | collective-permute-start | bytes 12296 | tf_op jit(solution)/shard_map/ppermute | solution.py:500
  60.1 3.0 %collective-permute-start.13 = (f32[8,128]{1,0:T(8,128)S(1)}, f32[8,128]{1,0:T(8,128)S(1)}, u32[]{:S(2)}, u32[]{:S(2)}) collective-permute-start(f32[8,128]{1,0:T(8,128)S(1)} %get-tuple-element.78), channel_id=1, source_target_pairs={{0,31},{1,16},{2,17},{3,18},{4,19},{5,20},{6,21},{7,22},{8,23},{9,... | collective-permute-start | bytes 12296 | tf_op jit(solution)/shard_map/ppermute | solution.py:500

commit v4 on v3

v4 whole, which is shorter than its diff:
```python
import functools

import jax
import jax.numpy as jnp
from jax import lax
from jax.experimental import pallas as pl
from jax.experimental.pallas import tpu as pltpu
from jax.sharding import PartitionSpec as P

HEAD_DIM = 128
RIM = 8
epsilon = 1e-06
norm_eps = 1e-05
f32 = jnp.float32
bf16 = jnp.bfloat16
VMEM_LIMIT = 24 * 1024 * 1024

DIMS = {
    "nn": (((1,), (0,)), ((), ())),
    "nt": (((1,), (1,)), ((), ())),
    "tn": (((0,), (0,)), ((), ())),
}


def split(a):
    high = a.astype(bf16)
    return high, (a - high.astype(f32)).astype(bf16)


def exact(a):
    return a, None


def rows_of(*parts):
    highs = jnp.concatenate([p[0] for p in parts], axis=0)
    lows = [jnp.zeros_like(p[0]) if p[1] is None else p[1] for p in parts]
    return highs, jnp.concatenate(lows, axis=0)


def cols_of(*parts):
    return tuple(jnp.concatenate([p[i] for p in parts], axis=1) for i in range(2))


def mm(a, b, form):
    width = b[0].shape[1]
    if form != "nt" and a[1] is not None and b[1] is not None and width == HEAD_DIM:
        right = jnp.concatenate(b, axis=1)
        left = jnp.concatenate(a, axis=0 if form == "tn" else 1)
        out = lax.dot_general(left, jnp.concatenate([right, right], axis=0), DIMS[form], preferred_element_type=f32)
        return out[:, :width] + out[:, width:]
    pairs = [(a[0], b[0])]
    if a[1] is not None:
        pairs.append((a[1], b[0]))
    if b[1] is not None:
        pairs.append((a[0], b[1]))
    left = jnp.concatenate([p[0] for p in pairs], axis=0 if form == "tn" else 1)
    right = jnp.concatenate([p[1] for p in pairs], axis=1 if form == "nt" else 0)
    return lax.dot_general(left, right, DIMS[form], preferred_element_type=f32)


def row_sums(a):
    high = a.astype(bf16)
    rest = a - high.astype(f32)
    mid = rest.astype(bf16)
    low = (rest - mid.astype(f32)).astype(bf16)
    terms = jnp.concatenate([high, mid, low], axis=1)
    ones = jnp.ones((RIM, terms.shape[1]), bf16)
    return lax.dot_general(ones, terms, DIMS["nt"], preferred_element_type=f32)


def down_rows(row):
    return jnp.transpose(jnp.broadcast_to(row[0:1], (HEAD_DIM, row.shape[1])))


def iotas(n=HEAD_DIM):
    return (
        lax.broadcasted_iota(jnp.int32, (n, n), 0),
        lax.broadcasted_iota(jnp.int32, (n, n), 1),
    )


def lane_slice(place):
    return pl.ds(pl.multiple_of(place * HEAD_DIM, HEAD_DIM), HEAD_DIM)


def prelude_kernel(
    x_hbm, go_hbm, kern_hbm, decay_hbm, beta_hbm, payload_ref, sums_ref, x_ref, go_ref, kern_ref, decay_ref, beta_ref, sems
):
    pairs = ((x_hbm, x_ref), (go_hbm, go_ref), (kern_hbm, kern_ref), (decay_hbm, decay_ref), (beta_hbm, beta_ref))
    copies = [pltpu.make_async_copy(src, dst, sems.at[n]) for n, (src, dst) in enumerate(pairs)]
    for copy in copies:
        copy.start()
    copies[0].wait()
    x = x_ref[...].astype(f32)
    channels = x.shape[1]
    sums = row_sums(x * x)
    sums_ref[...] = sums
    payload_ref[:, :channels] = x[x.shape[0] - RIM :]
    payload_ref[:, channels:] = sums
    for copy in copies[1:]:
        copy.wait()


def inverse_all(systems):
    row, col = iotas()
    own = row >> 3 == col >> 3
    row8 = lax.broadcasted_iota(jnp.int32, (RIM, HEAD_DIM), 0)
    col8 = lax.broadcasted_iota(jnp.int32, (RIM, HEAD_DIM), 1)
    found = []
    for n in systems:
        blocks = jnp.sum(jnp.where(own, n, 0.0).reshape(-1, RIM, HEAD_DIM), axis=0)
        rows = jnp.where(row8 == (col8 & 7), 1.0, 0.0)
        for s in range(RIM - 1):
            column = jnp.take_along_axis(blocks, ((col8 >> 3) << 3) + s, axis=1, mode="promise_in_bounds")
            rows = rows - column * rows[s : s + 1]
        found.append(jnp.where(own, jnp.concatenate([rows] * (HEAD_DIM // RIM), axis=0), 0.0))
    level = 3
    while (1 << level) < HEAD_DIM:
        mask = (row >> (level + 2) == col >> (level + 2)) & (row >> level != col >> level)
        parts = [split(d) for d in found]
        cross = [split(jnp.where(mask, n, 0.0)) for n in systems]
        maps = [split(mm(p, c, "nn")) for p, c in zip(parts, cross)]
        twice = [mm(m, cols_of(m, p), "nn") for m, p in zip(maps, parts)]
        less = [d - t[:, HEAD_DIM:] for d, t in zip(found, twice)]
        found = [y + mm(split(t[:, :HEAD_DIM]), split(y), "nn") for y, t in zip(less, twice)]
        level += 2
    return found


def mixes_of(normed, rim, kern):
    row8 = lax.broadcasted_iota(jnp.int32, (RIM, HEAD_DIM), 0)
    taps = kern.shape[1]
    shifted = [normed]
    for s in range(1, taps):
        moved = pltpu.roll(normed, s, 0)
        first = jnp.where(row8 < s, pltpu.roll(rim, s, 0), moved[:RIM])
        shifted.append(jnp.concatenate([first, moved[RIM:]], axis=0))
    return [
        sum(kern[j, i : i + 1] * shifted[taps - 1 - i] for i in range(taps)) for j in range(3)
    ]


def gates_kernel(decay_ref, beta_ref, e1_ref, e2_ref, edge_ref, rate_ref):
    length = decay_ref.shape[0]
    row, col = iotas()
    tril = jnp.where(row >= col, 1.0, 0.0).astype(bf16)
    tril = jnp.concatenate([tril] * 3, axis=1)
    for head in range(decay_ref.shape[1] // HEAD_DIM):
        here = slice(head * HEAD_DIM, (head + 1) * HEAD_DIM)
        decay = decay_ref[:, here]
        high = decay.astype(bf16)
        rest = decay - high.astype(f32)
        mid = rest.astype(bf16)
        low = (rest - mid.astype(f32)).astype(bf16)
        cumulative = lax.dot_general(
            tril, jnp.concatenate([high, mid, low], axis=0), DIMS["nn"], preferred_element_type=f32
        )
        middle = cumulative[length // 2 : length // 2 + 1]
        final = cumulative[length - 1 : length]
        e1_ref[:, here] = jnp.exp(cumulative - middle)
        e2_ref[:, here] = jnp.exp(middle - cumulative)
        edge_ref[0:8, here] = jnp.broadcast_to(jnp.exp(middle), (8, HEAD_DIM))
        edge_ref[8:16, here] = jnp.broadcast_to(jnp.exp(final - middle), (8, HEAD_DIM))
        edge_ref[16:24, here] = jnp.broadcast_to(jnp.exp(final), (8, HEAD_DIM))
        rate_ref[:, here] = down_rows(beta_ref[head : head + 1])


def scaled(x_ref, rim_ref, kern_ref, scale, rim_scale, at):
    x = x_ref[:, at].astype(f32)
    return mixes_of(x * scale, rim_ref[:, at] * rim_scale, kern_ref[:, :, at])


def scales(flags, scale_ref, rim_scale_ref):
    rim_scale = down_rows(rim_scale_ref[...])
    rim_scale = jnp.where(flags[4] != 0, rim_scale[rim_scale.shape[0] - RIM :], 0.0)
    return down_rows(scale_ref[...]), rim_scale


def keep_split(ref, j, n, parts):
    ref[j, n] = parts[0]
    ref[j, n + 1] = parts[1]


def kept(ref, j, n):
    return ref[j, n], ref[j, n + 1]


def local_kernel(
    slots, flags, x_ref, go_ref, kern_ref, e1_ref, e2_ref, edge_ref, rate_ref, rim_ref, scale_ref, rim_scale_ref,
    comp_ref, wide_ref, narrow_ref,
):
    length = x_ref.shape[0]
    row, col = iotas()
    strict, full = row > col, row >= col
    scale, rim_scale = scales(flags, scale_ref, rim_scale_ref)
    data = []
    for j, slot in enumerate(slots):
        at = lane_slice(slot ^ flags[0])
        mixes = scaled(x_ref, rim_ref, kern_ref, scale, rim_scale, at)
        act = [m / (1.0 + jnp.exp(-m)) for m in mixes]
        q, k = [a * lax.rsqrt(jnp.sum(a * a, axis=1, keepdims=True) + epsilon) for a in act[:2]]
        rate, e1, e2 = rate_ref[:, at], e1_ref[:, at], e2_ref[:, at]
        em, ecm, ef = [edge_ref[n : n + 1, at] for n in (0, 8, 16)]
        qf, kf, kb = q * e1, k * e1, k * e2
        skf, sqf, skb = split(kf), split(qf), split(kb)
        products = mm(rows_of(skf, sqf), skb, "nt")
        system = jnp.where(strict, rate * products[:length], 0.0)
        scores = split(jnp.where(full, products[length:], 0.0))
        go = exact(go_ref[:, at])
        fresh_grad = split(mm(scores, go, "tn"))
        wide_ref[j, 0], wide_ref[j, 1] = q, k
        for n, parts in enumerate((skf, sqf, skb, scores, fresh_grad)):
            keep_split(narrow_ref, j, 2 * n, parts)
        data.append(
            dict(system=system, go=go, rhs=cols_of(split(rate * kf * em), split(rate * act[2])), ke=split(kb * ecm),
                 qg=qf * em, fresh_grad=fresh_grad, ef=ef)
        )
    inverses = inverse_all([d["system"] for d in data])
    for j, (d, inverse) in enumerate(zip(data, inverses)):
        inverse = split(inverse)
        keep_split(narrow_ref, j, 14, inverse)
        solved = mm(inverse, d["rhs"], "nn")
        wide_ref[j, 2] = solved[:, HEAD_DIM:]
        d["solved"] = split(solved)
    for j, d in enumerate(data):
        solved = d["solved"]
        keep_split(narrow_ref, j, 10, (solved[0][:, :HEAD_DIM], solved[1][:, :HEAD_DIM]))
        keep_split(narrow_ref, j, 12, (solved[0][:, HEAD_DIM:], solved[1][:, HEAD_DIM:]))
        maps = mm(d["ke"], solved, "tn")
        comp_ref[j, 0:128] = jnp.where(row == col, d["ef"], 0.0) - maps[:, :HEAD_DIM]
        comp_ref[j, 128:256] = maps[:, HEAD_DIM:]
        w = (solved[0][:, :HEAD_DIM], solved[1][:, :HEAD_DIM])
        comp_ref[j, 256:384] = mm(split(d["qg"]), d["go"], "tn") - mm(w, d["fresh_grad"], "tn")


WIDE, NARROW = 3, 16


def ready_kernel(
    slots, flags, x_ref, kern_ref, e2_ref, edge_ref, rim_ref, scale_ref, rim_scale_ref, wide_ref, narrow_ref,
    more_ref, pairs_ref,
):
    scale, rim_scale = scales(flags, scale_ref, rim_scale_ref)
    for j, slot in enumerate(slots):
        at = lane_slice(slot ^ flags[0])
        mixes = scaled(x_ref, rim_ref, kern_ref, scale, rim_scale, at)
        sig = [1.0 / (1.0 + jnp.exp(-m)) for m in mixes]
        slope = [s * (1.0 + m * (1.0 - s)) for m, s in zip(mixes, sig)]
        act = [m * s for m, s in zip(mixes[:2], sig)]
        inv = [lax.rsqrt(jnp.sum(a * a, axis=1, keepdims=True) + epsilon) for a in act]
        em, ecm = edge_ref[0:1, at], edge_ref[8:9, at]
        scores, fresh_grad, inverse = [kept(narrow_ref, j, n) for n in (6, 8, 14)]
        solved = cols_of(kept(narrow_ref, j, 10), kept(narrow_ref, j, 12))
        seen = mm(scores, solved, "nn")
        ke = split(wide_ref[j, 1] * e2_ref[:, at] * ecm)
        back = mm(inverse, cols_of(fresh_grad, ke), "tn")
        more_ref[j, 0] = slope[0] * inv[0]
        more_ref[j, 1] = slope[1] * inv[1]
        more_ref[j, 2] = slope[2]
        more_ref[j, 3] = seen[:, HEAD_DIM:]
        more_ref[j, 4] = back[:, :HEAD_DIM]
        qf = narrow_ref[j, 2].astype(f32) + narrow_ref[j, 3].astype(f32)
        keep_split(pairs_ref, j, 0, split(qf * em - seen[:, :HEAD_DIM]))
        keep_split(pairs_ref, j, 2, split(back[:, HEAD_DIM:]))


MORE, PAIRS = 5, 4


def join_kernel(flags, keep_ref, recv_ref, *outs):
    later = flags[1] != 0
    outs = outs[-keep_ref.shape[0] :]
    for j, out in enumerate(outs):
        keep, recv = keep_ref[j], recv_ref[j]
        lo = jnp.where(later, recv, keep)
        hi = jnp.where(later, keep, recv)
        lo_map, hi_map = split(lo[0:128]), split(hi[0:128])
        forward = mm(hi_map, cols_of(lo_map, split(lo[128:256])), "nn")
        back = mm(lo_map, split(hi[256:384]), "tn")
        out[0:128] = forward[:, :HEAD_DIM]
        out[128:256] = forward[:, HEAD_DIM:] + hi[128:256]
        out[256:384] = back + lo[256:384]


def collect(place, parts, held):
    for n, part in enumerate(parts):
        held[place ^ n] = part[...]


def gather_kernel(count, waits, flags, *refs):
    parts, outs, held = refs[:count], refs[count + waits : -1], refs[-1]
    collect(flags[2], parts, held)
    maps = [split(held[p, 0:128]) for p in range(count)]
    state, grad = held[0, 128:256], held[count - 1, 256:384]
    whole = held[0, 0:128]
    for p in range(1, count):
        state = mm(maps[p], split(state), "nn") + held[p, 128:256]
        grad = mm(maps[count - 1 - p], split(grad), "tn") + held[count - 1 - p, 256:384]
        whole = mm(maps[p], split(whole), "nn")
    outs[0][...], outs[1][...], outs[2][...] = whole, state, grad


def hop_kernel(flags, t_ref, u_ref, g_ref, s_ref, e_ref, s_out, e_out):
    t = split(t_ref[...])
    s_out[...] = mm(t, split(s_ref[...]), "nn") + u_ref[...]
    e_out[...] = mm(t, split(e_ref[...]), "tn") + g_ref[...]


def spread_kernel(count, flags, *refs):
    parts, ins, outs, held, found = refs[:count], refs[count : -2 - count], refs[-2 - count : -2], refs[-2], refs[-1]
    collect(flags[2], parts, held)
    state, grad = ins[0][...], ins[1][...]
    for p in range(count):
        back = count - 1 - p
        found[p, 0:128] = state
        found[back, 128:256] = grad
        if p + 1 < count:
            state = mm(split(held[p, 0:128]), split(state), "nn") + held[p, 128:256]
            grad = mm(split(held[back, 0:128]), split(grad), "tn") + held[back, 256:384]
    for n, out in enumerate(outs):
        out[...] = found[flags[2] ^ n]


def two_gather_kernel(waits, flags, *refs):
    parts, outs = refs[:4], refs[4 + waits : -1]
    held = refs[-1]
    total_ref, known_ref, pairs_ref, found_ref = outs
    upper = flags[3] != 0
    collect(flags[2], parts, held)
    t = [split(held[p, 0:128]) for p in range(4)]
    u = [held[p, 128:256] for p in range(4)]
    g = [held[p, 256:384] for p in range(4)]
    last = mm(t[3], cols_of(t[2], split(u[2])), "nn")
    first = mm(t[1], cols_of(t[0], split(u[0])), "nn")
    second = first[:, HEAD_DIM:] + u[1]
    first, last, last_u = first[:, :HEAD_DIM], last[:, :HEAD_DIM], last[:, HEAD_DIM:]
    third = mm(t[2], split(g[3]), "tn") + g[2]
    low = mm(t[0], split(g[1]), "tn")
    s_second, s_third = split(second), split(third)
    forward = [jnp.zeros_like(second), u[0], second, mm(t[2], s_second, "nn") + u[2]]
    back = [mm(t[1], s_third, "tn") + g[1], third, g[3], jnp.zeros_like(third)]
    state = mm(split(last), s_second, "nn") + (last_u + u[3])
    grad = mm(split(first), s_third, "tn") + (low + g[0])
    total_ref[...] = jnp.where(upper, grad, state)
    pairs_ref[0], pairs_ref[1] = first, last
    for p in range(4):
        found_ref[p] = jnp.where(upper, back[p], forward[p])
        known_ref[p] = jnp.where(upper, forward[p], back[3 - p])


def reach_kernel(flags, *refs):
    parts, pairs_ref, found_ref, out_ref, early, held = refs[:4], refs[4], refs[5], refs[6], refs[7:11], refs[11]
    for n, out in enumerate(early):
        out[...] = found_ref[flags[2] ^ n]
    upper = flags[3] != 0
    collect(flags[2], parts, held)
    first, last = pairs_ref[0], pairs_ref[1]
    far_up = mm(split(held[2, 0:128]), split(first), "nn")
    far_down = mm(split(last), split(held[1, 0:128]), "nn")
    ups, downs = (held[0, 0:128], first, far_up), (held[3, 0:128], last, far_down)
    for n in range(3):
        high, low = split(jnp.where(upper, ups[n], jnp.transpose(downs[n])))
        out_ref[2 * n], out_ref[2 * n + 1] = high, low


def late_kernel(flags, recv_ref, known_ref, reach_ref, *refs):
    outs, found = refs[:-1], refs[-1]
    from_end = jnp.where(flags[3] != 0, 0, 3)
    recv = recv_ref[...]
    parts = split(recv)
    found[from_end] = recv
    for n in range(3):
        found[from_end ^ (n + 1)] = mm((reach_ref[2 * n], reach_ref[2 * n + 1]), parts, "nn") + known_ref[n + 1]
    for n, out in enumerate(outs):
        out[...] = found[flags[2] ^ n]


def part_kernel(flags, keep_ref, recv_ref, *refs):
    heads = keep_ref.shape[0]
    ins, (mine_ref, send_ref) = refs[:-2], refs[-2:]
    later, upper = flags[1] != 0, flags[3] != 0
    for j in range(heads):
        if len(ins) == heads:
            start, end = ins[j][0:128], ins[j][128:256]
        else:
            early, late = ins[j][...], ins[heads + j][...]
            start, end = jnp.where(upper, late, early), jnp.where(upper, early, late)
        keep, recv = keep_ref[j], recv_ref[j]
        lo = jnp.where(later, recv, keep)
        hi = jnp.where(later, keep, recv)
        start_hi = mm(split(lo[0:128]), split(start), "nn") + lo[128:256]
        end_lo = mm(split(hi[0:128]), split(end), "tn") + hi[256:384]
        mine_ref[j, 0:128] = jnp.where(later, start_hi, start)
        mine_ref[j, 128:256] = jnp.where(later, end, end_lo)
        send_ref[j, 0:128] = jnp.where(later, start, start_hi)
        send_ref[j, 128:256] = jnp.where(later, end_lo, end)


def back_kernel(
    slots, n_states, chained, last, flags, x_ref, go_ref, kern_ref, e1_ref, e2_ref, edge_ref, rate_ref, rim_ref, wide_ref,
    narrow_ref, more_ref, pairs_ref, *rest,
):
    state_refs, rest = rest[:n_states], rest[n_states:]
    if chained:
        sums_in, rim_grad_in, rest = rest[0], rest[1], rest[3:]
    out_hbm, grad_ref, sums_ref, rim_grad_ref, out_ref, sems = rest[:4] + rest[-2:]
    length = x_ref.shape[0]
    channels = x_ref.shape[1]
    row, col = iotas()
    row8 = lax.broadcasted_iota(jnp.int32, (RIM, HEAD_DIM), 0)
    strict, full = row > col, row >= col
    taps = kern_ref.shape[1]
    if chained:
        rim_grad_ref[...] = rim_grad_in[...]
    dot_all = rim_dot = 0.0
    data, copies = [], []
    states = [(ref, n) for ref in state_refs for n in range(ref.shape[0])]
    for j, slot in enumerate(slots):
        at = lane_slice(slot ^ flags[0])
        state_ref, n = states[j]
        start, end = split(state_ref[n, 0:128]), split(state_ref[n, 128:256])
        first = mm(rows_of(kept(pairs_ref, j, 0), kept(narrow_ref, j, 10)), start, "nn")
        z = more_ref[j, 4] + mm(kept(pairs_ref, j, 2), end, "nn")
        x = x_ref[:, at].astype(f32)
        out_ref[j] = (x + (more_ref[j, 3] + first[:length])).astype(bf16)
        copies.append(pltpu.make_async_copy(out_ref.at[j], out_hbm.at[:, at], sems.at[j]))
        copies[-1].start()
        data.append(dict(at=at, x=x, start=start, end=end, z=z, fresh=split(wide_ref[j, 2] - first[length:])))
    for j, d in enumerate(data):
        at = d["at"]
        q, k = wide_ref[j, 0], wide_ref[j, 1]
        gq, gk, gv = [more_ref[j, n] for n in range(3)]
        skf, sqf, skb = [kept(narrow_ref, j, n) for n in (0, 2, 4)]
        e1, e2, rate = e1_ref[:, at], e2_ref[:, at], rate_ref[:, at]
        em, ecm = edge_ref[0:1, at], edge_ref[8:9, at]
        go = exact(go_ref[:, at])
        second = mm(rows_of(go, split(d["z"])), rows_of(d["fresh"], d["start"]), "nt")
        score_grad = split(jnp.where(full, second[:length, :HEAD_DIM], 0.0))
        product_grad = split(jnp.where(strict, -rate * second[length:, :HEAD_DIM], 0.0))
        qg_grad = second[:length, HEAD_DIM:]
        kg_grad = -rate * second[length:, HEAD_DIM:]
        ke_grad = mm(d["fresh"], d["end"], "nt")
        pair = rows_of(score_grad, product_grad)
        third = mm(pair, skb, "nn")
        kb_grad = mm(pair, rows_of(sqf, skf), "tn")
        q_grad = e1 * (third[:length] + em * qg_grad)
        k_grad = e1 * (third[length:] + em * kg_grad) + e2 * (kb_grad + ecm * ke_grad)
        mix_grads = [
            gq * (q_grad - q * jnp.sum(q * q_grad, axis=1, keepdims=True)),
            gk * (k_grad - k * jnp.sum(k * k_grad, axis=1, keepdims=True)),
            gv * (rate * d["z"]),
        ]
        kern = kern_ref[:, :, at]
        normed_grad = rim_grad = 0.0
        for i in range(taps):
            each = sum(kern[n, i : i + 1] * mix_grads[n] for n in range(3))
            s = taps - 1 - i
            if s == 0:
                normed_grad = normed_grad + each
            else:
                moved = pltpu.roll(each, length - s, 0)
                normed_grad = normed_grad + jnp.where(row < length - s, moved, 0.0)
                rim_grad = rim_grad + jnp.where(row8 >= RIM - s, moved[length - RIM :], 0.0)
        grad_ref[j] = normed_grad
        rim_grad_ref[:, at] = rim_grad
        dot_all = dot_all + normed_grad * d["x"]
        rim_dot = rim_dot + rim_grad * rim_ref[:, at]
    sums = row_sums(dot_all)
    rim_sums = jnp.broadcast_to(jnp.sum(rim_dot, axis=1, keepdims=True), rim_dot.shape)
    if chained:
        sums, rim_sums = sums + sums_in[...], rim_sums + rim_grad_in[:, channels:]
    sums_ref[...] = sums
    rim_grad_ref[:, channels:] = rim_sums
    if last:
        rest[4][...] = rim_sums
    for copy in copies:
        copy.wait()


def finish_kernel(slots, width, flags, x_ref, go_ref, scale_ref, inner_ref, next_sums_ref, next_ref, *refs):
    grads, (out_hbm, out_ref, sems) = refs[:-3], refs[-3:]
    length = x_ref.shape[0]
    scale = down_rows(scale_ref[...])
    inner = down_rows(inner_ref[...])
    last = flags[5] == 0
    next_sums = jnp.where(last, 0.0, next_sums_ref[...])
    inner = jnp.concatenate([inner[: length - RIM], inner[length - RIM :] + next_sums], axis=0)
    cubed = scale * scale * scale * inner * (1.0 / width)
    copies = []
    places = [(ref, n) for ref in grads for n in range(ref.shape[0])]
    for j, (slot, (grad_ref, n)) in enumerate(zip(slots, places)):
        at = lane_slice(slot ^ flags[0])
        grad = grad_ref[n]
        next_grad = jnp.where(last, 0.0, next_ref[:, at])
        grad = jnp.concatenate([grad[: length - RIM], grad[length - RIM :] + next_grad], axis=0)
        total = go_ref[:, at].astype(f32) + grad * scale - x_ref[:, at].astype(f32) * cubed
        out_ref[j] = total.astype(bf16)
        copies.append(pltpu.make_async_copy(out_ref.at[j], out_hbm.at[:, at], sems.at[j]))
        copies[-1].start()
    for copy in copies:
        copy.wait()


def call(kernel, outs, *args, name=None, scratch=(), scalar=(), cost=None, far_in=False, far_out=(), unread=(), alias=None):
    spec, hbm = pl.BlockSpec(memory_space=pltpu.VMEM), pl.BlockSpec(memory_space=pltpu.HBM)
    in_specs = [hbm if far_in else spec] * len(args)
    in_specs += [pl.BlockSpec(memory_space=pl.ANY)] * len(unread)
    args = args + tuple(unread)
    aliases = {}
    if alias is not None:
        args, in_specs, aliases = args + (alias,), in_specs + [hbm], {len(args): 0}
    return pl.pallas_call(
        (lambda *refs: kernel(placed(*scalar), *refs)) if scalar else kernel,
        out_shape=list(outs),
        in_specs=in_specs,
        out_specs=[hbm if n in far_out else spec for n in range(len(outs))],
        scratch_shapes=scratch,
        input_output_aliases=aliases,
        compiler_params=pltpu.CompilerParams(vmem_limit_bytes=VMEM_LIMIT),
        cost_estimate=cost,
        name=name,
    )(*args)


BESIDE = pl.CostEstimate(flops=10**9, bytes_accessed=10**7, transcendentals=0)


def array(*shape, dtype=f32):
    return jax.ShapeDtypeStruct(shape, dtype)


def placed(per, spots):
    me = lax.axis_index("ctx")
    place, later = lax.rem(lax.shift_right_logical(me, 1), per), lax.rem(me, 2)
    row = lax.rem(lax.div(me, 2 * per), 2)
    return [later * per + place, later, place, row, me, spots - 1 - me]


def shards(inputs, out_grads, conv_weight, log_decay, beta):
    length, channels = inputs.shape
    heads = channels // HEAD_DIM
    sections, spots = lax.axis_size("section"), lax.axis_size("ctx")
    width = channels * sections
    per = heads // 2
    count = per
    slabs = spots // (2 * count)
    spot = functools.partial(call, scalar=(per, spots))

    def turned(value, sec, shift):
        route = [
            (s * spots + c, ((s + sec) % sections) * spots + (c + shift) % spots)
            for s in range(sections)
            for c in range(spots)
        ]
        return lax.ppermute(value, ("section", "ctx"), route)

    def swapped(value, distance):
        return lax.ppermute(value, "ctx", [(i, i ^ distance) for i in range(spots)])

    def moved(value, shift):
        return lax.ppermute(
            value, "ctx", [(i, i + shift) for i in range(spots) if 0 <= i + shift < spots]
        )

    payload, sums, x, go, kern, decay, rates = call(
        prelude_kernel,
        (
            array(RIM, channels + length), array(RIM, length), array(*inputs.shape, dtype=bf16),
            array(*inputs.shape, dtype=bf16), array(*conv_weight.shape), array(*inputs.shape), array(heads, length),
        ),
        *[pltpu.with_memory_space_constraint(a, pltpu.HBM) for a in (inputs, out_grads, conv_weight, log_decay, beta.T)],
        name="prelude", far_in=True, scratch=[pltpu.SemaphoreType.DMA((5,))],
    )
    total = sums
    rim_total = 0.0
    for sec in range(1, sections):
        total = total + turned(sums, sec, 0)
        rim_total = rim_total + turned(sums, sec, 1)
    rim = turned(payload, 0, 1)
    e1, e2, edge, rate = call(
        gates_kernel,
        (array(length, channels), array(length, channels), array(24, channels), array(length, channels)),
        decay, rates, name="gates", cost=BESIDE,
    )
    scale = lax.rsqrt(total / width + norm_eps)
    rim_scale = lax.rsqrt((rim_total + rim[:, channels:]) / width + norm_eps)

    shared = (x, go, kern, e1, e2, edge, rate, rim)
    tile = (HEAD_DIM, HEAD_DIM)

    def local(slots, name):
        n = len(slots)
        return spot(
            functools.partial(local_kernel, slots),
            (array(n, 384, HEAD_DIM), array(n, WIDE, *tile), array(n, NARROW, *tile, dtype=bf16)),
            *shared, scale, rim_scale, name=name,
        )

    def prepared(slots, saved, name):
        n = len(slots)
        return spot(
            functools.partial(ready_kernel, slots),
            (array(n, MORE, *tile), array(n, PAIRS, *tile, dtype=bf16)),
            x, kern, e2, edge, rim, scale, rim_scale, *saved, name=name, cost=BESIDE,
        )

    inner_slots, outer_slots = range(per), range(per, 2 * per)
    outer, *outer_saved = local(outer_slots, "local_outer")
    outer_recv = swapped(outer, 1)
    inner, *inner_saved = local(inner_slots, "local_inner")
    pairs = spot(join_kernel, (array(384, HEAD_DIM),) * per, inner, outer_recv, name="join")
    parts = [pairs[0]] + [swapped(pairs[n], 2 * n) for n in range(1, count)]
    outer_saved += prepared(outer_slots, outer_saved, "ready_outer")
    inner_saved += prepared(inner_slots, inner_saved, "ready_inner")
    ahead = [outer_saved[-1], inner_saved[-1]]

    held = pltpu.VMEM((count, 384, HEAD_DIM), f32)
    square = array(*tile)
    step = 2 * count

    def returned(values):
        return [values[0]] + [swapped(values[n], 2 * n) for n in range(1, count)]

    if slabs == 2 and count == 4:
        found = pltpu.VMEM((count, *tile), f32)
        total, known, products, sure = spot(
            functools.partial(two_gather_kernel, len(ahead)),
            (square, array(4, *tile), array(2, *tile), array(4, *tile)),
            *parts, name="gather", scratch=[held], unread=ahead,
        )
        other = swapped(total, step)
        reach, *early = spot(
            reach_kernel, (array(6, *tile, dtype=bf16),) + (square,) * 4,
            *parts, products, sure, name="reach", scratch=[held], cost=BESIDE,
        )
        early = returned(early)
        late = spot(late_kernel, (square,) * 4, other, known, reach, name="late", scratch=[found])
        states = early + returned(late)
    else:
        gathered = spot(
            functools.partial(gather_kernel, count, len(ahead)), (square,) * 3,
            *parts, name="gather", scratch=[held], unread=ahead,
        )
        ends = (jnp.zeros(tile, f32),) * 2
        for hop in range(slabs - 1):
            if hop == 0:
                ends = gathered[1:]
            else:
                ends = spot(hop_kernel, (square,) * 2, *gathered, *ends, name=f"hop{hop}")
            ends = (moved(ends[0], step), moved(ends[1], -step))
        states = returned(
            spot(
                functools.partial(spread_kernel, count), (array(256, HEAD_DIM),) * count,
                *parts, *ends, name="spread", scratch=[held, pltpu.VMEM((count, 256, HEAD_DIM), f32)],
            )
        )
    mine, send = spot(
        part_kernel, (array(per, 256, HEAD_DIM),) * 2, inner, outer_recv, *states, name="part"
    )
    far = swapped(send, 1)

    def backward(slots, saved, states, chain, name):
        n = len(slots)
        last = chain is not None
        before = (chain[2], chain[3]) if last else ()
        return spot(
            functools.partial(back_kernel, slots, len(states), last, last),
            (
                array(*inputs.shape, dtype=bf16), array(n, length, HEAD_DIM), array(RIM, length),
                array(RIM, channels + HEAD_DIM),
            )
            + (array(RIM, HEAD_DIM),) * last,
            *shared, *saved, *states, *before, name=name, far_out=(0,),
            alias=None if chain is None else chain[0],
            scratch=[pltpu.VMEM((n, length, HEAD_DIM), bf16), pltpu.SemaphoreType.DMA((n,))],
        )

    chain = backward(inner_slots, inner_saved, (mine,), None, "back_inner")
    grads = [chain[1]]
    chain = backward(outer_slots, outer_saved, (far,), chain, "back_outer")
    grads.append(chain[1])
    slots = [*inner_slots, *outer_slots]
    stream_out, _, inner_sum, rim_grad, rim_sums = chain

    inner_total, next_sums = inner_sum, 0.0
    for sec in range(1, sections):
        inner_total = inner_total + turned(inner_sum, sec, 0)
        next_sums = next_sums + turned(rim_sums, sec, -1)
    next_rim = turned(rim_grad, 0, -1)
    (input_grad,) = spot(
        functools.partial(finish_kernel, slots, width), (array(*inputs.shape, dtype=bf16),),
        x, go, scale, inner_total, next_sums + next_rim[:, channels:], next_rim, *grads, name="finish",
        far_out=(0,), scratch=[pltpu.VMEM((heads, length, HEAD_DIM), bf16), pltpu.SemaphoreType.DMA((heads,))],
    )
    return (stream_out, input_grad)


def solution(mesh):
    in_specs = (
        P("ctx", "section"),
        P("ctx", "section"),
        P(None, None, "section"),
        P("ctx", "section"),
        P("ctx", "section"),
    )
    out_specs = (P("ctx", "section"), P("ctx", "section"))
    return jax.shard_map(shards, mesh=mesh, in_specs=in_specs, out_specs=out_specs, check_vma=False)
```

time: 65.1 us -> 57.7 us (0.89)
  Pallas kernels: 25.2 us -> 17.7 us
  starting transfers between devices: 15.9 us -> 20.3 us
  waiting for transfers between devices: 22 us -> 18.8 us
  local copies, waits for them, and re-layouts: 0.77 us -> 0 us
    pallas_call x13 -> x14, Pallas kernels: 25.2 us -> 17.7 us  [call(): pl.pallas_call((lambda *refs: kernel(placed(*scalar), *refs)) if scalar e...]
    ppermute x9 -> x12, waiting for transfers between devices: 15.4 us -> 11.3 us  [swapped(): return lax.ppermute(value, 'ctx', [(i, i ^ distance) for i in range(spots)])]
    ppermute x9 -> x12, starting transfers between devices: 8.1 us -> 11.7 us  [swapped(): return lax.ppermute(value, 'ctx', [(i, i ^ distance) for i in range(spots)])]
    ppermute x6, starting transfers between devices: 7.77 us -> 8.63 us  [turned(): return lax.ppermute(value, ('section', 'ctx'), route)]
    ppermute x6, waiting for transfers between devices: 6.61 us -> 7.43 us  [turned(): return lax.ppermute(value, ('section', 'ctx'), route)]
    unnamed x2 -> x0, local copies, waits for them, and re-layouts: 0.69 us -> none
  transfers between devices with their start and end apart: 15 -> 18, of which waited for: 10 -> 11; matrix products, arithmetic and copies ran while one was open for 0% -> 0% of each run, Pallas kernels for 17% -> 15%
where the time goes in v4:
time: 57.7 us; the launch traced here: 57.5 us
  starting transfers between devices  20.3 us (35%)
  waiting for transfers between devices  18.8 us (33%)
  Pallas kernels  17.7 us (31%)
  between operations  0.78 us (1%)
    pallas_call x14, Pallas kernels, call(): pl.pallas_call((lambda *refs: kernel(placed(*scalar), *refs)) if scalar e...  17.7 us
    ppermute x12, starting transfers between devices, swapped(): return lax.ppermute(value, 'ctx', [(i, i ^ distance) for i in range(spots)])  11.7 us
    ppermute x12, waiting for transfers between devices, swapped(): return lax.ppermute(value, 'ctx', [(i, i ^ distance) for i in range(spots)])  11.3 us
    ppermute x6, starting transfers between devices, turned(): return lax.ppermute(value, ('section', 'ctx'), route)  8.63 us
    ppermute x6, waiting for transfers between devices, turned(): return lax.ppermute(value, ('section', 'ctx'), route)  7.43 us
  transfers between devices with their start and end apart: 18, of which 11 were waited for; matrix products, arithmetic and copies ran while one was open for 0% of the time, Pallas kernels for 15%

profile of v4, /device:TPU:0, one launch (start us, length us, event | category | flops | bytes accessed | tf_op | source)
XLA Modules:
  0.0 57.5 jit_solution(12530752214425971994)
XLA Ops:
  0.6 1.3 %prelude.1 = (f32[8,1152]{1,0:T(8,128)S(1)}, f32[8,128]{1,0:T(8,128)S(1)}, bf16[128,1024]{1,0:T(8,128)(2,1)S(1)}, bf16[128,1024]{1,0:T(8,128)(2,1)S(1)}, f32[3,4...) custom-call(bf16[128,1024]{1,0:T(8,128)(2,1)} %x_hbm.1, bf16[128,1024]{1,0:T(8,128)(2,1)} %go_hbm.1, ...), custom_call_target="tpu_custom_call" | custom-call | tf_op jit(solution)/shard_map/prelude/pallas_call | solution.py:512
  2.0 2.4 %collective-permute-start.2 = (f32[8,128]{1,0:T(8,128)S(1)}, f32[8,128]{1,0:T(8,128)S(1)}, u32[]{:S(2)}, u32[]{:S(2)}) collective-permute-start(f32[8,128]{1,0:T(8,128)S(1)} %get-tuple-element.61), channel_id=1, source_target_pairs={{0,17},{1,18},{2,19},{3,20},{4,21},{5,22},{6,23},{7,24},{8,25},{9,... | collective-permute-start | bytes 12296 | tf_op jit(solution)/shard_map/ppermute | solution.py:555
  4.4 0.6 %collective-permute-start.1 = (f32[8,128]{1,0:T(8,128)S(1)}, f32[8,128]{1,0:T(8,128)S(1)}, u32[]{:S(2)}, u32[]{:S(2)}) collective-permute-start(f32[8,128]{1,0:T(8,128)S(1)} %get-tuple-element.61), channel_id=1, source_target_pairs={{0,16},{1,17},{2,18},{3,19},{4,20},{5,21},{6,22},{7,23},{8,24},{9,... | collective-permute-start | bytes 12296 | tf_op jit(solution)/shard_map/ppermute | solution.py:555
  5.0 1.2 %collective-permute-start = (f32[8,1152]{1,0:T(8,128)S(1)}, f32[8,1152]{1,0:T(8,128)S(1)}, u32[]{:S(2)}, u32[]{:S(2)}) collective-permute-start(f32[8,1152]{1,0:T(8,128)S(1)} %get-tuple-element.60), channel_id=1, source_target_pairs={{0,1},{1,2},{2,3},{3,4},{4,5},{5,6},{6,7},{7,8},{8,9},{9,10},{10,1... | collective-permute-start | bytes 110600 | tf_op jit(solution)/shard_map/ppermute | solution.py:555
  6.3 0.4 gates.1
  6.7 1.3 %collective-permute-done.1 = f32[8,128]{1,0:T(8,128)S(1)} collective-permute-done((f32[8,128]{1,0:T(8,128)S(1)}, f32[8,128]{1,0:T(8,128)S(1)}, u32[]{:S(2)}, u32[]{:S(2)}) %collective-permute-start.1) | collective-permute-done | bytes 4128 | tf_op jit(solution)/shard_map/ppermute | solution.py:555
  8.0 1.7 %collective-permute-done.2 = f32[8,128]{1,0:T(8,128)S(1)} collective-permute-done((f32[8,128]{1,0:T(8,128)S(1)}, f32[8,128]{1,0:T(8,128)S(1)}, u32[]{:S(2)}, u32[]{:S(2)}) %collective-permute-start.2) | collective-permute-done | bytes 4128 | tf_op jit(solution)/shard_map/ppermute | solution.py:555
  9.7 1.4 %collective-permute-done.refs_7_.refs_4_ = f32[8,1152]{1,0:T(8,128)S(1)} collective-permute-done((f32[8,1152]{1,0:T(8,128)S(1)}, f32[8,1152]{1,0:T(8,128)S(1)}, u32[]{:S(2)}, u32[]{:S(2)}) %collective-permute-start) | collective-permute-done | bytes 36896 | tf_op jit(solution)/shard_map/ppermute | solution.py:555
  11.1 3.0 %local_outer.1 = (f32[4,384,128]{2,1,0:T(8,128)S(1)}, f32[4,3,128,128]{3,2,1,0:T(8,128)S(1)}, bf16[4,16,128,128]{3,2,1,0:T(8,128)(2,1)S(1)}) custom-call(bf16[128,1024]{1,0:T(8,128)(2,1)S(1)} %get-tuple-element.51.refs_0_, bf16[128,1024]{1,0:T(8,128)(2,1)S(1)} %get-tuple-element.52.refs_1_, f32[3,4,1024]{2,1,0:T(4,128)S(1)} %get-tuple-element.53.refs_2_.refs_1_, ...), custom_call_target="tpu_custom_call" | custom-call | tf_op jit(solution)/shard_map/local_outer/pallas_call | solution.py:512
  14.1 0.1 collective-permute-start.3
  14.2 3.0 %local_inner.1 = (f32[4,384,128]{2,1,0:T(8,128)S(1)}, f32[4,3,128,128]{3,2,1,0:T(8,128)S(1)}, bf16[4,16,128,128]{3,2,1,0:T(8,128)(2,1)S(1)}) custom-call(bf16[128,1024]{1,0:T(8,128)(2,1)S(1)} %get-tuple-element.51.refs_0_, bf16[128,1024]{1,0:T(8,128)(2,1)S(1)} %get-tuple-element.52.refs_1_, f32[3,4,1024]{2,1,0:T(4,128)S(1)} %get-tuple-element.53.refs_2_.refs_1_, ...), custom_call_target="tpu_custom_call" | custom-call | tf_op jit(solution)/shard_map/local_inner/pallas_call | solution.py:512
  17.2 0.0 collective-permute-done.3.refs_1_
  17.2 0.4 join.1
  17.6 0.1 collective-permute-start.4
  17.7 0.5 collective-permute-start.5
  18.2 3.0 %collective-permute-start.6 = (f32[384,128]{1,0:T(8,128)S(1)}, f32[384,128]{1,0:T(8,128)S(1)}, u32[]{:S(2)}, u32[]{:S(2)}) collective-permute-start(f32[384,128]{1,0:T(8,128)S(1)} %get-tuple-element.71), channel_id=1, source_target_pairs={{0,6},{1,7},{2,4},{3,5},{4,2},{5,3},{6,0},{7,1},{8,14},{9,15},{10,... | collective-permute-start | bytes 589832 | tf_op jit(solution)/shard_map/ppermute | solution.py:558
  21.2 0.9 %ready_inner.1 = (f32[4,5,128,128]{3,2,1,0:T(8,128)S(1)}, bf16[4,4,128,128]{3,2,1,0:T(8,128)(2,1)S(1)}) custom-call(bf16[128,1024]{1,0:T(8,128)(2,1)S(1)} %get-tuple-element.51.refs_0_, f32[3,4,1024]{2,1,0:T(4,128)S(1)} %get-tuple-element.53.refs_2_.refs_1_, f32[128,1024]{1,0:T(8,128)S(1)} %get-tuple-element.57.refs_4_.refs_2_, ...), custom_call_target="tpu_custom_call" | custom-call | flops 1000000000 | bytes 10000000 | tf_op jit(solution)/shard_map/ready_inner/pallas_call | solution.py:512
  22.1 0.9 %ready_outer.1 = (f32[4,5,128,128]{3,2,1,0:T(8,128)S(1)}, bf16[4,4,128,128]{3,2,1,0:T(8,128)(2,1)S(1)}) custom-call(bf16[128,1024]{1,0:T(8,128)(2,1)S(1)} %get-tuple-element.51.refs_0_, f32[3,4,1024]{2,1,0:T(4,128)S(1)} %get-tuple-element.53.refs_2_.refs_1_, f32[128,1024]{1,0:T(8,128)S(1)} %get-tuple-element.57.refs_4_.refs_2_, ...), custom_call_target="tpu_custom_call" | custom-call | flops 1000000000 | bytes 10000000 | tf_op jit(solution)/shard_map/ready_outer/pallas_call | solution.py:512
  23.0 2.0 %collective-permute-done.4.refs_1_ = f32[384,128]{1,0:T(8,128)S(1)} collective-permute-done((f32[384,128]{1,0:T(8,128)S(1)}, f32[384,128]{1,0:T(8,128)S(1)}, u32[]{:S(2)}, u32[]{:S(2)}) %collective-permute-start.4) | collective-permute-done | bytes 196640 | tf_op jit(solution)/shard_map/ppermute | solution.py:558
  25.0 0.5 collective-permute-done.5.refs_2_
  25.5 4.9 %collective-permute-done.6.refs_3_ = f32[384,128]{1,0:T(8,128)S(1)} collective-permute-done((f32[384,128]{1,0:T(8,128)S(1)}, f32[384,128]{1,0:T(8,128)S(1)}, u32[]{:S(2)}, u32[]{:S(2)}) %collective-permute-start.6) | collective-permute-done | bytes 196640 | tf_op jit(solution)/shard_map/ppermute | solution.py:558
  30.4 0.6 gather.1
  31.0 0.9 %collective-permute-start.10 = (f32[128,128]{1,0:T(8,128)S(1)}, f32[128,128]{1,0:T(8,128)S(1)}, u32[]{:S(2)}, u32[]{:S(2)}) collective-permute-start(f32[128,128]{1,0:T(8,128)S(1)} %get-tuple-element.81), channel_id=1, source_target_pairs={{0,8},{1,9},{2,10},{3,11},{4,12},{5,13},{6,14},{7,15},{8,0},{9,1},... | collective-permute-start | bytes 196616 | tf_op jit(solution)/shard_map/ppermute | solution.py:558
  31.8 0.3 reach.1
  32.2 0.7 %collective-permute-start.7 = (f32[128,128]{1,0:T(8,128)S(1)}, f32[128,128]{1,0:T(8,128)S(1)}, u32[]{:S(2)}, u32[]{:S(2)}) collective-permute-start(f32[128,128]{1,0:T(8,128)S(1)} %get-tuple-element.78), channel_id=1, source_target_pairs={{0,2},{1,3},{2,0},{3,1},{4,6},{5,7},{6,4},{7,5},{8,10},{9,11},{10,... | collective-permute-start | bytes 196616 | tf_op jit(solution)/shard_map/ppermute | solution.py:558
  32.9 1.6 %collective-permute-start.8 = (f32[128,128]{1,0:T(8,128)S(1)}, f32[128,128]{1,0:T(8,128)S(1)}, u32[]{:S(2)}, u32[]{:S(2)}) collective-permute-start(f32[128,128]{1,0:T(8,128)S(1)} %get-tuple-element.79), channel_id=1, source_target_pairs={{0,4},{1,5},{2,6},{3,7},{4,0},{5,1},{6,2},{7,3},{8,12},{9,13},{10,... | collective-permute-start | bytes 196616 | tf_op jit(solution)/shard_map/ppermute | solution.py:558
  34.4 1.3 %collective-permute-start.9 = (f32[128,128]{1,0:T(8,128)S(1)}, f32[128,128]{1,0:T(8,128)S(1)}, u32[]{:S(2)}, u32[]{:S(2)}) collective-permute-start(f32[128,128]{1,0:T(8,128)S(1)} %get-tuple-element.80), channel_id=1, source_target_pairs={{0,6},{1,7},{2,4},{3,5},{4,2},{5,3},{6,0},{7,1},{8,14},{9,15},{10,... | collective-permute-start | bytes 196616 | tf_op jit(solution)/shard_map/ppermute | solution.py:558
  35.7 1.0 %collective-permute-done.10.refs_0_ = f32[128,128]{1,0:T(8,128)S(1)} collective-permute-done((f32[128,128]{1,0:T(8,128)S(1)}, f32[128,128]{1,0:T(8,128)S(1)}, u32[]{:S(2)}, u32[]{:S(2)}) %collective-permute-start.10) | collective-permute-done | bytes 65568 | tf_op jit(solution)/shard_map/ppermute | solution.py:558
  36.8 0.2 late.1
  37.0 0.4 collective-permute-start.11
  37.4 0.8 %collective-permute-start.12 = (f32[128,128]{1,0:T(8,128)S(1)}, f32[128,128]{1,0:T(8,128)S(1)}, u32[]{:S(2)}, u32[]{:S(2)}) collective-permute-start(f32[128,128]{1,0:T(8,128)S(1)} %get-tuple-element.86), channel_id=1, source_target_pairs={{0,4},{1,5},{2,6},{3,7},{4,0},{5,1},{6,2},{7,3},{8,12},{9,13},{10,... | collective-permute-start | bytes 196616 | tf_op jit(solution)/shard_map/ppermute | solution.py:558
  38.2 0.0 collective-permute-done.7.refs_3_
  38.2 2.3 %collective-permute-start.13 = (f32[128,128]{1,0:T(8,128)S(1)}, f32[128,128]{1,0:T(8,128)S(1)}, u32[]{:S(2)}, u32[]{:S(2)}) collective-permute-start(f32[128,128]{1,0:T(8,128)S(1)} %get-tuple-element.87), channel_id=1, source_target_pairs={{0,6},{1,7},{2,4},{3,5},{4,2},{5,3},{6,0},{7,1},{8,14},{9,15},{10,... | collective-permute-start | bytes 196616 | tf_op jit(solution)/shard_map/ppermute | solution.py:558
  40.6 0.0 collective-permute-done.8.refs_4_
  40.6 0.0 collective-permute-done.9.refs_5_
  40.6 1.5 %collective-permute-done.11.refs_7_ = f32[128,128]{1,0:T(8,128)S(1)} collective-permute-done((f32[128,128]{1,0:T(8,128)S(1)}, f32[128,128]{1,0:T(8,128)S(1)}, u32[]{:S(2)}, u32[]{:S(2)}) %collective-permute-start.11) | collective-permute-done | bytes 65568 | tf_op jit(solution)/shard_map/ppermute | solution.py:558
  42.0 0.0 collective-permute-done.12.refs_8_
  42.0 1.5 %collective-permute-done.13.refs_9_ = f32[128,128]{1,0:T(8,128)S(1)} collective-permute-done((f32[128,128]{1,0:T(8,128)S(1)}, f32[128,128]{1,0:T(8,128)S(1)}, u32[]{:S(2)}, u32[]{:S(2)}) %collective-permute-start.13) | collective-permute-done | bytes 65568 | tf_op jit(solution)/shard_map/ppermute | solution.py:558
  43.5 0.3 part.1
  43.8 0.1 collective-permute-start.14
  43.9 2.6 %back_inner.1 = (bf16[128,1024]{1,0:T(8,128)(2,1)}, f32[4,128,128]{2,1,0:T(8,128)S(1)}, f32[8,128]{1,0:T(8,128)S(1)}, f32[8,1152]{1,0:T(8,128)S(1)}) custom-call(bf16[128,1024]{1,0:T(8,128)(2,1)S(1)} %get-tuple-element.51.refs_0_, bf16[128,1024]{1,0:T(8,128)(2,1)S(1)} %get-tuple-element.52.refs_1_, f32[3,4,1024]{2,1,0:T(4,128)S(1)} %get-tuple-element.53.refs_2_.refs_1_, ...), custom_call_target="tpu_custom_call" | custom-call | tf_op jit(solution)/shard_map/back_inner/pallas_call | solution.py:512
  46.5 0.0 collective-permute-done.14.refs_12_
  46.5 2.6 %back_outer.1 = (bf16[128,1024]{1,0:T(8,128)(2,1)}, f32[4,128,128]{2,1,0:T(8,128)S(1)}, f32[8,128]{1,0:T(8,128)S(1)}, f32[8,1152]{1,0:T(8,128)S(1)}, f32[8,128]{1,0:T(8,128)S(1)}) custom-call(bf16[128,1024]{1,0:T(8,128)(2,1)S(1)} %get-tuple-element.51.refs_0_, bf16[128,1024]{1,0:T(8,128)(2,1)S(1)} %get-tuple-element.52.refs_1_, ...), custom_call_target="tpu_custom_call", output_to_operand_aliasing={{0}: (15, {})} | custom-call | tf_op jit(solution)/shard_map/back_outer/pallas_call | solution.py:512
  49.1 2.9 %collective-permute-start.17 = (f32[8,1152]{1,0:T(8,128)S(1)}, f32[8,1152]{1,0:T(8,128)S(1)}, u32[]{:S(2)}, u32[]{:S(2)}) collective-permute-start(f32[8,1152]{1,0:T(8,128)S(1)} %get-tuple-element.97), channel_id=1, source_target_pairs={{0,15},{1,0},{2,1},{3,2},{4,3},{5,4},{6,5},{7,6},{8,7},{9,8},{10,9... | collective-permute-start | bytes 110600 | tf_op jit(solution)/shard_map/ppermute | solution.py:555
  52.0 1.4 %collective-permute-start.15 = (f32[8,128]{1,0:T(8,128)S(1)}, f32[8,128]{1,0:T(8,128)S(1)}, u32[]{:S(2)}, u32[]{:S(2)}) collective-permute-start(f32[8,128]{1,0:T(8,128)S(1)} %get-tuple-element.95), channel_id=1, source_target_pairs={{0,16},{1,17},{2,18},{3,19},{4,20},{5,21},{6,22},{7,23},{8,24},{9,... | collective-permute-start | bytes 12296 | tf_op jit(solution)/shard_map/ppermute | solution.py:555
  53.4 0.0 collective-permute-start.16
  53.4 2.2 %collective-permute-done.15 = f32[8,128]{1,0:T(8,128)S(1)} collective-permute-done((f32[8,128]{1,0:T(8,128)S(1)}, f32[8,128]{1,0:T(8,128)S(1)}, u32[]{:S(2)}, u32[]{:S(2)}) %collective-permute-start.15) | collective-permute-done | bytes 4128 | tf_op jit(solution)/shard_map/ppermute | solution.py:555
  55.7 0.8 %collective-permute-done.16 = f32[8,128]{1,0:T(8,128)S(1)} collective-permute-done((f32[8,128]{1,0:T(8,128)S(1)}, f32[8,128]{1,0:T(8,128)S(1)}, u32[]{:S(2)}, u32[]{:S(2)}) %collective-permute-start.16) | collective-permute-done | bytes 4128 | tf_op jit(solution)/shard_map/ppermute | solution.py:555
  56.5 0.0 collective-permute-done.17.refs_5_
  56.5 1.0 %finish.1 = bf16[128,1024]{1,0:T(8,128)(2,1)} custom-call(bf16[128,1024]{1,0:T(8,128)(2,1)S(1)} %get-tuple-element.51.refs_0_, bf16[128,1024]{1,0:T(8,128)(2,1)S(1)} %get-tuple-element.52.refs_1_, f32[8,128]{1,0:T(8,128)S(1)} %add_rsqrt_fusion.refs_8_.refs_5_.refs_2_, f32[8,128]{1,0:T(8,128)S(1)} %add.22.refs_3_, f32[8,128]{1,0:T(8,128)S(1)} %slice_add_fusion.refs_4_, ...), custom_call_target="tpu_custom_call" | custom-call | tf_op jit(solution)/shard_map/finish/pallas_call | solution.py:512
  (4 shorter events, 0.0 us)
Async XLA Ops:
  2.0 7.7 %collective-permute-start.2 = (f32[8,128]{1,0:T(8,128)S(1)}, f32[8,128]{1,0:T(8,128)S(1)}, u32[]{:S(2)}, u32[]{:S(2)}) collective-permute-start(f32[8,128]{1,0:T(8,128)S(1)} %get-tuple-element.61), channel_id=1, source_target_pairs={{0,17},{1,18},{2,19},{3,20},{4,21},{5,22},{6,23},{7,24},{8,25},{9,... | collective-permute-start | bytes 12296 | tf_op jit(solution)/shard_map/ppermute | solution.py:555
  4.4 3.6 %collective-permute-start.1 = (f32[8,128]{1,0:T(8,128)S(1)}, f32[8,128]{1,0:T(8,128)S(1)}, u32[]{:S(2)}, u32[]{:S(2)}) collective-permute-start(f32[8,128]{1,0:T(8,128)S(1)} %get-tuple-element.61), channel_id=1, source_target_pairs={{0,16},{1,17},{2,18},{3,19},{4,20},{5,21},{6,22},{7,23},{8,24},{9,... | collective-permute-start | bytes 12296 | tf_op jit(solution)/shard_map/ppermute | solution.py:555
  5.0 6.1 %collective-permute-start = (f32[8,1152]{1,0:T(8,128)S(1)}, f32[8,1152]{1,0:T(8,128)S(1)}, u32[]{:S(2)}, u32[]{:S(2)}) collective-permute-start(f32[8,1152]{1,0:T(8,128)S(1)} %get-tuple-element.60), channel_id=1, source_target_pairs={{0,1},{1,2},{2,3},{3,4},{4,5},{5,6},{6,7},{7,8},{8,9},{9,10},{10,1... | collective-permute-start | bytes 110600 | tf_op jit(solution)/shard_map/ppermute | solution.py:555
  14.1 3.1 %collective-permute-start.3 = (f32[4,384,128]{2,1,0:T(8,128)S(1)}, f32[4,384,128]{2,1,0:T(8,128)S(1)}, u32[]{:S(2)}, u32[]{:S(2)}) collective-permute-start(f32[4,384,128]{2,1,0:T(8,128)S(1)} %get-tuple-element.67), channel_id=1, source_target_pairs={{0,1},{1,0},{2,3},{3,2},{4,5},{5,4},{6,7},{7,6},{8,9},{9,8},{10,11... | collective-permute-start | bytes 2359304 | tf_op jit(solution)/shard_map/ppermute | solution.py:558
  17.6 7.4 %collective-permute-start.4 = (f32[384,128]{1,0:T(8,128)S(1)}, f32[384,128]{1,0:T(8,128)S(1)}, u32[]{:S(2)}, u32[]{:S(2)}) collective-permute-start(f32[384,128]{1,0:T(8,128)S(1)} %get-tuple-element.69), channel_id=1, source_target_pairs={{0,2},{1,3},{2,0},{3,1},{4,6},{5,7},{6,4},{7,5},{8,10},{9,11},{10,... | collective-permute-start | bytes 589832 | tf_op jit(solution)/shard_map/ppermute | solution.py:558
  17.7 7.8 %collective-permute-start.5 = (f32[384,128]{1,0:T(8,128)S(1)}, f32[384,128]{1,0:T(8,128)S(1)}, u32[]{:S(2)}, u32[]{:S(2)}) collective-permute-start(f32[384,128]{1,0:T(8,128)S(1)} %get-tuple-element.70), channel_id=1, source_target_pairs={{0,4},{1,5},{2,6},{3,7},{4,0},{5,1},{6,2},{7,3},{8,12},{9,13},{10,... | collective-permute-start | bytes 589832 | tf_op jit(solution)/shard_map/ppermute | solution.py:558
  18.2 12.2 %collective-permute-start.6 = (f32[384,128]{1,0:T(8,128)S(1)}, f32[384,128]{1,0:T(8,128)S(1)}, u32[]{:S(2)}, u32[]{:S(2)}) collective-permute-start(f32[384,128]{1,0:T(8,128)S(1)} %get-tuple-element.71), channel_id=1, source_target_pairs={{0,6},{1,7},{2,4},{3,5},{4,2},{5,3},{6,0},{7,1},{8,14},{9,15},{10,... | collective-permute-start | bytes 589832 | tf_op jit(solution)/shard_map/ppermute | solution.py:558
  31.0 5.8 %collective-permute-start.10 = (f32[128,128]{1,0:T(8,128)S(1)}, f32[128,128]{1,0:T(8,128)S(1)}, u32[]{:S(2)}, u32[]{:S(2)}) collective-permute-start(f32[128,128]{1,0:T(8,128)S(1)} %get-tuple-element.81), channel_id=1, source_target_pairs={{0,8},{1,9},{2,10},{3,11},{4,12},{5,13},{6,14},{7,15},{8,0},{9,1},... | collective-permute-start | bytes 196616 | tf_op jit(solution)/shard_map/ppermute | solution.py:558
  32.2 6.1 %collective-permute-start.7 = (f32[128,128]{1,0:T(8,128)S(1)}, f32[128,128]{1,0:T(8,128)S(1)}, u32[]{:S(2)}, u32[]{:S(2)}) collective-permute-start(f32[128,128]{1,0:T(8,128)S(1)} %get-tuple-element.78), channel_id=1, source_target_pairs={{0,2},{1,3},{2,0},{3,1},{4,6},{5,7},{6,4},{7,5},{8,10},{9,11},{10,... | collective-permute-start | bytes 196616 | tf_op jit(solution)/shard_map/ppermute | solution.py:558
  32.9 7.7 %collective-permute-start.8 = (f32[128,128]{1,0:T(8,128)S(1)}, f32[128,128]{1,0:T(8,128)S(1)}, u32[]{:S(2)}, u32[]{:S(2)}) collective-permute-start(f32[128,128]{1,0:T(8,128)S(1)} %get-tuple-element.79), channel_id=1, source_target_pairs={{0,4},{1,5},{2,6},{3,7},{4,0},{5,1},{6,2},{7,3},{8,12},{9,13},{10,... | collective-permute-start | bytes 196616 | tf_op jit(solution)/shard_map/ppermute | solution.py:558
  34.4 6.1 %collective-permute-start.9 = (f32[128,128]{1,0:T(8,128)S(1)}, f32[128,128]{1,0:T(8,128)S(1)}, u32[]{:S(2)}, u32[]{:S(2)}) collective-permute-start(f32[128,128]{1,0:T(8,128)S(1)} %get-tuple-element.80), channel_id=1, source_target_pairs={{0,6},{1,7},{2,4},{3,5},{4,2},{5,3},{6,0},{7,1},{8,14},{9,15},{10,... | collective-permute-start | bytes 196616 | tf_op jit(solution)/shard_map/ppermute | solution.py:558
  37.0 5.0 %collective-permute-start.11 = (f32[128,128]{1,0:T(8,128)S(1)}, f32[128,128]{1,0:T(8,128)S(1)}, u32[]{:S(2)}, u32[]{:S(2)}) collective-permute-start(f32[128,128]{1,0:T(8,128)S(1)} %get-tuple-element.85), channel_id=1, source_target_pairs={{0,2},{1,3},{2,0},{3,1},{4,6},{5,7},{6,4},{7,5},{8,10},{9,11},{10,... | collective-permute-start | bytes 196616 | tf_op jit(solution)/shard_map/ppermute | solution.py:558
  37.4 4.6 %collective-permute-start.12 = (f32[128,128]{1,0:T(8,128)S(1)}, f32[128,128]{1,0:T(8,128)S(1)}, u32[]{:S(2)}, u32[]{:S(2)}) collective-permute-start(f32[128,128]{1,0:T(8,128)S(1)} %get-tuple-element.86), channel_id=1, source_target_pairs={{0,4},{1,5},{2,6},{3,7},{4,0},{5,1},{6,2},{7,3},{8,12},{9,13},{10,... | collective-permute-start | bytes 196616 | tf_op jit(solution)/shard_map/ppermute | solution.py:558
  38.2 5.3 %collective-permute-start.13 = (f32[128,128]{1,0:T(8,128)S(1)}, f32[128,128]{1,0:T(8,128)S(1)}, u32[]{:S(2)}, u32[]{:S(2)}) collective-permute-start(f32[128,128]{1,0:T(8,128)S(1)} %get-tuple-element.87), channel_id=1, source_target_pairs={{0,6},{1,7},{2,4},{3,5},{4,2},{5,3},{6,0},{7,1},{8,14},{9,15},{10,... | collective-permute-start | bytes 196616 | tf_op jit(solution)/shard_map/ppermute | solution.py:558
  43.8 2.7 %collective-permute-start.14 = (f32[4,256,128]{2,1,0:T(8,128)S(1)}, f32[4,256,128]{2,1,0:T(8,128)S(1)}, u32[]{:S(2)}, u32[]{:S(2)}) collective-permute-start(f32[4,256,128]{2,1,0:T(8,128)S(1)} %get-tuple-element.88), channel_id=1, source_target_pairs={{0,1},{1,0},{2,3},{3,2},{4,5},{5,4},{6,7},{7,6},{8,9},{9,8},{10,11... | collective-permute-start | bytes 1572872 | tf_op jit(solution)/shard_map/ppermute | solution.py:558
  49.1 7.3 %collective-permute-start.17 = (f32[8,1152]{1,0:T(8,128)S(1)}, f32[8,1152]{1,0:T(8,128)S(1)}, u32[]{:S(2)}, u32[]{:S(2)}) collective-permute-start(f32[8,1152]{1,0:T(8,128)S(1)} %get-tuple-element.97), channel_id=1, source_target_pairs={{0,15},{1,0},{2,1},{3,2},{4,3},{5,4},{6,5},{7,6},{8,7},{9,8},{10,9... | collective-permute-start | bytes 110600 | tf_op jit(solution)/shard_map/ppermute | solution.py:555
  52.0 3.6 %collective-permute-start.15 = (f32[8,128]{1,0:T(8,128)S(1)}, f32[8,128]{1,0:T(8,128)S(1)}, u32[]{:S(2)}, u32[]{:S(2)}) collective-permute-start(f32[8,128]{1,0:T(8,128)S(1)} %get-tuple-element.95), channel_id=1, source_target_pairs={{0,16},{1,17},{2,18},{3,19},{4,20},{5,21},{6,22},{7,23},{8,24},{9,... | collective-permute-start | bytes 12296 | tf_op jit(solution)/shard_map/ppermute | solution.py:555
  53.4 3.0 %collective-permute-start.16 = (f32[8,128]{1,0:T(8,128)S(1)}, f32[8,128]{1,0:T(8,128)S(1)}, u32[]{:S(2)}, u32[]{:S(2)}) collective-permute-start(f32[8,128]{1,0:T(8,128)S(1)} %get-tuple-element.96), channel_id=1, source_target_pairs={{0,31},{1,16},{2,17},{3,18},{4,19},{5,20},{6,21},{7,22},{8,23},{9,... | collective-permute-start | bytes 12296 | tf_op jit(solution)/shard_map/ppermute | solution.py:555

commit v5 on v4

--- a/solution.py
+++ b/solution.py
@@ -101,20 +101,29 @@
         copy.wait()
 
 
+BASE = 5
+
+
 def inverse_all(systems):
     row, col = iotas()
-    own = row >> 3 == col >> 3
+    size = 1 << BASE
+    own = row >> BASE == col >> BASE
     row8 = lax.broadcasted_iota(jnp.int32, (RIM, HEAD_DIM), 0)
     col8 = lax.broadcasted_iota(jnp.int32, (RIM, HEAD_DIM), 1)
+    first = (col8 >> BASE) << BASE
     found = []
     for n in systems:
-        blocks = jnp.sum(jnp.where(own, n, 0.0).reshape(-1, RIM, HEAD_DIM), axis=0)
-        rows = jnp.where(row8 == (col8 & 7), 1.0, 0.0)
-        for s in range(RIM - 1):
-            column = jnp.take_along_axis(blocks, ((col8 >> 3) << 3) + s, axis=1, mode="promise_in_bounds")
-            rows = rows - column * rows[s : s + 1]
-        found.append(jnp.where(own, jnp.concatenate([rows] * (HEAD_DIM // RIM), axis=0), 0.0))
-    level = 3
+        blocks = jnp.sum(jnp.where(own, n, 0.0).reshape(-1, size, HEAD_DIM), axis=0)
+        tiles = [jnp.where(row8 + RIM * t == (col8 & (size - 1)), 1.0, 0.0) for t in range(size // RIM)]
+        for s in range(size - 1):
+            done = tiles[s // RIM][s % RIM : s % RIM + 1]
+            for t in range(s // RIM, size // RIM):
+                column = jnp.take_along_axis(
+                    blocks[RIM * t : RIM * (t + 1)], first + s, axis=1, mode="promise_in_bounds"
+                )
+                tiles[t] = tiles[t] - column * done
+        found.append(jnp.where(own, jnp.concatenate(tiles * (HEAD_DIM // size), axis=0), 0.0))
+    level = BASE
     while (1 << level) < HEAD_DIM:
         mask = (row >> (level + 2) == col >> (level + 2)) & (row >> level != col >> level)
         parts = [split(d) for d in found]
@@ -187,8 +196,9 @@
 
 def local_kernel(
     slots, flags, x_ref, go_ref, kern_ref, e1_ref, e2_ref, edge_ref, rate_ref, rim_ref, scale_ref, rim_scale_ref,
-    comp_ref, wide_ref, narrow_ref,
+    *rest,
 ):
+    comp_ref, wide_ref, narrow_ref = rest[-3:]
     length = x_ref.shape[0]
     row, col = iotas()
     strict, full = row > col, row >= col
@@ -375,17 +385,17 @@
         out[...] = found[flags[2] ^ n]
 
 
-def part_kernel(flags, keep_ref, recv_ref, *refs):
-    heads = keep_ref.shape[0]
-    ins, (mine_ref, send_ref) = refs[:-2], refs[-2:]
+def part_kernel(sets, per_head, flags, *refs):
+    maps = [(keep, recv, n) for keep, recv in zip(refs[:sets], refs[sets : 2 * sets]) for n in range(keep.shape[0])]
+    ins, (mine_ref, send_ref) = refs[2 * sets : -2], refs[-2:]
     later, upper = flags[1] != 0, flags[3] != 0
-    for j in range(heads):
-        if len(ins) == heads:
+    for j, (keep_ref, recv_ref, n) in enumerate(maps):
+        if per_head == 1:
             start, end = ins[j][0:128], ins[j][128:256]
         else:
-            early, late = ins[j][...], ins[heads + j][...]
+            early, late = ins[2 * j][...], ins[2 * j + 1][...]
             start, end = jnp.where(upper, late, early), jnp.where(upper, early, late)
-        keep, recv = keep_ref[j], recv_ref[j]
+        keep, recv = keep_ref[n], recv_ref[n]
         lo = jnp.where(later, recv, keep)
         hi = jnp.where(later, keep, recv)
         start_hi = mm(split(lo[0:128]), split(start), "nn") + lo[128:256]
@@ -397,10 +407,11 @@
 
 
 def back_kernel(
-    slots, n_states, chained, last, flags, x_ref, go_ref, kern_ref, e1_ref, e2_ref, edge_ref, rate_ref, rim_ref, wide_ref,
-    narrow_ref, more_ref, pairs_ref, *rest,
+    slots, homes, chained, flags, x_ref, go_ref, kern_ref, e1_ref, e2_ref, edge_ref, rate_ref, rim_ref, state_ref,
+    *rest,
 ):
-    state_refs, rest = rest[:n_states], rest[n_states:]
+    sets = 1 + max(n for n, _ in homes)
+    saved, rest = [rest[4 * n : 4 * n + 4] for n in range(sets)], rest[4 * sets :]
     if chained:
         sums_in, rim_grad_in, rest = rest[0], rest[1], rest[3:]
     out_hbm, grad_ref, sums_ref, rim_grad_ref, out_ref, sems = rest[:4] + rest[-2:]
@@ -414,23 +425,23 @@
         rim_grad_ref[...] = rim_grad_in[...]
     dot_all = rim_dot = 0.0
     data, copies = [], []
-    states = [(ref, n) for ref in state_refs for n in range(ref.shape[0])]
-    for j, slot in enumerate(slots):
+    for j, (slot, (n, i)) in enumerate(zip(slots, homes)):
         at = lane_slice(slot ^ flags[0])
-        state_ref, n = states[j]
-        start, end = split(state_ref[n, 0:128]), split(state_ref[n, 128:256])
-        first = mm(rows_of(kept(pairs_ref, j, 0), kept(narrow_ref, j, 10)), start, "nn")
-        z = more_ref[j, 4] + mm(kept(pairs_ref, j, 2), end, "nn")
+        wide_ref, narrow_ref, more_ref, pairs_ref = saved[n]
+        start, end = split(state_ref[j, 0:128]), split(state_ref[j, 128:256])
+        first = mm(rows_of(kept(pairs_ref, i, 0), kept(narrow_ref, i, 10)), start, "nn")
+        z = more_ref[i, 4] + mm(kept(pairs_ref, i, 2), end, "nn")
         x = x_ref[:, at].astype(f32)
-        out_ref[j] = (x + (more_ref[j, 3] + first[:length])).astype(bf16)
+        out_ref[j] = (x + (more_ref[i, 3] + first[:length])).astype(bf16)
         copies.append(pltpu.make_async_copy(out_ref.at[j], out_hbm.at[:, at], sems.at[j]))
         copies[-1].start()
-        data.append(dict(at=at, x=x, start=start, end=end, z=z, fresh=split(wide_ref[j, 2] - first[length:])))
-    for j, d in enumerate(data):
+        data.append(dict(at=at, x=x, start=start, end=end, z=z, fresh=split(wide_ref[i, 2] - first[length:])))
+    for j, (d, (n, i)) in enumerate(zip(data, homes)):
         at = d["at"]
-        q, k = wide_ref[j, 0], wide_ref[j, 1]
-        gq, gk, gv = [more_ref[j, n] for n in range(3)]
-        skf, sqf, skb = [kept(narrow_ref, j, n) for n in (0, 2, 4)]
+        wide_ref, narrow_ref, more_ref, _ = saved[n]
+        q, k = wide_ref[i, 0], wide_ref[i, 1]
+        gq, gk, gv = [more_ref[i, n] for n in range(3)]
+        skf, sqf, skb = [kept(narrow_ref, i, n) for n in (0, 2, 4)]
         e1, e2, rate = e1_ref[:, at], e2_ref[:, at], rate_ref[:, at]
         em, ecm = edge_ref[0:1, at], edge_ref[8:9, at]
         go = exact(go_ref[:, at])
@@ -471,7 +482,7 @@
         sums, rim_sums = sums + sums_in[...], rim_sums + rim_grad_in[:, channels:]
     sums_ref[...] = sums
     rim_grad_ref[:, channels:] = rim_sums
-    if last:
+    if chained:
         rest[4][...] = rim_sums
     for copy in copies:
         copy.wait()
@@ -588,12 +599,12 @@
     shared = (x, go, kern, e1, e2, edge, rate, rim)
     tile = (HEAD_DIM, HEAD_DIM)
 
-    def local(slots, name):
+    def local(slots, name, unread=()):
         n = len(slots)
         return spot(
             functools.partial(local_kernel, slots),
             (array(n, 384, HEAD_DIM), array(n, WIDE, *tile), array(n, NARROW, *tile, dtype=bf16)),
-            *shared, scale, rim_scale, name=name,
+            *shared, scale, rim_scale, name=name, unread=unread,
         )
 
     def prepared(slots, saved, name):
@@ -604,15 +615,25 @@
             x, kern, e2, edge, rim, scale, rim_scale, *saved, name=name, cost=BESIDE,
         )
 
-    inner_slots, outer_slots = range(per), range(per, 2 * per)
-    outer, *outer_saved = local(outer_slots, "local_outer")
-    outer_recv = swapped(outer, 1)
-    inner, *inner_saved = local(inner_slots, "local_inner")
-    pairs = spot(join_kernel, (array(384, HEAD_DIM),) * per, inner, outer_recv, name="join")
-    parts = [pairs[0]] + [swapped(pairs[n], 2 * n) for n in range(1, count)]
-    outer_saved += prepared(outer_slots, outer_saved, "ready_outer")
-    inner_saved += prepared(inner_slots, inner_saved, "ready_inner")
-    ahead = [outer_saved[-1], inner_saved[-1]]
+    inner_slots, outer_slots, rest_slots = range(1, per), range(per + 1, 2 * per), (0, per)
+    some = per > 1
+    parts, ahead, pairs = [None], [], ()
+    if some:
+        outer, *outer_saved = local(outer_slots, "local_outer")
+        outer_recv = swapped(outer, 1)
+        inner, *inner_saved = local(inner_slots, "local_inner")
+        pairs = spot(join_kernel, (array(384, HEAD_DIM),) * (per - 1), inner, outer_recv, name="join_inner")
+        parts += [swapped(pairs[n - 1], 2 * n) for n in range(1, count)]
+    rest, *rest_saved = local(rest_slots, "local_rest", pairs)
+    rest_recv = swapped(rest[1:], 1)
+    rest = rest[:1]
+    (parts[0],) = spot(join_kernel, (array(384, HEAD_DIM),), rest, rest_recv, name="join_rest")
+    rest_saved += prepared(rest_slots, rest_saved, "ready_rest")
+    ahead = [rest_saved[-1]]
+    if some:
+        outer_saved += prepared(outer_slots, outer_saved, "ready_outer")
+        inner_saved += prepared(inner_slots, inner_saved, "ready_inner")
+        ahead += [outer_saved[-1], inner_saved[-1]]
 
     held = pltpu.VMEM((count, 384, HEAD_DIM), f32)
     square = array(*tile)
@@ -635,7 +656,7 @@
         )
         early = returned(early)
         late = spot(late_kernel, (square,) * 4, other, known, reach, name="late", scratch=[found])
-        states = early + returned(late)
+        states = list(zip(early, returned(late)))
     else:
         gathered = spot(
             functools.partial(gather_kernel, count, len(ahead)), (square,) * 3,
@@ -648,38 +669,47 @@
             else:
                 ends = spot(hop_kernel, (square,) * 2, *gathered, *ends, name=f"hop{hop}")
             ends = (moved(ends[0], step), moved(ends[1], -step))
-        states = returned(
+        spread = returned(
             spot(
                 functools.partial(spread_kernel, count), (array(256, HEAD_DIM),) * count,
                 *parts, *ends, name="spread", scratch=[held, pltpu.VMEM((count, 256, HEAD_DIM), f32)],
             )
         )
+        states = [(a,) for a in spread]
+
+    keeps, recvs = ((rest, inner), (rest_recv, outer_recv)) if some else ((rest,), (rest_recv,))
     mine, send = spot(
-        part_kernel, (array(per, 256, HEAD_DIM),) * 2, inner, outer_recv, *states, name="part"
+        functools.partial(part_kernel, len(keeps), len(states[0])), (array(per, 256, HEAD_DIM),) * 2,
+        *keeps, *recvs, *(a for pair in states for a in pair), name="part",
     )
     far = swapped(send, 1)
 
-    def backward(slots, saved, states, chain, name):
+    def backward(slots, saved, homes, states, chain, name):
         n = len(slots)
-        last = chain is not None
-        before = (chain[2], chain[3]) if last else ()
+        chained = chain is not None
+        before = (chain[2], chain[3]) if chained else ()
         return spot(
-            functools.partial(back_kernel, slots, len(states), last, last),
+            functools.partial(back_kernel, slots, homes, chained),
             (
                 array(*inputs.shape, dtype=bf16), array(n, length, HEAD_DIM), array(RIM, length),
                 array(RIM, channels + HEAD_DIM),
             )
-            + (array(RIM, HEAD_DIM),) * last,
-            *shared, *saved, *states, *before, name=name, far_out=(0,),
-            alias=None if chain is None else chain[0],
+            + (array(RIM, HEAD_DIM),) * chained,
+            *shared, states, *(a for group in saved for a in group), *before, name=name, far_out=(0,),
+            alias=chain[0] if chained else None,
             scratch=[pltpu.VMEM((n, length, HEAD_DIM), bf16), pltpu.SemaphoreType.DMA((n,))],
         )
 
-    chain = backward(inner_slots, inner_saved, (mine,), None, "back_inner")
+    slots = range(heads)
+    homes = [[(0, n)] + [(1, i) for i in range(per - 1)] for n in range(2)]
+    chain = backward(
+        slots[:per], [rest_saved] + ([inner_saved] if some else []), homes[0], mine, None, "back_inner"
+    )
     grads = [chain[1]]
-    chain = backward(outer_slots, outer_saved, (far,), chain, "back_outer")
+    chain = backward(
+        slots[per:], [rest_saved] + ([outer_saved] if some else []), homes[1], far, chain, "back_outer"
+    )
     grads.append(chain[1])
-    slots = [*inner_slots, *outer_slots]
     stream_out, _, inner_sum, rim_grad, rim_sums = chain
 
     inner_total, next_sums = inner_sum, 0.0

time: 57.7 us -> 56.6 us (0.981)
  waiting for transfers between devices: 18.8 us -> 16.3 us
  Pallas kernels: 17.7 us -> 18.8 us
    ppermute x12 -> x13, waiting for transfers between devices: 11.3 us -> 8.86 us  [swapped(): return lax.ppermute(value, 'ctx', [(i, i ^ distance) for i in range(spots)])]
    pallas_call x14 -> x17, Pallas kernels: 17.7 us -> 18.8 us  [call(): pl.pallas_call((lambda *refs: kernel(placed(*scalar), *refs)) if scalar e...]
    ppermute x12 -> x13, starting transfers between devices: 11.7 us -> 11.7 us  [swapped(): return lax.ppermute(value, 'ctx', [(i, i ^ distance) for i in range(spots)])]
  transfers between devices with their start and end apart: 18 -> 19, of which waited for: 11 -> 9; matrix products, arithmetic and copies ran while one was open for 0% -> 0% of each run, Pallas kernels for 15% -> 18%
where the time goes in v5:
time: 56.6 us; the launch traced here: 56.5 us
  starting transfers between devices  20.3 us (36%)
  Pallas kernels  18.8 us (33%)
  waiting for transfers between devices  16.3 us (29%)
  between operations  1 us (2%)
    pallas_call x17, Pallas kernels, call(): pl.pallas_call((lambda *refs: kernel(placed(*scalar), *refs)) if scalar e...  18.8 us
    ppermute x13, starting transfers between devices, swapped(): return lax.ppermute(value, 'ctx', [(i, i ^ distance) for i in range(spots)])  11.7 us
    ppermute x13, waiting for transfers between devices, swapped(): return lax.ppermute(value, 'ctx', [(i, i ^ distance) for i in range(spots)])  8.86 us
    ppermute x6, starting transfers between devices, turned(): return lax.ppermute(value, ('section', 'ctx'), route)  8.63 us
    ppermute x6, waiting for transfers between devices, turned(): return lax.ppermute(value, ('section', 'ctx'), route)  7.44 us
  transfers between devices with their start and end apart: 19, of which 9 were waited for; matrix products, arithmetic and copies ran while one was open for 0% of the time, Pallas kernels for 18%

profile of v5, /device:TPU:0, one launch (start us, length us, event | category | flops | bytes accessed | tf_op | source)
XLA Modules:
  0.0 56.5 jit_solution(14559310409628487154)
XLA Ops:
  0.6 1.3 %prelude.1 = (f32[8,1152]{1,0:T(8,128)S(1)}, f32[8,128]{1,0:T(8,128)S(1)}, bf16[128,1024]{1,0:T(8,128)(2,1)S(1)}, bf16[128,1024]{1,0:T(8,128)(2,1)S(1)}, f32[3,4...) custom-call(bf16[128,1024]{1,0:T(8,128)(2,1)} %x_hbm.1, bf16[128,1024]{1,0:T(8,128)(2,1)} %go_hbm.1, ...), custom_call_target="tpu_custom_call" | custom-call | tf_op jit(solution)/shard_map/prelude/pallas_call | solution.py:523
  2.0 2.4 %collective-permute-start.2 = (f32[8,128]{1,0:T(8,128)S(1)}, f32[8,128]{1,0:T(8,128)S(1)}, u32[]{:S(2)}, u32[]{:S(2)}) collective-permute-start(f32[8,128]{1,0:T(8,128)S(1)} %get-tuple-element.65), channel_id=1, source_target_pairs={{0,17},{1,18},{2,19},{3,20},{4,21},{5,22},{6,23},{7,24},{8,25},{9,... | collective-permute-start | bytes 12296 | tf_op jit(solution)/shard_map/ppermute | solution.py:566
  4.4 0.6 %collective-permute-start.1 = (f32[8,128]{1,0:T(8,128)S(1)}, f32[8,128]{1,0:T(8,128)S(1)}, u32[]{:S(2)}, u32[]{:S(2)}) collective-permute-start(f32[8,128]{1,0:T(8,128)S(1)} %get-tuple-element.65), channel_id=1, source_target_pairs={{0,16},{1,17},{2,18},{3,19},{4,20},{5,21},{6,22},{7,23},{8,24},{9,... | collective-permute-start | bytes 12296 | tf_op jit(solution)/shard_map/ppermute | solution.py:566
  5.0 1.2 %collective-permute-start = (f32[8,1152]{1,0:T(8,128)S(1)}, f32[8,1152]{1,0:T(8,128)S(1)}, u32[]{:S(2)}, u32[]{:S(2)}) collective-permute-start(f32[8,1152]{1,0:T(8,128)S(1)} %get-tuple-element.64), channel_id=1, source_target_pairs={{0,1},{1,2},{2,3},{3,4},{4,5},{5,6},{6,7},{7,8},{8,9},{9,10},{10,1... | collective-permute-start | bytes 110600 | tf_op jit(solution)/shard_map/ppermute | solution.py:566
  6.3 0.4 gates.1
  6.7 1.3 %collective-permute-done.1 = f32[8,128]{1,0:T(8,128)S(1)} collective-permute-done((f32[8,128]{1,0:T(8,128)S(1)}, f32[8,128]{1,0:T(8,128)S(1)}, u32[]{:S(2)}, u32[]{:S(2)}) %collective-permute-start.1) | collective-permute-done | bytes 4128 | tf_op jit(solution)/shard_map/ppermute | solution.py:566
  8.0 1.7 %collective-permute-done.2 = f32[8,128]{1,0:T(8,128)S(1)} collective-permute-done((f32[8,128]{1,0:T(8,128)S(1)}, f32[8,128]{1,0:T(8,128)S(1)}, u32[]{:S(2)}, u32[]{:S(2)}) %collective-permute-start.2) | collective-permute-done | bytes 4128 | tf_op jit(solution)/shard_map/ppermute | solution.py:566
  9.7 1.4 %collective-permute-done.refs_7_.refs_4_ = f32[8,1152]{1,0:T(8,128)S(1)} collective-permute-done((f32[8,1152]{1,0:T(8,128)S(1)}, f32[8,1152]{1,0:T(8,128)S(1)}, u32[]{:S(2)}, u32[]{:S(2)}) %collective-permute-start) | collective-permute-done | bytes 36896 | tf_op jit(solution)/shard_map/ppermute | solution.py:566
  11.1 2.3 %local_outer.1 = (f32[3,384,128]{2,1,0:T(8,128)S(1)}, f32[3,3,128,128]{3,2,1,0:T(8,128)S(1)}, bf16[3,16,128,128]{3,2,1,0:T(8,128)(2,1)S(1)}) custom-call(bf16[128,1024]{1,0:T(8,128)(2,1)S(1)} %get-tuple-element.55.refs_0_, bf16[128,1024]{1,0:T(8,128)(2,1)S(1)} %get-tuple-element.56.refs_1_, f32[3,4,1024]{2,1,0:T(4,128)S(1)} %get-tuple-element.57.refs_2_.refs_1_, ...), custom_call_target="tpu_custom_call" | custom-call | tf_op jit(solution)/shard_map/local_outer/pallas_call | solution.py:523
  13.5 0.1 collective-permute-start.3
  13.6 2.3 %local_inner.1 = (f32[3,384,128]{2,1,0:T(8,128)S(1)}, f32[3,3,128,128]{3,2,1,0:T(8,128)S(1)}, bf16[3,16,128,128]{3,2,1,0:T(8,128)(2,1)S(1)}) custom-call(bf16[128,1024]{1,0:T(8,128)(2,1)S(1)} %get-tuple-element.55.refs_0_, bf16[128,1024]{1,0:T(8,128)(2,1)S(1)} %get-tuple-element.56.refs_1_, f32[3,4,1024]{2,1,0:T(4,128)S(1)} %get-tuple-element.57.refs_2_.refs_1_, ...), custom_call_target="tpu_custom_call" | custom-call | tf_op jit(solution)/shard_map/local_inner/pallas_call | solution.py:523
  15.9 0.0 collective-permute-done.3.refs_1_.refs_3_
  15.9 0.3 join_inner.1
  16.2 0.1 collective-permute-start.5
  16.3 0.5 collective-permute-start.6
  16.8 3.0 %collective-permute-start.7 = (f32[384,128]{1,0:T(8,128)S(1)}, f32[384,128]{1,0:T(8,128)S(1)}, u32[]{:S(2)}, u32[]{:S(2)}) collective-permute-start(f32[384,128]{1,0:T(8,128)S(1)} %get-tuple-element.70.refs_12_), channel_id=1, source_target_pairs={{0,6},{1,7},{2,4},{3,5},{4,2},{5,3},{6,0},{7,1},{8,14},{9,15},{10,... | collective-permute-start | bytes 589832 | tf_op jit(solution)/shard_map/ppermute | solution.py:569
  19.8 2.0 %local_rest.1 = (f32[2,384,128]{2,1,0:T(8,128)S(1)}, f32[2,3,128,128]{3,2,1,0:T(8,128)S(1)}, bf16[2,16,128,128]{3,2,1,0:T(8,128)(2,1)S(1)}) custom-call(bf16[128,1024]{1,0:T(8,128)(2,1)S(1)} %get-tuple-element.55.refs_0_, bf16[128,1024]{1,0:T(8,128)(2,1)S(1)} %get-tuple-element.56.refs_1_, f32[3,4,1024]{2,1,0:T(4,128)S(1)} %get-tuple-element.57.refs_2_.refs_1_, ...), custom_call_target="tpu_custom_call" | custom-call | tf_op jit(solution)/shard_map/local_rest/pallas_call | solution.py:523
  21.9 0.1 collective-permute-start.4
  21.9 0.7 %ready_outer.1 = (f32[3,5,128,128]{3,2,1,0:T(8,128)S(1)}, bf16[3,4,128,128]{3,2,1,0:T(8,128)(2,1)S(1)}) custom-call(bf16[128,1024]{1,0:T(8,128)(2,1)S(1)} %get-tuple-element.55.refs_0_, f32[3,4,1024]{2,1,0:T(4,128)S(1)} %get-tuple-element.57.refs_2_.refs_1_, f32[128,1024]{1,0:T(8,128)S(1)} %get-tuple-element.61.refs_4_.refs_2_, ...), custom_call_target="tpu_custom_call" | custom-call | flops 1000000000 | bytes 10000000 | tf_op jit(solution)/shard_map/ready_outer/pallas_call | solution.py:523
  22.6 0.7 %ready_inner.1 = (f32[3,5,128,128]{3,2,1,0:T(8,128)S(1)}, bf16[3,4,128,128]{3,2,1,0:T(8,128)(2,1)S(1)}) custom-call(bf16[128,1024]{1,0:T(8,128)(2,1)S(1)} %get-tuple-element.55.refs_0_, f32[3,4,1024]{2,1,0:T(4,128)S(1)} %get-tuple-element.57.refs_2_.refs_1_, f32[128,1024]{1,0:T(8,128)S(1)} %get-tuple-element.61.refs_4_.refs_2_, ...), custom_call_target="tpu_custom_call" | custom-call | flops 1000000000 | bytes 10000000 | tf_op jit(solution)/shard_map/ready_inner/pallas_call | solution.py:523
  23.4 0.5 ready_rest.1
  23.9 0.0 collective-permute-done.4.refs_1_.refs_2_
  23.9 0.2 join_rest.1.refs_0_
  24.1 0.0 collective-permute-done.5.refs_1_
  24.1 0.0 collective-permute-done.6.refs_2_
  24.1 4.9 %collective-permute-done.7.refs_3_ = f32[384,128]{1,0:T(8,128)S(1)} collective-permute-done((f32[384,128]{1,0:T(8,128)S(1)}, f32[384,128]{1,0:T(8,128)S(1)}, u32[]{:S(2)}, u32[]{:S(2)}) %collective-permute-start.7) | collective-permute-done | bytes 196640 | tf_op jit(solution)/shard_map/ppermute | solution.py:569
  29.0 0.6 gather.1
  29.6 0.9 %collective-permute-start.8 = (f32[128,128]{1,0:T(8,128)S(1)}, f32[128,128]{1,0:T(8,128)S(1)}, u32[]{:S(2)}, u32[]{:S(2)}) collective-permute-start(f32[128,128]{1,0:T(8,128)S(1)} %get-tuple-element.84), channel_id=1, source_target_pairs={{0,8},{1,9},{2,10},{3,11},{4,12},{5,13},{6,14},{7,15},{8,0},{9,1},... | collective-permute-start | bytes 196616 | tf_op jit(solution)/shard_map/ppermute | solution.py:569
  30.4 0.3 reach.1
  30.8 0.7 %collective-permute-start.9 = (f32[128,128]{1,0:T(8,128)S(1)}, f32[128,128]{1,0:T(8,128)S(1)}, u32[]{:S(2)}, u32[]{:S(2)}) collective-permute-start(f32[128,128]{1,0:T(8,128)S(1)} %get-tuple-element.88), channel_id=1, source_target_pairs={{0,2},{1,3},{2,0},{3,1},{4,6},{5,7},{6,4},{7,5},{8,10},{9,11},{10,... | collective-permute-start | bytes 196616 | tf_op jit(solution)/shard_map/ppermute | solution.py:569
  31.5 1.6 %collective-permute-start.11 = (f32[128,128]{1,0:T(8,128)S(1)}, f32[128,128]{1,0:T(8,128)S(1)}, u32[]{:S(2)}, u32[]{:S(2)}) collective-permute-start(f32[128,128]{1,0:T(8,128)S(1)} %get-tuple-element.90), channel_id=1, source_target_pairs={{0,4},{1,5},{2,6},{3,7},{4,0},{5,1},{6,2},{7,3},{8,12},{9,13},{10,... | collective-permute-start | bytes 196616 | tf_op jit(solution)/shard_map/ppermute | solution.py:569
  33.0 1.3 %collective-permute-start.13 = (f32[128,128]{1,0:T(8,128)S(1)}, f32[128,128]{1,0:T(8,128)S(1)}, u32[]{:S(2)}, u32[]{:S(2)}) collective-permute-start(f32[128,128]{1,0:T(8,128)S(1)} %get-tuple-element.92), channel_id=1, source_target_pairs={{0,6},{1,7},{2,4},{3,5},{4,2},{5,3},{6,0},{7,1},{8,14},{9,15},{10,... | collective-permute-start | bytes 196616 | tf_op jit(solution)/shard_map/ppermute | solution.py:569
  34.3 1.0 %collective-permute-done.8.refs_0_ = f32[128,128]{1,0:T(8,128)S(1)} collective-permute-done((f32[128,128]{1,0:T(8,128)S(1)}, f32[128,128]{1,0:T(8,128)S(1)}, u32[]{:S(2)}, u32[]{:S(2)}) %collective-permute-start.8) | collective-permute-done | bytes 65568 | tf_op jit(solution)/shard_map/ppermute | solution.py:569
  35.4 0.2 late.1
  35.6 0.4 collective-permute-start.10
  36.0 0.8 %collective-permute-start.12 = (f32[128,128]{1,0:T(8,128)S(1)}, f32[128,128]{1,0:T(8,128)S(1)}, u32[]{:S(2)}, u32[]{:S(2)}) collective-permute-start(f32[128,128]{1,0:T(8,128)S(1)} %get-tuple-element.91), channel_id=1, source_target_pairs={{0,4},{1,5},{2,6},{3,7},{4,0},{5,1},{6,2},{7,3},{8,12},{9,13},{10,... | collective-permute-start | bytes 196616 | tf_op jit(solution)/shard_map/ppermute | solution.py:569
  36.8 0.0 collective-permute-done.9.refs_6_
  36.8 2.3 %collective-permute-start.14 = (f32[128,128]{1,0:T(8,128)S(1)}, f32[128,128]{1,0:T(8,128)S(1)}, u32[]{:S(2)}, u32[]{:S(2)}) collective-permute-start(f32[128,128]{1,0:T(8,128)S(1)} %get-tuple-element.93), channel_id=1, source_target_pairs={{0,6},{1,7},{2,4},{3,5},{4,2},{5,3},{6,0},{7,1},{8,14},{9,15},{10,... | collective-permute-start | bytes 196616 | tf_op jit(solution)/shard_map/ppermute | solution.py:569
  39.2 0.0 collective-permute-done.11.refs_8_
  39.2 0.0 collective-permute-done.13.refs_10_
  39.2 1.5 %collective-permute-done.10.refs_7_ = f32[128,128]{1,0:T(8,128)S(1)} collective-permute-done((f32[128,128]{1,0:T(8,128)S(1)}, f32[128,128]{1,0:T(8,128)S(1)}, u32[]{:S(2)}, u32[]{:S(2)}) %collective-permute-start.10) | collective-permute-done | bytes 65568 | tf_op jit(solution)/shard_map/ppermute | solution.py:569
  40.6 0.0 collective-permute-done.12.refs_9_
  40.6 1.5 %collective-permute-done.14.refs_11_ = f32[128,128]{1,0:T(8,128)S(1)} collective-permute-done((f32[128,128]{1,0:T(8,128)S(1)}, f32[128,128]{1,0:T(8,128)S(1)}, u32[]{:S(2)}, u32[]{:S(2)}) %collective-permute-start.14) | collective-permute-done | bytes 65568 | tf_op jit(solution)/shard_map/ppermute | solution.py:569
  42.1 0.4 part.1
  42.5 0.1 collective-permute-start.15
  42.5 2.8 %back_inner.1 = (bf16[128,1024]{1,0:T(8,128)(2,1)}, f32[4,128,128]{2,1,0:T(8,128)S(1)}, f32[8,128]{1,0:T(8,128)S(1)}, f32[8,1152]{1,0:T(8,128)S(1)}) custom-call(bf16[128,1024]{1,0:T(8,128)(2,1)S(1)} %get-tuple-element.55.refs_0_, bf16[128,1024]{1,0:T(8,128)(2,1)S(1)} %get-tuple-element.56.refs_1_, f32[3,4,1024]{2,1,0:T(4,128)S(1)} %get-tuple-element.57.refs_2_.refs_1_, ...), custom_call_target="tpu_custom_call" | custom-call | tf_op jit(solution)/shard_map/back_inner/pallas_call | solution.py:523
  45.3 0.0 collective-permute-done.15.refs_8_
  45.3 2.6 %back_outer.1 = (bf16[128,1024]{1,0:T(8,128)(2,1)}, f32[4,128,128]{2,1,0:T(8,128)S(1)}, f32[8,128]{1,0:T(8,128)S(1)}, f32[8,1152]{1,0:T(8,128)S(1)}, f32[8,128]{1,0:T(8,128)S(1)}) custom-call(bf16[128,1024]{1,0:T(8,128)(2,1)S(1)} %get-tuple-element.55.refs_0_, bf16[128,1024]{1,0:T(8,128)(2,1)S(1)} %get-tuple-element.56.refs_1_, ...), custom_call_target="tpu_custom_call", output_to_operand_aliasing={{0}: (19, {})} | custom-call | tf_op jit(solution)/shard_map/back_outer/pallas_call | solution.py:523
  47.9 2.9 %collective-permute-start.18 = (f32[8,1152]{1,0:T(8,128)S(1)}, f32[8,1152]{1,0:T(8,128)S(1)}, u32[]{:S(2)}, u32[]{:S(2)}) collective-permute-start(f32[8,1152]{1,0:T(8,128)S(1)} %get-tuple-element.105), channel_id=1, source_target_pairs={{0,15},{1,0},{2,1},{3,2},{4,3},{5,4},{6,5},{7,6},{8,7},{9,8},{10,9... | collective-permute-start | bytes 110600 | tf_op jit(solution)/shard_map/ppermute | solution.py:566
  50.9 1.4 %collective-permute-start.16 = (f32[8,128]{1,0:T(8,128)S(1)}, f32[8,128]{1,0:T(8,128)S(1)}, u32[]{:S(2)}, u32[]{:S(2)}) collective-permute-start(f32[8,128]{1,0:T(8,128)S(1)} %get-tuple-element.103), channel_id=1, source_target_pairs={{0,16},{1,17},{2,18},{3,19},{4,20},{5,21},{6,22},{7,23},{8,24},{9,... | collective-permute-start | bytes 12296 | tf_op jit(solution)/shard_map/ppermute | solution.py:566
  52.2 0.0 collective-permute-start.17
  52.2 2.2 %collective-permute-done.16 = f32[8,128]{1,0:T(8,128)S(1)} collective-permute-done((f32[8,128]{1,0:T(8,128)S(1)}, f32[8,128]{1,0:T(8,128)S(1)}, u32[]{:S(2)}, u32[]{:S(2)}) %collective-permute-start.16) | collective-permute-done | bytes 4128 | tf_op jit(solution)/shard_map/ppermute | solution.py:566
  54.5 0.8 %collective-permute-done.17 = f32[8,128]{1,0:T(8,128)S(1)} collective-permute-done((f32[8,128]{1,0:T(8,128)S(1)}, f32[8,128]{1,0:T(8,128)S(1)}, u32[]{:S(2)}, u32[]{:S(2)}) %collective-permute-start.17) | collective-permute-done | bytes 4128 | tf_op jit(solution)/shard_map/ppermute | solution.py:566
  55.3 0.0 collective-permute-done.18.refs_5_
  55.3 1.0 %finish.1 = bf16[128,1024]{1,0:T(8,128)(2,1)} custom-call(bf16[128,1024]{1,0:T(8,128)(2,1)S(1)} %get-tuple-element.55.refs_0_, bf16[128,1024]{1,0:T(8,128)(2,1)S(1)} %get-tuple-element.56.refs_1_, f32[8,128]{1,0:T(8,128)S(1)} %add_rsqrt_fusion.refs_8_.refs_5_.refs_2_, f32[8,128]{1,0:T(8,128)S(1)} %add.22.refs_3_, f32[8,128]{1,0:T(8,128)S(1)} %slice_add_fusion.refs_4_, ...), custom_call_target="tpu_custom_call" | custom-call | tf_op jit(solution)/shard_map/finish/pallas_call | solution.py:523
  (5 shorter events, 0.0 us)
Async XLA Ops:
  2.0 7.7 %collective-permute-start.2 = (f32[8,128]{1,0:T(8,128)S(1)}, f32[8,128]{1,0:T(8,128)S(1)}, u32[]{:S(2)}, u32[]{:S(2)}) collective-permute-start(f32[8,128]{1,0:T(8,128)S(1)} %get-tuple-element.65), channel_id=1, source_target_pairs={{0,17},{1,18},{2,19},{3,20},{4,21},{5,22},{6,23},{7,24},{8,25},{9,... | collective-permute-start | bytes 12296 | tf_op jit(solution)/shard_map/ppermute | solution.py:566
  4.4 3.6 %collective-permute-start.1 = (f32[8,128]{1,0:T(8,128)S(1)}, f32[8,128]{1,0:T(8,128)S(1)}, u32[]{:S(2)}, u32[]{:S(2)}) collective-permute-start(f32[8,128]{1,0:T(8,128)S(1)} %get-tuple-element.65), channel_id=1, source_target_pairs={{0,16},{1,17},{2,18},{3,19},{4,20},{5,21},{6,22},{7,23},{8,24},{9,... | collective-permute-start | bytes 12296 | tf_op jit(solution)/shard_map/ppermute | solution.py:566
  5.0 6.1 %collective-permute-start = (f32[8,1152]{1,0:T(8,128)S(1)}, f32[8,1152]{1,0:T(8,128)S(1)}, u32[]{:S(2)}, u32[]{:S(2)}) collective-permute-start(f32[8,1152]{1,0:T(8,128)S(1)} %get-tuple-element.64), channel_id=1, source_target_pairs={{0,1},{1,2},{2,3},{3,4},{4,5},{5,6},{6,7},{7,8},{8,9},{9,10},{10,1... | collective-permute-start | bytes 110600 | tf_op jit(solution)/shard_map/ppermute | solution.py:566
  13.5 2.4 %collective-permute-start.3 = (f32[3,384,128]{2,1,0:T(8,128)S(1)}, f32[3,384,128]{2,1,0:T(8,128)S(1)}, u32[]{:S(2)}, u32[]{:S(2)}) collective-permute-start(f32[3,384,128]{2,1,0:T(8,128)S(1)} %get-tuple-element.67), channel_id=1, source_target_pairs={{0,1},{1,0},{2,3},{3,2},{4,5},{5,4},{6,7},{7,6},{8,9},{9,8},{10,11... | collective-permute-start | bytes 1769480 | tf_op jit(solution)/shard_map/ppermute | solution.py:569
  16.2 7.9 %collective-permute-start.5 = (f32[384,128]{1,0:T(8,128)S(1)}, f32[384,128]{1,0:T(8,128)S(1)}, u32[]{:S(2)}, u32[]{:S(2)}) collective-permute-start(f32[384,128]{1,0:T(8,128)S(1)} %get-tuple-element.68.refs_10_), channel_id=1, source_target_pairs={{0,2},{1,3},{2,0},{3,1},{4,6},{5,7},{6,4},{7,5},{8,10},{9,11},{10,... | collective-permute-start | bytes 589832 | tf_op jit(solution)/shard_map/ppermute | solution.py:569
  16.3 7.8 %collective-permute-start.6 = (f32[384,128]{1,0:T(8,128)S(1)}, f32[384,128]{1,0:T(8,128)S(1)}, u32[]{:S(2)}, u32[]{:S(2)}) collective-permute-start(f32[384,128]{1,0:T(8,128)S(1)} %get-tuple-element.69.refs_11_), channel_id=1, source_target_pairs={{0,4},{1,5},{2,6},{3,7},{4,0},{5,1},{6,2},{7,3},{8,12},{9,13},{10,... | collective-permute-start | bytes 589832 | tf_op jit(solution)/shard_map/ppermute | solution.py:569
  16.8 12.2 %collective-permute-start.7 = (f32[384,128]{1,0:T(8,128)S(1)}, f32[384,128]{1,0:T(8,128)S(1)}, u32[]{:S(2)}, u32[]{:S(2)}) collective-permute-start(f32[384,128]{1,0:T(8,128)S(1)} %get-tuple-element.70.refs_12_), channel_id=1, source_target_pairs={{0,6},{1,7},{2,4},{3,5},{4,2},{5,3},{6,0},{7,1},{8,14},{9,15},{10,... | collective-permute-start | bytes 589832 | tf_op jit(solution)/shard_map/ppermute | solution.py:569
  21.9 2.0 %collective-permute-start.4 = (f32[1,384,128]{2,1,0:T(8,128)S(1)}, f32[1,384,128]{2,1,0:T(8,128)S(1)}, u32[]{:S(2)}, u32[]{:S(2)}) collective-permute-start(f32[1,384,128]{2,1,0:T(8,128)S(1)} %get-tuple-element.108), channel_id=1, source_target_pairs={{0,1},{1,0},{2,3},{3,2},{4,5},{5,4},{6,7},{7,6},{8,9},{9,8},{10,11... | collective-permute-start | bytes 589832 | tf_op jit(solution)/shard_map/ppermute | solution.py:569
  29.6 5.8 %collective-permute-start.8 = (f32[128,128]{1,0:T(8,128)S(1)}, f32[128,128]{1,0:T(8,128)S(1)}, u32[]{:S(2)}, u32[]{:S(2)}) collective-permute-start(f32[128,128]{1,0:T(8,128)S(1)} %get-tuple-element.84), channel_id=1, source_target_pairs={{0,8},{1,9},{2,10},{3,11},{4,12},{5,13},{6,14},{7,15},{8,0},{9,1},... | collective-permute-start | bytes 196616 | tf_op jit(solution)/shard_map/ppermute | solution.py:569
  30.8 6.1 %collective-permute-start.9 = (f32[128,128]{1,0:T(8,128)S(1)}, f32[128,128]{1,0:T(8,128)S(1)}, u32[]{:S(2)}, u32[]{:S(2)}) collective-permute-start(f32[128,128]{1,0:T(8,128)S(1)} %get-tuple-element.88), channel_id=1, source_target_pairs={{0,2},{1,3},{2,0},{3,1},{4,6},{5,7},{6,4},{7,5},{8,10},{9,11},{10,... | collective-permute-start | bytes 196616 | tf_op jit(solution)/shard_map/ppermute | solution.py:569
  31.5 7.7 %collective-permute-start.11 = (f32[128,128]{1,0:T(8,128)S(1)}, f32[128,128]{1,0:T(8,128)S(1)}, u32[]{:S(2)}, u32[]{:S(2)}) collective-permute-start(f32[128,128]{1,0:T(8,128)S(1)} %get-tuple-element.90), channel_id=1, source_target_pairs={{0,4},{1,5},{2,6},{3,7},{4,0},{5,1},{6,2},{7,3},{8,12},{9,13},{10,... | collective-permute-start | bytes 196616 | tf_op jit(solution)/shard_map/ppermute | solution.py:569
  33.0 6.1 %collective-permute-start.13 = (f32[128,128]{1,0:T(8,128)S(1)}, f32[128,128]{1,0:T(8,128)S(1)}, u32[]{:S(2)}, u32[]{:S(2)}) collective-permute-start(f32[128,128]{1,0:T(8,128)S(1)} %get-tuple-element.92), channel_id=1, source_target_pairs={{0,6},{1,7},{2,4},{3,5},{4,2},{5,3},{6,0},{7,1},{8,14},{9,15},{10,... | collective-permute-start | bytes 196616 | tf_op jit(solution)/shard_map/ppermute | solution.py:569
  35.6 5.0 %collective-permute-start.10 = (f32[128,128]{1,0:T(8,128)S(1)}, f32[128,128]{1,0:T(8,128)S(1)}, u32[]{:S(2)}, u32[]{:S(2)}) collective-permute-start(f32[128,128]{1,0:T(8,128)S(1)} %get-tuple-element.89), channel_id=1, source_target_pairs={{0,2},{1,3},{2,0},{3,1},{4,6},{5,7},{6,4},{7,5},{8,10},{9,11},{10,... | collective-permute-start | bytes 196616 | tf_op jit(solution)/shard_map/ppermute | solution.py:569
  36.0 4.6 %collective-permute-start.12 = (f32[128,128]{1,0:T(8,128)S(1)}, f32[128,128]{1,0:T(8,128)S(1)}, u32[]{:S(2)}, u32[]{:S(2)}) collective-permute-start(f32[128,128]{1,0:T(8,128)S(1)} %get-tuple-element.91), channel_id=1, source_target_pairs={{0,4},{1,5},{2,6},{3,7},{4,0},{5,1},{6,2},{7,3},{8,12},{9,13},{10,... | collective-permute-start | bytes 196616 | tf_op jit(solution)/shard_map/ppermute | solution.py:569
  36.8 5.3 %collective-permute-start.14 = (f32[128,128]{1,0:T(8,128)S(1)}, f32[128,128]{1,0:T(8,128)S(1)}, u32[]{:S(2)}, u32[]{:S(2)}) collective-permute-start(f32[128,128]{1,0:T(8,128)S(1)} %get-tuple-element.93), channel_id=1, source_target_pairs={{0,6},{1,7},{2,4},{3,5},{4,2},{5,3},{6,0},{7,1},{8,14},{9,15},{10,... | collective-permute-start | bytes 196616 | tf_op jit(solution)/shard_map/ppermute | solution.py:569
  42.5 2.9 %collective-permute-start.15 = (f32[4,256,128]{2,1,0:T(8,128)S(1)}, f32[4,256,128]{2,1,0:T(8,128)S(1)}, u32[]{:S(2)}, u32[]{:S(2)}) collective-permute-start(f32[4,256,128]{2,1,0:T(8,128)S(1)} %get-tuple-element.94), channel_id=1, source_target_pairs={{0,1},{1,0},{2,3},{3,2},{4,5},{5,4},{6,7},{7,6},{8,9},{9,8},{10,11... | collective-permute-start | bytes 1572872 | tf_op jit(solution)/shard_map/ppermute | solution.py:569
  47.9 7.3 %collective-permute-start.18 = (f32[8,1152]{1,0:T(8,128)S(1)}, f32[8,1152]{1,0:T(8,128)S(1)}, u32[]{:S(2)}, u32[]{:S(2)}) collective-permute-start(f32[8,1152]{1,0:T(8,128)S(1)} %get-tuple-element.105), channel_id=1, source_target_pairs={{0,15},{1,0},{2,1},{3,2},{4,3},{5,4},{6,5},{7,6},{8,7},{9,8},{10,9... | collective-permute-start | bytes 110600 | tf_op jit(solution)/shard_map/ppermute | solution.py:566
  50.9 3.6 %collective-permute-start.16 = (f32[8,128]{1,0:T(8,128)S(1)}, f32[8,128]{1,0:T(8,128)S(1)}, u32[]{:S(2)}, u32[]{:S(2)}) collective-permute-start(f32[8,128]{1,0:T(8,128)S(1)} %get-tuple-element.103), channel_id=1, source_target_pairs={{0,16},{1,17},{2,18},{3,19},{4,20},{5,21},{6,22},{7,23},{8,24},{9,... | collective-permute-start | bytes 12296 | tf_op jit(solution)/shard_map/ppermute | solution.py:566
  52.2 3.0 %collective-permute-start.17 = (f32[8,128]{1,0:T(8,128)S(1)}, f32[8,128]{1,0:T(8,128)S(1)}, u32[]{:S(2)}, u32[]{:S(2)}) collective-permute-start(f32[8,128]{1,0:T(8,128)S(1)} %get-tuple-element.104), channel_id=1, source_target_pairs={{0,31},{1,16},{2,17},{3,18},{4,19},{5,20},{6,21},{7,22},{8,23},{9,... | collective-permute-start | bytes 12296 | tf_op jit(solution)/shard_map/ppermute | solution.py:566

commit v6 on v5

--- a/solution.py
+++ b/solution.py
@@ -84,7 +84,8 @@
 
 
 def prelude_kernel(
-    x_hbm, go_hbm, kern_hbm, decay_hbm, beta_hbm, payload_ref, sums_ref, x_ref, go_ref, kern_ref, decay_ref, beta_ref, sems
+    x_hbm, go_hbm, kern_hbm, decay_hbm, beta_hbm, payload_ref, sums_ref, last_sums_ref, x_ref, go_ref, kern_ref,
+    decay_ref, beta_ref, sems,
 ):
     pairs = ((x_hbm, x_ref), (go_hbm, go_ref), (kern_hbm, kern_ref), (decay_hbm, decay_ref), (beta_hbm, beta_ref))
     copies = [pltpu.make_async_copy(src, dst, sems.at[n]) for n, (src, dst) in enumerate(pairs)]
@@ -92,11 +93,15 @@
         copy.start()
     copies[0].wait()
     x = x_ref[...].astype(f32)
-    channels = x.shape[1]
-    sums = row_sums(x * x)
-    sums_ref[...] = sums
-    payload_ref[:, :channels] = x[x.shape[0] - RIM :]
-    payload_ref[:, channels:] = sums
+    length, channels = x.shape
+    blocks = [x[:, n : n + HEAD_DIM] for n in range(0, channels, HEAD_DIM)]
+    squares = sum(block * block for block in blocks)
+    sums_ref[...] = row_sums(squares)
+    last = jnp.sum(squares[length - RIM :], axis=1, keepdims=True)
+    last = jnp.broadcast_to(last, (RIM, HEAD_DIM))
+    last_sums_ref[...] = last
+    payload_ref[:, :channels] = x[length - RIM :]
+    payload_ref[:, channels:] = last
     for copy in copies[1:]:
         copy.wait()
 
@@ -149,7 +154,8 @@
     ]
 
 
-def gates_kernel(decay_ref, beta_ref, e1_ref, e2_ref, edge_ref, rate_ref):
+def gates_kernel(width, decay_ref, beta_ref, sums_ref, e1_ref, e2_ref, edge_ref, rate_ref, scale_ref):
+    scale_ref[...] = down_rows(lax.rsqrt(sums_ref[...] / width + norm_eps))
     length = decay_ref.shape[0]
     row, col = iotas()
     tril = jnp.where(row >= col, 1.0, 0.0).astype(bf16)
@@ -180,9 +186,7 @@
 
 
 def scales(flags, scale_ref, rim_scale_ref):
-    rim_scale = down_rows(rim_scale_ref[...])
-    rim_scale = jnp.where(flags[4] != 0, rim_scale[rim_scale.shape[0] - RIM :], 0.0)
-    return down_rows(scale_ref[...]), rim_scale
+    return scale_ref[...], jnp.where(flags[4] != 0, rim_scale_ref[...], 0.0)
 
 
 def keep_split(ref, j, n, parts):
@@ -491,7 +495,7 @@
 def finish_kernel(slots, width, flags, x_ref, go_ref, scale_ref, inner_ref, next_sums_ref, next_ref, *refs):
     grads, (out_hbm, out_ref, sems) = refs[:-3], refs[-3:]
     length = x_ref.shape[0]
-    scale = down_rows(scale_ref[...])
+    scale = scale_ref[...]
     inner = down_rows(inner_ref[...])
     last = flags[5] == 0
     next_sums = jnp.where(last, 0.0, next_sums_ref[...])
@@ -573,10 +577,10 @@
             value, "ctx", [(i, i + shift) for i in range(spots) if 0 <= i + shift < spots]
         )
 
-    payload, sums, x, go, kern, decay, rates = call(
+    payload, sums, last_sums, x, go, kern, decay, rates = call(
         prelude_kernel,
         (
-            array(RIM, channels + length), array(RIM, length), array(*inputs.shape, dtype=bf16),
+            array(RIM, channels + HEAD_DIM), array(RIM, length), array(RIM, HEAD_DIM), array(*inputs.shape, dtype=bf16),
             array(*inputs.shape, dtype=bf16), array(*conv_weight.shape), array(*inputs.shape), array(heads, length),
         ),
         *[pltpu.with_memory_space_constraint(a, pltpu.HBM) for a in (inputs, out_grads, conv_weight, log_decay, beta.T)],
@@ -586,14 +590,14 @@
     rim_total = 0.0
     for sec in range(1, sections):
         total = total + turned(sums, sec, 0)
-        rim_total = rim_total + turned(sums, sec, 1)
+        rim_total = rim_total + turned(last_sums, sec, 1)
     rim = turned(payload, 0, 1)
-    e1, e2, edge, rate = call(
-        gates_kernel,
-        (array(length, channels), array(length, channels), array(24, channels), array(length, channels)),
-        decay, rates, name="gates", cost=BESIDE,
+    e1, e2, edge, rate, scale = call(
+        functools.partial(gates_kernel, width),
+        (array(length, channels), array(length, channels), array(24, channels), array(length, channels),
+         array(length, HEAD_DIM)),
+        decay, rates, total, name="gates", cost=BESIDE,
     )
-    scale = lax.rsqrt(total / width + norm_eps)
     rim_scale = lax.rsqrt((rim_total + rim[:, channels:]) / width + norm_eps)
 
     shared = (x, go, kern, e1, e2, edge, rate, rim)

time: 56.6 us -> 56.4 us (level)
  transfers between devices with their start and end apart: 19 -> 19, of which waited for: 9 -> 7; matrix products, arithmetic and copies ran while one was open for 0% -> 0% of each run, Pallas kernels for 18% -> 18%
where the time goes in v6:
time: 56.4 us; the launch traced here: 56.2 us
  starting transfers between devices  20.6 us (37%)
  Pallas kernels  18.5 us (33%)
  waiting for transfers between devices  16.2 us (29%)
  between operations  0.99 us (2%)
    pallas_call x17, Pallas kernels, call(): pl.pallas_call((lambda *refs: kernel(placed(*scalar), *refs)) if scalar e...  18.5 us
    ppermute x13, starting transfers between devices, swapped(): return lax.ppermute(value, 'ctx', [(i, i ^ distance) for i in range(spots)])  11.7 us
    ppermute x13, waiting for transfers between devices, swapped(): return lax.ppermute(value, 'ctx', [(i, i ^ distance) for i in range(spots)])  8.87 us
    ppermute x6, starting transfers between devices, turned(): return lax.ppermute(value, ('section', 'ctx'), route)  8.84 us
    ppermute x6, waiting for transfers between devices, turned(): return lax.ppermute(value, ('section', 'ctx'), route)  7.31 us
  transfers between devices with their start and end apart: 19, of which 7 were waited for; matrix products, arithmetic and copies ran while one was open for 0% of the time, Pallas kernels for 18%

profile of v6, /device:TPU:0, one launch (start us, length us, event | category | flops | bytes accessed | tf_op | source)
XLA Modules:
  0.0 56.2 jit_solution(12255640696359308192)
XLA Ops:
  0.6 1.3 %prelude.1 = (f32[8,1152]{1,0:T(8,128)S(1)}, f32[8,128]{1,0:T(8,128)S(1)}, f32[8,128]{1,0:T(8,128)S(1)}, bf16[128,1024]{1,0:T(8,128)(2,1)S(1)}, bf16[128,1024]{1...) custom-call(bf16[128,1024]{1,0:T(8,128)(2,1)} %x_hbm.1, ...), custom_call_target="tpu_custom_call" | custom-call | tf_op jit(solution)/shard_map/prelude/pallas_call | solution.py:527
  1.9 3.0 %collective-permute-start = (f32[8,128]{1,0:T(8,128)S(1)}, f32[8,128]{1,0:T(8,128)S(1)}, u32[]{:S(2)}, u32[]{:S(2)}) collective-permute-start(f32[8,128]{1,0:T(8,128)S(1)} %get-tuple-element.62), channel_id=1, source_target_pairs={{0,16},{1,17},{2,18},{3,19},{4,20},{5,21},{6,22},{7,23},{8,24},{9,... | collective-permute-start | bytes 12296 | tf_op jit(solution)/shard_map/ppermute | solution.py:570
  4.9 0.0 collective-permute-start.2
  4.9 1.6 %collective-permute-start.1 = (f32[8,1152]{1,0:T(8,128)S(1)}, f32[8,1152]{1,0:T(8,128)S(1)}, u32[]{:S(2)}, u32[]{:S(2)}) collective-permute-start(f32[8,1152]{1,0:T(8,128)S(1)} %get-tuple-element.67), channel_id=1, source_target_pairs={{0,1},{1,2},{2,3},{3,4},{4,5},{5,6},{6,7},{7,8},{8,9},{9,10},{10,1... | collective-permute-start | bytes 110600 | tf_op jit(solution)/shard_map/ppermute | solution.py:570
  6.5 0.0 collective-permute-done
  6.5 0.4 gates.1
  7.0 4.6 %collective-permute-done.2 = f32[8,128]{1,0:T(8,128)S(1)} collective-permute-done((f32[8,128]{1,0:T(8,128)S(1)}, f32[8,128]{1,0:T(8,128)S(1)}, u32[]{:S(2)}, u32[]{:S(2)}) %collective-permute-start.2) | collective-permute-done | bytes 4128 | tf_op jit(solution)/shard_map/ppermute | solution.py:570
  11.5 0.0 collective-permute-done.1.refs_7_.refs_4_
  11.5 2.3 %local_outer.1 = (f32[3,384,128]{2,1,0:T(8,128)S(1)}, f32[3,3,128,128]{3,2,1,0:T(8,128)S(1)}, bf16[3,16,128,128]{3,2,1,0:T(8,128)(2,1)S(1)}) custom-call(bf16[128,1024]{1,0:T(8,128)(2,1)S(1)} %get-tuple-element.57.refs_0_, bf16[128,1024]{1,0:T(8,128)(2,1)S(1)} %get-tuple-element.58.refs_1_, f32[3,4,1024]{2,1,0:T(4,128)S(1)} %get-tuple-element.59.refs_2_.refs_1_, ...), custom_call_target="tpu_custom_call" | custom-call | tf_op jit(solution)/shard_map/local_outer/pallas_call | solution.py:527
  13.8 0.1 collective-permute-start.3
  13.9 2.3 %local_inner.1 = (f32[3,384,128]{2,1,0:T(8,128)S(1)}, f32[3,3,128,128]{3,2,1,0:T(8,128)S(1)}, bf16[3,16,128,128]{3,2,1,0:T(8,128)(2,1)S(1)}) custom-call(bf16[128,1024]{1,0:T(8,128)(2,1)S(1)} %get-tuple-element.57.refs_0_, bf16[128,1024]{1,0:T(8,128)(2,1)S(1)} %get-tuple-element.58.refs_1_, f32[3,4,1024]{2,1,0:T(4,128)S(1)} %get-tuple-element.59.refs_2_.refs_1_, ...), custom_call_target="tpu_custom_call" | custom-call | tf_op jit(solution)/shard_map/local_inner/pallas_call | solution.py:527
  16.2 0.0 collective-permute-done.3.refs_1_.refs_3_
  16.2 0.3 join_inner.1
  16.5 0.1 collective-permute-start.5
  16.6 0.4 collective-permute-start.6
  17.0 3.1 %collective-permute-start.7 = (f32[384,128]{1,0:T(8,128)S(1)}, f32[384,128]{1,0:T(8,128)S(1)}, u32[]{:S(2)}, u32[]{:S(2)}) collective-permute-start(f32[384,128]{1,0:T(8,128)S(1)} %get-tuple-element.74.refs_12_), channel_id=1, source_target_pairs={{0,6},{1,7},{2,4},{3,5},{4,2},{5,3},{6,0},{7,1},{8,14},{9,15},{10,... | collective-permute-start | bytes 589832 | tf_op jit(solution)/shard_map/ppermute | solution.py:573
  20.1 1.9 %local_rest.1 = (f32[2,384,128]{2,1,0:T(8,128)S(1)}, f32[2,3,128,128]{3,2,1,0:T(8,128)S(1)}, bf16[2,16,128,128]{3,2,1,0:T(8,128)(2,1)S(1)}) custom-call(bf16[128,1024]{1,0:T(8,128)(2,1)S(1)} %get-tuple-element.57.refs_0_, bf16[128,1024]{1,0:T(8,128)(2,1)S(1)} %get-tuple-element.58.refs_1_, f32[3,4,1024]{2,1,0:T(4,128)S(1)} %get-tuple-element.59.refs_2_.refs_1_, ...), custom_call_target="tpu_custom_call" | custom-call | tf_op jit(solution)/shard_map/local_rest/pallas_call | solution.py:527
  22.1 0.1 collective-permute-start.4
  22.1 0.7 %ready_outer.1 = (f32[3,5,128,128]{3,2,1,0:T(8,128)S(1)}, bf16[3,4,128,128]{3,2,1,0:T(8,128)(2,1)S(1)}) custom-call(bf16[128,1024]{1,0:T(8,128)(2,1)S(1)} %get-tuple-element.57.refs_0_, f32[3,4,1024]{2,1,0:T(4,128)S(1)} %get-tuple-element.59.refs_2_.refs_1_, f32[128,1024]{1,0:T(8,128)S(1)} %get-tuple-element.64.refs_4_.refs_2_, ...), custom_call_target="tpu_custom_call" | custom-call | flops 1000000000 | bytes 10000000 | tf_op jit(solution)/shard_map/ready_outer/pallas_call | solution.py:527
  22.9 0.7 %ready_inner.1 = (f32[3,5,128,128]{3,2,1,0:T(8,128)S(1)}, bf16[3,4,128,128]{3,2,1,0:T(8,128)(2,1)S(1)}) custom-call(bf16[128,1024]{1,0:T(8,128)(2,1)S(1)} %get-tuple-element.57.refs_0_, f32[3,4,1024]{2,1,0:T(4,128)S(1)} %get-tuple-element.59.refs_2_.refs_1_, f32[128,1024]{1,0:T(8,128)S(1)} %get-tuple-element.64.refs_4_.refs_2_, ...), custom_call_target="tpu_custom_call" | custom-call | flops 1000000000 | bytes 10000000 | tf_op jit(solution)/shard_map/ready_inner/pallas_call | solution.py:527
  23.6 0.5 ready_rest.1
  24.1 0.0 collective-permute-done.4.refs_1_.refs_2_
  24.1 0.2 join_rest.1.refs_0_
  24.3 0.0 collective-permute-done.5.refs_1_
  24.3 0.0 collective-permute-done.6.refs_2_
  24.4 4.9 %collective-permute-done.7.refs_3_ = f32[384,128]{1,0:T(8,128)S(1)} collective-permute-done((f32[384,128]{1,0:T(8,128)S(1)}, f32[384,128]{1,0:T(8,128)S(1)}, u32[]{:S(2)}, u32[]{:S(2)}) %collective-permute-start.7) | collective-permute-done | bytes 196640 | tf_op jit(solution)/shard_map/ppermute | solution.py:573
  29.3 0.6 gather.1
  29.8 0.9 %collective-permute-start.8 = (f32[128,128]{1,0:T(8,128)S(1)}, f32[128,128]{1,0:T(8,128)S(1)}, u32[]{:S(2)}, u32[]{:S(2)}) collective-permute-start(f32[128,128]{1,0:T(8,128)S(1)} %get-tuple-element.88), channel_id=1, source_target_pairs={{0,8},{1,9},{2,10},{3,11},{4,12},{5,13},{6,14},{7,15},{8,0},{9,1},... | collective-permute-start | bytes 196616 | tf_op jit(solution)/shard_map/ppermute | solution.py:573
  30.7 0.3 reach.1
  31.1 0.7 %collective-permute-start.9 = (f32[128,128]{1,0:T(8,128)S(1)}, f32[128,128]{1,0:T(8,128)S(1)}, u32[]{:S(2)}, u32[]{:S(2)}) collective-permute-start(f32[128,128]{1,0:T(8,128)S(1)} %get-tuple-element.92), channel_id=1, source_target_pairs={{0,2},{1,3},{2,0},{3,1},{4,6},{5,7},{6,4},{7,5},{8,10},{9,11},{10,... | collective-permute-start | bytes 196616 | tf_op jit(solution)/shard_map/ppermute | solution.py:573
  31.7 1.6 %collective-permute-start.11 = (f32[128,128]{1,0:T(8,128)S(1)}, f32[128,128]{1,0:T(8,128)S(1)}, u32[]{:S(2)}, u32[]{:S(2)}) collective-permute-start(f32[128,128]{1,0:T(8,128)S(1)} %get-tuple-element.94), channel_id=1, source_target_pairs={{0,4},{1,5},{2,6},{3,7},{4,0},{5,1},{6,2},{7,3},{8,12},{9,13},{10,... | collective-permute-start | bytes 196616 | tf_op jit(solution)/shard_map/ppermute | solution.py:573
  33.3 1.3 %collective-permute-start.13 = (f32[128,128]{1,0:T(8,128)S(1)}, f32[128,128]{1,0:T(8,128)S(1)}, u32[]{:S(2)}, u32[]{:S(2)}) collective-permute-start(f32[128,128]{1,0:T(8,128)S(1)} %get-tuple-element.96), channel_id=1, source_target_pairs={{0,6},{1,7},{2,4},{3,5},{4,2},{5,3},{6,0},{7,1},{8,14},{9,15},{10,... | collective-permute-start | bytes 196616 | tf_op jit(solution)/shard_map/ppermute | solution.py:573
  34.6 1.0 %collective-permute-done.8.refs_0_ = f32[128,128]{1,0:T(8,128)S(1)} collective-permute-done((f32[128,128]{1,0:T(8,128)S(1)}, f32[128,128]{1,0:T(8,128)S(1)}, u32[]{:S(2)}, u32[]{:S(2)}) %collective-permute-start.8) | collective-permute-done | bytes 65568 | tf_op jit(solution)/shard_map/ppermute | solution.py:573
  35.6 0.2 late.1
  35.8 0.4 collective-permute-start.10
  36.3 0.9 %collective-permute-start.12 = (f32[128,128]{1,0:T(8,128)S(1)}, f32[128,128]{1,0:T(8,128)S(1)}, u32[]{:S(2)}, u32[]{:S(2)}) collective-permute-start(f32[128,128]{1,0:T(8,128)S(1)} %get-tuple-element.95), channel_id=1, source_target_pairs={{0,4},{1,5},{2,6},{3,7},{4,0},{5,1},{6,2},{7,3},{8,12},{9,13},{10,... | collective-permute-start | bytes 196616 | tf_op jit(solution)/shard_map/ppermute | solution.py:573
  37.1 0.0 collective-permute-done.9.refs_6_
  37.1 2.3 %collective-permute-start.14 = (f32[128,128]{1,0:T(8,128)S(1)}, f32[128,128]{1,0:T(8,128)S(1)}, u32[]{:S(2)}, u32[]{:S(2)}) collective-permute-start(f32[128,128]{1,0:T(8,128)S(1)} %get-tuple-element.97), channel_id=1, source_target_pairs={{0,6},{1,7},{2,4},{3,5},{4,2},{5,3},{6,0},{7,1},{8,14},{9,15},{10,... | collective-permute-start | bytes 196616 | tf_op jit(solution)/shard_map/ppermute | solution.py:573
  39.4 0.0 collective-permute-done.11.refs_8_
  39.4 0.0 collective-permute-done.13.refs_10_
  39.4 1.2 %collective-permute-done.10.refs_7_ = f32[128,128]{1,0:T(8,128)S(1)} collective-permute-done((f32[128,128]{1,0:T(8,128)S(1)}, f32[128,128]{1,0:T(8,128)S(1)}, u32[]{:S(2)}, u32[]{:S(2)}) %collective-permute-start.10) | collective-permute-done | bytes 65568 | tf_op jit(solution)/shard_map/ppermute | solution.py:573
  40.6 0.0 collective-permute-done.12.refs_9_
  40.6 1.7 %collective-permute-done.14.refs_11_ = f32[128,128]{1,0:T(8,128)S(1)} collective-permute-done((f32[128,128]{1,0:T(8,128)S(1)}, f32[128,128]{1,0:T(8,128)S(1)}, u32[]{:S(2)}, u32[]{:S(2)}) %collective-permute-start.14) | collective-permute-done | bytes 65568 | tf_op jit(solution)/shard_map/ppermute | solution.py:573
  42.3 0.4 part.1
  42.7 0.1 collective-permute-start.15
  42.8 2.7 %back_inner.1 = (bf16[128,1024]{1,0:T(8,128)(2,1)}, f32[4,128,128]{2,1,0:T(8,128)S(1)}, f32[8,128]{1,0:T(8,128)S(1)}, f32[8,1152]{1,0:T(8,128)S(1)}) custom-call(bf16[128,1024]{1,0:T(8,128)(2,1)S(1)} %get-tuple-element.57.refs_0_, bf16[128,1024]{1,0:T(8,128)(2,1)S(1)} %get-tuple-element.58.refs_1_, f32[3,4,1024]{2,1,0:T(4,128)S(1)} %get-tuple-element.59.refs_2_.refs_1_, ...), custom_call_target="tpu_custom_call" | custom-call | tf_op jit(solution)/shard_map/back_inner/pallas_call | solution.py:527
  45.5 0.0 collective-permute-done.15.refs_8_
  45.5 2.6 %back_outer.1 = (bf16[128,1024]{1,0:T(8,128)(2,1)}, f32[4,128,128]{2,1,0:T(8,128)S(1)}, f32[8,128]{1,0:T(8,128)S(1)}, f32[8,1152]{1,0:T(8,128)S(1)}, f32[8,128]{1,0:T(8,128)S(1)}) custom-call(bf16[128,1024]{1,0:T(8,128)(2,1)S(1)} %get-tuple-element.57.refs_0_, bf16[128,1024]{1,0:T(8,128)(2,1)S(1)} %get-tuple-element.58.refs_1_, ...), custom_call_target="tpu_custom_call", output_to_operand_aliasing={{0}: (19, {})} | custom-call | tf_op jit(solution)/shard_map/back_outer/pallas_call | solution.py:527
  48.1 3.0 %collective-permute-start.18 = (f32[8,1152]{1,0:T(8,128)S(1)}, f32[8,1152]{1,0:T(8,128)S(1)}, u32[]{:S(2)}, u32[]{:S(2)}) collective-permute-start(f32[8,1152]{1,0:T(8,128)S(1)} %get-tuple-element.109), channel_id=1, source_target_pairs={{0,15},{1,0},{2,1},{3,2},{4,3},{5,4},{6,5},{7,6},{8,7},{9,8},{10,9... | collective-permute-start | bytes 110600 | tf_op jit(solution)/shard_map/ppermute | solution.py:570
  51.1 0.9 %collective-permute-start.16 = (f32[8,128]{1,0:T(8,128)S(1)}, f32[8,128]{1,0:T(8,128)S(1)}, u32[]{:S(2)}, u32[]{:S(2)}) collective-permute-start(f32[8,128]{1,0:T(8,128)S(1)} %get-tuple-element.107), channel_id=1, source_target_pairs={{0,16},{1,17},{2,18},{3,19},{4,20},{5,21},{6,22},{7,23},{8,24},{9,... | collective-permute-start | bytes 12296 | tf_op jit(solution)/shard_map/ppermute | solution.py:570
  52.0 0.3 collective-permute-start.17
  52.4 2.3 %collective-permute-done.16 = f32[8,128]{1,0:T(8,128)S(1)} collective-permute-done((f32[8,128]{1,0:T(8,128)S(1)}, f32[8,128]{1,0:T(8,128)S(1)}, u32[]{:S(2)}, u32[]{:S(2)}) %collective-permute-start.16) | collective-permute-done | bytes 4128 | tf_op jit(solution)/shard_map/ppermute | solution.py:570
  54.7 0.4 collective-permute-done.17
  55.1 0.0 collective-permute-done.18.refs_5_
  55.1 1.0 %finish.1 = bf16[128,1024]{1,0:T(8,128)(2,1)} custom-call(bf16[128,1024]{1,0:T(8,128)(2,1)S(1)} %get-tuple-element.57.refs_0_, bf16[128,1024]{1,0:T(8,128)(2,1)S(1)} %get-tuple-element.58.refs_1_, f32[128,128]{1,0:T(8,128)S(1)} %get-tuple-element.68.refs_8_.refs_5_.refs_2_, f32[8,128]{1,0:T(8,128)S(1)} %add.22.refs_3_, f32[8,128]{1,0:T(8,128)S(1)} %slice_add_fusion.refs_4_, ...), custom_call_target="tpu_custom_call" | custom-call | tf_op jit(solution)/shard_map/finish/pallas_call | solution.py:527
  (5 shorter events, 0.0 us)
Async XLA Ops:
  1.9 4.6 %collective-permute-start = (f32[8,128]{1,0:T(8,128)S(1)}, f32[8,128]{1,0:T(8,128)S(1)}, u32[]{:S(2)}, u32[]{:S(2)}) collective-permute-start(f32[8,128]{1,0:T(8,128)S(1)} %get-tuple-element.62), channel_id=1, source_target_pairs={{0,16},{1,17},{2,18},{3,19},{4,20},{5,21},{6,22},{7,23},{8,24},{9,... | collective-permute-start | bytes 12296 | tf_op jit(solution)/shard_map/ppermute | solution.py:570
  4.9 6.6 %collective-permute-start.2 = (f32[8,128]{1,0:T(8,128)S(1)}, f32[8,128]{1,0:T(8,128)S(1)}, u32[]{:S(2)}, u32[]{:S(2)}) collective-permute-start(f32[8,128]{1,0:T(8,128)S(1)} %get-tuple-element.69), channel_id=1, source_target_pairs={{0,17},{1,18},{2,19},{3,20},{4,21},{5,22},{6,23},{7,24},{8,25},{9,... | collective-permute-start | bytes 12296 | tf_op jit(solution)/shard_map/ppermute | solution.py:570
  4.9 6.6 %collective-permute-start.1 = (f32[8,1152]{1,0:T(8,128)S(1)}, f32[8,1152]{1,0:T(8,128)S(1)}, u32[]{:S(2)}, u32[]{:S(2)}) collective-permute-start(f32[8,1152]{1,0:T(8,128)S(1)} %get-tuple-element.67), channel_id=1, source_target_pairs={{0,1},{1,2},{2,3},{3,4},{4,5},{5,6},{6,7},{7,8},{8,9},{9,10},{10,1... | collective-permute-start | bytes 110600 | tf_op jit(solution)/shard_map/ppermute | solution.py:570
  13.8 2.4 %collective-permute-start.3 = (f32[3,384,128]{2,1,0:T(8,128)S(1)}, f32[3,384,128]{2,1,0:T(8,128)S(1)}, u32[]{:S(2)}, u32[]{:S(2)}) collective-permute-start(f32[3,384,128]{2,1,0:T(8,128)S(1)} %get-tuple-element.71), channel_id=1, source_target_pairs={{0,1},{1,0},{2,3},{3,2},{4,5},{5,4},{6,7},{7,6},{8,9},{9,8},{10,11... | collective-permute-start | bytes 1769480 | tf_op jit(solution)/shard_map/ppermute | solution.py:573
  16.5 7.8 %collective-permute-start.5 = (f32[384,128]{1,0:T(8,128)S(1)}, f32[384,128]{1,0:T(8,128)S(1)}, u32[]{:S(2)}, u32[]{:S(2)}) collective-permute-start(f32[384,128]{1,0:T(8,128)S(1)} %get-tuple-element.72.refs_10_), channel_id=1, source_target_pairs={{0,2},{1,3},{2,0},{3,1},{4,6},{5,7},{6,4},{7,5},{8,10},{9,11},{10,... | collective-permute-start | bytes 589832 | tf_op jit(solution)/shard_map/ppermute | solution.py:573
  16.6 7.8 %collective-permute-start.6 = (f32[384,128]{1,0:T(8,128)S(1)}, f32[384,128]{1,0:T(8,128)S(1)}, u32[]{:S(2)}, u32[]{:S(2)}) collective-permute-start(f32[384,128]{1,0:T(8,128)S(1)} %get-tuple-element.73.refs_11_), channel_id=1, source_target_pairs={{0,4},{1,5},{2,6},{3,7},{4,0},{5,1},{6,2},{7,3},{8,12},{9,13},{10,... | collective-permute-start | bytes 589832 | tf_op jit(solution)/shard_map/ppermute | solution.py:573
  17.0 12.3 %collective-permute-start.7 = (f32[384,128]{1,0:T(8,128)S(1)}, f32[384,128]{1,0:T(8,128)S(1)}, u32[]{:S(2)}, u32[]{:S(2)}) collective-permute-start(f32[384,128]{1,0:T(8,128)S(1)} %get-tuple-element.74.refs_12_), channel_id=1, source_target_pairs={{0,6},{1,7},{2,4},{3,5},{4,2},{5,3},{6,0},{7,1},{8,14},{9,15},{10,... | collective-permute-start | bytes 589832 | tf_op jit(solution)/shard_map/ppermute | solution.py:573
  22.1 2.0 %collective-permute-start.4 = (f32[1,384,128]{2,1,0:T(8,128)S(1)}, f32[1,384,128]{2,1,0:T(8,128)S(1)}, u32[]{:S(2)}, u32[]{:S(2)}) collective-permute-start(f32[1,384,128]{2,1,0:T(8,128)S(1)} %get-tuple-element.112), channel_id=1, source_target_pairs={{0,1},{1,0},{2,3},{3,2},{4,5},{5,4},{6,7},{7,6},{8,9},{9,8},{10,11... | collective-permute-start | bytes 589832 | tf_op jit(solution)/shard_map/ppermute | solution.py:573
  29.8 5.7 %collective-permute-start.8 = (f32[128,128]{1,0:T(8,128)S(1)}, f32[128,128]{1,0:T(8,128)S(1)}, u32[]{:S(2)}, u32[]{:S(2)}) collective-permute-start(f32[128,128]{1,0:T(8,128)S(1)} %get-tuple-element.88), channel_id=1, source_target_pairs={{0,8},{1,9},{2,10},{3,11},{4,12},{5,13},{6,14},{7,15},{8,0},{9,1},... | collective-permute-start | bytes 196616 | tf_op jit(solution)/shard_map/ppermute | solution.py:573
  31.1 6.1 %collective-permute-start.9 = (f32[128,128]{1,0:T(8,128)S(1)}, f32[128,128]{1,0:T(8,128)S(1)}, u32[]{:S(2)}, u32[]{:S(2)}) collective-permute-start(f32[128,128]{1,0:T(8,128)S(1)} %get-tuple-element.92), channel_id=1, source_target_pairs={{0,2},{1,3},{2,0},{3,1},{4,6},{5,7},{6,4},{7,5},{8,10},{9,11},{10,... | collective-permute-start | bytes 196616 | tf_op jit(solution)/shard_map/ppermute | solution.py:573
  31.7 7.7 %collective-permute-start.11 = (f32[128,128]{1,0:T(8,128)S(1)}, f32[128,128]{1,0:T(8,128)S(1)}, u32[]{:S(2)}, u32[]{:S(2)}) collective-permute-start(f32[128,128]{1,0:T(8,128)S(1)} %get-tuple-element.94), channel_id=1, source_target_pairs={{0,4},{1,5},{2,6},{3,7},{4,0},{5,1},{6,2},{7,3},{8,12},{9,13},{10,... | collective-permute-start | bytes 196616 | tf_op jit(solution)/shard_map/ppermute | solution.py:573
  33.3 6.1 %collective-permute-start.13 = (f32[128,128]{1,0:T(8,128)S(1)}, f32[128,128]{1,0:T(8,128)S(1)}, u32[]{:S(2)}, u32[]{:S(2)}) collective-permute-start(f32[128,128]{1,0:T(8,128)S(1)} %get-tuple-element.96), channel_id=1, source_target_pairs={{0,6},{1,7},{2,4},{3,5},{4,2},{5,3},{6,0},{7,1},{8,14},{9,15},{10,... | collective-permute-start | bytes 196616 | tf_op jit(solution)/shard_map/ppermute | solution.py:573
  35.8 4.8 %collective-permute-start.10 = (f32[128,128]{1,0:T(8,128)S(1)}, f32[128,128]{1,0:T(8,128)S(1)}, u32[]{:S(2)}, u32[]{:S(2)}) collective-permute-start(f32[128,128]{1,0:T(8,128)S(1)} %get-tuple-element.93), channel_id=1, source_target_pairs={{0,2},{1,3},{2,0},{3,1},{4,6},{5,7},{6,4},{7,5},{8,10},{9,11},{10,... | collective-permute-start | bytes 196616 | tf_op jit(solution)/shard_map/ppermute | solution.py:573
  36.3 4.3 %collective-permute-start.12 = (f32[128,128]{1,0:T(8,128)S(1)}, f32[128,128]{1,0:T(8,128)S(1)}, u32[]{:S(2)}, u32[]{:S(2)}) collective-permute-start(f32[128,128]{1,0:T(8,128)S(1)} %get-tuple-element.95), channel_id=1, source_target_pairs={{0,4},{1,5},{2,6},{3,7},{4,0},{5,1},{6,2},{7,3},{8,12},{9,13},{10,... | collective-permute-start | bytes 196616 | tf_op jit(solution)/shard_map/ppermute | solution.py:573
  37.1 5.2 %collective-permute-start.14 = (f32[128,128]{1,0:T(8,128)S(1)}, f32[128,128]{1,0:T(8,128)S(1)}, u32[]{:S(2)}, u32[]{:S(2)}) collective-permute-start(f32[128,128]{1,0:T(8,128)S(1)} %get-tuple-element.97), channel_id=1, source_target_pairs={{0,6},{1,7},{2,4},{3,5},{4,2},{5,3},{6,0},{7,1},{8,14},{9,15},{10,... | collective-permute-start | bytes 196616 | tf_op jit(solution)/shard_map/ppermute | solution.py:573
  42.7 2.8 %collective-permute-start.15 = (f32[4,256,128]{2,1,0:T(8,128)S(1)}, f32[4,256,128]{2,1,0:T(8,128)S(1)}, u32[]{:S(2)}, u32[]{:S(2)}) collective-permute-start(f32[4,256,128]{2,1,0:T(8,128)S(1)} %get-tuple-element.98), channel_id=1, source_target_pairs={{0,1},{1,0},{2,3},{3,2},{4,5},{5,4},{6,7},{7,6},{8,9},{9,8},{10,11... | collective-permute-start | bytes 1572872 | tf_op jit(solution)/shard_map/ppermute | solution.py:573
  48.1 7.0 %collective-permute-start.18 = (f32[8,1152]{1,0:T(8,128)S(1)}, f32[8,1152]{1,0:T(8,128)S(1)}, u32[]{:S(2)}, u32[]{:S(2)}) collective-permute-start(f32[8,1152]{1,0:T(8,128)S(1)} %get-tuple-element.109), channel_id=1, source_target_pairs={{0,15},{1,0},{2,1},{3,2},{4,3},{5,4},{6,5},{7,6},{8,7},{9,8},{10,9... | collective-permute-start | bytes 110600 | tf_op jit(solution)/shard_map/ppermute | solution.py:570
  51.1 3.6 %collective-permute-start.16 = (f32[8,128]{1,0:T(8,128)S(1)}, f32[8,128]{1,0:T(8,128)S(1)}, u32[]{:S(2)}, u32[]{:S(2)}) collective-permute-start(f32[8,128]{1,0:T(8,128)S(1)} %get-tuple-element.107), channel_id=1, source_target_pairs={{0,16},{1,17},{2,18},{3,19},{4,20},{5,21},{6,22},{7,23},{8,24},{9,... | collective-permute-start | bytes 12296 | tf_op jit(solution)/shard_map/ppermute | solution.py:570
  52.0 3.0 %collective-permute-start.17 = (f32[8,128]{1,0:T(8,128)S(1)}, f32[8,128]{1,0:T(8,128)S(1)}, u32[]{:S(2)}, u32[]{:S(2)}) collective-permute-start(f32[8,128]{1,0:T(8,128)S(1)} %get-tuple-element.108), channel_id=1, source_target_pairs={{0,31},{1,16},{2,17},{3,18},{4,19},{5,20},{6,21},{7,22},{8,23},{9,... | collective-permute-start | bytes 12296 | tf_op jit(solution)/shard_map/ppermute | solution.py:570

commit v7 on v6

--- a/solution.py
+++ b/solution.py
@@ -282,18 +282,23 @@
 
 
 def join_kernel(flags, keep_ref, recv_ref, *outs):
-    later = flags[1] != 0
-    outs = outs[-keep_ref.shape[0] :]
-    for j, out in enumerate(outs):
+    later, upper = flags[1] != 0, flags[3] != 0
+    heads = keep_ref.shape[0]
+    for j in range(heads):
         keep, recv = keep_ref[j], recv_ref[j]
         lo = jnp.where(later, recv, keep)
         hi = jnp.where(later, keep, recv)
         lo_map, hi_map = split(lo[0:128]), split(hi[0:128])
         forward = mm(hi_map, cols_of(lo_map, split(lo[128:256])), "nn")
-        back = mm(lo_map, split(hi[256:384]), "tn")
+        grad = mm(lo_map, split(hi[256:384]), "tn") + lo[256:384]
+        state = forward[:, HEAD_DIM:] + hi[128:256]
+        out = outs[j]
         out[0:128] = forward[:, :HEAD_DIM]
-        out[128:256] = forward[:, HEAD_DIM:] + hi[128:256]
-        out[256:384] = back + lo[256:384]
+        if len(outs) == heads:
+            out[128:256], out[256:384] = state, grad
+        else:
+            out[128:256] = jnp.where(upper, grad, state)
+            outs[heads + j][...] = jnp.where(upper, state, grad)
 
 
 def collect(place, parts, held):
@@ -338,28 +343,42 @@
 def two_gather_kernel(waits, flags, *refs):
     parts, outs = refs[:4], refs[4 + waits : -1]
     held = refs[-1]
-    total_ref, known_ref, pairs_ref, found_ref = outs
+    total_ref, pairs_ref, found_ref = outs
     upper = flags[3] != 0
     collect(flags[2], parts, held)
     t = [split(held[p, 0:128]) for p in range(4)]
     u = [held[p, 128:256] for p in range(4)]
-    g = [held[p, 256:384] for p in range(4)]
-    last = mm(t[3], cols_of(t[2], split(u[2])), "nn")
-    first = mm(t[1], cols_of(t[0], split(u[0])), "nn")
+    su = [split(a) for a in u]
+    last = mm(t[3], cols_of(t[2], su[2]), "nn")
+    first = mm(t[1], cols_of(t[0], su[0]), "nn")
     second = first[:, HEAD_DIM:] + u[1]
     first, last, last_u = first[:, :HEAD_DIM], last[:, :HEAD_DIM], last[:, HEAD_DIM:]
-    third = mm(t[2], split(g[3]), "tn") + g[2]
-    low = mm(t[0], split(g[1]), "tn")
+    third = mm(t[2], su[3], "tn") + u[2]
+    low = mm(t[0], su[1], "tn")
     s_second, s_third = split(second), split(third)
     forward = [jnp.zeros_like(second), u[0], second, mm(t[2], s_second, "nn") + u[2]]
-    back = [mm(t[1], s_third, "tn") + g[1], third, g[3], jnp.zeros_like(third)]
+    back = [mm(t[1], s_third, "tn") + u[1], third, u[3], jnp.zeros_like(third)]
     state = mm(split(last), s_second, "nn") + (last_u + u[3])
-    grad = mm(split(first), s_third, "tn") + (low + g[0])
+    grad = mm(split(first), s_third, "tn") + (low + u[0])
     total_ref[...] = jnp.where(upper, grad, state)
     pairs_ref[0], pairs_ref[1] = first, last
     for p in range(4):
         found_ref[p] = jnp.where(upper, back[p], forward[p])
-        known_ref[p] = jnp.where(upper, forward[p], back[3 - p])
+
+
+def known_kernel(flags, *refs):
+    parts, others, known_ref, held, values = refs[:4], refs[4:8], refs[8], refs[9], refs[10]
+    upper = flags[3] != 0
+    collect(flags[2], parts, held)
+    collect(flags[2], others, values)
+    t = [split(held[p, 0:128]) for p in (1, 2)]
+    second = mm(t[0], split(values[0]), "nn") + values[1]
+    third = mm(t[1], split(second), "nn") + values[2]
+    below = mm(t[1], split(values[3]), "tn") + values[2]
+    lowest = mm(t[0], split(below), "tn") + values[1]
+    for n, (up, down) in enumerate(((values[0], values[3]), (second, below), (third, lowest))):
+        known_ref[n + 1] = jnp.where(upper, up, down)
+    known_ref[0] = jnp.zeros_like(second)
 
 
 def reach_kernel(flags, *refs):
@@ -537,7 +556,7 @@
     )(*args)
 
 
-BESIDE = pl.CostEstimate(flops=10**9, bytes_accessed=10**7, transcendentals=0)
+BESIDE = pl.CostEstimate(flops=0, bytes_accessed=0, transcendentals=0)
 
 
 def array(*shape, dtype=f32):
@@ -559,6 +578,7 @@
     per = heads // 2
     count = per
     slabs = spots // (2 * count)
+    rows = slabs == 2 and count == 4
     spot = functools.partial(call, scalar=(per, spots))
 
     def turned(value, sec, shift):
@@ -608,7 +628,7 @@
         return spot(
             functools.partial(local_kernel, slots),
             (array(n, 384, HEAD_DIM), array(n, WIDE, *tile), array(n, NARROW, *tile, dtype=bf16)),
-            *shared, scale, rim_scale, name=name, unread=unread,
+            *shared, scale, rim_scale, name=name, unread=unread, cost=BESIDE,
         )
 
     def prepared(slots, saved, name):
@@ -619,38 +639,30 @@
             x, kern, e2, edge, rim, scale, rim_scale, *saved, name=name, cost=BESIDE,
         )
 
-    inner_slots, outer_slots, rest_slots = range(1, per), range(per + 1, 2 * per), (0, per)
-    some = per > 1
-    parts, ahead, pairs = [None], [], ()
-    if some:
-        outer, *outer_saved = local(outer_slots, "local_outer")
-        outer_recv = swapped(outer, 1)
-        inner, *inner_saved = local(inner_slots, "local_inner")
-        pairs = spot(join_kernel, (array(384, HEAD_DIM),) * (per - 1), inner, outer_recv, name="join_inner")
-        parts += [swapped(pairs[n - 1], 2 * n) for n in range(1, count)]
-    rest, *rest_saved = local(rest_slots, "local_rest", pairs)
-    rest_recv = swapped(rest[1:], 1)
-    rest = rest[:1]
-    (parts[0],) = spot(join_kernel, (array(384, HEAD_DIM),), rest, rest_recv, name="join_rest")
-    rest_saved += prepared(rest_slots, rest_saved, "ready_rest")
-    ahead = [rest_saved[-1]]
-    if some:
-        outer_saved += prepared(outer_slots, outer_saved, "ready_outer")
-        inner_saved += prepared(inner_slots, inner_saved, "ready_inner")
-        ahead += [outer_saved[-1], inner_saved[-1]]
-
-    held = pltpu.VMEM((count, 384, HEAD_DIM), f32)
+    inner_slots, outer_slots = range(per), range(per, 2 * per)
+    joined, others = ((array(256, HEAD_DIM),), (array(*tile),)) if rows else ((array(384, HEAD_DIM),), ())
+    outer, *outer_saved = local(outer_slots, "local_outer")
+    outer_recv = swapped(outer, 1)
+    inner, *inner_saved = local(inner_slots, "local_inner")
+    pairs = spot(join_kernel, joined * per + others * per, inner, outer_recv, name="join")
+    parts = [pairs[0]] + [swapped(pairs[n], 2 * n) for n in range(1, count)]
+    second = [pairs[per]] + [swapped(pairs[per + n], 2 * n) for n in range(1, count)] if rows else []
+    outer_saved += prepared(outer_slots, outer_saved, "ready_outer")
+    inner_saved += prepared(inner_slots, inner_saved, "ready_inner")
+    ahead = [outer_saved[-1], inner_saved[-1]]
+
+    held = pltpu.VMEM((count, 256 if rows else 384, HEAD_DIM), f32)
     square = array(*tile)
     step = 2 * count
 
     def returned(values):
         return [values[0]] + [swapped(values[n], 2 * n) for n in range(1, count)]
 
-    if slabs == 2 and count == 4:
+    if rows:
         found = pltpu.VMEM((count, *tile), f32)
-        total, known, products, sure = spot(
+        total, products, sure = spot(
             functools.partial(two_gather_kernel, len(ahead)),
-            (square, array(4, *tile), array(2, *tile), array(4, *tile)),
+            (square, array(2, *tile), array(4, *tile)),
             *parts, name="gather", scratch=[held], unread=ahead,
         )
         other = swapped(total, step)
@@ -659,6 +671,9 @@
             *parts, products, sure, name="reach", scratch=[held], cost=BESIDE,
         )
         early = returned(early)
+        (known,) = spot(
+            known_kernel, (array(4, *tile),), *parts, *second, name="known", scratch=[held, found], cost=BESIDE
+        )
         late = spot(late_kernel, (square,) * 4, other, known, reach, name="late", scratch=[found])
         states = list(zip(early, returned(late)))
     else:
@@ -681,7 +696,7 @@
         )
         states = [(a,) for a in spread]
 
-    keeps, recvs = ((rest, inner), (rest_recv, outer_recv)) if some else ((rest,), (rest_recv,))
+    keeps, recvs = (inner,), (outer_recv,)
     mine, send = spot(
         functools.partial(part_kernel, len(keeps), len(states[0])), (array(per, 256, HEAD_DIM),) * 2,
         *keeps, *recvs, *(a for pair in states for a in pair), name="part",
@@ -705,14 +720,10 @@
         )
 
     slots = range(heads)
-    homes = [[(0, n)] + [(1, i) for i in range(per - 1)] for n in range(2)]
-    chain = backward(
-        slots[:per], [rest_saved] + ([inner_saved] if some else []), homes[0], mine, None, "back_inner"
-    )
+    homes = [(0, n) for n in range(per)]
+    chain = backward(slots[:per], [inner_saved], homes, mine, None, "back_inner")
     grads = [chain[1]]
-    chain = backward(
-        slots[per:], [rest_saved] + ([outer_saved] if some else []), homes[1], far, chain, "back_outer"
-    )
+    chain = backward(slots[per:], [outer_saved], homes, far, chain, "back_outer")
     grads.append(chain[1])
     stream_out, _, inner_sum, rim_grad, rim_sums = chain
 

time: 56.4 us -> 55.9 us (level)
  starting transfers between devices: 20.6 us -> 24 us
  waiting for transfers between devices: 16.2 us -> 12.8 us
    ppermute x13 -> x15, starting transfers between devices: 11.7 us -> 15.2 us  [swapped(): return lax.ppermute(value, 'ctx', [(i, i ^ distance) for i in range(spots)])]
    ppermute x13 -> x15, waiting for transfers between devices: 8.87 us -> 5.68 us  [swapped(): return lax.ppermute(value, 'ctx', [(i, i ^ distance) for i in range(spots)])]
    pallas_call x17 -> x15, Pallas kernels: 18.5 us -> 18 us  [call(): pl.pallas_call((lambda *refs: kernel(placed(*scalar), *refs)) if scalar e...]
  transfers between devices with their start and end apart: 19 -> 21, of which waited for: 7 -> 8; matrix products, arithmetic and copies ran while one was open for 0% -> 0% of each run, Pallas kernels for 18% -> 17%
where the time goes in v7:
time: 55.9 us; the launch traced here: 55.7 us
  starting transfers between devices  24 us (43%)
  Pallas kernels  18 us (32%)
  waiting for transfers between devices  12.8 us (23%)
  between operations  0.96 us (2%)
    pallas_call x15, Pallas kernels, call(): pl.pallas_call((lambda *refs: kernel(placed(*scalar), *refs)) if scalar e...  18 us
    ppermute x15, starting transfers between devices, swapped(): return lax.ppermute(value, 'ctx', [(i, i ^ distance) for i in range(spots)])  15.2 us
    ppermute x6, starting transfers between devices, turned(): return lax.ppermute(value, ('section', 'ctx'), route)  8.77 us
    ppermute x6, waiting for transfers between devices, turned(): return lax.ppermute(value, ('section', 'ctx'), route)  7.13 us
    ppermute x15, waiting for transfers between devices, swapped(): return lax.ppermute(value, 'ctx', [(i, i ^ distance) for i in range(spots)])  5.68 us
  transfers between devices with their start and end apart: 21, of which 8 were waited for; matrix products, arithmetic and copies ran while one was open for 0% of the time, Pallas kernels for 17%

profile of v7, /device:TPU:0, one launch (start us, length us, event | category | flops | bytes accessed | tf_op | source)
XLA Modules:
  0.0 55.7 jit_solution(3425139984453268944)
XLA Ops:
  0.6 1.3 %prelude.1 = (f32[8,1152]{1,0:T(8,128)S(1)}, f32[8,128]{1,0:T(8,128)S(1)}, f32[8,128]{1,0:T(8,128)S(1)}, bf16[128,1024]{1,0:T(8,128)(2,1)S(1)}, bf16[128,1024]{1...) custom-call(bf16[128,1024]{1,0:T(8,128)(2,1)} %x_hbm.1, ...), custom_call_target="tpu_custom_call" | custom-call | tf_op jit(solution)/shard_map/prelude/pallas_call | solution.py:546
  1.9 0.5 collective-permute-start.1
  2.4 2.6 %collective-permute-start = (f32[8,128]{1,0:T(8,128)S(1)}, f32[8,128]{1,0:T(8,128)S(1)}, u32[]{:S(2)}, u32[]{:S(2)}) collective-permute-start(f32[8,128]{1,0:T(8,128)S(1)} %get-tuple-element.61), channel_id=1, source_target_pairs={{0,16},{1,17},{2,18},{3,19},{4,20},{5,21},{6,22},{7,23},{8,24},{9,... | collective-permute-start | bytes 12296 | tf_op jit(solution)/shard_map/ppermute | solution.py:590
  5.0 1.4 %collective-permute-start.2 = (f32[8,128]{1,0:T(8,128)S(1)}, f32[8,128]{1,0:T(8,128)S(1)}, u32[]{:S(2)}, u32[]{:S(2)}) collective-permute-start(f32[8,128]{1,0:T(8,128)S(1)} %get-tuple-element.68), channel_id=1, source_target_pairs={{0,17},{1,18},{2,19},{3,20},{4,21},{5,22},{6,23},{7,24},{8,25},{9,... | collective-permute-start | bytes 12296 | tf_op jit(solution)/shard_map/ppermute | solution.py:590
  6.4 0.2 collective-permute-done
  6.6 0.4 gates.1
  7.0 4.6 %collective-permute-done.2 = f32[8,128]{1,0:T(8,128)S(1)} collective-permute-done((f32[8,128]{1,0:T(8,128)S(1)}, f32[8,128]{1,0:T(8,128)S(1)}, u32[]{:S(2)}, u32[]{:S(2)}) %collective-permute-start.2) | collective-permute-done | bytes 4128 | tf_op jit(solution)/shard_map/ppermute | solution.py:590
  11.6 0.0 collective-permute-done.1.refs_7_.refs_4_
  11.6 2.9 %local_outer.1 = (f32[4,384,128]{2,1,0:T(8,128)S(1)}, f32[4,3,128,128]{3,2,1,0:T(8,128)S(1)}, bf16[4,16,128,128]{3,2,1,0:T(8,128)(2,1)S(1)}) custom-call(bf16[128,1024]{1,0:T(8,128)(2,1)S(1)} %get-tuple-element.56.refs_0_, bf16[128,1024]{1,0:T(8,128)(2,1)S(1)} %get-tuple-element.57.refs_1_, f32[3,4,1024]{2,1,0:T(4,128)S(1)} %get-tuple-element.58.refs_2_.refs_1_, ...), custom_call_target="tpu_custom_call" | custom-call | tf_op jit(solution)/shard_map/local_outer/pallas_call | solution.py:546
  14.5 0.1 collective-permute-start.3
  14.6 2.9 %local_inner.1 = (f32[4,384,128]{2,1,0:T(8,128)S(1)}, f32[4,3,128,128]{3,2,1,0:T(8,128)S(1)}, bf16[4,16,128,128]{3,2,1,0:T(8,128)(2,1)S(1)}) custom-call(bf16[128,1024]{1,0:T(8,128)(2,1)S(1)} %get-tuple-element.56.refs_0_, bf16[128,1024]{1,0:T(8,128)(2,1)S(1)} %get-tuple-element.57.refs_1_, f32[3,4,1024]{2,1,0:T(4,128)S(1)} %get-tuple-element.58.refs_2_.refs_1_, ...), custom_call_target="tpu_custom_call" | custom-call | tf_op jit(solution)/shard_map/local_inner/pallas_call | solution.py:546
  17.5 0.0 collective-permute-done.3.refs_1_
  17.5 0.4 join.1
  18.0 0.1 collective-permute-start.4
  18.1 0.7 %collective-permute-start.5 = (f32[256,128]{1,0:T(8,128)S(1)}, f32[256,128]{1,0:T(8,128)S(1)}, u32[]{:S(2)}, u32[]{:S(2)}) collective-permute-start(f32[256,128]{1,0:T(8,128)S(1)} %get-tuple-element.73), channel_id=1, source_target_pairs={{0,4},{1,5},{2,6},{3,7},{4,0},{5,1},{6,2},{7,3},{8,12},{9,13},{10,... | collective-permute-start | bytes 393224 | tf_op jit(solution)/shard_map/ppermute | solution.py:593
  18.8 2.7 %collective-permute-start.6 = (f32[256,128]{1,0:T(8,128)S(1)}, f32[256,128]{1,0:T(8,128)S(1)}, u32[]{:S(2)}, u32[]{:S(2)}) collective-permute-start(f32[256,128]{1,0:T(8,128)S(1)} %get-tuple-element.74), channel_id=1, source_target_pairs={{0,6},{1,7},{2,4},{3,5},{4,2},{5,3},{6,0},{7,1},{8,14},{9,15},{10,... | collective-permute-start | bytes 393224 | tf_op jit(solution)/shard_map/ppermute | solution.py:593
  21.5 0.9 %ready_outer.1 = (f32[4,5,128,128]{3,2,1,0:T(8,128)S(1)}, bf16[4,4,128,128]{3,2,1,0:T(8,128)(2,1)S(1)}) custom-call(bf16[128,1024]{1,0:T(8,128)(2,1)S(1)} %get-tuple-element.56.refs_0_, f32[3,4,1024]{2,1,0:T(4,128)S(1)} %get-tuple-element.58.refs_2_.refs_1_, f32[128,1024]{1,0:T(8,128)S(1)} %get-tuple-element.63.refs_4_.refs_2_, ...), custom_call_target="tpu_custom_call" | custom-call | tf_op jit(solution)/shard_map/ready_outer/pallas_call | solution.py:546
  22.4 0.9 %ready_inner.1 = (f32[4,5,128,128]{3,2,1,0:T(8,128)S(1)}, bf16[4,4,128,128]{3,2,1,0:T(8,128)(2,1)S(1)}) custom-call(bf16[128,1024]{1,0:T(8,128)(2,1)S(1)} %get-tuple-element.56.refs_0_, f32[3,4,1024]{2,1,0:T(4,128)S(1)} %get-tuple-element.58.refs_2_.refs_1_, f32[128,1024]{1,0:T(8,128)S(1)} %get-tuple-element.63.refs_4_.refs_2_, ...), custom_call_target="tpu_custom_call" | custom-call | tf_op jit(solution)/shard_map/ready_inner/pallas_call | solution.py:546
  23.3 0.2 collective-permute-start.8
  23.5 0.7 %collective-permute-start.9 = (f32[128,128]{1,0:T(8,128)S(1)}, f32[128,128]{1,0:T(8,128)S(1)}, u32[]{:S(2)}, u32[]{:S(2)}) collective-permute-start(f32[128,128]{1,0:T(8,128)S(1)} %get-tuple-element.87), channel_id=1, source_target_pairs={{0,4},{1,5},{2,6},{3,7},{4,0},{5,1},{6,2},{7,3},{8,12},{9,13},{10,... | collective-permute-start | bytes 196616 | tf_op jit(solution)/shard_map/ppermute | solution.py:593
  24.2 0.0 collective-permute-done.4.refs_1_
  24.2 2.7 %collective-permute-start.10 = (f32[128,128]{1,0:T(8,128)S(1)}, f32[128,128]{1,0:T(8,128)S(1)}, u32[]{:S(2)}, u32[]{:S(2)}) collective-permute-start(f32[128,128]{1,0:T(8,128)S(1)} %get-tuple-element.88), channel_id=1, source_target_pairs={{0,6},{1,7},{2,4},{3,5},{4,2},{5,3},{6,0},{7,1},{8,14},{9,15},{10,... | collective-permute-start | bytes 196616 | tf_op jit(solution)/shard_map/ppermute | solution.py:593
  26.9 0.0 collective-permute-done.5.refs_2_
  26.9 1.8 %collective-permute-done.6.refs_3_ = f32[256,128]{1,0:T(8,128)S(1)} collective-permute-done((f32[256,128]{1,0:T(8,128)S(1)}, f32[256,128]{1,0:T(8,128)S(1)}, u32[]{:S(2)}, u32[]{:S(2)}) %collective-permute-start.6) | collective-permute-done | bytes 131104 | tf_op jit(solution)/shard_map/ppermute | solution.py:593
  28.7 0.5 gather.1
  29.2 0.9 %collective-permute-start.7 = (f32[128,128]{1,0:T(8,128)S(1)}, f32[128,128]{1,0:T(8,128)S(1)}, u32[]{:S(2)}, u32[]{:S(2)}) collective-permute-start(f32[128,128]{1,0:T(8,128)S(1)} %get-tuple-element.84), channel_id=1, source_target_pairs={{0,8},{1,9},{2,10},{3,11},{4,12},{5,13},{6,14},{7,15},{8,0},{9,1},... | collective-permute-start | bytes 196616 | tf_op jit(solution)/shard_map/ppermute | solution.py:593
  30.1 0.3 reach.1
  30.4 0.6 %collective-permute-start.11 = (f32[128,128]{1,0:T(8,128)S(1)}, f32[128,128]{1,0:T(8,128)S(1)}, u32[]{:S(2)}, u32[]{:S(2)}) collective-permute-start(f32[128,128]{1,0:T(8,128)S(1)} %get-tuple-element.91), channel_id=1, source_target_pairs={{0,2},{1,3},{2,0},{3,1},{4,6},{5,7},{6,4},{7,5},{8,10},{9,11},{10,... | collective-permute-start | bytes 196616 | tf_op jit(solution)/shard_map/ppermute | solution.py:593
  31.0 0.0 collective-permute-done.8.refs_5_
  31.0 1.6 %collective-permute-start.13 = (f32[128,128]{1,0:T(8,128)S(1)}, f32[128,128]{1,0:T(8,128)S(1)}, u32[]{:S(2)}, u32[]{:S(2)}) collective-permute-start(f32[128,128]{1,0:T(8,128)S(1)} %get-tuple-element.93), channel_id=1, source_target_pairs={{0,4},{1,5},{2,6},{3,7},{4,0},{5,1},{6,2},{7,3},{8,12},{9,13},{10,... | collective-permute-start | bytes 196616 | tf_op jit(solution)/shard_map/ppermute | solution.py:593
  32.7 0.0 collective-permute-done.9.refs_6_
  32.7 1.3 %collective-permute-start.15 = (f32[128,128]{1,0:T(8,128)S(1)}, f32[128,128]{1,0:T(8,128)S(1)}, u32[]{:S(2)}, u32[]{:S(2)}) collective-permute-start(f32[128,128]{1,0:T(8,128)S(1)} %get-tuple-element.95), channel_id=1, source_target_pairs={{0,6},{1,7},{2,4},{3,5},{4,2},{5,3},{6,0},{7,1},{8,14},{9,15},{10,... | collective-permute-start | bytes 196616 | tf_op jit(solution)/shard_map/ppermute | solution.py:593
  34.0 0.0 collective-permute-done.10.refs_7_
  34.0 0.4 known.1.refs_1_
  34.5 0.4 collective-permute-done.7.refs_0_
  34.8 0.2 late.1
  35.1 0.5 collective-permute-start.12
  35.6 1.4 %collective-permute-start.14 = (f32[128,128]{1,0:T(8,128)S(1)}, f32[128,128]{1,0:T(8,128)S(1)}, u32[]{:S(2)}, u32[]{:S(2)}) collective-permute-start(f32[128,128]{1,0:T(8,128)S(1)} %get-tuple-element.94), channel_id=1, source_target_pairs={{0,4},{1,5},{2,6},{3,7},{4,0},{5,1},{6,2},{7,3},{8,12},{9,13},{10,... | collective-permute-start | bytes 196616 | tf_op jit(solution)/shard_map/ppermute | solution.py:593
  37.0 0.0 collective-permute-done.11.refs_4_
  37.0 1.7 %collective-permute-start.16 = (f32[128,128]{1,0:T(8,128)S(1)}, f32[128,128]{1,0:T(8,128)S(1)}, u32[]{:S(2)}, u32[]{:S(2)}) collective-permute-start(f32[128,128]{1,0:T(8,128)S(1)} %get-tuple-element.96), channel_id=1, source_target_pairs={{0,6},{1,7},{2,4},{3,5},{4,2},{5,3},{6,0},{7,1},{8,14},{9,15},{10,... | collective-permute-start | bytes 196616 | tf_op jit(solution)/shard_map/ppermute | solution.py:593
  38.7 0.0 collective-permute-done.13.refs_6_
  38.7 0.0 collective-permute-done.15.refs_8_
  38.7 1.0 %collective-permute-done.12.refs_5_ = f32[128,128]{1,0:T(8,128)S(1)} collective-permute-done((f32[128,128]{1,0:T(8,128)S(1)}, f32[128,128]{1,0:T(8,128)S(1)}, u32[]{:S(2)}, u32[]{:S(2)}) %collective-permute-start.12) | collective-permute-done | bytes 65568 | tf_op jit(solution)/shard_map/ppermute | solution.py:593
  39.7 0.2 collective-permute-done.14.refs_7_
  39.9 2.3 %collective-permute-done.16.refs_9_ = f32[128,128]{1,0:T(8,128)S(1)} collective-permute-done((f32[128,128]{1,0:T(8,128)S(1)}, f32[128,128]{1,0:T(8,128)S(1)}, u32[]{:S(2)}, u32[]{:S(2)}) %collective-permute-start.16) | collective-permute-done | bytes 65568 | tf_op jit(solution)/shard_map/ppermute | solution.py:593
  42.1 0.3 part.1
  42.5 0.1 collective-permute-start.17
  42.6 2.8 %back_inner.1 = (bf16[128,1024]{1,0:T(8,128)(2,1)}, f32[4,128,128]{2,1,0:T(8,128)S(1)}, f32[8,128]{1,0:T(8,128)S(1)}, f32[8,1152]{1,0:T(8,128)S(1)}) custom-call(bf16[128,1024]{1,0:T(8,128)(2,1)S(1)} %get-tuple-element.56.refs_0_, bf16[128,1024]{1,0:T(8,128)(2,1)S(1)} %get-tuple-element.57.refs_1_, f32[3,4,1024]{2,1,0:T(4,128)S(1)} %get-tuple-element.58.refs_2_.refs_1_, ...), custom_call_target="tpu_custom_call" | custom-call | tf_op jit(solution)/shard_map/back_inner/pallas_call | solution.py:546
  45.3 0.0 collective-permute-done.17.refs_8_
  45.3 2.6 %back_outer.1 = (bf16[128,1024]{1,0:T(8,128)(2,1)}, f32[4,128,128]{2,1,0:T(8,128)S(1)}, f32[8,128]{1,0:T(8,128)S(1)}, f32[8,1152]{1,0:T(8,128)S(1)}, f32[8,128]{1,0:T(8,128)S(1)}) custom-call(bf16[128,1024]{1,0:T(8,128)(2,1)S(1)} %get-tuple-element.56.refs_0_, bf16[128,1024]{1,0:T(8,128)(2,1)S(1)} %get-tuple-element.57.refs_1_, ...), custom_call_target="tpu_custom_call", output_to_operand_aliasing={{0}: (15, {})} | custom-call | tf_op jit(solution)/shard_map/back_outer/pallas_call | solution.py:546
  47.9 3.0 %collective-permute-start.20 = (f32[8,1152]{1,0:T(8,128)S(1)}, f32[8,1152]{1,0:T(8,128)S(1)}, u32[]{:S(2)}, u32[]{:S(2)}) collective-permute-start(f32[8,1152]{1,0:T(8,128)S(1)} %get-tuple-element.107), channel_id=1, source_target_pairs={{0,15},{1,0},{2,1},{3,2},{4,3},{5,4},{6,5},{7,6},{8,7},{9,8},{10,9... | collective-permute-start | bytes 110600 | tf_op jit(solution)/shard_map/ppermute | solution.py:590
  51.0 0.2 collective-permute-start.18
  51.2 1.1 %collective-permute-start.19 = (f32[8,128]{1,0:T(8,128)S(1)}, f32[8,128]{1,0:T(8,128)S(1)}, u32[]{:S(2)}, u32[]{:S(2)}) collective-permute-start(f32[8,128]{1,0:T(8,128)S(1)} %get-tuple-element.106), channel_id=1, source_target_pairs={{0,31},{1,16},{2,17},{3,18},{4,19},{5,20},{6,21},{7,22},{8,23},{9,... | collective-permute-start | bytes 12296 | tf_op jit(solution)/shard_map/ppermute | solution.py:590
  52.2 2.3 %collective-permute-done.18 = f32[8,128]{1,0:T(8,128)S(1)} collective-permute-done((f32[8,128]{1,0:T(8,128)S(1)}, f32[8,128]{1,0:T(8,128)S(1)}, u32[]{:S(2)}, u32[]{:S(2)}) %collective-permute-start.18) | collective-permute-done | bytes 4128 | tf_op jit(solution)/shard_map/ppermute | solution.py:590
  54.6 0.0 collective-permute-done.19
  54.6 0.0 collective-permute-done.20.refs_5_
  54.6 1.0 %finish.1 = bf16[128,1024]{1,0:T(8,128)(2,1)} custom-call(bf16[128,1024]{1,0:T(8,128)(2,1)S(1)} %get-tuple-element.56.refs_0_, bf16[128,1024]{1,0:T(8,128)(2,1)S(1)} %get-tuple-element.57.refs_1_, f32[128,128]{1,0:T(8,128)S(1)} %get-tuple-element.67.refs_8_.refs_5_.refs_2_, f32[8,128]{1,0:T(8,128)S(1)} %add.22.refs_3_, f32[8,128]{1,0:T(8,128)S(1)} %slice_add_fusion.refs_4_, ...), custom_call_target="tpu_custom_call" | custom-call | tf_op jit(solution)/shard_map/finish/pallas_call | solution.py:546
  (4 shorter events, 0.0 us)
Async XLA Ops:
  1.9 9.7 %collective-permute-start.1 = (f32[8,1152]{1,0:T(8,128)S(1)}, f32[8,1152]{1,0:T(8,128)S(1)}, u32[]{:S(2)}, u32[]{:S(2)}) collective-permute-start(f32[8,1152]{1,0:T(8,128)S(1)} %get-tuple-element.66), channel_id=1, source_target_pairs={{0,1},{1,2},{2,3},{3,4},{4,5},{5,6},{6,7},{7,8},{8,9},{9,10},{10,1... | collective-permute-start | bytes 110600 | tf_op jit(solution)/shard_map/ppermute | solution.py:590
  2.4 4.2 %collective-permute-start = (f32[8,128]{1,0:T(8,128)S(1)}, f32[8,128]{1,0:T(8,128)S(1)}, u32[]{:S(2)}, u32[]{:S(2)}) collective-permute-start(f32[8,128]{1,0:T(8,128)S(1)} %get-tuple-element.61), channel_id=1, source_target_pairs={{0,16},{1,17},{2,18},{3,19},{4,20},{5,21},{6,22},{7,23},{8,24},{9,... | collective-permute-start | bytes 12296 | tf_op jit(solution)/shard_map/ppermute | solution.py:590
  5.0 6.6 %collective-permute-start.2 = (f32[8,128]{1,0:T(8,128)S(1)}, f32[8,128]{1,0:T(8,128)S(1)}, u32[]{:S(2)}, u32[]{:S(2)}) collective-permute-start(f32[8,128]{1,0:T(8,128)S(1)} %get-tuple-element.68), channel_id=1, source_target_pairs={{0,17},{1,18},{2,19},{3,20},{4,21},{5,22},{6,23},{7,24},{8,25},{9,... | collective-permute-start | bytes 12296 | tf_op jit(solution)/shard_map/ppermute | solution.py:590
  14.5 3.0 %collective-permute-start.3 = (f32[4,384,128]{2,1,0:T(8,128)S(1)}, f32[4,384,128]{2,1,0:T(8,128)S(1)}, u32[]{:S(2)}, u32[]{:S(2)}) collective-permute-start(f32[4,384,128]{2,1,0:T(8,128)S(1)} %get-tuple-element.70), channel_id=1, source_target_pairs={{0,1},{1,0},{2,3},{3,2},{4,5},{5,4},{6,7},{7,6},{8,9},{9,8},{10,11... | collective-permute-start | bytes 2359304 | tf_op jit(solution)/shard_map/ppermute | solution.py:593
  18.0 6.2 %collective-permute-start.4 = (f32[256,128]{1,0:T(8,128)S(1)}, f32[256,128]{1,0:T(8,128)S(1)}, u32[]{:S(2)}, u32[]{:S(2)}) collective-permute-start(f32[256,128]{1,0:T(8,128)S(1)} %get-tuple-element.72), channel_id=1, source_target_pairs={{0,2},{1,3},{2,0},{3,1},{4,6},{5,7},{6,4},{7,5},{8,10},{9,11},{10,... | collective-permute-start | bytes 393224 | tf_op jit(solution)/shard_map/ppermute | solution.py:593
  18.1 8.8 %collective-permute-start.5 = (f32[256,128]{1,0:T(8,128)S(1)}, f32[256,128]{1,0:T(8,128)S(1)}, u32[]{:S(2)}, u32[]{:S(2)}) collective-permute-start(f32[256,128]{1,0:T(8,128)S(1)} %get-tuple-element.73), channel_id=1, source_target_pairs={{0,4},{1,5},{2,6},{3,7},{4,0},{5,1},{6,2},{7,3},{8,12},{9,13},{10,... | collective-permute-start | bytes 393224 | tf_op jit(solution)/shard_map/ppermute | solution.py:593
  18.8 9.9 %collective-permute-start.6 = (f32[256,128]{1,0:T(8,128)S(1)}, f32[256,128]{1,0:T(8,128)S(1)}, u32[]{:S(2)}, u32[]{:S(2)}) collective-permute-start(f32[256,128]{1,0:T(8,128)S(1)} %get-tuple-element.74), channel_id=1, source_target_pairs={{0,6},{1,7},{2,4},{3,5},{4,2},{5,3},{6,0},{7,1},{8,14},{9,15},{10,... | collective-permute-start | bytes 393224 | tf_op jit(solution)/shard_map/ppermute | solution.py:593
  23.3 7.7 %collective-permute-start.8 = (f32[128,128]{1,0:T(8,128)S(1)}, f32[128,128]{1,0:T(8,128)S(1)}, u32[]{:S(2)}, u32[]{:S(2)}) collective-permute-start(f32[128,128]{1,0:T(8,128)S(1)} %get-tuple-element.86), channel_id=1, source_target_pairs={{0,2},{1,3},{2,0},{3,1},{4,6},{5,7},{6,4},{7,5},{8,10},{9,11},{10,... | collective-permute-start | bytes 196616 | tf_op jit(solution)/shard_map/ppermute | solution.py:593
  23.5 9.2 %collective-permute-start.9 = (f32[128,128]{1,0:T(8,128)S(1)}, f32[128,128]{1,0:T(8,128)S(1)}, u32[]{:S(2)}, u32[]{:S(2)}) collective-permute-start(f32[128,128]{1,0:T(8,128)S(1)} %get-tuple-element.87), channel_id=1, source_target_pairs={{0,4},{1,5},{2,6},{3,7},{4,0},{5,1},{6,2},{7,3},{8,12},{9,13},{10,... | collective-permute-start | bytes 196616 | tf_op jit(solution)/shard_map/ppermute | solution.py:593
  24.2 9.8 %collective-permute-start.10 = (f32[128,128]{1,0:T(8,128)S(1)}, f32[128,128]{1,0:T(8,128)S(1)}, u32[]{:S(2)}, u32[]{:S(2)}) collective-permute-start(f32[128,128]{1,0:T(8,128)S(1)} %get-tuple-element.88), channel_id=1, source_target_pairs={{0,6},{1,7},{2,4},{3,5},{4,2},{5,3},{6,0},{7,1},{8,14},{9,15},{10,... | collective-permute-start | bytes 196616 | tf_op jit(solution)/shard_map/ppermute | solution.py:593
  29.2 5.6 %collective-permute-start.7 = (f32[128,128]{1,0:T(8,128)S(1)}, f32[128,128]{1,0:T(8,128)S(1)}, u32[]{:S(2)}, u32[]{:S(2)}) collective-permute-start(f32[128,128]{1,0:T(8,128)S(1)} %get-tuple-element.84), channel_id=1, source_target_pairs={{0,8},{1,9},{2,10},{3,11},{4,12},{5,13},{6,14},{7,15},{8,0},{9,1},... | collective-permute-start | bytes 196616 | tf_op jit(solution)/shard_map/ppermute | solution.py:593
  30.4 6.5 %collective-permute-start.11 = (f32[128,128]{1,0:T(8,128)S(1)}, f32[128,128]{1,0:T(8,128)S(1)}, u32[]{:S(2)}, u32[]{:S(2)}) collective-permute-start(f32[128,128]{1,0:T(8,128)S(1)} %get-tuple-element.91), channel_id=1, source_target_pairs={{0,2},{1,3},{2,0},{3,1},{4,6},{5,7},{6,4},{7,5},{8,10},{9,11},{10,... | collective-permute-start | bytes 196616 | tf_op jit(solution)/shard_map/ppermute | solution.py:593
  31.0 7.6 %collective-permute-start.13 = (f32[128,128]{1,0:T(8,128)S(1)}, f32[128,128]{1,0:T(8,128)S(1)}, u32[]{:S(2)}, u32[]{:S(2)}) collective-permute-start(f32[128,128]{1,0:T(8,128)S(1)} %get-tuple-element.93), channel_id=1, source_target_pairs={{0,4},{1,5},{2,6},{3,7},{4,0},{5,1},{6,2},{7,3},{8,12},{9,13},{10,... | collective-permute-start | bytes 196616 | tf_op jit(solution)/shard_map/ppermute | solution.py:593
  32.7 6.0 %collective-permute-start.15 = (f32[128,128]{1,0:T(8,128)S(1)}, f32[128,128]{1,0:T(8,128)S(1)}, u32[]{:S(2)}, u32[]{:S(2)}) collective-permute-start(f32[128,128]{1,0:T(8,128)S(1)} %get-tuple-element.95), channel_id=1, source_target_pairs={{0,6},{1,7},{2,4},{3,5},{4,2},{5,3},{6,0},{7,1},{8,14},{9,15},{10,... | collective-permute-start | bytes 196616 | tf_op jit(solution)/shard_map/ppermute | solution.py:593
  35.1 4.6 %collective-permute-start.12 = (f32[128,128]{1,0:T(8,128)S(1)}, f32[128,128]{1,0:T(8,128)S(1)}, u32[]{:S(2)}, u32[]{:S(2)}) collective-permute-start(f32[128,128]{1,0:T(8,128)S(1)} %get-tuple-element.92), channel_id=1, source_target_pairs={{0,2},{1,3},{2,0},{3,1},{4,6},{5,7},{6,4},{7,5},{8,10},{9,11},{10,... | collective-permute-start | bytes 196616 | tf_op jit(solution)/shard_map/ppermute | solution.py:593
  35.6 4.3 %collective-permute-start.14 = (f32[128,128]{1,0:T(8,128)S(1)}, f32[128,128]{1,0:T(8,128)S(1)}, u32[]{:S(2)}, u32[]{:S(2)}) collective-permute-start(f32[128,128]{1,0:T(8,128)S(1)} %get-tuple-element.94), channel_id=1, source_target_pairs={{0,4},{1,5},{2,6},{3,7},{4,0},{5,1},{6,2},{7,3},{8,12},{9,13},{10,... | collective-permute-start | bytes 196616 | tf_op jit(solution)/shard_map/ppermute | solution.py:593
  37.0 5.2 %collective-permute-start.16 = (f32[128,128]{1,0:T(8,128)S(1)}, f32[128,128]{1,0:T(8,128)S(1)}, u32[]{:S(2)}, u32[]{:S(2)}) collective-permute-start(f32[128,128]{1,0:T(8,128)S(1)} %get-tuple-element.96), channel_id=1, source_target_pairs={{0,6},{1,7},{2,4},{3,5},{4,2},{5,3},{6,0},{7,1},{8,14},{9,15},{10,... | collective-permute-start | bytes 196616 | tf_op jit(solution)/shard_map/ppermute | solution.py:593
  42.5 2.8 %collective-permute-start.17 = (f32[4,256,128]{2,1,0:T(8,128)S(1)}, f32[4,256,128]{2,1,0:T(8,128)S(1)}, u32[]{:S(2)}, u32[]{:S(2)}) collective-permute-start(f32[4,256,128]{2,1,0:T(8,128)S(1)} %get-tuple-element.97), channel_id=1, source_target_pairs={{0,1},{1,0},{2,3},{3,2},{4,5},{5,4},{6,7},{7,6},{8,9},{9,8},{10,11... | collective-permute-start | bytes 1572872 | tf_op jit(solution)/shard_map/ppermute | solution.py:593
  47.9 6.6 %collective-permute-start.20 = (f32[8,1152]{1,0:T(8,128)S(1)}, f32[8,1152]{1,0:T(8,128)S(1)}, u32[]{:S(2)}, u32[]{:S(2)}) collective-permute-start(f32[8,1152]{1,0:T(8,128)S(1)} %get-tuple-element.107), channel_id=1, source_target_pairs={{0,15},{1,0},{2,1},{3,2},{4,3},{5,4},{6,5},{7,6},{8,7},{9,8},{10,9... | collective-permute-start | bytes 110600 | tf_op jit(solution)/shard_map/ppermute | solution.py:590
  51.0 3.6 %collective-permute-start.18 = (f32[8,128]{1,0:T(8,128)S(1)}, f32[8,128]{1,0:T(8,128)S(1)}, u32[]{:S(2)}, u32[]{:S(2)}) collective-permute-start(f32[8,128]{1,0:T(8,128)S(1)} %get-tuple-element.105), channel_id=1, source_target_pairs={{0,16},{1,17},{2,18},{3,19},{4,20},{5,21},{6,22},{7,23},{8,24},{9,... | collective-permute-start | bytes 12296 | tf_op jit(solution)/shard_map/ppermute | solution.py:590
  51.2 3.4 %collective-permute-start.19 = (f32[8,128]{1,0:T(8,128)S(1)}, f32[8,128]{1,0:T(8,128)S(1)}, u32[]{:S(2)}, u32[]{:S(2)}) collective-permute-start(f32[8,128]{1,0:T(8,128)S(1)} %get-tuple-element.106), channel_id=1, source_target_pairs={{0,31},{1,16},{2,17},{3,18},{4,19},{5,20},{6,21},{7,22},{8,23},{9,... | collective-permute-start | bytes 12296 | tf_op jit(solution)/shard_map/ppermute | solution.py:590

commit v8 on v7

--- a/solution.py
+++ b/solution.py
@@ -221,15 +221,17 @@
         system = jnp.where(strict, rate * products[:length], 0.0)
         scores = split(jnp.where(full, products[length:], 0.0))
         go = exact(go_ref[:, at])
-        fresh_grad = split(mm(scores, go, "tn"))
         wide_ref[j, 0], wide_ref[j, 1] = q, k
-        for n, parts in enumerate((skf, sqf, skb, scores, fresh_grad)):
+        for n, parts in enumerate((skf, sqf, skb, scores)):
             keep_split(narrow_ref, j, 2 * n, parts)
         data.append(
             dict(system=system, go=go, rhs=cols_of(split(rate * kf * em), split(rate * act[2])), ke=split(kb * ecm),
-                 qg=qf * em, fresh_grad=fresh_grad, ef=ef)
+                 qg=qf * em, scores=scores, ef=ef)
         )
     inverses = inverse_all([d["system"] for d in data])
+    for j, d in enumerate(data):
+        d["fresh_grad"] = split(mm(d["scores"], d["go"], "tn"))
+        keep_split(narrow_ref, j, 8, d["fresh_grad"])
     for j, (d, inverse) in enumerate(zip(data, inverses)):
         inverse = split(inverse)
         keep_split(narrow_ref, j, 14, inverse)

time: 55.9 us -> 55.1 us (0.986)
  Pallas kernels: 18 us -> 17.4 us
    pallas_call x15, Pallas kernels: 18 us -> 17.4 us  [call(): pl.pallas_call((lambda *refs: kernel(placed(*scalar), *refs)) if scalar e...]
  transfers between devices with their start and end apart: 21 -> 21, of which waited for: 8 -> 8; matrix products, arithmetic and copies ran while one was open for 0% -> 0% of each run, Pallas kernels for 17% -> 16%
where the time goes in v8:
time: 55.1 us; the launch traced here: 55 us
  starting transfers between devices  24 us (44%)
  Pallas kernels  17.4 us (32%)
  waiting for transfers between devices  12.8 us (23%)
  between operations  0.8 us (1%)
    pallas_call x15, Pallas kernels, call(): pl.pallas_call((lambda *refs: kernel(placed(*scalar), *refs)) if scalar e...  17.4 us
    ppermute x15, starting transfers between devices, swapped(): return lax.ppermute(value, 'ctx', [(i, i ^ distance) for i in range(spots)])  15.2 us
    ppermute x6, starting transfers between devices, turned(): return lax.ppermute(value, ('section', 'ctx'), route)  8.78 us
    ppermute x6, waiting for transfers between devices, turned(): return lax.ppermute(value, ('section', 'ctx'), route)  7.13 us
    ppermute x15, waiting for transfers between devices, swapped(): return lax.ppermute(value, 'ctx', [(i, i ^ distance) for i in range(spots)])  5.67 us
  transfers between devices with their start and end apart: 21, of which 8 were waited for; matrix products, arithmetic and copies ran while one was open for 0% of the time, Pallas kernels for 16%

profile of v8, /device:TPU:0, one launch (start us, length us, event | category | flops | bytes accessed | tf_op | source)
XLA Modules:
  0.0 55.0 jit_solution(18395616401752817572)
XLA Ops:
  0.6 1.3 %prelude.1 = (f32[8,1152]{1,0:T(8,128)S(1)}, f32[8,128]{1,0:T(8,128)S(1)}, f32[8,128]{1,0:T(8,128)S(1)}, bf16[128,1024]{1,0:T(8,128)(2,1)S(1)}, bf16[128,1024]{1...) custom-call(bf16[128,1024]{1,0:T(8,128)(2,1)} %x_hbm.1, ...), custom_call_target="tpu_custom_call" | custom-call | tf_op jit(solution)/shard_map/prelude/pallas_call | solution.py:548
  1.9 0.5 collective-permute-start.1
  2.4 2.6 %collective-permute-start = (f32[8,128]{1,0:T(8,128)S(1)}, f32[8,128]{1,0:T(8,128)S(1)}, u32[]{:S(2)}, u32[]{:S(2)}) collective-permute-start(f32[8,128]{1,0:T(8,128)S(1)} %get-tuple-element.61), channel_id=1, source_target_pairs={{0,16},{1,17},{2,18},{3,19},{4,20},{5,21},{6,22},{7,23},{8,24},{9,... | collective-permute-start | bytes 12296 | tf_op jit(solution)/shard_map/ppermute | solution.py:592
  5.0 1.4 %collective-permute-start.2 = (f32[8,128]{1,0:T(8,128)S(1)}, f32[8,128]{1,0:T(8,128)S(1)}, u32[]{:S(2)}, u32[]{:S(2)}) collective-permute-start(f32[8,128]{1,0:T(8,128)S(1)} %get-tuple-element.68), channel_id=1, source_target_pairs={{0,17},{1,18},{2,19},{3,20},{4,21},{5,22},{6,23},{7,24},{8,25},{9,... | collective-permute-start | bytes 12296 | tf_op jit(solution)/shard_map/ppermute | solution.py:592
  6.4 0.2 collective-permute-done
  6.6 0.4 gates.1
  7.0 4.6 %collective-permute-done.2 = f32[8,128]{1,0:T(8,128)S(1)} collective-permute-done((f32[8,128]{1,0:T(8,128)S(1)}, f32[8,128]{1,0:T(8,128)S(1)}, u32[]{:S(2)}, u32[]{:S(2)}) %collective-permute-start.2) | collective-permute-done | bytes 4128 | tf_op jit(solution)/shard_map/ppermute | solution.py:592
  11.6 0.0 collective-permute-done.1.refs_7_.refs_4_
  11.6 2.7 %local_outer.1 = (f32[4,384,128]{2,1,0:T(8,128)S(1)}, f32[4,3,128,128]{3,2,1,0:T(8,128)S(1)}, bf16[4,16,128,128]{3,2,1,0:T(8,128)(2,1)S(1)}) custom-call(bf16[128,1024]{1,0:T(8,128)(2,1)S(1)} %get-tuple-element.56.refs_0_, bf16[128,1024]{1,0:T(8,128)(2,1)S(1)} %get-tuple-element.57.refs_1_, f32[3,4,1024]{2,1,0:T(4,128)S(1)} %get-tuple-element.58.refs_2_.refs_1_, ...), custom_call_target="tpu_custom_call" | custom-call | tf_op jit(solution)/shard_map/local_outer/pallas_call | solution.py:548
  14.3 0.1 collective-permute-start.3
  14.4 2.7 %local_inner.1 = (f32[4,384,128]{2,1,0:T(8,128)S(1)}, f32[4,3,128,128]{3,2,1,0:T(8,128)S(1)}, bf16[4,16,128,128]{3,2,1,0:T(8,128)(2,1)S(1)}) custom-call(bf16[128,1024]{1,0:T(8,128)(2,1)S(1)} %get-tuple-element.56.refs_0_, bf16[128,1024]{1,0:T(8,128)(2,1)S(1)} %get-tuple-element.57.refs_1_, f32[3,4,1024]{2,1,0:T(4,128)S(1)} %get-tuple-element.58.refs_2_.refs_1_, ...), custom_call_target="tpu_custom_call" | custom-call | tf_op jit(solution)/shard_map/local_inner/pallas_call | solution.py:548
  17.1 0.0 collective-permute-done.3.refs_1_
  17.1 0.4 join.1
  17.6 0.1 collective-permute-start.4
  17.6 0.7 %collective-permute-start.5 = (f32[256,128]{1,0:T(8,128)S(1)}, f32[256,128]{1,0:T(8,128)S(1)}, u32[]{:S(2)}, u32[]{:S(2)}) collective-permute-start(f32[256,128]{1,0:T(8,128)S(1)} %get-tuple-element.73), channel_id=1, source_target_pairs={{0,4},{1,5},{2,6},{3,7},{4,0},{5,1},{6,2},{7,3},{8,12},{9,13},{10,... | collective-permute-start | bytes 393224 | tf_op jit(solution)/shard_map/ppermute | solution.py:595
  18.4 2.8 %collective-permute-start.6 = (f32[256,128]{1,0:T(8,128)S(1)}, f32[256,128]{1,0:T(8,128)S(1)}, u32[]{:S(2)}, u32[]{:S(2)}) collective-permute-start(f32[256,128]{1,0:T(8,128)S(1)} %get-tuple-element.74), channel_id=1, source_target_pairs={{0,6},{1,7},{2,4},{3,5},{4,2},{5,3},{6,0},{7,1},{8,14},{9,15},{10,... | collective-permute-start | bytes 393224 | tf_op jit(solution)/shard_map/ppermute | solution.py:595
  21.1 0.9 %ready_outer.1 = (f32[4,5,128,128]{3,2,1,0:T(8,128)S(1)}, bf16[4,4,128,128]{3,2,1,0:T(8,128)(2,1)S(1)}) custom-call(bf16[128,1024]{1,0:T(8,128)(2,1)S(1)} %get-tuple-element.56.refs_0_, f32[3,4,1024]{2,1,0:T(4,128)S(1)} %get-tuple-element.58.refs_2_.refs_1_, f32[128,1024]{1,0:T(8,128)S(1)} %get-tuple-element.63.refs_4_.refs_2_, ...), custom_call_target="tpu_custom_call" | custom-call | tf_op jit(solution)/shard_map/ready_outer/pallas_call | solution.py:548
  22.0 0.9 %ready_inner.1 = (f32[4,5,128,128]{3,2,1,0:T(8,128)S(1)}, bf16[4,4,128,128]{3,2,1,0:T(8,128)(2,1)S(1)}) custom-call(bf16[128,1024]{1,0:T(8,128)(2,1)S(1)} %get-tuple-element.56.refs_0_, f32[3,4,1024]{2,1,0:T(4,128)S(1)} %get-tuple-element.58.refs_2_.refs_1_, f32[128,1024]{1,0:T(8,128)S(1)} %get-tuple-element.63.refs_4_.refs_2_, ...), custom_call_target="tpu_custom_call" | custom-call | tf_op jit(solution)/shard_map/ready_inner/pallas_call | solution.py:548
  22.9 0.1 collective-permute-start.8
  23.1 0.7 %collective-permute-start.9 = (f32[128,128]{1,0:T(8,128)S(1)}, f32[128,128]{1,0:T(8,128)S(1)}, u32[]{:S(2)}, u32[]{:S(2)}) collective-permute-start(f32[128,128]{1,0:T(8,128)S(1)} %get-tuple-element.87), channel_id=1, source_target_pairs={{0,4},{1,5},{2,6},{3,7},{4,0},{5,1},{6,2},{7,3},{8,12},{9,13},{10,... | collective-permute-start | bytes 196616 | tf_op jit(solution)/shard_map/ppermute | solution.py:595
  23.7 0.0 collective-permute-done.4.refs_1_
  23.7 2.7 %collective-permute-start.10 = (f32[128,128]{1,0:T(8,128)S(1)}, f32[128,128]{1,0:T(8,128)S(1)}, u32[]{:S(2)}, u32[]{:S(2)}) collective-permute-start(f32[128,128]{1,0:T(8,128)S(1)} %get-tuple-element.88), channel_id=1, source_target_pairs={{0,6},{1,7},{2,4},{3,5},{4,2},{5,3},{6,0},{7,1},{8,14},{9,15},{10,... | collective-permute-start | bytes 196616 | tf_op jit(solution)/shard_map/ppermute | solution.py:595
  26.5 0.0 collective-permute-done.5.refs_2_
  26.5 1.8 %collective-permute-done.6.refs_3_ = f32[256,128]{1,0:T(8,128)S(1)} collective-permute-done((f32[256,128]{1,0:T(8,128)S(1)}, f32[256,128]{1,0:T(8,128)S(1)}, u32[]{:S(2)}, u32[]{:S(2)}) %collective-permute-start.6) | collective-permute-done | bytes 131104 | tf_op jit(solution)/shard_map/ppermute | solution.py:595
  28.3 0.5 gather.1
  28.8 0.9 %collective-permute-start.7 = (f32[128,128]{1,0:T(8,128)S(1)}, f32[128,128]{1,0:T(8,128)S(1)}, u32[]{:S(2)}, u32[]{:S(2)}) collective-permute-start(f32[128,128]{1,0:T(8,128)S(1)} %get-tuple-element.84), channel_id=1, source_target_pairs={{0,8},{1,9},{2,10},{3,11},{4,12},{5,13},{6,14},{7,15},{8,0},{9,1},... | collective-permute-start | bytes 196616 | tf_op jit(solution)/shard_map/ppermute | solution.py:595
  29.7 0.3 reach.1
  30.0 0.6 %collective-permute-start.11 = (f32[128,128]{1,0:T(8,128)S(1)}, f32[128,128]{1,0:T(8,128)S(1)}, u32[]{:S(2)}, u32[]{:S(2)}) collective-permute-start(f32[128,128]{1,0:T(8,128)S(1)} %get-tuple-element.91), channel_id=1, source_target_pairs={{0,2},{1,3},{2,0},{3,1},{4,6},{5,7},{6,4},{7,5},{8,10},{9,11},{10,... | collective-permute-start | bytes 196616 | tf_op jit(solution)/shard_map/ppermute | solution.py:595
  30.6 0.0 collective-permute-done.8.refs_5_
  30.6 1.7 %collective-permute-start.13 = (f32[128,128]{1,0:T(8,128)S(1)}, f32[128,128]{1,0:T(8,128)S(1)}, u32[]{:S(2)}, u32[]{:S(2)}) collective-permute-start(f32[128,128]{1,0:T(8,128)S(1)} %get-tuple-element.93), channel_id=1, source_target_pairs={{0,4},{1,5},{2,6},{3,7},{4,0},{5,1},{6,2},{7,3},{8,12},{9,13},{10,... | collective-permute-start | bytes 196616 | tf_op jit(solution)/shard_map/ppermute | solution.py:595
  32.3 0.0 collective-permute-done.9.refs_6_
  32.3 1.3 %collective-permute-start.15 = (f32[128,128]{1,0:T(8,128)S(1)}, f32[128,128]{1,0:T(8,128)S(1)}, u32[]{:S(2)}, u32[]{:S(2)}) collective-permute-start(f32[128,128]{1,0:T(8,128)S(1)} %get-tuple-element.95), channel_id=1, source_target_pairs={{0,6},{1,7},{2,4},{3,5},{4,2},{5,3},{6,0},{7,1},{8,14},{9,15},{10,... | collective-permute-start | bytes 196616 | tf_op jit(solution)/shard_map/ppermute | solution.py:595
  33.6 0.0 collective-permute-done.10.refs_7_
  33.6 0.4 known.1.refs_1_
  34.0 0.4 collective-permute-done.7.refs_0_
  34.4 0.2 late.1
  34.7 0.5 collective-permute-start.12
  35.2 1.4 %collective-permute-start.14 = (f32[128,128]{1,0:T(8,128)S(1)}, f32[128,128]{1,0:T(8,128)S(1)}, u32[]{:S(2)}, u32[]{:S(2)}) collective-permute-start(f32[128,128]{1,0:T(8,128)S(1)} %get-tuple-element.94), channel_id=1, source_target_pairs={{0,4},{1,5},{2,6},{3,7},{4,0},{5,1},{6,2},{7,3},{8,12},{9,13},{10,... | collective-permute-start | bytes 196616 | tf_op jit(solution)/shard_map/ppermute | solution.py:595
  36.5 0.0 collective-permute-done.11.refs_4_
  36.5 1.7 %collective-permute-start.16 = (f32[128,128]{1,0:T(8,128)S(1)}, f32[128,128]{1,0:T(8,128)S(1)}, u32[]{:S(2)}, u32[]{:S(2)}) collective-permute-start(f32[128,128]{1,0:T(8,128)S(1)} %get-tuple-element.96), channel_id=1, source_target_pairs={{0,6},{1,7},{2,4},{3,5},{4,2},{5,3},{6,0},{7,1},{8,14},{9,15},{10,... | collective-permute-start | bytes 196616 | tf_op jit(solution)/shard_map/ppermute | solution.py:595
  38.2 0.0 collective-permute-done.13.refs_6_
  38.2 0.0 collective-permute-done.15.refs_8_
  38.2 1.0 %collective-permute-done.12.refs_5_ = f32[128,128]{1,0:T(8,128)S(1)} collective-permute-done((f32[128,128]{1,0:T(8,128)S(1)}, f32[128,128]{1,0:T(8,128)S(1)}, u32[]{:S(2)}, u32[]{:S(2)}) %collective-permute-start.12) | collective-permute-done | bytes 65568 | tf_op jit(solution)/shard_map/ppermute | solution.py:595
  39.2 0.2 collective-permute-done.14.refs_7_
  39.4 2.3 %collective-permute-done.16.refs_9_ = f32[128,128]{1,0:T(8,128)S(1)} collective-permute-done((f32[128,128]{1,0:T(8,128)S(1)}, f32[128,128]{1,0:T(8,128)S(1)}, u32[]{:S(2)}, u32[]{:S(2)}) %collective-permute-start.16) | collective-permute-done | bytes 65568 | tf_op jit(solution)/shard_map/ppermute | solution.py:595
  41.7 0.3 part.1
  42.1 0.1 collective-permute-start.17
  42.1 2.6 %back_inner.1 = (bf16[128,1024]{1,0:T(8,128)(2,1)}, f32[4,128,128]{2,1,0:T(8,128)S(1)}, f32[8,128]{1,0:T(8,128)S(1)}, f32[8,1152]{1,0:T(8,128)S(1)}) custom-call(bf16[128,1024]{1,0:T(8,128)(2,1)S(1)} %get-tuple-element.56.refs_0_, bf16[128,1024]{1,0:T(8,128)(2,1)S(1)} %get-tuple-element.57.refs_1_, f32[3,4,1024]{2,1,0:T(4,128)S(1)} %get-tuple-element.58.refs_2_.refs_1_, ...), custom_call_target="tpu_custom_call" | custom-call | tf_op jit(solution)/shard_map/back_inner/pallas_call | solution.py:548
  44.7 0.0 collective-permute-done.17.refs_8_
  44.7 2.6 %back_outer.1 = (bf16[128,1024]{1,0:T(8,128)(2,1)}, f32[4,128,128]{2,1,0:T(8,128)S(1)}, f32[8,128]{1,0:T(8,128)S(1)}, f32[8,1152]{1,0:T(8,128)S(1)}, f32[8,128]{1,0:T(8,128)S(1)}) custom-call(bf16[128,1024]{1,0:T(8,128)(2,1)S(1)} %get-tuple-element.56.refs_0_, bf16[128,1024]{1,0:T(8,128)(2,1)S(1)} %get-tuple-element.57.refs_1_, ...), custom_call_target="tpu_custom_call", output_to_operand_aliasing={{0}: (15, {})} | custom-call | tf_op jit(solution)/shard_map/back_outer/pallas_call | solution.py:548
  47.3 3.0 %collective-permute-start.20 = (f32[8,1152]{1,0:T(8,128)S(1)}, f32[8,1152]{1,0:T(8,128)S(1)}, u32[]{:S(2)}, u32[]{:S(2)}) collective-permute-start(f32[8,1152]{1,0:T(8,128)S(1)} %get-tuple-element.107), channel_id=1, source_target_pairs={{0,15},{1,0},{2,1},{3,2},{4,3},{5,4},{6,5},{7,6},{8,7},{9,8},{10,9... | collective-permute-start | bytes 110600 | tf_op jit(solution)/shard_map/ppermute | solution.py:592
  50.4 0.2 collective-permute-start.18
  50.6 1.1 %collective-permute-start.19 = (f32[8,128]{1,0:T(8,128)S(1)}, f32[8,128]{1,0:T(8,128)S(1)}, u32[]{:S(2)}, u32[]{:S(2)}) collective-permute-start(f32[8,128]{1,0:T(8,128)S(1)} %get-tuple-element.106), channel_id=1, source_target_pairs={{0,31},{1,16},{2,17},{3,18},{4,19},{5,20},{6,21},{7,22},{8,23},{9,... | collective-permute-start | bytes 12296 | tf_op jit(solution)/shard_map/ppermute | solution.py:592
  51.6 2.3 %collective-permute-done.18 = f32[8,128]{1,0:T(8,128)S(1)} collective-permute-done((f32[8,128]{1,0:T(8,128)S(1)}, f32[8,128]{1,0:T(8,128)S(1)}, u32[]{:S(2)}, u32[]{:S(2)}) %collective-permute-start.18) | collective-permute-done | bytes 4128 | tf_op jit(solution)/shard_map/ppermute | solution.py:592
  54.0 0.0 collective-permute-done.19
  54.0 0.0 collective-permute-done.20.refs_5_
  54.0 1.0 %finish.1 = bf16[128,1024]{1,0:T(8,128)(2,1)} custom-call(bf16[128,1024]{1,0:T(8,128)(2,1)S(1)} %get-tuple-element.56.refs_0_, bf16[128,1024]{1,0:T(8,128)(2,1)S(1)} %get-tuple-element.57.refs_1_, f32[128,128]{1,0:T(8,128)S(1)} %get-tuple-element.67.refs_8_.refs_5_.refs_2_, f32[8,128]{1,0:T(8,128)S(1)} %add.22.refs_3_, f32[8,128]{1,0:T(8,128)S(1)} %slice_add_fusion.refs_4_, ...), custom_call_target="tpu_custom_call" | custom-call | tf_op jit(solution)/shard_map/finish/pallas_call | solution.py:548
  (4 shorter events, 0.0 us)
Async XLA Ops:
  1.9 9.7 %collective-permute-start.1 = (f32[8,1152]{1,0:T(8,128)S(1)}, f32[8,1152]{1,0:T(8,128)S(1)}, u32[]{:S(2)}, u32[]{:S(2)}) collective-permute-start(f32[8,1152]{1,0:T(8,128)S(1)} %get-tuple-element.66), channel_id=1, source_target_pairs={{0,1},{1,2},{2,3},{3,4},{4,5},{5,6},{6,7},{7,8},{8,9},{9,10},{10,1... | collective-permute-start | bytes 110600 | tf_op jit(solution)/shard_map/ppermute | solution.py:592
  2.4 4.2 %collective-permute-start = (f32[8,128]{1,0:T(8,128)S(1)}, f32[8,128]{1,0:T(8,128)S(1)}, u32[]{:S(2)}, u32[]{:S(2)}) collective-permute-start(f32[8,128]{1,0:T(8,128)S(1)} %get-tuple-element.61), channel_id=1, source_target_pairs={{0,16},{1,17},{2,18},{3,19},{4,20},{5,21},{6,22},{7,23},{8,24},{9,... | collective-permute-start | bytes 12296 | tf_op jit(solution)/shard_map/ppermute | solution.py:592
  5.0 6.6 %collective-permute-start.2 = (f32[8,128]{1,0:T(8,128)S(1)}, f32[8,128]{1,0:T(8,128)S(1)}, u32[]{:S(2)}, u32[]{:S(2)}) collective-permute-start(f32[8,128]{1,0:T(8,128)S(1)} %get-tuple-element.68), channel_id=1, source_target_pairs={{0,17},{1,18},{2,19},{3,20},{4,21},{5,22},{6,23},{7,24},{8,25},{9,... | collective-permute-start | bytes 12296 | tf_op jit(solution)/shard_map/ppermute | solution.py:592
  14.3 2.8 %collective-permute-start.3 = (f32[4,384,128]{2,1,0:T(8,128)S(1)}, f32[4,384,128]{2,1,0:T(8,128)S(1)}, u32[]{:S(2)}, u32[]{:S(2)}) collective-permute-start(f32[4,384,128]{2,1,0:T(8,128)S(1)} %get-tuple-element.70), channel_id=1, source_target_pairs={{0,1},{1,0},{2,3},{3,2},{4,5},{5,4},{6,7},{7,6},{8,9},{9,8},{10,11... | collective-permute-start | bytes 2359304 | tf_op jit(solution)/shard_map/ppermute | solution.py:595
  17.6 6.2 %collective-permute-start.4 = (f32[256,128]{1,0:T(8,128)S(1)}, f32[256,128]{1,0:T(8,128)S(1)}, u32[]{:S(2)}, u32[]{:S(2)}) collective-permute-start(f32[256,128]{1,0:T(8,128)S(1)} %get-tuple-element.72), channel_id=1, source_target_pairs={{0,2},{1,3},{2,0},{3,1},{4,6},{5,7},{6,4},{7,5},{8,10},{9,11},{10,... | collective-permute-start | bytes 393224 | tf_op jit(solution)/shard_map/ppermute | solution.py:595
  17.6 8.8 %collective-permute-start.5 = (f32[256,128]{1,0:T(8,128)S(1)}, f32[256,128]{1,0:T(8,128)S(1)}, u32[]{:S(2)}, u32[]{:S(2)}) collective-permute-start(f32[256,128]{1,0:T(8,128)S(1)} %get-tuple-element.73), channel_id=1, source_target_pairs={{0,4},{1,5},{2,6},{3,7},{4,0},{5,1},{6,2},{7,3},{8,12},{9,13},{10,... | collective-permute-start | bytes 393224 | tf_op jit(solution)/shard_map/ppermute | solution.py:595
  18.4 9.9 %collective-permute-start.6 = (f32[256,128]{1,0:T(8,128)S(1)}, f32[256,128]{1,0:T(8,128)S(1)}, u32[]{:S(2)}, u32[]{:S(2)}) collective-permute-start(f32[256,128]{1,0:T(8,128)S(1)} %get-tuple-element.74), channel_id=1, source_target_pairs={{0,6},{1,7},{2,4},{3,5},{4,2},{5,3},{6,0},{7,1},{8,14},{9,15},{10,... | collective-permute-start | bytes 393224 | tf_op jit(solution)/shard_map/ppermute | solution.py:595
  22.9 7.7 %collective-permute-start.8 = (f32[128,128]{1,0:T(8,128)S(1)}, f32[128,128]{1,0:T(8,128)S(1)}, u32[]{:S(2)}, u32[]{:S(2)}) collective-permute-start(f32[128,128]{1,0:T(8,128)S(1)} %get-tuple-element.86), channel_id=1, source_target_pairs={{0,2},{1,3},{2,0},{3,1},{4,6},{5,7},{6,4},{7,5},{8,10},{9,11},{10,... | collective-permute-start | bytes 196616 | tf_op jit(solution)/shard_map/ppermute | solution.py:595
  23.1 9.2 %collective-permute-start.9 = (f32[128,128]{1,0:T(8,128)S(1)}, f32[128,128]{1,0:T(8,128)S(1)}, u32[]{:S(2)}, u32[]{:S(2)}) collective-permute-start(f32[128,128]{1,0:T(8,128)S(1)} %get-tuple-element.87), channel_id=1, source_target_pairs={{0,4},{1,5},{2,6},{3,7},{4,0},{5,1},{6,2},{7,3},{8,12},{9,13},{10,... | collective-permute-start | bytes 196616 | tf_op jit(solution)/shard_map/ppermute | solution.py:595
  23.7 9.8 %collective-permute-start.10 = (f32[128,128]{1,0:T(8,128)S(1)}, f32[128,128]{1,0:T(8,128)S(1)}, u32[]{:S(2)}, u32[]{:S(2)}) collective-permute-start(f32[128,128]{1,0:T(8,128)S(1)} %get-tuple-element.88), channel_id=1, source_target_pairs={{0,6},{1,7},{2,4},{3,5},{4,2},{5,3},{6,0},{7,1},{8,14},{9,15},{10,... | collective-permute-start | bytes 196616 | tf_op jit(solution)/shard_map/ppermute | solution.py:595
  28.8 5.6 %collective-permute-start.7 = (f32[128,128]{1,0:T(8,128)S(1)}, f32[128,128]{1,0:T(8,128)S(1)}, u32[]{:S(2)}, u32[]{:S(2)}) collective-permute-start(f32[128,128]{1,0:T(8,128)S(1)} %get-tuple-element.84), channel_id=1, source_target_pairs={{0,8},{1,9},{2,10},{3,11},{4,12},{5,13},{6,14},{7,15},{8,0},{9,1},... | collective-permute-start | bytes 196616 | tf_op jit(solution)/shard_map/ppermute | solution.py:595
  30.0 6.5 %collective-permute-start.11 = (f32[128,128]{1,0:T(8,128)S(1)}, f32[128,128]{1,0:T(8,128)S(1)}, u32[]{:S(2)}, u32[]{:S(2)}) collective-permute-start(f32[128,128]{1,0:T(8,128)S(1)} %get-tuple-element.91), channel_id=1, source_target_pairs={{0,2},{1,3},{2,0},{3,1},{4,6},{5,7},{6,4},{7,5},{8,10},{9,11},{10,... | collective-permute-start | bytes 196616 | tf_op jit(solution)/shard_map/ppermute | solution.py:595
  30.6 7.6 %collective-permute-start.13 = (f32[128,128]{1,0:T(8,128)S(1)}, f32[128,128]{1,0:T(8,128)S(1)}, u32[]{:S(2)}, u32[]{:S(2)}) collective-permute-start(f32[128,128]{1,0:T(8,128)S(1)} %get-tuple-element.93), channel_id=1, source_target_pairs={{0,4},{1,5},{2,6},{3,7},{4,0},{5,1},{6,2},{7,3},{8,12},{9,13},{10,... | collective-permute-start | bytes 196616 | tf_op jit(solution)/shard_map/ppermute | solution.py:595
  32.3 6.0 %collective-permute-start.15 = (f32[128,128]{1,0:T(8,128)S(1)}, f32[128,128]{1,0:T(8,128)S(1)}, u32[]{:S(2)}, u32[]{:S(2)}) collective-permute-start(f32[128,128]{1,0:T(8,128)S(1)} %get-tuple-element.95), channel_id=1, source_target_pairs={{0,6},{1,7},{2,4},{3,5},{4,2},{5,3},{6,0},{7,1},{8,14},{9,15},{10,... | collective-permute-start | bytes 196616 | tf_op jit(solution)/shard_map/ppermute | solution.py:595
  34.7 4.6 %collective-permute-start.12 = (f32[128,128]{1,0:T(8,128)S(1)}, f32[128,128]{1,0:T(8,128)S(1)}, u32[]{:S(2)}, u32[]{:S(2)}) collective-permute-start(f32[128,128]{1,0:T(8,128)S(1)} %get-tuple-element.92), channel_id=1, source_target_pairs={{0,2},{1,3},{2,0},{3,1},{4,6},{5,7},{6,4},{7,5},{8,10},{9,11},{10,... | collective-permute-start | bytes 196616 | tf_op jit(solution)/shard_map/ppermute | solution.py:595
  35.2 4.3 %collective-permute-start.14 = (f32[128,128]{1,0:T(8,128)S(1)}, f32[128,128]{1,0:T(8,128)S(1)}, u32[]{:S(2)}, u32[]{:S(2)}) collective-permute-start(f32[128,128]{1,0:T(8,128)S(1)} %get-tuple-element.94), channel_id=1, source_target_pairs={{0,4},{1,5},{2,6},{3,7},{4,0},{5,1},{6,2},{7,3},{8,12},{9,13},{10,... | collective-permute-start | bytes 196616 | tf_op jit(solution)/shard_map/ppermute | solution.py:595
  36.5 5.2 %collective-permute-start.16 = (f32[128,128]{1,0:T(8,128)S(1)}, f32[128,128]{1,0:T(8,128)S(1)}, u32[]{:S(2)}, u32[]{:S(2)}) collective-permute-start(f32[128,128]{1,0:T(8,128)S(1)} %get-tuple-element.96), channel_id=1, source_target_pairs={{0,6},{1,7},{2,4},{3,5},{4,2},{5,3},{6,0},{7,1},{8,14},{9,15},{10,... | collective-permute-start | bytes 196616 | tf_op jit(solution)/shard_map/ppermute | solution.py:595
  42.1 2.7 %collective-permute-start.17 = (f32[4,256,128]{2,1,0:T(8,128)S(1)}, f32[4,256,128]{2,1,0:T(8,128)S(1)}, u32[]{:S(2)}, u32[]{:S(2)}) collective-permute-start(f32[4,256,128]{2,1,0:T(8,128)S(1)} %get-tuple-element.97), channel_id=1, source_target_pairs={{0,1},{1,0},{2,3},{3,2},{4,5},{5,4},{6,7},{7,6},{8,9},{9,8},{10,11... | collective-permute-start | bytes 1572872 | tf_op jit(solution)/shard_map/ppermute | solution.py:595
  47.3 6.6 %collective-permute-start.20 = (f32[8,1152]{1,0:T(8,128)S(1)}, f32[8,1152]{1,0:T(8,128)S(1)}, u32[]{:S(2)}, u32[]{:S(2)}) collective-permute-start(f32[8,1152]{1,0:T(8,128)S(1)} %get-tuple-element.107), channel_id=1, source_target_pairs={{0,15},{1,0},{2,1},{3,2},{4,3},{5,4},{6,5},{7,6},{8,7},{9,8},{10,9... | collective-permute-start | bytes 110600 | tf_op jit(solution)/shard_map/ppermute | solution.py:592
  50.4 3.6 %collective-permute-start.18 = (f32[8,128]{1,0:T(8,128)S(1)}, f32[8,128]{1,0:T(8,128)S(1)}, u32[]{:S(2)}, u32[]{:S(2)}) collective-permute-start(f32[8,128]{1,0:T(8,128)S(1)} %get-tuple-element.105), channel_id=1, source_target_pairs={{0,16},{1,17},{2,18},{3,19},{4,20},{5,21},{6,22},{7,23},{8,24},{9,... | collective-permute-start | bytes 12296 | tf_op jit(solution)/shard_map/ppermute | solution.py:592
  50.6 3.4 %collective-permute-start.19 = (f32[8,128]{1,0:T(8,128)S(1)}, f32[8,128]{1,0:T(8,128)S(1)}, u32[]{:S(2)}, u32[]{:S(2)}) collective-permute-start(f32[8,128]{1,0:T(8,128)S(1)} %get-tuple-element.106), channel_id=1, source_target_pairs={{0,31},{1,16},{2,17},{3,18},{4,19},{5,20},{6,21},{7,22},{8,23},{9,... | collective-permute-start | bytes 12296 | tf_op jit(solution)/shard_map/ppermute | solution.py:592

commit v9 on v8

--- a/solution.py
+++ b/solution.py
@@ -59,11 +59,7 @@
 
 
 def row_sums(a):
-    high = a.astype(bf16)
-    rest = a - high.astype(f32)
-    mid = rest.astype(bf16)
-    low = (rest - mid.astype(f32)).astype(bf16)
-    terms = jnp.concatenate([high, mid, low], axis=1)
+    terms = jnp.concatenate(split(a), axis=1)
     ones = jnp.ones((RIM, terms.shape[1]), bf16)
     return lax.dot_general(ones, terms, DIMS["nt"], preferred_element_type=f32)
 

time: 55.1 us -> 55.2 us (level)
  no operation moved by 1% of the time
where the time goes in v9:
time: 55.2 us; the launch traced here: 55 us
  starting transfers between devices  24 us (43%)
  Pallas kernels  17.4 us (32%)
  waiting for transfers between devices  12.8 us (23%)
  between operations  0.8 us (1%)
    pallas_call x15, Pallas kernels, call(): pl.pallas_call((lambda *refs: kernel(placed(*scalar), *refs)) if scalar e...  17.4 us
    ppermute x15, starting transfers between devices, swapped(): return lax.ppermute(value, 'ctx', [(i, i ^ distance) for i in range(spots)])  15.2 us
    ppermute x6, starting transfers between devices, turned(): return lax.ppermute(value, ('section', 'ctx'), route)  8.79 us
    ppermute x6, waiting for transfers between devices, turned(): return lax.ppermute(value, ('section', 'ctx'), route)  7.13 us
    ppermute x15, waiting for transfers between devices, swapped(): return lax.ppermute(value, 'ctx', [(i, i ^ distance) for i in range(spots)])  5.67 us
  transfers between devices with their start and end apart: 21, of which 8 were waited for; matrix products, arithmetic and copies ran while one was open for 0% of the time, Pallas kernels for 16%

profile of v9, /device:TPU:0, one launch (start us, length us, event | category | flops | bytes accessed | tf_op | source)
XLA Modules:
  0.0 55.0 jit_solution(8246105858499953432)
XLA Ops:
  0.6 1.3 %prelude.1 = (f32[8,1152]{1,0:T(8,128)S(1)}, f32[8,128]{1,0:T(8,128)S(1)}, f32[8,128]{1,0:T(8,128)S(1)}, bf16[128,1024]{1,0:T(8,128)(2,1)S(1)}, bf16[128,1024]{1...) custom-call(bf16[128,1024]{1,0:T(8,128)(2,1)} %x_hbm.1, ...), custom_call_target="tpu_custom_call" | custom-call | tf_op jit(solution)/shard_map/prelude/pallas_call | solution.py:544
  1.9 0.5 collective-permute-start.1
  2.4 2.6 %collective-permute-start = (f32[8,128]{1,0:T(8,128)S(1)}, f32[8,128]{1,0:T(8,128)S(1)}, u32[]{:S(2)}, u32[]{:S(2)}) collective-permute-start(f32[8,128]{1,0:T(8,128)S(1)} %get-tuple-element.61), channel_id=1, source_target_pairs={{0,16},{1,17},{2,18},{3,19},{4,20},{5,21},{6,22},{7,23},{8,24},{9,... | collective-permute-start | bytes 12296 | tf_op jit(solution)/shard_map/ppermute | solution.py:588
  5.0 1.4 %collective-permute-start.2 = (f32[8,128]{1,0:T(8,128)S(1)}, f32[8,128]{1,0:T(8,128)S(1)}, u32[]{:S(2)}, u32[]{:S(2)}) collective-permute-start(f32[8,128]{1,0:T(8,128)S(1)} %get-tuple-element.68), channel_id=1, source_target_pairs={{0,17},{1,18},{2,19},{3,20},{4,21},{5,22},{6,23},{7,24},{8,25},{9,... | collective-permute-start | bytes 12296 | tf_op jit(solution)/shard_map/ppermute | solution.py:588
  6.4 0.2 collective-permute-done
  6.6 0.4 gates.1
  7.0 4.6 %collective-permute-done.2 = f32[8,128]{1,0:T(8,128)S(1)} collective-permute-done((f32[8,128]{1,0:T(8,128)S(1)}, f32[8,128]{1,0:T(8,128)S(1)}, u32[]{:S(2)}, u32[]{:S(2)}) %collective-permute-start.2) | collective-permute-done | bytes 4128 | tf_op jit(solution)/shard_map/ppermute | solution.py:588
  11.6 0.0 collective-permute-done.1.refs_7_.refs_4_
  11.6 2.7 %local_outer.1 = (f32[4,384,128]{2,1,0:T(8,128)S(1)}, f32[4,3,128,128]{3,2,1,0:T(8,128)S(1)}, bf16[4,16,128,128]{3,2,1,0:T(8,128)(2,1)S(1)}) custom-call(bf16[128,1024]{1,0:T(8,128)(2,1)S(1)} %get-tuple-element.56.refs_0_, bf16[128,1024]{1,0:T(8,128)(2,1)S(1)} %get-tuple-element.57.refs_1_, f32[3,4,1024]{2,1,0:T(4,128)S(1)} %get-tuple-element.58.refs_2_.refs_1_, ...), custom_call_target="tpu_custom_call" | custom-call | tf_op jit(solution)/shard_map/local_outer/pallas_call | solution.py:544
  14.3 0.1 collective-permute-start.3
  14.4 2.7 %local_inner.1 = (f32[4,384,128]{2,1,0:T(8,128)S(1)}, f32[4,3,128,128]{3,2,1,0:T(8,128)S(1)}, bf16[4,16,128,128]{3,2,1,0:T(8,128)(2,1)S(1)}) custom-call(bf16[128,1024]{1,0:T(8,128)(2,1)S(1)} %get-tuple-element.56.refs_0_, bf16[128,1024]{1,0:T(8,128)(2,1)S(1)} %get-tuple-element.57.refs_1_, f32[3,4,1024]{2,1,0:T(4,128)S(1)} %get-tuple-element.58.refs_2_.refs_1_, ...), custom_call_target="tpu_custom_call" | custom-call | tf_op jit(solution)/shard_map/local_inner/pallas_call | solution.py:544
  17.1 0.0 collective-permute-done.3.refs_1_
  17.1 0.4 join.1
  17.6 0.1 collective-permute-start.4
  17.6 0.7 %collective-permute-start.5 = (f32[256,128]{1,0:T(8,128)S(1)}, f32[256,128]{1,0:T(8,128)S(1)}, u32[]{:S(2)}, u32[]{:S(2)}) collective-permute-start(f32[256,128]{1,0:T(8,128)S(1)} %get-tuple-element.73), channel_id=1, source_target_pairs={{0,4},{1,5},{2,6},{3,7},{4,0},{5,1},{6,2},{7,3},{8,12},{9,13},{10,... | collective-permute-start | bytes 393224 | tf_op jit(solution)/shard_map/ppermute | solution.py:591
  18.4 2.8 %collective-permute-start.6 = (f32[256,128]{1,0:T(8,128)S(1)}, f32[256,128]{1,0:T(8,128)S(1)}, u32[]{:S(2)}, u32[]{:S(2)}) collective-permute-start(f32[256,128]{1,0:T(8,128)S(1)} %get-tuple-element.74), channel_id=1, source_target_pairs={{0,6},{1,7},{2,4},{3,5},{4,2},{5,3},{6,0},{7,1},{8,14},{9,15},{10,... | collective-permute-start | bytes 393224 | tf_op jit(solution)/shard_map/ppermute | solution.py:591
  21.1 0.9 %ready_outer.1 = (f32[4,5,128,128]{3,2,1,0:T(8,128)S(1)}, bf16[4,4,128,128]{3,2,1,0:T(8,128)(2,1)S(1)}) custom-call(bf16[128,1024]{1,0:T(8,128)(2,1)S(1)} %get-tuple-element.56.refs_0_, f32[3,4,1024]{2,1,0:T(4,128)S(1)} %get-tuple-element.58.refs_2_.refs_1_, f32[128,1024]{1,0:T(8,128)S(1)} %get-tuple-element.63.refs_4_.refs_2_, ...), custom_call_target="tpu_custom_call" | custom-call | tf_op jit(solution)/shard_map/ready_outer/pallas_call | solution.py:544
  22.0 0.9 %ready_inner.1 = (f32[4,5,128,128]{3,2,1,0:T(8,128)S(1)}, bf16[4,4,128,128]{3,2,1,0:T(8,128)(2,1)S(1)}) custom-call(bf16[128,1024]{1,0:T(8,128)(2,1)S(1)} %get-tuple-element.56.refs_0_, f32[3,4,1024]{2,1,0:T(4,128)S(1)} %get-tuple-element.58.refs_2_.refs_1_, f32[128,1024]{1,0:T(8,128)S(1)} %get-tuple-element.63.refs_4_.refs_2_, ...), custom_call_target="tpu_custom_call" | custom-call | tf_op jit(solution)/shard_map/ready_inner/pallas_call | solution.py:544
  22.9 0.1 collective-permute-start.8
  23.1 0.7 %collective-permute-start.9 = (f32[128,128]{1,0:T(8,128)S(1)}, f32[128,128]{1,0:T(8,128)S(1)}, u32[]{:S(2)}, u32[]{:S(2)}) collective-permute-start(f32[128,128]{1,0:T(8,128)S(1)} %get-tuple-element.87), channel_id=1, source_target_pairs={{0,4},{1,5},{2,6},{3,7},{4,0},{5,1},{6,2},{7,3},{8,12},{9,13},{10,... | collective-permute-start | bytes 196616 | tf_op jit(solution)/shard_map/ppermute | solution.py:591
  23.7 0.0 collective-permute-done.4.refs_1_
  23.7 2.7 %collective-permute-start.10 = (f32[128,128]{1,0:T(8,128)S(1)}, f32[128,128]{1,0:T(8,128)S(1)}, u32[]{:S(2)}, u32[]{:S(2)}) collective-permute-start(f32[128,128]{1,0:T(8,128)S(1)} %get-tuple-element.88), channel_id=1, source_target_pairs={{0,6},{1,7},{2,4},{3,5},{4,2},{5,3},{6,0},{7,1},{8,14},{9,15},{10,... | collective-permute-start | bytes 196616 | tf_op jit(solution)/shard_map/ppermute | solution.py:591
  26.5 0.0 collective-permute-done.5.refs_2_
  26.5 1.8 %collective-permute-done.6.refs_3_ = f32[256,128]{1,0:T(8,128)S(1)} collective-permute-done((f32[256,128]{1,0:T(8,128)S(1)}, f32[256,128]{1,0:T(8,128)S(1)}, u32[]{:S(2)}, u32[]{:S(2)}) %collective-permute-start.6) | collective-permute-done | bytes 131104 | tf_op jit(solution)/shard_map/ppermute | solution.py:591
  28.3 0.5 gather.1
  28.8 0.9 %collective-permute-start.7 = (f32[128,128]{1,0:T(8,128)S(1)}, f32[128,128]{1,0:T(8,128)S(1)}, u32[]{:S(2)}, u32[]{:S(2)}) collective-permute-start(f32[128,128]{1,0:T(8,128)S(1)} %get-tuple-element.84), channel_id=1, source_target_pairs={{0,8},{1,9},{2,10},{3,11},{4,12},{5,13},{6,14},{7,15},{8,0},{9,1},... | collective-permute-start | bytes 196616 | tf_op jit(solution)/shard_map/ppermute | solution.py:591
  29.7 0.3 reach.1
  30.0 0.6 %collective-permute-start.11 = (f32[128,128]{1,0:T(8,128)S(1)}, f32[128,128]{1,0:T(8,128)S(1)}, u32[]{:S(2)}, u32[]{:S(2)}) collective-permute-start(f32[128,128]{1,0:T(8,128)S(1)} %get-tuple-element.91), channel_id=1, source_target_pairs={{0,2},{1,3},{2,0},{3,1},{4,6},{5,7},{6,4},{7,5},{8,10},{9,11},{10,... | collective-permute-start | bytes 196616 | tf_op jit(solution)/shard_map/ppermute | solution.py:591
  30.6 0.0 collective-permute-done.8.refs_5_
  30.6 1.7 %collective-permute-start.13 = (f32[128,128]{1,0:T(8,128)S(1)}, f32[128,128]{1,0:T(8,128)S(1)}, u32[]{:S(2)}, u32[]{:S(2)}) collective-permute-start(f32[128,128]{1,0:T(8,128)S(1)} %get-tuple-element.93), channel_id=1, source_target_pairs={{0,4},{1,5},{2,6},{3,7},{4,0},{5,1},{6,2},{7,3},{8,12},{9,13},{10,... | collective-permute-start | bytes 196616 | tf_op jit(solution)/shard_map/ppermute | solution.py:591
  32.3 0.0 collective-permute-done.9.refs_6_
  32.3 1.3 %collective-permute-start.15 = (f32[128,128]{1,0:T(8,128)S(1)}, f32[128,128]{1,0:T(8,128)S(1)}, u32[]{:S(2)}, u32[]{:S(2)}) collective-permute-start(f32[128,128]{1,0:T(8,128)S(1)} %get-tuple-element.95), channel_id=1, source_target_pairs={{0,6},{1,7},{2,4},{3,5},{4,2},{5,3},{6,0},{7,1},{8,14},{9,15},{10,... | collective-permute-start | bytes 196616 | tf_op jit(solution)/shard_map/ppermute | solution.py:591
  33.6 0.0 collective-permute-done.10.refs_7_
  33.6 0.4 known.1.refs_1_
  34.0 0.4 collective-permute-done.7.refs_0_
  34.4 0.2 late.1
  34.7 0.5 collective-permute-start.12
  35.2 1.4 %collective-permute-start.14 = (f32[128,128]{1,0:T(8,128)S(1)}, f32[128,128]{1,0:T(8,128)S(1)}, u32[]{:S(2)}, u32[]{:S(2)}) collective-permute-start(f32[128,128]{1,0:T(8,128)S(1)} %get-tuple-element.94), channel_id=1, source_target_pairs={{0,4},{1,5},{2,6},{3,7},{4,0},{5,1},{6,2},{7,3},{8,12},{9,13},{10,... | collective-permute-start | bytes 196616 | tf_op jit(solution)/shard_map/ppermute | solution.py:591
  36.5 0.0 collective-permute-done.11.refs_4_
  36.5 1.7 %collective-permute-start.16 = (f32[128,128]{1,0:T(8,128)S(1)}, f32[128,128]{1,0:T(8,128)S(1)}, u32[]{:S(2)}, u32[]{:S(2)}) collective-permute-start(f32[128,128]{1,0:T(8,128)S(1)} %get-tuple-element.96), channel_id=1, source_target_pairs={{0,6},{1,7},{2,4},{3,5},{4,2},{5,3},{6,0},{7,1},{8,14},{9,15},{10,... | collective-permute-start | bytes 196616 | tf_op jit(solution)/shard_map/ppermute | solution.py:591
  38.2 0.0 collective-permute-done.13.refs_6_
  38.2 0.0 collective-permute-done.15.refs_8_
  38.2 1.0 %collective-permute-done.12.refs_5_ = f32[128,128]{1,0:T(8,128)S(1)} collective-permute-done((f32[128,128]{1,0:T(8,128)S(1)}, f32[128,128]{1,0:T(8,128)S(1)}, u32[]{:S(2)}, u32[]{:S(2)}) %collective-permute-start.12) | collective-permute-done | bytes 65568 | tf_op jit(solution)/shard_map/ppermute | solution.py:591
  39.2 0.2 collective-permute-done.14.refs_7_
  39.4 2.3 %collective-permute-done.16.refs_9_ = f32[128,128]{1,0:T(8,128)S(1)} collective-permute-done((f32[128,128]{1,0:T(8,128)S(1)}, f32[128,128]{1,0:T(8,128)S(1)}, u32[]{:S(2)}, u32[]{:S(2)}) %collective-permute-start.16) | collective-permute-done | bytes 65568 | tf_op jit(solution)/shard_map/ppermute | solution.py:591
  41.7 0.3 part.1
  42.1 0.1 collective-permute-start.17
  42.1 2.6 %back_inner.1 = (bf16[128,1024]{1,0:T(8,128)(2,1)}, f32[4,128,128]{2,1,0:T(8,128)S(1)}, f32[8,128]{1,0:T(8,128)S(1)}, f32[8,1152]{1,0:T(8,128)S(1)}) custom-call(bf16[128,1024]{1,0:T(8,128)(2,1)S(1)} %get-tuple-element.56.refs_0_, bf16[128,1024]{1,0:T(8,128)(2,1)S(1)} %get-tuple-element.57.refs_1_, f32[3,4,1024]{2,1,0:T(4,128)S(1)} %get-tuple-element.58.refs_2_.refs_1_, ...), custom_call_target="tpu_custom_call" | custom-call | tf_op jit(solution)/shard_map/back_inner/pallas_call | solution.py:544
  44.7 0.0 collective-permute-done.17.refs_8_
  44.7 2.6 %back_outer.1 = (bf16[128,1024]{1,0:T(8,128)(2,1)}, f32[4,128,128]{2,1,0:T(8,128)S(1)}, f32[8,128]{1,0:T(8,128)S(1)}, f32[8,1152]{1,0:T(8,128)S(1)}, f32[8,128]{1,0:T(8,128)S(1)}) custom-call(bf16[128,1024]{1,0:T(8,128)(2,1)S(1)} %get-tuple-element.56.refs_0_, bf16[128,1024]{1,0:T(8,128)(2,1)S(1)} %get-tuple-element.57.refs_1_, ...), custom_call_target="tpu_custom_call", output_to_operand_aliasing={{0}: (15, {})} | custom-call | tf_op jit(solution)/shard_map/back_outer/pallas_call | solution.py:544
  47.3 3.0 %collective-permute-start.20 = (f32[8,1152]{1,0:T(8,128)S(1)}, f32[8,1152]{1,0:T(8,128)S(1)}, u32[]{:S(2)}, u32[]{:S(2)}) collective-permute-start(f32[8,1152]{1,0:T(8,128)S(1)} %get-tuple-element.107), channel_id=1, source_target_pairs={{0,15},{1,0},{2,1},{3,2},{4,3},{5,4},{6,5},{7,6},{8,7},{9,8},{10,9... | collective-permute-start | bytes 110600 | tf_op jit(solution)/shard_map/ppermute | solution.py:588
  50.4 0.2 collective-permute-start.18
  50.6 1.1 %collective-permute-start.19 = (f32[8,128]{1,0:T(8,128)S(1)}, f32[8,128]{1,0:T(8,128)S(1)}, u32[]{:S(2)}, u32[]{:S(2)}) collective-permute-start(f32[8,128]{1,0:T(8,128)S(1)} %get-tuple-element.106), channel_id=1, source_target_pairs={{0,31},{1,16},{2,17},{3,18},{4,19},{5,20},{6,21},{7,22},{8,23},{9,... | collective-permute-start | bytes 12296 | tf_op jit(solution)/shard_map/ppermute | solution.py:588
  51.6 2.3 %collective-permute-done.18 = f32[8,128]{1,0:T(8,128)S(1)} collective-permute-done((f32[8,128]{1,0:T(8,128)S(1)}, f32[8,128]{1,0:T(8,128)S(1)}, u32[]{:S(2)}, u32[]{:S(2)}) %collective-permute-start.18) | collective-permute-done | bytes 4128 | tf_op jit(solution)/shard_map/ppermute | solution.py:588
  54.0 0.0 collective-permute-done.19
  54.0 0.0 collective-permute-done.20.refs_5_
  54.0 1.0 %finish.1 = bf16[128,1024]{1,0:T(8,128)(2,1)} custom-call(bf16[128,1024]{1,0:T(8,128)(2,1)S(1)} %get-tuple-element.56.refs_0_, bf16[128,1024]{1,0:T(8,128)(2,1)S(1)} %get-tuple-element.57.refs_1_, f32[128,128]{1,0:T(8,128)S(1)} %get-tuple-element.67.refs_8_.refs_5_.refs_2_, f32[8,128]{1,0:T(8,128)S(1)} %add.22.refs_3_, f32[8,128]{1,0:T(8,128)S(1)} %slice_add_fusion.refs_4_, ...), custom_call_target="tpu_custom_call" | custom-call | tf_op jit(solution)/shard_map/finish/pallas_call | solution.py:544
  (4 shorter events, 0.0 us)
Async XLA Ops:
  1.9 9.7 %collective-permute-start.1 = (f32[8,1152]{1,0:T(8,128)S(1)}, f32[8,1152]{1,0:T(8,128)S(1)}, u32[]{:S(2)}, u32[]{:S(2)}) collective-permute-start(f32[8,1152]{1,0:T(8,128)S(1)} %get-tuple-element.66), channel_id=1, source_target_pairs={{0,1},{1,2},{2,3},{3,4},{4,5},{5,6},{6,7},{7,8},{8,9},{9,10},{10,1... | collective-permute-start | bytes 110600 | tf_op jit(solution)/shard_map/ppermute | solution.py:588
  2.4 4.2 %collective-permute-start = (f32[8,128]{1,0:T(8,128)S(1)}, f32[8,128]{1,0:T(8,128)S(1)}, u32[]{:S(2)}, u32[]{:S(2)}) collective-permute-start(f32[8,128]{1,0:T(8,128)S(1)} %get-tuple-element.61), channel_id=1, source_target_pairs={{0,16},{1,17},{2,18},{3,19},{4,20},{5,21},{6,22},{7,23},{8,24},{9,... | collective-permute-start | bytes 12296 | tf_op jit(solution)/shard_map/ppermute | solution.py:588
  5.0 6.6 %collective-permute-start.2 = (f32[8,128]{1,0:T(8,128)S(1)}, f32[8,128]{1,0:T(8,128)S(1)}, u32[]{:S(2)}, u32[]{:S(2)}) collective-permute-start(f32[8,128]{1,0:T(8,128)S(1)} %get-tuple-element.68), channel_id=1, source_target_pairs={{0,17},{1,18},{2,19},{3,20},{4,21},{5,22},{6,23},{7,24},{8,25},{9,... | collective-permute-start | bytes 12296 | tf_op jit(solution)/shard_map/ppermute | solution.py:588
  14.3 2.8 %collective-permute-start.3 = (f32[4,384,128]{2,1,0:T(8,128)S(1)}, f32[4,384,128]{2,1,0:T(8,128)S(1)}, u32[]{:S(2)}, u32[]{:S(2)}) collective-permute-start(f32[4,384,128]{2,1,0:T(8,128)S(1)} %get-tuple-element.70), channel_id=1, source_target_pairs={{0,1},{1,0},{2,3},{3,2},{4,5},{5,4},{6,7},{7,6},{8,9},{9,8},{10,11... | collective-permute-start | bytes 2359304 | tf_op jit(solution)/shard_map/ppermute | solution.py:591
  17.6 6.2 %collective-permute-start.4 = (f32[256,128]{1,0:T(8,128)S(1)}, f32[256,128]{1,0:T(8,128)S(1)}, u32[]{:S(2)}, u32[]{:S(2)}) collective-permute-start(f32[256,128]{1,0:T(8,128)S(1)} %get-tuple-element.72), channel_id=1, source_target_pairs={{0,2},{1,3},{2,0},{3,1},{4,6},{5,7},{6,4},{7,5},{8,10},{9,11},{10,... | collective-permute-start | bytes 393224 | tf_op jit(solution)/shard_map/ppermute | solution.py:591
  17.6 8.8 %collective-permute-start.5 = (f32[256,128]{1,0:T(8,128)S(1)}, f32[256,128]{1,0:T(8,128)S(1)}, u32[]{:S(2)}, u32[]{:S(2)}) collective-permute-start(f32[256,128]{1,0:T(8,128)S(1)} %get-tuple-element.73), channel_id=1, source_target_pairs={{0,4},{1,5},{2,6},{3,7},{4,0},{5,1},{6,2},{7,3},{8,12},{9,13},{10,... | collective-permute-start | bytes 393224 | tf_op jit(solution)/shard_map/ppermute | solution.py:591
  18.4 9.9 %collective-permute-start.6 = (f32[256,128]{1,0:T(8,128)S(1)}, f32[256,128]{1,0:T(8,128)S(1)}, u32[]{:S(2)}, u32[]{:S(2)}) collective-permute-start(f32[256,128]{1,0:T(8,128)S(1)} %get-tuple-element.74), channel_id=1, source_target_pairs={{0,6},{1,7},{2,4},{3,5},{4,2},{5,3},{6,0},{7,1},{8,14},{9,15},{10,... | collective-permute-start | bytes 393224 | tf_op jit(solution)/shard_map/ppermute | solution.py:591
  22.9 7.7 %collective-permute-start.8 = (f32[128,128]{1,0:T(8,128)S(1)}, f32[128,128]{1,0:T(8,128)S(1)}, u32[]{:S(2)}, u32[]{:S(2)}) collective-permute-start(f32[128,128]{1,0:T(8,128)S(1)} %get-tuple-element.86), channel_id=1, source_target_pairs={{0,2},{1,3},{2,0},{3,1},{4,6},{5,7},{6,4},{7,5},{8,10},{9,11},{10,... | collective-permute-start | bytes 196616 | tf_op jit(solution)/shard_map/ppermute | solution.py:591
  23.1 9.2 %collective-permute-start.9 = (f32[128,128]{1,0:T(8,128)S(1)}, f32[128,128]{1,0:T(8,128)S(1)}, u32[]{:S(2)}, u32[]{:S(2)}) collective-permute-start(f32[128,128]{1,0:T(8,128)S(1)} %get-tuple-element.87), channel_id=1, source_target_pairs={{0,4},{1,5},{2,6},{3,7},{4,0},{5,1},{6,2},{7,3},{8,12},{9,13},{10,... | collective-permute-start | bytes 196616 | tf_op jit(solution)/shard_map/ppermute | solution.py:591
  23.7 9.8 %collective-permute-start.10 = (f32[128,128]{1,0:T(8,128)S(1)}, f32[128,128]{1,0:T(8,128)S(1)}, u32[]{:S(2)}, u32[]{:S(2)}) collective-permute-start(f32[128,128]{1,0:T(8,128)S(1)} %get-tuple-element.88), channel_id=1, source_target_pairs={{0,6},{1,7},{2,4},{3,5},{4,2},{5,3},{6,0},{7,1},{8,14},{9,15},{10,... | collective-permute-start | bytes 196616 | tf_op jit(solution)/shard_map/ppermute | solution.py:591
  28.8 5.6 %collective-permute-start.7 = (f32[128,128]{1,0:T(8,128)S(1)}, f32[128,128]{1,0:T(8,128)S(1)}, u32[]{:S(2)}, u32[]{:S(2)}) collective-permute-start(f32[128,128]{1,0:T(8,128)S(1)} %get-tuple-element.84), channel_id=1, source_target_pairs={{0,8},{1,9},{2,10},{3,11},{4,12},{5,13},{6,14},{7,15},{8,0},{9,1},... | collective-permute-start | bytes 196616 | tf_op jit(solution)/shard_map/ppermute | solution.py:591
  30.0 6.5 %collective-permute-start.11 = (f32[128,128]{1,0:T(8,128)S(1)}, f32[128,128]{1,0:T(8,128)S(1)}, u32[]{:S(2)}, u32[]{:S(2)}) collective-permute-start(f32[128,128]{1,0:T(8,128)S(1)} %get-tuple-element.91), channel_id=1, source_target_pairs={{0,2},{1,3},{2,0},{3,1},{4,6},{5,7},{6,4},{7,5},{8,10},{9,11},{10,... | collective-permute-start | bytes 196616 | tf_op jit(solution)/shard_map/ppermute | solution.py:591
  30.6 7.6 %collective-permute-start.13 = (f32[128,128]{1,0:T(8,128)S(1)}, f32[128,128]{1,0:T(8,128)S(1)}, u32[]{:S(2)}, u32[]{:S(2)}) collective-permute-start(f32[128,128]{1,0:T(8,128)S(1)} %get-tuple-element.93), channel_id=1, source_target_pairs={{0,4},{1,5},{2,6},{3,7},{4,0},{5,1},{6,2},{7,3},{8,12},{9,13},{10,... | collective-permute-start | bytes 196616 | tf_op jit(solution)/shard_map/ppermute | solution.py:591
  32.3 6.0 %collective-permute-start.15 = (f32[128,128]{1,0:T(8,128)S(1)}, f32[128,128]{1,0:T(8,128)S(1)}, u32[]{:S(2)}, u32[]{:S(2)}) collective-permute-start(f32[128,128]{1,0:T(8,128)S(1)} %get-tuple-element.95), channel_id=1, source_target_pairs={{0,6},{1,7},{2,4},{3,5},{4,2},{5,3},{6,0},{7,1},{8,14},{9,15},{10,... | collective-permute-start | bytes 196616 | tf_op jit(solution)/shard_map/ppermute | solution.py:591
  34.7 4.6 %collective-permute-start.12 = (f32[128,128]{1,0:T(8,128)S(1)}, f32[128,128]{1,0:T(8,128)S(1)}, u32[]{:S(2)}, u32[]{:S(2)}) collective-permute-start(f32[128,128]{1,0:T(8,128)S(1)} %get-tuple-element.92), channel_id=1, source_target_pairs={{0,2},{1,3},{2,0},{3,1},{4,6},{5,7},{6,4},{7,5},{8,10},{9,11},{10,... | collective-permute-start | bytes 196616 | tf_op jit(solution)/shard_map/ppermute | solution.py:591
  35.2 4.3 %collective-permute-start.14 = (f32[128,128]{1,0:T(8,128)S(1)}, f32[128,128]{1,0:T(8,128)S(1)}, u32[]{:S(2)}, u32[]{:S(2)}) collective-permute-start(f32[128,128]{1,0:T(8,128)S(1)} %get-tuple-element.94), channel_id=1, source_target_pairs={{0,4},{1,5},{2,6},{3,7},{4,0},{5,1},{6,2},{7,3},{8,12},{9,13},{10,... | collective-permute-start | bytes 196616 | tf_op jit(solution)/shard_map/ppermute | solution.py:591
  36.5 5.2 %collective-permute-start.16 = (f32[128,128]{1,0:T(8,128)S(1)}, f32[128,128]{1,0:T(8,128)S(1)}, u32[]{:S(2)}, u32[]{:S(2)}) collective-permute-start(f32[128,128]{1,0:T(8,128)S(1)} %get-tuple-element.96), channel_id=1, source_target_pairs={{0,6},{1,7},{2,4},{3,5},{4,2},{5,3},{6,0},{7,1},{8,14},{9,15},{10,... | collective-permute-start | bytes 196616 | tf_op jit(solution)/shard_map/ppermute | solution.py:591
  42.1 2.7 %collective-permute-start.17 = (f32[4,256,128]{2,1,0:T(8,128)S(1)}, f32[4,256,128]{2,1,0:T(8,128)S(1)}, u32[]{:S(2)}, u32[]{:S(2)}) collective-permute-start(f32[4,256,128]{2,1,0:T(8,128)S(1)} %get-tuple-element.97), channel_id=1, source_target_pairs={{0,1},{1,0},{2,3},{3,2},{4,5},{5,4},{6,7},{7,6},{8,9},{9,8},{10,11... | collective-permute-start | bytes 1572872 | tf_op jit(solution)/shard_map/ppermute | solution.py:591
  47.3 6.7 %collective-permute-start.20 = (f32[8,1152]{1,0:T(8,128)S(1)}, f32[8,1152]{1,0:T(8,128)S(1)}, u32[]{:S(2)}, u32[]{:S(2)}) collective-permute-start(f32[8,1152]{1,0:T(8,128)S(1)} %get-tuple-element.107), channel_id=1, source_target_pairs={{0,15},{1,0},{2,1},{3,2},{4,3},{5,4},{6,5},{7,6},{8,7},{9,8},{10,9... | collective-permute-start | bytes 110600 | tf_op jit(solution)/shard_map/ppermute | solution.py:588
  50.4 3.6 %collective-permute-start.18 = (f32[8,128]{1,0:T(8,128)S(1)}, f32[8,128]{1,0:T(8,128)S(1)}, u32[]{:S(2)}, u32[]{:S(2)}) collective-permute-start(f32[8,128]{1,0:T(8,128)S(1)} %get-tuple-element.105), channel_id=1, source_target_pairs={{0,16},{1,17},{2,18},{3,19},{4,20},{5,21},{6,22},{7,23},{8,24},{9,... | collective-permute-start | bytes 12296 | tf_op jit(solution)/shard_map/ppermute | solution.py:588
  50.6 3.4 %collective-permute-start.19 = (f32[8,128]{1,0:T(8,128)S(1)}, f32[8,128]{1,0:T(8,128)S(1)}, u32[]{:S(2)}, u32[]{:S(2)}) collective-permute-start(f32[8,128]{1,0:T(8,128)S(1)} %get-tuple-element.106), channel_id=1, source_target_pairs={{0,31},{1,16},{2,17},{3,18},{4,19},{5,20},{6,21},{7,22},{8,23},{9,... | collective-permute-start | bytes 12296 | tf_op jit(solution)/shard_map/ppermute | solution.py:588
